TPU v7x, 128 devices: a whole 4x4x4 slice. The times are simulated.
128 devices in a mesh: dp: 32 (over y, x, core), ctx: 4 (over z).
Axes of the slice: x: 4, y: 4, z: 4, core: 2. Of those that a mesh axis runs over, the one named last changes fastest.
Arguments:
- conv_input: bfloat16 [32, 1024, 2816], P('dp', 'ctx'), may hold values from -6 to 6
- gate_input: bfloat16 [32, 1024, 2560], P('dp', 'ctx'), may hold values from -6 to 6
- step_input: float32 [32, 40, 1024], P('dp', None, 'ctx'), may hold values from -2.2 to 11.2
- step_bias: float32 [40], replicated, may hold values from -7 to -5
- log_rates: float32 [40], replicated, may hold values from -3 to 3.6
- skip_gain: float32 [40], replicated, may hold values from 0.5 to 1.5
- conv_weight: float32 [4, 2816], replicated, may hold values from -3 to 3
- conv_bias: float32 [2816], replicated, may hold values from -3 to 3
- norm_gain: float32 [2560], replicated, may hold values from 0.5 to 1.5
- doc_ids: int32 [32, 1024], P('dp', 'ctx'), may hold values from 0 to 2, never falling along the last dimension, each value on 1 to 512 neighbouring positions
- cotangent: bfloat16 [32, 1024, 1280], P('dp', 'ctx'), may hold values from -0.03125 to 0.03125
Outputs:
- normed_out: bfloat16 [32, 1024, 2560], P('dp', 'ctx')
- weight_grad: float32 [2560, 1280], P(('dp', 'ctx'))
Inputs may be any that keep to these rules, and one draw needn't show every extreme that they name: `doc_ids`: document numbers never fall along a sequence; each sequence holds 3 documents of 1 to 512 positions, one of exactly 512.
All inputs are finite; a program needn't handle non-finite values.
Results may differ from a plain program's by a relative error of at most 0.013.
Values may be sent and summed in bfloat16 or wider, within the bound.
No kernel may reach another device: no remote copies, remote signals or barrier semaphores. Data moves between devices by JAX's collectives and lax.ppermute only.
A program may use at most 64 MiB of HBM per device.

v0:
```python
import jax
import jax.numpy as jnp
from jax import lax
from jax.sharding import PartitionSpec as P

BLOCK = 256


def shifted(value, axis, by):
    size = lax.axis_size(axis)
    pairs = [(i, i + by) for i in range(size) if 0 <= i + by < size]
    return lax.ppermute(value, axis, pairs)


def filter_rows(conv_rows, prev_rows, doc_values, prev_docs, conv_weight, conv_bias):
    tap_count = conv_weight.shape[0]
    joined = jnp.concatenate([prev_rows, conv_rows], 0)
    joined_docs = jnp.concatenate([prev_docs, doc_values], 0)
    length = conv_rows.shape[0]
    summed = jnp.zeros(conv_rows.shape, jnp.float32) + conv_bias[None, :]
    for offset in range(tap_count):
        window = joined[offset : offset + length].astype(jnp.float32)
        same_doc = (joined_docs[offset : offset + length] == doc_values).astype(jnp.float32)
        summed = summed + conv_weight[offset][None, :] * window * same_doc[:, None]
    return summed


def read_state(map_rows, state):
    heads, head_size, state_size = state.shape
    flat = state.transpose(2, 0, 1).reshape(state_size, heads * head_size)
    upper = flat.astype(jnp.bfloat16)
    lower = (flat - upper.astype(jnp.float32)).astype(jnp.bfloat16)
    total = jnp.dot(map_rows, upper, preferred_element_type=jnp.float32)
    total = total + jnp.dot(map_rows, lower, preferred_element_type=jnp.float32)
    return total.reshape(map_rows.shape[0], heads, head_size)


def run_blocks(head_values, input_map, output_map, log_decay, step_sizes, doc_list, block_len):
    count_blocks = head_values.shape[0] // block_len
    heads = head_values.shape[1]
    head_size = head_values.shape[2]
    state_size = input_map.shape[1]
    items = (
        head_values.reshape(count_blocks, block_len, heads, head_size),
        input_map.reshape(count_blocks, block_len, state_size),
        output_map.reshape(count_blocks, block_len, state_size),
        log_decay.reshape(heads, count_blocks, block_len).transpose(1, 0, 2),
        step_sizes.reshape(heads, count_blocks, block_len).transpose(1, 0, 2),
        doc_list.reshape(count_blocks, block_len),
    )
    positions = jnp.arange(block_len)
    causal = positions[:, None] >= positions[None, :]

    def one_block(carry, block_items):
        state, last_tag = carry
        vals_block, in_block, out_block, decay_block, step_block, doc_block = block_items
        cumul = jnp.cumsum(decay_block, axis=1)
        same_doc = jnp.logical_and(doc_block[:, None] == doc_block[None, :], causal)[None]
        spread = cumul[:, :, None] - cumul[:, None, :]
        decay_mat = jnp.where(same_doc, jnp.exp(jnp.where(same_doc, spread, 0.0)), 0.0)
        scores = jnp.dot(out_block, in_block.T, preferred_element_type=jnp.float32)
        weights = (scores[None] * decay_mat * step_block[:, None, :]).astype(jnp.bfloat16)
        inside = jnp.einsum("hts,shp->thp", weights, vals_block, preferred_element_type=jnp.float32)
        keep_in = (doc_block == last_tag).astype(jnp.float32)
        reading = read_state(out_block, state)
        inter = reading * (jnp.exp(cumul).T * keep_in[:, None])[:, :, None]
        last_doc = doc_block[-1]
        tail_doc = (doc_block == last_doc).astype(jnp.float32)
        factor = step_block * jnp.exp(cumul[:, -1:] - cumul) * tail_doc[None, :]
        scaled = (vals_block.astype(jnp.float32) * factor.T[:, :, None]).astype(jnp.bfloat16)
        local_state = jnp.einsum(
            "shp,sn->hpn", scaled, in_block, preferred_element_type=jnp.float32
        )
        carry_on = (last_doc == last_tag).astype(jnp.float32)
        new_state = jnp.exp(cumul[:, -1])[:, None, None] * carry_on * state + local_state
        return ((new_state, last_doc), inside + inter)

    start = (jnp.zeros((heads, head_size, state_size), jnp.float32), jnp.array(-1, dtype=jnp.int32))
    (state, last_tag), outputs = lax.scan(one_block, start, items)
    return (outputs.reshape(count_blocks * block_len, heads, head_size), state, last_tag)


def per_device(
    conv_input,
    gate_input,
    step_input,
    step_bias,
    log_rates,
    skip_gain,
    conv_weight,
    conv_bias,
    norm_gain,
    doc_ids,
    cotangent,
):
    conv_rows = conv_input[0]
    doc_list = doc_ids[0]
    doc_values = doc_list.astype(jnp.float32)
    edge_count = conv_weight.shape[0] - 1
    local_len = conv_rows.shape[0]
    inner = gate_input.shape[2]
    heads = step_bias.shape[0]
    head_size = inner // heads
    state_size = (conv_rows.shape[1] - inner) // 2
    prev_rows, prev_docs = shifted(
        (
            conv_rows[local_len - edge_count :],
            doc_values[local_len - edge_count :].astype(jnp.bfloat16),
        ),
        "ctx",
        1,
    )
    filtered = filter_rows(
        conv_rows, prev_rows, doc_values, prev_docs.astype(jnp.float32), conv_weight, conv_bias
    )
    activated = lax.optimization_barrier(jax.nn.silu(filtered).astype(jnp.bfloat16))
    head_values = activated[:, :inner].reshape(local_len, heads, head_size)
    input_map = activated[:, inner : inner + state_size]
    output_map = activated[:, inner + state_size :]
    step_sizes = jax.nn.softplus(step_input[0] + step_bias[:, None])
    log_decay = -jnp.exp(log_rates)[:, None] * step_sizes
    local_out, end_state, last_tag = run_blocks(
        head_values, input_map, output_map, log_decay, step_sizes, doc_list, BLOCK
    )
    whole_decay = jnp.exp(jnp.sum(log_decay, axis=1))
    own_tag = last_tag.astype(jnp.float32).reshape(1)
    prefix_state = jnp.zeros_like(end_state)
    prefix_tag = jnp.zeros((1,), jnp.float32)
    for turn in range(lax.axis_size("ctx") - 1):
        linked = (prefix_tag[0] == own_tag[0]).astype(jnp.float32)
        outgoing = whole_decay[:, None, None] * linked * prefix_state + end_state
        prefix_state, prefix_tag = shifted((outgoing, own_tag), "ctx", 1)
    running = jnp.cumsum(log_decay, axis=1)
    matched = (doc_values == prefix_tag[0]).astype(jnp.float32)
    reading = read_state(output_map, prefix_state)
    correction = reading * (jnp.exp(running).T * matched[:, None])[:, :, None]
    mixed = local_out + correction + skip_gain[None, :, None] * head_values.astype(jnp.float32)
    mixer_out = lax.optimization_barrier(mixed.reshape(local_len, inner).astype(jnp.bfloat16))
    gated = mixer_out.astype(jnp.float32) * jax.nn.silu(gate_input[0].astype(jnp.float32))
    normed = (
        gated
        * lax.rsqrt(jnp.mean(gated * gated, axis=1, keepdims=True) + 1e-05)
        * norm_gain[None, :]
    ).astype(jnp.bfloat16)
    cot_rows = cotangent[0]
    weight_grad = lax.psum_scatter(
        jnp.einsum("tr,td->rd", normed, cot_rows, preferred_element_type=jnp.float32),
        ("dp", "ctx"),
        scatter_dimension=0,
        tiled=True,
    )
    return (normed[None], weight_grad)


def solution(mesh):
    in_specs = (
        P("dp", "ctx", None),
        P("dp", "ctx", None),
        P("dp", None, "ctx"),
        P(),
        P(),
        P(),
        P(),
        P(),
        P(),
        P("dp", "ctx"),
        P("dp", "ctx", None),
    )
    out_specs = (P("dp", "ctx", None), P(("dp", "ctx"), None))
    return jax.shard_map(
        per_device, mesh=mesh, in_specs=in_specs, out_specs=out_specs, check_vma=False
    )
```

profile of v0, /device:TPU:6, one launch (start us, length us, event | category | flops | bytes accessed | tf_op | source)
XLA Modules:
  0.0 611.0 jit_solution(3859218998205327611)
XLA Ops:
  1.5 3.8 collective-permute-start.1
  7.2 5.1 collective-permute-start.2
  13.1 3.5 collective-permute-start
  25.4 1.4 compare_convert_fusion.6
  27.6 6.0 multiply_convert_fusion.2
  33.7 1.5 copy.24
  35.2 1.8 broadcast_add_fusion
  37.0 2.0 collective-permute-start.3
  39.1 26.8 %collective-permute-done.3 = f32[40,64,128]{2,1,0:T(8,128)S(1)} collective-permute-done((f32[40,64,128]{2,1,0:T(8,128)S(1)}, f32[40,64,128]{2,1,0:T(8,128)S(1)}, u32[]{:S(2)}, u32[]{:S(2)}) %collective-permute-start.3) | collective-permute-done | bytes 1310752 | tf_op jit(solution)/shard_map/ppermute | solution.py:12
  67.2 4.5 collective-permute-start.4
  71.9 1.7 mul.365
  73.6 3.2 copy.28
  76.9 21.0 %collective-permute-done.4 = f32[40,64,128]{2,1,0:T(8,128)S(1)} collective-permute-done((f32[40,64,128]{2,1,0:T(8,128)}, f32[40,64,128]{2,1,0:T(8,128)S(1)}, u32[]{:S(2)}, u32[]{:S(2)}) %collective-permute-start.4) | collective-permute-done | bytes 1310752 | tf_op jit(solution)/shard_map/ppermute | solution.py:12
  99.1 5.3 collective-permute-start.5
  105.6 2.1 copy.27
  108.8 6.1 %bitcast_add_fusion = f32[256,40,64]{0,2,1:T(8,128)} fusion(f32[256,40,64]{0,2,1:T(8,128)} %bitcast.69, bf16[256,40,64]{0,2,1:T(8,128)(2,1)} %bitcast.68, f32[40,256]{1,0:T(8,128)S(1)} %get-tuple-element.31, f32[40,256]{1,0:T(8,128)S(1)} %copy-done.26, f32[256,256]{1,0:T(8,128)S(1)} %fusion.26, pred[256,256]{1,0:T(8,128)(4,1)S(1)} %fusion.23, ...), kind=kOutput, calls=%fused_computation.21 | convolution fusion | flops 352583680 | bytes 7004160 | tf_op jit(solution)/shard_map/while/body/eval_jaxpr/hts,shp->thp/dot_general | solution.py:63
  115.0 2.1 copy.29
  117.1 11.6 %collective-permute-done.5 = f32[40,64,128]{2,1,0:T(8,128)} collective-permute-done((f32[40,64,128]{2,1,0:T(8,128)}, f32[40,64,128]{2,1,0:T(8,128)}, u32[]{:S(2)}, u32[]{:S(2)}) %collective-permute-start.5) | collective-permute-done | bytes 1310752 | tf_op jit(solution)/shard_map/ppermute | solution.py:12
  128.7 1.5 fusion.18
  131.6 2.4 fusion.11
  136.1 6.6 %fusion.20 = f32[2560,1280]{1,0:T(8,128)} fusion(bf16[256,2560]{1,0:T(8,128)(2,1)S(1)} %multiply_convert_fusion.3, bf16[1,256,1280]{2,1,0:T(8,128)(2,1)S(1)} %copy-done), kind=kOutput, calls=%fused_computation.37 | convolution fusion | flops 1677721600 | bytes 15073280 | tf_op jit(solution)/shard_map/tr,td->rd/dot_general | solution.py:147
  142.7 311.9 %fusion = f32[24,1280]{1,0:T(8,128)S(1)} fusion(f32[2560,1280]{1,0:T(8,128)} %fusion.20), kind=kCustom, calls=%all-reduce-scatter | all-reduce-scatter fusion | flops 3932161 | bytes 13230080
  454.6 6.7 %collective-permute-start.10 = (f32[24,1280]{1,0:T(8,128)S(1)}, f32[24,1280]{1,0:T(8,128)S(1)}, u32[]{:S(2)}, u32[]{:S(2)}) collective-permute-start(f32[24,1280]{1,0:T(8,128)S(1)} %fusion), channel_id=1, source_target_pairs={{0,5},{1,6},{2,7},{3,8},{4,9},{5,10},{6,11},{7,12},{8,13},{9,14},{... | collective-permute-start | bytes 368648
  461.3 1.9 collective-permute-start.27
  463.3 10.1 %collective-permute-start.11 = (f32[24,1280]{1,0:T(8,128)S(1)}, f32[24,1280]{1,0:T(8,128)S(1)}, u32[]{:S(2)}, u32[]{:S(2)}) collective-permute-start(f32[24,1280]{1,0:T(8,128)S(1)} %fusion), channel_id=1, source_target_pairs={{0,6},{1,7},{2,8},{3,9},{4,10},{5,11},{6,12},{7,13},{8,14},{9,15},... | collective-permute-start | bytes 368648
  473.3 11.3 %collective-permute-start.12 = (f32[24,1280]{1,0:T(8,128)S(1)}, f32[24,1280]{1,0:T(8,128)S(1)}, u32[]{:S(2)}, u32[]{:S(2)}) collective-permute-start(f32[24,1280]{1,0:T(8,128)S(1)} %fusion), channel_id=1, source_target_pairs={{0,7},{1,8},{2,9},{3,10},{4,11},{5,12},{6,13},{7,14},{8,15},{9,16}... | collective-permute-start | bytes 368648
  484.6 1.9 collective-permute-start.13
  486.6 25.9 %collective-permute-done.27 = f32[4,1280]{1,0:T(4,128)S(1)} collective-permute-done((f32[4,1280]{1,0:T(4,128)S(1)}, f32[4,1280]{1,0:T(4,128)S(1)}, u32[]{:S(2)}, u32[]{:S(2)}) %collective-permute-start.27) | collective-permute-done | bytes 20512
  512.5 1.9 collective-permute-start.14
  514.4 1.9 collective-permute-start.15
  516.4 1.9 collective-permute-start.16
  518.3 1.9 collective-permute-start.17
  520.3 22.9 %collective-permute-start.18 = (f32[24,1280]{1,0:T(8,128)S(1)}, f32[24,1280]{1,0:T(8,128)S(1)}, u32[]{:S(2)}, u32[]{:S(2)}) collective-permute-start(f32[24,1280]{1,0:T(8,128)S(1)} %fusion), channel_id=1, source_target_pairs={{0,13},{1,14},{2,15},{3,16},{4,17},{5,18},{6,19},{7,20},{8,21},{9,... | collective-permute-start | bytes 368648
  543.2 2.5 collective-permute-start.19
  545.7 2.6 collective-permute-start.20
  548.3 1.9 collective-permute-start.21
  550.3 1.9 collective-permute-start.22
  552.2 3.0 collective-permute-start.23
  555.3 3.0 collective-permute-start.24
  558.3 1.9 collective-permute-start.25
  560.3 1.9 collective-permute-start.26
  562.2 14.6 %collective-permute-start.6 = (f32[24,1280]{1,0:T(8,128)S(1)}, f32[24,1280]{1,0:T(8,128)S(1)}, u32[]{:S(2)}, u32[]{:S(2)}) collective-permute-start(f32[24,1280]{1,0:T(8,128)S(1)} %fusion), channel_id=1, source_target_pairs={{0,1},{1,2},{2,3},{3,4},{4,5},{5,6},{6,7},{7,8},{8,9},{9,10},{10,1... | collective-permute-start | bytes 368648
  576.8 1.9 collective-permute-start.7
  578.8 1.9 collective-permute-start.8
  580.7 1.9 collective-permute-start.9
  582.8 2.6 collective-permute-done.7
  586.7 2.1 collective-permute-done.9
  588.8 21.5 %concatenate.8 = f32[532,1280]{1,0:T(8,128)S(1)} concatenate(f32[4,1280]{1,0:T(4,128)S(1)} %collective-permute-done.27, f32[24,1280]{1,0:T(8,128)} %copy-done.21, f32[24,1280]{1,0:T(8,128)} %copy-done.20, f32[24,1280]{1,0:T(8,128)} %copy-done.19, f32[24,1280]{1,0:T(8,128)} %copy-done.18, f32[24,1280]{1,0:T(8,128)} %copy-done.17, f32[24,1280]{1,0:T(8,128)} %copy-done.16, ...), dimensions={0} | concatenate | bytes 5447680
  (120 shorter events, 21.7 us)
Async XLA Ops:
  0.6 135.4 %copy-start = (bf16[1,256,1280]{2,1,0:T(8,128)(2,1)S(1)}, bf16[1,256,1280]{2,1,0:T(8,128)(2,1)}, u32[]{:S(2)}) copy-start(bf16[1,256,1280]{2,1,0:T(8,128)(2,1)} %param.21) | copy-start | bytes 1966084
  1.5 23.9 %collective-permute-start.1 = (bf16[3]{0:T(256)(128)(2,1)S(1)}, bf16[3]{0:T(256)(128)(2,1)S(1)}, u32[]{:S(2)}, u32[]{:S(2)}) collective-permute-start(bf16[3]{0:T(256)(128)(2,1)S(1)} %slice.71), channel_id=1, source_target_pairs={{0,1},{1,2},{2,3},{4,5},{5,6},{6,7},{8,9},{9,10},{10,11},{12,13},{... | collective-permute-start | bytes 26 | tf_op jit(solution)/shard_map/ppermute | solution.py:12
  7.2 17.5 %collective-permute-start.2 = (f32[1]{0:T(128)}, f32[1]{0:T(128)}, u32[]{:S(2)}, u32[]{:S(2)}) collective-permute-start(f32[1]{0:T(128)} %bitcast.10), channel_id=1, source_target_pairs={{0,1},{1,2},{2,3},{4,5},{5,6},{6,7},{8,9},{9,10},{10,11},{12,13},{... | collective-permute-start | bytes 20 | tf_op jit(solution)/shard_map/ppermute | solution.py:12
  13.1 14.5 %collective-permute-start = (bf16[3,2816]{1,0:T(4,128)(2,1)S(1)}, bf16[3,2816]{1,0:T(4,128)(2,1)S(1)}, u32[]{:S(2)}, u32[]{:S(2)}) collective-permute-start(bf16[3,2816]{1,0:T(4,128)(2,1)S(1)} %slice_bitcast_fusion), channel_id=1, source_target_pairs={{0,1},{1,2},{2,3},{4,5},{5,6},{6,7},{8,9},{9,10},{10,11},{12,13},{... | collective-permute-start | bytes 50696 | tf_op jit(solution)/shard_map/ppermute | solution.py:12
  37.0 34.6 %copy-start.30 = (f32[40]{0:T(128)S(1)}, f32[40]{0:T(128)}, u32[]{:S(2)}) copy-start(f32[40]{0:T(128)} %param.16) | copy-start | bytes 484
  37.0 34.7 %copy-start.28 = (s32[1,256]{1,0:T(1,128)S(1)}, s32[1,256]{1,0:T(1,128)}, u32[]{:S(2)}) copy-start(s32[1,256]{1,0:T(1,128)} %param.20) | copy-start | bytes 3076
  37.0 28.8 %collective-permute-start.3 = (f32[40,64,128]{2,1,0:T(8,128)S(1)}, f32[40,64,128]{2,1,0:T(8,128)S(1)}, u32[]{:S(2)}, u32[]{:S(2)}) collective-permute-start(f32[40,64,128]{2,1,0:T(8,128)S(1)} %get-tuple-element.54), channel_id=1, source_target_pairs={{0,1},{1,2},{2,3},{4,5},{5,6},{6,7},{8,9},{9,10},{10,11},{12,13},{... | collective-permute-start | bytes 3932168 | tf_op jit(solution)/shard_map/ppermute | solution.py:12
  67.2 30.7 %collective-permute-start.4 = (f32[40,64,128]{2,1,0:T(8,128)}, f32[40,64,128]{2,1,0:T(8,128)S(1)}, u32[]{:S(2)}, u32[]{:S(2)}) collective-permute-start(f32[40,64,128]{2,1,0:T(8,128)} %multiply_add_fusion.1), channel_id=1, source_target_pairs={{0,1},{1,2},{2,3},{4,5},{5,6},{6,7},{8,9},{9,10},{10,11},{12,13},{... | collective-permute-start | bytes 3932168 | tf_op jit(solution)/shard_map/ppermute | solution.py:12
  99.1 29.6 %collective-permute-start.5 = (f32[40,64,128]{2,1,0:T(8,128)}, f32[40,64,128]{2,1,0:T(8,128)}, u32[]{:S(2)}, u32[]{:S(2)}) collective-permute-start(f32[40,64,128]{2,1,0:T(8,128)} %multiply_add_fusion), channel_id=1, source_target_pairs={{0,1},{1,2},{2,3},{4,5},{5,6},{6,7},{8,9},{9,10},{10,11},{12,13},{... | collective-permute-start | bytes 3932168 | tf_op jit(solution)/shard_map/ppermute | solution.py:12
  117.1 14.4 %copy-start.1 = (f32[256,2560]{1,0:T(8,128)S(1)}, f32[256,2560]{1,0:T(8,128)}, u32[]{:S(2)}) copy-start(f32[256,2560]{1,0:T(8,128)} %copy.28) | copy-start | bytes 7864324
  136.1 6.7 %copy-start.3 = (bf16[256,2560]{1,0:T(8,128)(2,1)}, bf16[256,2560]{1,0:T(8,128)(2,1)S(1)}, u32[]{:S(2)}) copy-start(bf16[256,2560]{1,0:T(8,128)(2,1)S(1)} %multiply_convert_fusion.3) | copy-start | bytes 3932164
  454.6 59.8 %collective-permute-start.10 = (f32[24,1280]{1,0:T(8,128)S(1)}, f32[24,1280]{1,0:T(8,128)S(1)}, u32[]{:S(2)}, u32[]{:S(2)}) collective-permute-start(f32[24,1280]{1,0:T(8,128)S(1)} %fusion), channel_id=1, source_target_pairs={{0,5},{1,6},{2,7},{3,8},{4,9},{5,10},{6,11},{7,12},{8,13},{9,14},{... | collective-permute-start | bytes 368648
  461.3 51.2 %collective-permute-start.27 = (f32[4,1280]{1,0:T(4,128)S(1)}, f32[4,1280]{1,0:T(4,128)S(1)}, u32[]{:S(2)}, u32[]{:S(2)}) collective-permute-start(f32[4,1280]{1,0:T(4,128)S(1)} %slice.96), channel_id=1, source_target_pairs={{0,22},{1,23},{2,24},{3,25},{4,26},{5,27},{6,28},{7,29},{8,30},{9,... | collective-permute-start | bytes 61448
  463.3 53.1 %collective-permute-start.11 = (f32[24,1280]{1,0:T(8,128)S(1)}, f32[24,1280]{1,0:T(8,128)S(1)}, u32[]{:S(2)}, u32[]{:S(2)}) collective-permute-start(f32[24,1280]{1,0:T(8,128)S(1)} %fusion), channel_id=1, source_target_pairs={{0,6},{1,7},{2,8},{3,9},{4,10},{5,11},{6,12},{7,13},{8,14},{9,15},... | collective-permute-start | bytes 368648
  473.3 45.0 %collective-permute-start.12 = (f32[24,1280]{1,0:T(8,128)S(1)}, f32[24,1280]{1,0:T(8,128)S(1)}, u32[]{:S(2)}, u32[]{:S(2)}) collective-permute-start(f32[24,1280]{1,0:T(8,128)S(1)} %fusion), channel_id=1, source_target_pairs={{0,7},{1,8},{2,9},{3,10},{4,11},{5,12},{6,13},{7,14},{8,15},{9,16}... | collective-permute-start | bytes 368648
  484.6 35.6 %collective-permute-start.13 = (f32[24,1280]{1,0:T(8,128)S(1)}, f32[24,1280]{1,0:T(8,128)S(1)}, u32[]{:S(2)}, u32[]{:S(2)}) collective-permute-start(f32[24,1280]{1,0:T(8,128)S(1)} %fusion), channel_id=1, source_target_pairs={{0,8},{1,9},{2,10},{3,11},{4,12},{5,13},{6,14},{7,15},{8,16},{9,17... | collective-permute-start | bytes 368648
  512.5 30.7 %collective-permute-start.14 = (f32[24,1280]{1,0:T(8,128)S(1)}, f32[24,1280]{1,0:T(8,128)S(1)}, u32[]{:S(2)}, u32[]{:S(2)}) collective-permute-start(f32[24,1280]{1,0:T(8,128)S(1)} %fusion), channel_id=1, source_target_pairs={{0,9},{1,10},{2,11},{3,12},{4,13},{5,14},{6,15},{7,16},{8,17},{9,1... | collective-permute-start | bytes 368648
  514.4 66.3 %copy-start.5 = (f32[24,1280]{1,0:T(8,128)}, f32[24,1280]{1,0:T(8,128)S(1)}, u32[]{:S(2)}) copy-start(f32[24,1280]{1,0:T(8,128)S(1)} %collective-permute-done.10) | copy-start | bytes 368644
  514.4 31.2 %collective-permute-start.15 = (f32[24,1280]{1,0:T(8,128)S(1)}, f32[24,1280]{1,0:T(8,128)S(1)}, u32[]{:S(2)}, u32[]{:S(2)}) collective-permute-start(f32[24,1280]{1,0:T(8,128)S(1)} %fusion), channel_id=1, source_target_pairs={{0,10},{1,11},{2,12},{3,13},{4,14},{5,15},{6,16},{7,17},{8,18},{9,... | collective-permute-start | bytes 368648
  516.4 66.3 %copy-start.6 = (f32[24,1280]{1,0:T(8,128)}, f32[24,1280]{1,0:T(8,128)S(1)}, u32[]{:S(2)}) copy-start(f32[24,1280]{1,0:T(8,128)S(1)} %collective-permute-done.11) | copy-start | bytes 368644
  516.4 31.9 %collective-permute-start.16 = (f32[24,1280]{1,0:T(8,128)S(1)}, f32[24,1280]{1,0:T(8,128)S(1)}, u32[]{:S(2)}, u32[]{:S(2)}) collective-permute-start(f32[24,1280]{1,0:T(8,128)S(1)} %fusion), channel_id=1, source_target_pairs={{0,11},{1,12},{2,13},{3,14},{4,15},{5,16},{6,17},{7,18},{8,19},{9,... | collective-permute-start | bytes 368648
  518.3 64.3 %copy-start.7 = (f32[24,1280]{1,0:T(8,128)}, f32[24,1280]{1,0:T(8,128)S(1)}, u32[]{:S(2)}) copy-start(f32[24,1280]{1,0:T(8,128)S(1)} %collective-permute-done.12) | copy-start | bytes 368644
  518.3 31.9 %collective-permute-start.17 = (f32[24,1280]{1,0:T(8,128)S(1)}, f32[24,1280]{1,0:T(8,128)S(1)}, u32[]{:S(2)}, u32[]{:S(2)}) collective-permute-start(f32[24,1280]{1,0:T(8,128)S(1)} %fusion), channel_id=1, source_target_pairs={{0,12},{1,13},{2,14},{3,15},{4,16},{5,17},{6,18},{7,19},{8,20},{9,... | collective-permute-start | bytes 368648
  520.3 62.4 %copy-start.8 = (f32[24,1280]{1,0:T(8,128)}, f32[24,1280]{1,0:T(8,128)S(1)}, u32[]{:S(2)}) copy-start(f32[24,1280]{1,0:T(8,128)S(1)} %collective-permute-done.13) | copy-start | bytes 368644
  520.3 31.9 %collective-permute-start.18 = (f32[24,1280]{1,0:T(8,128)S(1)}, f32[24,1280]{1,0:T(8,128)S(1)}, u32[]{:S(2)}, u32[]{:S(2)}) collective-permute-start(f32[24,1280]{1,0:T(8,128)S(1)} %fusion), channel_id=1, source_target_pairs={{0,13},{1,14},{2,15},{3,16},{4,17},{5,18},{6,19},{7,20},{8,21},{9,... | collective-permute-start | bytes 368648
  543.2 39.5 %copy-start.9 = (f32[24,1280]{1,0:T(8,128)}, f32[24,1280]{1,0:T(8,128)S(1)}, u32[]{:S(2)}) copy-start(f32[24,1280]{1,0:T(8,128)S(1)} %collective-permute-done.14) | copy-start | bytes 368644
  543.2 12.1 %collective-permute-start.19 = (f32[24,1280]{1,0:T(8,128)S(1)}, f32[24,1280]{1,0:T(8,128)S(1)}, u32[]{:S(2)}, u32[]{:S(2)}) collective-permute-start(f32[24,1280]{1,0:T(8,128)S(1)} %fusion), channel_id=1, source_target_pairs={{0,14},{1,15},{2,16},{3,17},{4,18},{5,19},{6,20},{7,21},{8,22},{9,... | collective-permute-start | bytes 368648
  545.7 37.0 %copy-start.10 = (f32[24,1280]{1,0:T(8,128)}, f32[24,1280]{1,0:T(8,128)S(1)}, u32[]{:S(2)}) copy-start(f32[24,1280]{1,0:T(8,128)S(1)} %collective-permute-done.15) | copy-start | bytes 368644
  545.7 12.6 %collective-permute-start.20 = (f32[24,1280]{1,0:T(8,128)S(1)}, f32[24,1280]{1,0:T(8,128)S(1)}, u32[]{:S(2)}, u32[]{:S(2)}) collective-permute-start(f32[24,1280]{1,0:T(8,128)S(1)} %fusion), channel_id=1, source_target_pairs={{0,15},{1,16},{2,17},{3,18},{4,19},{5,20},{6,21},{7,22},{8,23},{9,... | collective-permute-start | bytes 368648
  548.3 34.4 %copy-start.11 = (f32[24,1280]{1,0:T(8,128)}, f32[24,1280]{1,0:T(8,128)S(1)}, u32[]{:S(2)}) copy-start(f32[24,1280]{1,0:T(8,128)S(1)} %collective-permute-done.16) | copy-start | bytes 368644
  548.3 11.9 %collective-permute-start.21 = (f32[24,1280]{1,0:T(8,128)S(1)}, f32[24,1280]{1,0:T(8,128)S(1)}, u32[]{:S(2)}, u32[]{:S(2)}) collective-permute-start(f32[24,1280]{1,0:T(8,128)S(1)} %fusion), channel_id=1, source_target_pairs={{0,16},{1,17},{2,18},{3,19},{4,20},{5,21},{6,22},{7,23},{8,24},{9,... | collective-permute-start | bytes 368648
  550.3 32.4 %copy-start.12 = (f32[24,1280]{1,0:T(8,128)}, f32[24,1280]{1,0:T(8,128)S(1)}, u32[]{:S(2)}) copy-start(f32[24,1280]{1,0:T(8,128)S(1)} %collective-permute-done.17) | copy-start | bytes 368644
  550.3 11.9 %collective-permute-start.22 = (f32[24,1280]{1,0:T(8,128)S(1)}, f32[24,1280]{1,0:T(8,128)S(1)}, u32[]{:S(2)}, u32[]{:S(2)}) collective-permute-start(f32[24,1280]{1,0:T(8,128)S(1)} %fusion), channel_id=1, source_target_pairs={{0,17},{1,18},{2,19},{3,20},{4,21},{5,22},{6,23},{7,24},{8,25},{9,... | collective-permute-start | bytes 368648
  552.2 30.5 %copy-start.13 = (f32[24,1280]{1,0:T(8,128)}, f32[24,1280]{1,0:T(8,128)S(1)}, u32[]{:S(2)}) copy-start(f32[24,1280]{1,0:T(8,128)S(1)} %collective-permute-done.18) | copy-start | bytes 368644
  552.2 24.6 %collective-permute-start.23 = (f32[24,1280]{1,0:T(8,128)S(1)}, f32[24,1280]{1,0:T(8,128)S(1)}, u32[]{:S(2)}, u32[]{:S(2)}) collective-permute-start(f32[24,1280]{1,0:T(8,128)S(1)} %fusion), channel_id=1, source_target_pairs={{0,18},{1,19},{2,20},{3,21},{4,22},{5,23},{6,24},{7,25},{8,26},{9,... | collective-permute-start | bytes 368648
  555.3 27.5 %copy-start.14 = (f32[24,1280]{1,0:T(8,128)}, f32[24,1280]{1,0:T(8,128)S(1)}, u32[]{:S(2)}) copy-start(f32[24,1280]{1,0:T(8,128)S(1)} %collective-permute-done.19) | copy-start | bytes 368644
  555.3 23.5 %collective-permute-start.24 = (f32[24,1280]{1,0:T(8,128)S(1)}, f32[24,1280]{1,0:T(8,128)S(1)}, u32[]{:S(2)}, u32[]{:S(2)}) collective-permute-start(f32[24,1280]{1,0:T(8,128)S(1)} %fusion), channel_id=1, source_target_pairs={{0,19},{1,20},{2,21},{3,22},{4,23},{5,24},{6,25},{7,26},{8,27},{9,... | collective-permute-start | bytes 368648
  558.3 24.4 %copy-start.15 = (f32[24,1280]{1,0:T(8,128)}, f32[24,1280]{1,0:T(8,128)S(1)}, u32[]{:S(2)}) copy-start(f32[24,1280]{1,0:T(8,128)S(1)} %collective-permute-done.20) | copy-start | bytes 368644
  558.3 22.4 %collective-permute-start.25 = (f32[24,1280]{1,0:T(8,128)S(1)}, f32[24,1280]{1,0:T(8,128)S(1)}, u32[]{:S(2)}, u32[]{:S(2)}) collective-permute-start(f32[24,1280]{1,0:T(8,128)S(1)} %fusion), channel_id=1, source_target_pairs={{0,20},{1,21},{2,22},{3,23},{4,24},{5,25},{6,26},{7,27},{8,28},{9,... | collective-permute-start | bytes 368648
  560.3 22.5 %copy-start.16 = (f32[24,1280]{1,0:T(8,128)}, f32[24,1280]{1,0:T(8,128)S(1)}, u32[]{:S(2)}) copy-start(f32[24,1280]{1,0:T(8,128)S(1)} %collective-permute-done.21) | copy-start | bytes 368644
  560.3 22.5 %collective-permute-start.26 = (f32[24,1280]{1,0:T(8,128)S(1)}, f32[24,1280]{1,0:T(8,128)S(1)}, u32[]{:S(2)}, u32[]{:S(2)}) collective-permute-start(f32[24,1280]{1,0:T(8,128)S(1)} %fusion), channel_id=1, source_target_pairs={{0,21},{1,22},{2,23},{3,24},{4,25},{5,26},{6,27},{7,28},{8,29},{9,... | collective-permute-start | bytes 368648
  562.2 20.5 %copy-start.17 = (f32[24,1280]{1,0:T(8,128)}, f32[24,1280]{1,0:T(8,128)S(1)}, u32[]{:S(2)}) copy-start(f32[24,1280]{1,0:T(8,128)S(1)} %collective-permute-done.22) | copy-start | bytes 368644
  562.2 20.6 %collective-permute-start.6 = (f32[24,1280]{1,0:T(8,128)S(1)}, f32[24,1280]{1,0:T(8,128)S(1)}, u32[]{:S(2)}, u32[]{:S(2)}) collective-permute-start(f32[24,1280]{1,0:T(8,128)S(1)} %fusion), channel_id=1, source_target_pairs={{0,1},{1,2},{2,3},{3,4},{4,5},{5,6},{6,7},{7,8},{8,9},{9,10},{10,1... | collective-permute-start | bytes 368648
  576.8 6.0 copy-start.18
  576.8 8.6 %collective-permute-start.7 = (f32[24,1280]{1,0:T(8,128)S(1)}, f32[24,1280]{1,0:T(8,128)S(1)}, u32[]{:S(2)}, u32[]{:S(2)}) collective-permute-start(f32[24,1280]{1,0:T(8,128)S(1)} %fusion), channel_id=1, source_target_pairs={{0,2},{1,3},{2,4},{3,5},{4,6},{5,7},{6,8},{7,9},{8,10},{9,11},{10,... | collective-permute-start | bytes 368648
  578.7 4.0 copy-start.19
  578.8 7.1 %collective-permute-start.8 = (f32[24,1280]{1,0:T(8,128)S(1)}, f32[24,1280]{1,0:T(8,128)S(1)}, u32[]{:S(2)}, u32[]{:S(2)}) collective-permute-start(f32[24,1280]{1,0:T(8,128)S(1)} %fusion), channel_id=1, source_target_pairs={{0,3},{1,4},{2,5},{3,6},{4,7},{5,8},{6,9},{7,10},{8,11},{9,12},{10... | collective-permute-start | bytes 368648
  580.7 8.1 %collective-permute-start.9 = (f32[24,1280]{1,0:T(8,128)S(1)}, f32[24,1280]{1,0:T(8,128)}, u32[]{:S(2)}, u32[]{:S(2)}) collective-permute-start(f32[24,1280]{1,0:T(8,128)S(1)} %fusion), channel_id=1, source_target_pairs={{0,4},{1,5},{2,6},{3,7},{4,8},{5,9},{6,10},{7,11},{8,12},{9,13},{1... | collective-permute-start | bytes 368648
  (11 other events, 24.7 us)
where the time goes:
time: 614 us; the launch traced here: 611 us
  blocking collectives  312 us (51%)
  starting transfers between devices  126 us (21%)
  waiting for transfers between devices  90.5 us (15%)
  local copies, waits for them, and re-layouts  38.5 us (6%)
  matrix products  20.6 us (3%)
  other arithmetic  20.3 us (3%)
    unnamed x1, blocking collectives  312 us
    unnamed x22, starting transfers between devices  102 us
    ppermute x6, waiting for transfers between devices, shifted(): return lax.ppermute(value, axis, pairs)  59.3 us
    unnamed x22, waiting for transfers between devices  31.1 us
    ppermute x6, starting transfers between devices, shifted(): return lax.ppermute(value, axis, pairs)  24.2 us
    unnamed x65, local copies, waits for them, and re-layouts  23.2 us
  transfers between devices with their start and end apart: 28, of which 7 were waited for; matrix products, arithmetic and copies ran while one was open for 5% of the time, Pallas kernels for 0%

commit v1 on v0

v1 whole, which is shorter than its diff:
```python
import jax
import jax.numpy as jnp
from jax import lax
from jax.experimental import pallas as pl
from jax.experimental.pallas import tpu as pltpu
from jax.sharding import Mesh
from jax.sharding import PartitionSpec as P

T = 256
H = 40
HD = 64
N = 128
INNER = 2560
C_ALL = 2816
D = 1280
LANES = 128
XCHUNKS = INNER // LANES
MSG = N + 16
F32 = jnp.float32
BF16 = jnp.bfloat16
HIGH = lax.Precision.HIGHEST
VMEM = pltpu.VMEM


def silu(v):
    return 0.5 * v * (1.0 + jnp.tanh(0.5 * v))


def dot(a, b, dims=((1,), (0,)), precision=None):
    return lax.dot_general(a, b, (dims, ((), ())), preferred_element_type=F32, precision=precision)


def split_rows(v):
    hi = v.astype(BF16).astype(F32)
    rest = v - hi
    mid = rest.astype(BF16).astype(F32)
    low = rest - mid
    return jnp.concatenate([hi, mid, low, jnp.zeros((8, v.shape[1]), F32)], 0)


def head_pick(chunk, width):
    rows = lax.broadcasted_iota(jnp.int32, (LANES, width), 0)
    rows = jnp.where(rows >= 2 * H, rows - 2 * H, jnp.where(rows >= H, rows - H, rows))
    real = lax.broadcasted_iota(jnp.int32, (LANES, width), 0) < 3 * H
    lanes = lax.broadcasted_iota(jnp.int32, (LANES, width), 1)
    head = 2 * chunk + jnp.where(lanes >= width // 2, 1, 0)
    return jnp.where(jnp.logical_and(real, rows == head), 1.0, 0.0).astype(BF16)


def front_kernel(conv, halo, step_in, bias, rates, w, cb, doc_row, docb, act, msg, cum_o, step_o, win, dwin, masks, xs, fac):
    step = jax.nn.softplus(step_in[...] + bias[...])
    decay = -jnp.exp(rates[...]) * step
    tri = (
        lax.broadcasted_iota(jnp.int32, (T, T), 0) <= lax.broadcasted_iota(jnp.int32, (T, T), 1)
    ).astype(F32)
    cum = dot(decay, tri, precision=HIGH)
    cum_o[...] = cum
    step_o[...] = step
    docs = doc_row[...]
    tail = (docs == docs[:, T - 1 : T]).astype(F32)
    total = cum[:, T - 1 : T]
    factor = step * jnp.exp(total - cum) * tail
    whole = jnp.broadcast_to(jnp.exp(total), (H, LANES))
    fac[...] = split_rows(jnp.concatenate([factor, whole], 1)).T.astype(BF16)
    dwin[0:8, :] = halo[:, C_ALL:].astype(F32)
    dwin[8:, :] = docb[...].astype(F32)
    own = dwin[8:, :]
    for k in range(3):
        masks[k] = (dwin[5 + k : 5 + k + T, :] == own).astype(F32)
    tag = docb[T - 16 :, :].astype(F32)[15:16, :]

    def conv_chunk(j):
        at = pl.ds(pl.multiple_of(j * LANES, LANES), LANES)
        win[0:8, :] = halo[:, at].astype(F32)
        win[8:, :] = conv[:, at].astype(F32)
        taps = w[:, at]
        total = cb[:, at] + taps[3:4] * win[8:, :]
        for k in range(3):
            total = total + (taps[k : k + 1] * win[5 + k : 5 + k + T, :]) * masks[k]
        out = silu(total).astype(BF16)
        act[:, at] = out
        return at, out

    def value_chunk(j, carry):
        at, out = conv_chunk(j)
        wide = dot(fac[0 : T + 16, :], head_pick(j, LANES))
        xs[:, at] = (out.astype(F32) * wide[0:T]).astype(BF16)
        row = lax.broadcasted_iota(jnp.int32, (16, LANES), 0)
        end = wide[T : T + 16]
        hi = end.astype(BF16).astype(F32)
        info = jnp.where(row == 0, hi, jnp.where(row == 1, end - hi, jnp.where(row == 2, tag, 0.0)))
        msg[N:, at] = info.astype(BF16)
        return carry

    def map_chunk(j, carry):
        conv_chunk(j)
        return carry

    lax.fori_loop(XCHUNKS, XCHUNKS + 2, map_chunk, 0)
    lax.fori_loop(0, XCHUNKS, value_chunk, 0)
    b_t = act[:, INNER : INNER + N].astype(F32).T.astype(BF16)
    for k in range(5):
        at = slice(512 * k, 512 * k + 512)
        msg[0:N, at] = dot(b_t, xs[:, at]).astype(BF16)


def middle_kernel(act, cum, step, doc_row, docb, halo, gate, skip, local, reach, sgate, scores, fac, efac):
    c_map = act[:, INNER + N :]
    b_map = act[:, INNER : INNER + N]
    doc_col = docb[...].astype(F32)
    for s in range(2):
        at = slice(s * LANES, s * LANES + LANES)
        g = dot(c_map, b_map[at], ((1,), (1,)))
        order = lax.broadcasted_iota(jnp.int32, (T, LANES), 0) >= (
            lax.broadcasted_iota(jnp.int32, (T, LANES), 1) + s * LANES
        )
        same = jnp.logical_and(order, doc_col == doc_row[:, at].astype(F32))
        scores[:, at] = jnp.where(same, g, 0.0)
    all_cum = cum[...]
    fac[...] = split_rows(all_cum).T.astype(BF16)
    prev_tag = halo[:, C_ALL : C_ALL + LANES].astype(F32)[7:8, :]
    prev_tag = jnp.concatenate([prev_tag, prev_tag], 1)
    matched = (doc_row[...].astype(F32) == prev_tag).astype(F32)
    efac[...] = split_rows(jnp.exp(all_cum) * matched).T.astype(BF16)
    half = T // 2

    def pair(j, carry):
        at = pl.ds(pl.multiple_of(j * LANES, LANES), LANES)
        vals = act[:, at]
        lanes = lax.broadcasted_iota(jnp.int32, (T, LANES), 1)
        cols = dot(fac[...], head_pick(j, 2 * LANES))
        top = jnp.zeros((half, LANES), F32)
        low = jnp.zeros((half, LANES), F32)
        for k in range(2):
            mine = jnp.where((lanes >= HD) == (k == 1), vals.astype(F32), 0.0).astype(BF16)
            col = cols[:, k * LANES : (k + 1) * LANES]
            row = cum[pl.ds(2 * j + k, 1), :]
            size = step[pl.ds(2 * j + k, 1), :]

            def weights(t, s):
                ts = slice(t * half, t * half + half)
                ss = slice(s * LANES, s * LANES + LANES)
                spread = jnp.minimum(col[ts] - row[:, ss], 0.0)
                return (scores[ts, ss] * jnp.exp(spread) * size[:, ss]).astype(BF16)

            top = top + dot(weights(0, 0), mine[0:half])
            low = low + dot(jnp.concatenate([weights(1, 0), weights(1, 1)], 1), mine)
        gain = skip[:, at]
        local[0:half, at] = top + gain * vals[0:half].astype(F32)
        local[half:, at] = low + gain * vals[half:].astype(F32)
        reach[:, at] = dot(efac[...], head_pick(j, LANES))
        sgate[:, at] = silu(gate[:, at].astype(F32))
        return carry

    lax.fori_loop(0, XCHUNKS, pair, 0)


def back_kernel(local, reach, sgate, act, one, two, gain, normed, parts, gated, squares):
    c_map = act[:, INNER + N :]
    squares[...] = jnp.zeros_like(squares)

    def first(j, carry):
        at = pl.ds(pl.multiple_of(j * LANES, LANES), LANES)
        info = one[N:, at].astype(F32)
        other = two[N:, at].astype(F32)
        linked = (info[2:3] == other[2:3]).astype(F32)
        weight = (info[0:1] + info[1:2]) * linked
        state = one[0:N, at].astype(F32) + weight * two[0:N, at].astype(F32)
        reading = dot(c_map, state.astype(BF16))
        mixed = local[:, at] + reading * reach[:, at]
        value = mixed.astype(BF16).astype(F32) * sgate[:, at]
        gated[:, at] = value
        squares[...] += value * value
        return carry

    lax.fori_loop(0, XCHUNKS, first, 0)
    mean = jnp.sum(squares[...], axis=1, keepdims=True) * (1.0 / INNER)
    squares[...] = jnp.broadcast_to(lax.rsqrt(mean + 1e-05), squares.shape)
    for p in range(4):

        def second(j, carry):
            src = pl.ds(pl.multiple_of((5 * p + j) * LANES, LANES), LANES)
            dst = pl.ds(pl.multiple_of(j * LANES, LANES), LANES)
            value = (gated[:, src] * squares[...] * gain[:, src]).astype(BF16)
            normed[:, src] = value
            parts[p, :, dst] = value
            return carry

        lax.fori_loop(0, 5, second, 0)


def pack_kernel(own, other, out, flat):
    for x in range(4):
        for z in range(4):
            rows = slice(20 * z, 20 * z + 20)
            for k in range(10):
                at = slice(k * LANES, k * LANES + LANES)
                flat[4 * x + z, 20 * k : 20 * k + 20, :] = own[x, rows, at] + other[x, rows, at].astype(F32)
    for i in range(16):
        out[i] = flat[i].astype(BF16)


def sum_kernel(pieces, out, flat):
    total = pieces[0].astype(F32)
    for i in range(1, 16):
        total = total + pieces[i].astype(F32)
    flat[...] = total
    for k in range(10):
        out[:, k * LANES : k * LANES + LANES] = flat[20 * k : 20 * k + 20, :]


def call(kernel, name, out, scratch, limit, flops=0, moved=0, special=0):
    return pl.pallas_call(
        kernel,
        name=name,
        out_shape=out,
        scratch_shapes=scratch,
        compiler_params=pltpu.CompilerParams(vmem_limit_bytes=limit << 20),
        cost_estimate=pl.CostEstimate(flops=flops, bytes_accessed=moved, transcendentals=special),
    )


def shape(dims, kind=F32):
    return jax.ShapeDtypeStruct(dims, kind)


def shifted(value, by):
    return lax.ppermute(value, "z", [(i, i + by) for i in range(4 - by)])


def per_device(conv_input, gate_input, step_input, step_bias, log_rates, skip_gain, conv_weight, conv_bias, norm_gain, doc_ids, cotangent):
    conv = conv_input[0]
    docb = jnp.broadcast_to(doc_ids[0].astype(BF16)[:, None], (T, LANES))
    halo = shifted(jnp.concatenate([conv[T - 8 :], docb[T - 8 :]], 1), 1)
    cots = lax.all_gather(cotangent[0], "y")
    act, msg, cum, step = call(
        front_kernel,
        "front",
        (shape((T, C_ALL), BF16), shape((MSG, INNER), BF16), shape((H, T)), shape((H, T))),
        [
            VMEM((T + 8, LANES), F32),
            VMEM((T + 8, LANES), F32),
            VMEM((3, T, LANES), F32),
            VMEM((T, INNER), BF16),
            VMEM((T + LANES, LANES), BF16),
        ],
        16,
        flops=10**9,
        moved=4 * 10**6,
        special=10**6,
    )(
        conv,
        halo,
        step_input[0],
        step_bias[:, None],
        log_rates[:, None],
        conv_weight,
        conv_bias[None],
        doc_ids,
        docb,
    )
    one = shifted(msg, 1)
    two = shifted(msg, 2)
    local, reach, sgate = call(
        middle_kernel,
        "middle",
        (shape((T, INNER)), shape((T, INNER)), shape((T, INNER))),
        [VMEM((T, T), F32), VMEM((T, LANES), BF16), VMEM((T, LANES), BF16)],
        24,
        flops=2 * 10**9,
        moved=12 * 10**6,
        special=4 * 10**6,
    )(act, cum, step, doc_ids, docb, halo, gate_input[0], jnp.repeat(skip_gain, HD)[None])
    normed, parts = call(
        back_kernel,
        "back",
        (shape((T, INNER), BF16), shape((4, T, INNER // 4), BF16)),
        [VMEM((T, INNER), F32), VMEM((T, LANES), F32)],
        24,
        flops=10**9,
        moved=12 * 10**6,
    )(local, reach, sgate, act, one, two, norm_gain[None])
    rows = lax.all_to_all(parts, "y", 0, 0)
    part = jnp.einsum("ytr,ytd->rd", rows, cots, preferred_element_type=F32)
    part = part.reshape(4, 2, 80, D)
    core = lax.axis_index("c")
    own = jnp.where(core == 0, part[:, 0], part[:, 1])
    send = jnp.where(core == 0, part[:, 1], part[:, 0]).astype(BF16)
    other = lax.ppermute(send, "c", [(0, 1), (1, 0)])
    packed = call(
        pack_kernel, "pack", shape((16, 200, LANES), BF16), [VMEM((16, 200, LANES), F32)], 12, moved=4 * 10**6
    )(own, other)
    pieces = lax.all_to_all(packed, ("x", "z"), 0, 0)
    grad = call(sum_kernel, "total", shape((20, D)), [VMEM((200, LANES), F32)], 8, moved=10**6)(pieces)
    return (normed[None], grad)


def solution(mesh):
    fine = Mesh(mesh.devices.reshape(4, 4, 2, 4), ("y", "x", "c", "z"))
    dp = ("y", "x", "c")
    in_specs = (
        P(dp, "z", None),
        P(dp, "z", None),
        P(dp, None, "z"),
        P(),
        P(),
        P(),
        P(),
        P(),
        P(),
        P(dp, "z"),
        P(dp, "z", None),
    )
    out_specs = (P(dp, "z", None), P(dp + ("z",), None))
    return jax.shard_map(per_device, mesh=fine, in_specs=in_specs, out_specs=out_specs, check_vma=False)
```

time: 614 us -> 126 us (0.21)
  the two profiles are of different devices: /device:TPU:6 before, /device:TPU:0 now
where the time goes in v1:
time: 126 us; the launch traced here: 125 us
  waiting for transfers between devices  36.8 us (29%)
  blocking collectives  22.3 us (18%)
  Pallas kernels  21 us (17%)
  starting transfers between devices  17.1 us (14%)
  between operations  14.2 us (11%)
  local copies, waits for them, and re-layouts  8.32 us (7%)
  matrix products  3.68 us (3%)
  other arithmetic  1.72 us (1%)
    all_to_all x1, blocking collectives, per_device(): pieces = lax.all_to_all(packed, ('x', 'z'), 0, 0)  22.3 us
    ppermute x3, waiting for transfers between devices, shifted(): return lax.ppermute(value, 'z', [(i, i + by) for i in range(4 - by)])  17.3 us
    all_to_all x1, waiting for transfers between devices, per_device(): rows = lax.all_to_all(parts, 'y', 0, 0)  16.7 us
    ppermute x3, starting transfers between devices, shifted(): return lax.ppermute(value, 'z', [(i, i + by) for i in range(4 - by)])  12.5 us
    pallas_call x1, Pallas kernels, per_device(): call(middle_kernel, 'middle', (shape((T, INNER)), shape((T, INNER)), shap...  8.02 us
    pallas_call x1, Pallas kernels, per_device(): call(back_kernel, 'back', (shape((T, INNER), BF16), shape((4, T, INNER //...  6.05 us
    pallas_call x1, Pallas kernels, per_device(): call(front_kernel, 'front', (shape((T, C_ALL), BF16), shape((MSG, INNER),...  5.9 us
    unnamed x16, local copies, waits for them, and re-layouts  4.92 us
  transfers between devices with their start and end apart: 6, of which 4 were waited for; matrix products, arithmetic and copies ran while one was open for 4% of the time, Pallas kernels for 16%

profile of v1, /device:TPU:0, one launch (start us, length us, event | category | flops | bytes accessed | tf_op | source)
XLA Modules:
  0.0 125.0 jit_solution(1152758092703993476)
XLA Ops:
  7.2 0.0 all-gather.2.cloned.1.call-start
  7.2 0.7 all-gather.2.cloned.1.call-update
  7.9 0.7 convert_element_type.21
  8.6 0.1 slice_bitcast_fusion.3
  8.7 0.8 slice_bitcast_fusion.2
  9.4 0.1 broadcast_in_dim.26
  9.5 3.9 %collective-permute-start = (bf16[8,2944]{1,0:T(8,128)(2,1)S(1)}, bf16[8,2944]{1,0:T(8,128)(2,1)S(1)}, u32[]{:S(2)}, u32[]{:S(2)}) collective-permute-start(bf16[8,2944]{1,0:T(8,128)(2,1)S(1)} %pad_maximum_fusion), channel_id=1, source_target_pairs={{0,1},{1,2},{2,3},{4,5},{5,6},{6,7},{8,9},{9,10},{10,11},{12,13},{... | collective-permute-start | bytes 141320 | tf_op jit(solution)/shard_map/ppermute | solution.py:228
  13.4 0.7 convert_reduce_fusion
  14.1 0.7 copy.21.bias
  14.9 0.7 copy.22.rates
  15.6 0.7 broadcast_in_dim.29.cb
  16.3 0.0 collective-permute-done.halo
  16.3 0.1 broadcast_in_dim.30.docb
  16.4 0.0 copy-start
  16.4 1.4 %copy-done = bf16[1,256,2816]{2,1,0:T(8,128)(2,1)S(1)} copy-done((bf16[1,256,2816]{2,1,0:T(8,128)(2,1)S(1)}, bf16[1,256,2816]{2,1,0:T(8,128)(2,1)}, u32[]{:S(2)}) %copy-start) | copy-done | bytes 1441816
  17.8 0.0 copy-start.1
  17.8 0.7 copy-done.1
  18.5 0.0 copy-start.4
  18.5 0.8 copy-done.4
  19.3 0.0 copy-start.5
  19.3 0.8 copy-done.5
  20.0 0.0 copy-start.7
  20.0 0.0 copy-start.6
  20.1 5.9 %front.1 = (bf16[256,2816]{1,0:T(8,128)(2,1)S(1)}, bf16[144,2560]{1,0:T(8,128)(2,1)}, f32[40,256]{1,0:T(8,128)S(1)}, f32[40,256]{1,0:T(8,128)S(1)}) custom-call(bf16[256,2816]{1,0:T(8,128)(2,1)S(1)} %bitcast.35, bf16[8,2944]{1,0:T(8,128)(2,1)S(1)} %collective-permute-done.halo, f32[40,256]{1,0:T(8,128)S(1)} %bitcast.37, f32[40,1]{1,0:T(8,128)S(1)} %copy.21.bias, ...), custom_call_target="tpu_custom_call" | custom-call | flops 1000000000 | bytes 4000000 | tf_op jit(solution)/shard_map/front/pallas_call | solution.py:236
  26.0 3.9 %collective-permute-start.1 = (bf16[144,2560]{1,0:T(8,128)(2,1)}, bf16[144,2560]{1,0:T(8,128)(2,1)S(1)}, u32[]{:S(2)}, u32[]{:S(2)}) collective-permute-start(bf16[144,2560]{1,0:T(8,128)(2,1)} %get-tuple-element.17), channel_id=1, source_target_pairs={{0,1},{1,2},{2,3},{4,5},{5,6},{6,7},{8,9},{9,10},{10,11},{12,13},{... | collective-permute-start | bytes 2211848 | tf_op jit(solution)/shard_map/ppermute | solution.py:228
  29.8 4.7 %collective-permute-start.2 = (bf16[144,2560]{1,0:T(8,128)(2,1)}, bf16[144,2560]{1,0:T(8,128)(2,1)S(1)}, u32[]{:S(2)}, u32[]{:S(2)}) collective-permute-start(bf16[144,2560]{1,0:T(8,128)(2,1)} %get-tuple-element.17), channel_id=1, source_target_pairs={{0,2},{1,3},{4,6},{5,7},{8,10},{9,11},{12,14},{13,15},{16,18},{17,... | collective-permute-start | bytes 2211848 | tf_op jit(solution)/shard_map/ppermute | solution.py:228
  34.6 0.0 copy-done.7
  34.6 0.1 broadcast_in_dim.31
  34.6 0.1 broadcast_in_dim_reshape.3.skip
  34.7 0.0 copy-done.6
  34.8 0.0 copy-done.2
  34.8 0.0 copy-start.3
  34.8 1.3 %copy-done.3 = bf16[1,256,2560]{2,1,0:T(8,128)(2,1)S(1)} copy-done((bf16[1,256,2560]{2,1,0:T(8,128)(2,1)S(1)}, bf16[1,256,2560]{2,1,0:T(8,128)(2,1)}, u32[]{:S(2)}) %copy-start.3) | copy-done | bytes 1310744
  36.1 8.0 %middle.1 = (f32[256,2560]{1,0:T(8,128)S(1)}, f32[256,2560]{1,0:T(8,128)S(1)}, f32[256,2560]{1,0:T(8,128)S(1)}) custom-call(bf16[256,2816]{1,0:T(8,128)(2,1)S(1)} %get-tuple-element.11.act, f32[40,256]{1,0:T(8,128)S(1)} %get-tuple-element.12.cum, f32[40,256]{1,0:T(8,128)S(1)} %get-tuple-element.13.step, s32[1,256]{1,0:T(1,128)S(1)} %copy-done.2, ...), custom_call_target="tpu_custom_call" | custom-call | flops 2000000000 | bytes 12000000 | tf_op jit(solution)/shard_map/middle/pallas_call | solution.py:264
  44.1 2.9 %collective-permute-done.1.one = bf16[144,2560]{1,0:T(8,128)(2,1)S(1)} collective-permute-done((bf16[144,2560]{1,0:T(8,128)(2,1)}, bf16[144,2560]{1,0:T(8,128)(2,1)S(1)}, u32[]{:S(2)}, u32[]{:S(2)}) %collective-permute-start.1) | collective-permute-done | bytes 737312 | tf_op jit(solution)/shard_map/ppermute | solution.py:228
  47.0 14.4 %collective-permute-done.2.two = bf16[144,2560]{1,0:T(8,128)(2,1)S(1)} collective-permute-done((bf16[144,2560]{1,0:T(8,128)(2,1)}, bf16[144,2560]{1,0:T(8,128)(2,1)S(1)}, u32[]{:S(2)}, u32[]{:S(2)}) %collective-permute-start.2) | collective-permute-done | bytes 737312 | tf_op jit(solution)/shard_map/ppermute | solution.py:228
  61.4 6.1 %back.1 = (bf16[256,2560]{1,0:T(8,128)(2,1)}, bf16[4,256,640]{2,1,0:T(8,128)(2,1)}) custom-call(f32[256,2560]{1,0:T(8,128)S(1)} %get-tuple-element.14.local, f32[256,2560]{1,0:T(8,128)S(1)} %get-tuple-element.15.reach, f32[256,2560]{1,0:T(8,128)S(1)} %get-tuple-element.16.sgate, bf16[256,2816]{1,0:T(8,128)(2,1)S(1)} %get-tuple-element.11.act, ...), custom_call_target="tpu_custom_call" | custom-call | flops 1000000000 | bytes 12000000 | tf_op jit(solution)/shard_map/back/pallas_call | solution.py:274
  67.4 4.5 %all-to-all-start = ((bf16[4,256,640]{2,1,0:T(8,128)(2,1)}), bf16[4,256,640]{2,1,0:T(8,128)(2,1)S(1)}, u32[]{:S(2)}, u32[]{:S(2)}) async-start(bf16[4,256,640]{2,1,0:T(8,128)(2,1)} %get-tuple-element.19), calls=%async_computation | async-start | bytes 2621440 | tf_op jit(solution)/shard_map/all_to_all | solution.py:283
  71.9 16.7 %all-to-all-done = bf16[4,256,640]{2,1,0:T(8,128)(2,1)S(1)} async-done(((bf16[4,256,640]{2,1,0:T(8,128)(2,1)}), bf16[4,256,640]{2,1,0:T(8,128)(2,1)S(1)}, u32[]{:S(2)}, u32[]{:S(2)}) %all-to-all-start) | async-done | bytes 1310752 | tf_op jit(solution)/shard_map/all_to_all | solution.py:283
  88.6 0.0 all-gather.2.cloned.1.call-done
  88.6 3.7 %fusion.1 = f32[640,1280,1]{1,0,2:T(8,128)S(1)} fusion(bf16[4,256,640]{2,1,0:T(8,128)(2,1)S(1)} %all-to-all-done, bf16[4,256,1280]{2,1,0:T(8,128)(2,1)} %all-gather.2.cloned.1.call-done), kind=kOutput, calls=%fused_computation.9 | convolution fusion | flops 1677721600 | bytes 7208960 | tf_op jit(solution)/shard_map/ytr,ytd->rd/dot_general | solution.py:284
  92.3 0.1 fusion
  92.5 0.1 collective-permute-start.3
  92.6 0.2 select_bitcast_fusion.own
  92.7 2.1 %collective-permute-done.3.other = bf16[4,80,1280]{2,1,0:T(8,128)(2,1)S(1)} collective-permute-done((bf16[4,80,1280]{2,1,0:T(8,128)(2,1)S(1)}, bf16[4,80,1280]{2,1,0:T(8,128)(2,1)S(1)}, u32[]{:S(2)}, u32[]{:S(2)}) %collective-permute-start.3) | collective-permute-done | bytes 819232 | tf_op jit(solution)/shard_map/ppermute | solution.py:289
  94.9 0.3 pack.1
  95.1 22.3 %all_to_all.10.pieces = bf16[16,200,128]{2,1,0:T(8,128)(2,1)S(1)} all-to-all(bf16[16,200,128]{2,1,0:T(8,128)(2,1)S(1)} %pack.1), channel_id=1, replica_groups=mesh['y'=4,'x'=4,'c'=2,'z'=4] {'x','z'}, dimensions={0} | all-to-all | bytes 1638400 | tf_op jit(solution)/shard_map/all_to_all | solution.py:293
  117.4 0.8 total.1
  (3 shorter events, 0.0 us)
Async XLA Ops:
  7.2 81.5 %all-gather.2.cloned.1.call-start = ((), (), s32[]{:S(2)}) async-start(), calls=%async_computation.2 | async-start | bytes 3276800 | tf_op jit(solution)/shard_map/all_gather | solution.py:235
  9.5 6.8 %collective-permute-start = (bf16[8,2944]{1,0:T(8,128)(2,1)S(1)}, bf16[8,2944]{1,0:T(8,128)(2,1)S(1)}, u32[]{:S(2)}, u32[]{:S(2)}) collective-permute-start(bf16[8,2944]{1,0:T(8,128)(2,1)S(1)} %pad_maximum_fusion), channel_id=1, source_target_pairs={{0,1},{1,2},{2,3},{4,5},{5,6},{6,7},{8,9},{9,10},{10,11},{12,13},{... | collective-permute-start | bytes 141320 | tf_op jit(solution)/shard_map/ppermute | solution.py:228
  16.4 1.4 %copy-start = (bf16[1,256,2816]{2,1,0:T(8,128)(2,1)S(1)}, bf16[1,256,2816]{2,1,0:T(8,128)(2,1)}, u32[]{:S(2)}) copy-start(bf16[1,256,2816]{2,1,0:T(8,128)(2,1)} %param.11) | copy-start | bytes 4325380
  17.8 0.7 copy-start.1
  18.5 0.8 copy-start.4
  19.3 0.8 copy-start.5
  20.0 14.5 %copy-start.7 = (f32[40]{0:T(128)S(1)}, f32[40]{0:T(128)}, u32[]{:S(2)}) copy-start(f32[40]{0:T(128)} %param.16) | copy-start | bytes 484
  20.0 14.7 %copy-start.6 = (f32[2560]{0:T(1024)S(1)}, f32[2560]{0:T(1024)}, u32[]{:S(2)}) copy-start(f32[2560]{0:T(1024)} %param.19) | copy-start | bytes 30724
  20.1 14.7 %copy-start.2 = (s32[1,256]{1,0:T(1,128)S(1)}, s32[1,256]{1,0:T(1,128)}, u32[]{:S(2)}) copy-start(s32[1,256]{1,0:T(1,128)} %doc_row.3) | copy-start | bytes 3076
  26.0 21.1 %collective-permute-start.1 = (bf16[144,2560]{1,0:T(8,128)(2,1)}, bf16[144,2560]{1,0:T(8,128)(2,1)S(1)}, u32[]{:S(2)}, u32[]{:S(2)}) collective-permute-start(bf16[144,2560]{1,0:T(8,128)(2,1)} %get-tuple-element.17), channel_id=1, source_target_pairs={{0,1},{1,2},{2,3},{4,5},{5,6},{6,7},{8,9},{9,10},{10,11},{12,13},{... | collective-permute-start | bytes 2211848 | tf_op jit(solution)/shard_map/ppermute | solution.py:228
  29.8 31.6 %collective-permute-start.2 = (bf16[144,2560]{1,0:T(8,128)(2,1)}, bf16[144,2560]{1,0:T(8,128)(2,1)S(1)}, u32[]{:S(2)}, u32[]{:S(2)}) collective-permute-start(bf16[144,2560]{1,0:T(8,128)(2,1)} %get-tuple-element.17), channel_id=1, source_target_pairs={{0,2},{1,3},{4,6},{5,7},{8,10},{9,11},{12,14},{13,15},{16,18},{17,... | collective-permute-start | bytes 2211848 | tf_op jit(solution)/shard_map/ppermute | solution.py:228
  34.8 1.3 %copy-start.3 = (bf16[1,256,2560]{2,1,0:T(8,128)(2,1)S(1)}, bf16[1,256,2560]{2,1,0:T(8,128)(2,1)}, u32[]{:S(2)}) copy-start(bf16[1,256,2560]{2,1,0:T(8,128)(2,1)} %param.12) | copy-start | bytes 3932164
  67.4 21.2 %all-to-all-start = ((bf16[4,256,640]{2,1,0:T(8,128)(2,1)}), bf16[4,256,640]{2,1,0:T(8,128)(2,1)S(1)}, u32[]{:S(2)}, u32[]{:S(2)}) async-start(bf16[4,256,640]{2,1,0:T(8,128)(2,1)} %get-tuple-element.19), calls=%async_computation | async-start | bytes 2621440 | tf_op jit(solution)/shard_map/all_to_all | solution.py:283
  92.5 2.4 %collective-permute-start.3 = (bf16[4,80,1280]{2,1,0:T(8,128)(2,1)S(1)}, bf16[4,80,1280]{2,1,0:T(8,128)(2,1)S(1)}, u32[]{:S(2)}, u32[]{:S(2)}) collective-permute-start(bf16[4,80,1280]{2,1,0:T(8,128)(2,1)S(1)} %fusion), channel_id=1, source_target_pairs={{0,4},{4,0},{1,5},{5,1},{2,6},{6,2},{3,7},{7,3},{8,12},{12,8},{9,1... | collective-permute-start | bytes 2457608 | tf_op jit(solution)/shard_map/ppermute | solution.py:289
Sparse Core Ops, SparseCore 0:
  9.7 37.6 all-gather.1

commit v2 on v1

v2 whole, which is shorter than its diff:
```python
import jax
import jax.numpy as jnp
from jax import lax
from jax.experimental import pallas as pl
from jax.experimental.pallas import tpu as pltpu
from jax.sharding import Mesh
from jax.sharding import PartitionSpec as P

T = 256
H = 40
HD = 64
N = 128
INNER = 2560
C_ALL = 2816
D = 1280
LANES = 128
XCHUNKS = INNER // LANES
MSG = N + 16
F32 = jnp.float32
BF16 = jnp.bfloat16
HIGH = lax.Precision.HIGHEST
VMEM = pltpu.VMEM


def silu(v):
    return 0.5 * v * (1.0 + jnp.tanh(0.5 * v))


def dot(a, b, dims=((1,), (0,)), precision=None):
    return lax.dot_general(a, b, (dims, ((), ())), preferred_element_type=F32, precision=precision)


def split_rows(v):
    hi = v.astype(BF16).astype(F32)
    rest = v - hi
    mid = rest.astype(BF16).astype(F32)
    low = rest - mid
    return jnp.concatenate([hi, mid, low, jnp.zeros((8, v.shape[1]), F32)], 0)


def head_pick(chunk, width):
    rows = lax.broadcasted_iota(jnp.int32, (LANES, width), 0)
    rows = jnp.where(rows >= 2 * H, rows - 2 * H, jnp.where(rows >= H, rows - H, rows))
    real = lax.broadcasted_iota(jnp.int32, (LANES, width), 0) < 3 * H
    lanes = lax.broadcasted_iota(jnp.int32, (LANES, width), 1)
    head = 2 * chunk + jnp.where(lanes >= width // 2, 1, 0)
    return jnp.where(jnp.logical_and(real, rows == head), 1.0, 0.0).astype(BF16)


def column(row, width):
    n = row.shape[1]
    diag = lax.broadcasted_iota(jnp.int32, (n, n), 0) == lax.broadcasted_iota(jnp.int32, (n, n), 1)
    diag = jnp.where(diag, jnp.broadcast_to(row, (n, n)), 0.0).astype(BF16)
    return dot(diag, jnp.ones((n, width), BF16))


def upright(row):
    n = row.shape[1]
    diag = lax.broadcasted_iota(jnp.int32, (n, n), 0) == lax.broadcasted_iota(jnp.int32, (n, n), 1)
    return jnp.sum(jnp.where(diag, jnp.broadcast_to(row, (n, n)), 0.0), axis=1, keepdims=True)


def edge_kernel(rows, docs, out):
    out[:, 0:C_ALL] = rows[8:16, :]
    out[:, C_ALL:] = column(docs[...].astype(F32), LANES)[T - 8 :].astype(BF16)


def front_kernel(conv, step_in, bias, rates, w, cb, docs, act, state, info, top, cum_o, step_o, win, dwin, masks, xs, fac):
    step = jax.nn.softplus(step_in[...] + upright(bias[...]))
    decay = -jnp.exp(upright(rates[...])) * step
    tri = (
        lax.broadcasted_iota(jnp.int32, (T, T), 0) <= lax.broadcasted_iota(jnp.int32, (T, T), 1)
    ).astype(F32)
    cum = dot(decay, tri, precision=HIGH)
    cum_o[...] = cum
    step_o[...] = step
    doc_row = docs[...].astype(F32)
    tail = (doc_row == doc_row[:, T - 1 : T]).astype(F32)
    total = cum[:, T - 1 : T]
    factor = step * jnp.exp(total - cum) * tail
    whole = jnp.broadcast_to(jnp.exp(total), (H, LANES))
    fac[...] = split_rows(jnp.concatenate([factor, whole], 1)).T.astype(BF16)
    docb = column(doc_row, LANES)
    dwin[0:8, :] = jnp.zeros((8, LANES), F32)
    dwin[8:, :] = docb
    for k in range(3):
        masks[k] = (dwin[5 + k : 5 + k + T, :] == docb).astype(F32)
    tag = docb[T - 8 :][7:8]
    win[:, 0:8, :] = jnp.zeros((2, 8, LANES), F32)
    xs[0:16, :] = jnp.zeros((16, INNER), BF16)

    def conv_chunk(j, slot):
        at = pl.ds(pl.multiple_of(j * LANES, LANES), LANES)
        win[slot, 8:, :] = conv[:, at].astype(F32)
        taps = w[:, at]
        total = cb[:, at] + taps[3:4] * win[slot, 8:, :]
        for k in range(3):
            total = total + (taps[k : k + 1] * win[slot, 5 + k : 5 + k + T, :]) * masks[k]
        out = silu(total).astype(BF16)
        act[:, at] = out
        return at, out

    def value_chunk(j, slot):
        at, out = conv_chunk(j, slot)
        wide = dot(fac[0 : T + 16, :], head_pick(j, LANES))
        xs[16:, at] = (out[16:].astype(F32) * wide[16:T]).astype(BF16)
        top[:, at] = wide[0:16]
        row = lax.broadcasted_iota(jnp.int32, (16, LANES), 0)
        end = wide[T : T + 16]
        hi = end.astype(BF16).astype(F32)
        rows = jnp.where(row == 0, hi, jnp.where(row == 1, end - hi, jnp.where(row == 2, tag, 0.0)))
        info[:, at] = rows.astype(BF16)

    def value_pair(i, carry):
        for slot in range(2):
            value_chunk(2 * i + slot, slot)
        return carry

    for slot in range(2):
        conv_chunk(XCHUNKS + slot, slot)
    lax.fori_loop(0, XCHUNKS // 2, value_pair, 0)
    b_t = act[:, INNER : INNER + N].astype(F32).T.astype(BF16)
    for k in range(5):
        at = slice(512 * k, 512 * k + 512)
        state[:, at] = dot(b_t, xs[:, at])


def fix_kernel(halo, rows, w, cb, docs, old, state, info, top, act, msg):
    own = column(docs[...].astype(F32), LANES)[0:16]
    joined = jnp.concatenate([halo[:, C_ALL:].astype(F32), own], 0)
    masks = [(joined[5 + k : 21 + k] == own).astype(F32) for k in range(3)]

    def chunk(j):
        at = slice(j * LANES, j * LANES + LANES)
        win = jnp.concatenate([halo[:, at].astype(F32), rows[:, at].astype(F32)], 0)
        total = cb[:, at] + w[3:4, at] * win[8:24]
        for k in range(3):
            total = total + (w[k : k + 1, at] * win[5 + k : 21 + k]) * masks[k]
        out = silu(total).astype(BF16)
        act[:, at] = out
        return at, out

    _, b_rows = chunk(XCHUNKS)
    chunk(XCHUNKS + 1)
    b_t = jnp.concatenate([b_rows.astype(F32), jnp.zeros((LANES - 16, LANES), F32)], 0).T.astype(BF16)
    for j in range(XCHUNKS):
        at, out = chunk(j)
        scaled = (out.astype(F32) * top[:, at]).astype(BF16)
        scaled = jnp.concatenate([scaled, jnp.zeros((LANES - 16, LANES), BF16)], 0)
        msg[0:N, at] = (state[:, at] + dot(b_t, scaled)).astype(BF16)
        msg[N:, at] = info[:, at]


def middle_kernel(act, cum, step, docs, halo, gate, skip, local, reach, sgate, scores, fac, efac):
    doc_row = docs[...].astype(F32)
    c_map = act[:, INNER + N :]
    b_map = act[:, INNER : INNER + N]
    doc_col = column(doc_row, LANES)
    for s in range(2):
        at = slice(s * LANES, s * LANES + LANES)
        g = dot(c_map, b_map[at], ((1,), (1,)))
        order = lax.broadcasted_iota(jnp.int32, (T, LANES), 0) >= (
            lax.broadcasted_iota(jnp.int32, (T, LANES), 1) + s * LANES
        )
        same = jnp.logical_and(order, doc_col == doc_row[:, at])
        scores[:, at] = jnp.where(same, g, 0.0)
    all_cum = cum[...]
    fac[...] = split_rows(all_cum).T.astype(BF16)
    prev_tag = halo[:, C_ALL : C_ALL + LANES].astype(F32)[7:8, :]
    prev_tag = jnp.concatenate([prev_tag, prev_tag], 1)
    matched = (doc_row == prev_tag).astype(F32)
    efac[...] = split_rows(jnp.exp(all_cum) * matched).T.astype(BF16)
    half = T // 2

    def pair(j, carry):
        at = pl.ds(pl.multiple_of(j * LANES, LANES), LANES)
        vals = act[:, at]
        lanes = lax.broadcasted_iota(jnp.int32, (T, LANES), 1)
        cols = dot(fac[...], head_pick(j, 2 * LANES))
        top = jnp.zeros((half, LANES), F32)
        low = jnp.zeros((half, LANES), F32)
        for k in range(2):
            mine = jnp.where((lanes >= HD) == (k == 1), vals.astype(F32), 0.0).astype(BF16)
            col = cols[:, k * LANES : (k + 1) * LANES]
            row = cum[pl.ds(2 * j + k, 1), :]
            size = step[pl.ds(2 * j + k, 1), :]

            def weights(t, s):
                ts = slice(t * half, t * half + half)
                ss = slice(s * LANES, s * LANES + LANES)
                spread = jnp.minimum(col[ts] - row[:, ss], 0.0)
                return (scores[ts, ss] * jnp.exp(spread) * size[:, ss]).astype(BF16)

            top = top + dot(weights(0, 0), mine[0:half])
            low = low + dot(jnp.concatenate([weights(1, 0), weights(1, 1)], 1), mine)
        gain = skip[:, at]
        local[0:half, at] = top + gain * vals[0:half].astype(F32)
        local[half:, at] = low + gain * vals[half:].astype(F32)
        reach[:, at] = dot(efac[...], head_pick(j, LANES))
        sgate[:, at] = silu(gate[:, at].astype(F32))
        return carry

    lax.fori_loop(0, XCHUNKS, pair, 0)


def back_kernel(local, reach, sgate, act, one, two, gain, place, normed, mine, give, gated, squares, turned):
    c_map = act[:, INNER + N :]
    squares[...] = jnp.zeros_like(squares)

    def first(j):
        at = pl.ds(pl.multiple_of(j * LANES, LANES), LANES)
        info = one[N:, at].astype(F32)
        other = two[N:, at].astype(F32)
        linked = (info[2:3] == other[2:3]).astype(F32)
        weight = (info[0:1] + info[1:2]) * linked
        state = one[0:N, at].astype(F32) + weight * two[0:N, at].astype(F32)
        reading = dot(c_map, state.astype(BF16))
        mixed = local[:, at] + reading * reach[:, at]
        value = mixed.astype(BF16).astype(F32) * sgate[:, at]
        gated[:, at] = value
        return value * value

    def first_pair(i, carry):
        squares[...] += first(2 * i) + first(2 * i + 1)
        return carry

    lax.fori_loop(0, XCHUNKS // 2, first_pair, 0)
    mean = jnp.sum(squares[...], axis=1, keepdims=True) * (1.0 / INNER)
    squares[...] = jnp.broadcast_to(lax.rsqrt(mean + 1e-05), squares.shape)
    eye = (
        lax.broadcasted_iota(jnp.int32, (LANES, LANES), 0) == lax.broadcasted_iota(jnp.int32, (LANES, LANES), 1)
    ).astype(BF16)

    def second(i, carry):
        for k in range(2):
            at = pl.ds(pl.multiple_of((2 * i + k) * LANES, LANES), LANES)
            value = (gated[:, at] * squares[...] * gain[:, at]).astype(BF16)
            normed[:, at] = value
            turned[at, :] = dot(eye, value, ((1,), (1,))).astype(BF16)
        return carry

    lax.fori_loop(0, XCHUNKS // 2, second, 0)
    y, x, c = place[0], place[1], place[2]

    def deal(i, carry):
        far_y, far_x = lax.rem(i // 4 - y + 4, 4), lax.rem(lax.rem(i, 4) - x + 4, 4)
        blocks = [turned[pl.ds(pl.multiple_of(160 * i + 80 * k, 16), 80), :] for k in range(2)]

        @pl.when(c == 0)
        def _():
            mine[far_y, far_x] = blocks[0]
            give[far_x, far_y] = blocks[1]

        @pl.when(c == 1)
        def _():
            give[far_y, far_x] = blocks[0]
            mine[far_x, far_y] = blocks[1]

        return carry

    lax.fori_loop(0, 16, deal, 0)


def grad_kernel(mine, got, r1, r2, r3, c0, c1, c2, c3, keep, s1, s2, s3):
    left = [mine[0].reshape(320, T), got[0].reshape(320, T)]
    right = [c0[0], c0[1]]
    for r, c in ((r1, c1), (r2, c2), (r3, c3)):
        for k in range(2):
            left.append(r[k].reshape(320, T))
            right.append(c[k])
    for n in range(5):
        at = slice(256 * n, 256 * n + 256)
        total = dot(left[0], right[0][:, at])
        for k in range(1, 8):
            total = total + dot(left[k], right[k][:, at])
        keep[:, at] = total[0:80]
        for k, out in enumerate((s1, s2, s3)):
            out[:, at] = total[80 * k + 80 : 80 * k + 160].astype(BF16)


def join_kernel(keep, r1, r2, r3, out, total, flat):
    total[...] = keep[...] + r1[...].astype(F32) + r2[...].astype(F32) + r3[...].astype(F32)
    for z in range(4):
        for k in range(10):
            flat[z, 20 * k : 20 * k + 20, :] = total[20 * z : 20 * z + 20, k * LANES : k * LANES + LANES]
        out[z] = flat[z].astype(BF16)


def sum_kernel(pieces, out, flat):
    total = pieces[0].astype(F32)
    for i in range(1, 4):
        total = total + pieces[i].astype(F32)
    flat[...] = total
    for k in range(10):
        out[:, k * LANES : k * LANES + LANES] = flat[20 * k : 20 * k + 20, :]


def call(kernel, name, out, scratch, limit, flops=0, moved=0, special=0, **kw):
    return pl.pallas_call(
        kernel,
        name=name,
        out_shape=out,
        scratch_shapes=scratch,
        compiler_params=pltpu.CompilerParams(vmem_limit_bytes=limit << 20),
        cost_estimate=pl.CostEstimate(flops=flops, bytes_accessed=moved, transcendentals=special),
        **kw,
    )


def shape(dims, kind=F32):
    return jax.ShapeDtypeStruct(dims, kind)


def shifted(value, by):
    return lax.ppermute(value, "z", [(i, i + by) for i in range(4 - by)])


def around(value, by, first_axis):
    pairs = []
    for y in range(4):
        for x in range(4):
            for c in range(2):
                along_y = (c == 0) == (first_axis == "y")
                to_y, to_x = ((y + by) % 4, x) if along_y else (y, (x + by) % 4)
                pairs.append(((y * 4 + x) * 2 + c, (to_y * 4 + to_x) * 2 + c))
    return lax.ppermute(value, ("y", "x", "c"), pairs)


def swapped(value):
    return lax.ppermute(value, "c", [(0, 1), (1, 0)])


def whole(dims):
    return pl.BlockSpec(dims, lambda i: (0,) * len(dims))


def per_device(conv_input, gate_input, step_input, step_bias, log_rates, skip_gain, conv_weight, conv_bias, norm_gain, doc_ids, cotangent):
    conv = conv_input[0]
    halo = call(
        edge_kernel,
        "edge",
        shape((8, C_ALL + LANES), BF16),
        [],
        8,
        moved=10**5,
        grid=(1,),
        in_specs=[pl.BlockSpec((16, C_ALL), lambda i: (T // 16 - 1, 0)), whole((1, T))],
        out_specs=whole((8, C_ALL + LANES)),
    )(conv, doc_ids)
    halo = shifted(halo, 1)
    cots = jnp.stack([cotangent[0], swapped(cotangent[0])])
    place = jnp.stack([lax.axis_index(a) for a in ("y", "x", "c")]).astype(jnp.int32)
    act, state, info, top, cum, step = call(
        front_kernel,
        "front",
        (
            shape((T, C_ALL), BF16),
            shape((N, INNER)),
            shape((16, INNER), BF16),
            shape((16, INNER)),
            shape((H, T)),
            shape((H, T)),
        ),
        [
            VMEM((2, T + 8, LANES), F32),
            VMEM((T + 8, LANES), F32),
            VMEM((3, T, LANES), F32),
            VMEM((T, INNER), BF16),
            VMEM((T + LANES, LANES), BF16),
        ],
        16,
        flops=10**9,
        moved=4 * 10**6,
        special=10**6,
    )(conv, step_input[0], step_bias[None], log_rates[None], conv_weight, conv_bias[None], doc_ids)
    act, msg = call(
        fix_kernel,
        "fix",
        (shape((T, C_ALL), BF16), shape((MSG, INNER), BF16)),
        [],
        8,
        moved=2 * 10**6,
        grid=(1,),
        in_specs=[
            whole((8, C_ALL + LANES)),
            whole((16, C_ALL)),
            whole((4, C_ALL)),
            whole((1, C_ALL)),
            whole((1, T)),
            whole((16, C_ALL)),
            whole((N, INNER)),
            whole((16, INNER)),
            whole((16, INNER)),
        ],
        out_specs=(whole((16, C_ALL)), whole((MSG, INNER))),
        input_output_aliases={5: 0},
    )(halo, conv, conv_weight, conv_bias[None], doc_ids, act, state, info, top)
    one = shifted(msg, 1)
    two = shifted(msg, 2)
    c1, c2, c3 = [around(cots, k, "y") for k in (1, 2, 3)]
    local, reach, sgate = call(
        middle_kernel,
        "middle",
        (shape((T, INNER)), shape((T, INNER)), shape((T, INNER))),
        [VMEM((T, T), F32), VMEM((T, LANES), BF16), VMEM((T, LANES), BF16)],
        24,
        flops=2 * 10**9,
        moved=12 * 10**6,
        special=4 * 10**6,
    )(act, cum, step, doc_ids, halo, gate_input[0], jnp.repeat(skip_gain, HD)[None])
    block = (4, 4, 80, T)
    vmem = pl.BlockSpec(memory_space=VMEM)
    normed, mine, give = call(
        back_kernel,
        "back",
        (shape((T, INNER), BF16), shape(block, BF16), shape(block, BF16)),
        [VMEM((T, INNER), F32), VMEM((T, LANES), F32), VMEM((INNER, T), BF16)],
        24,
        flops=10**9,
        moved=12 * 10**6,
        in_specs=[vmem] * 7 + [pl.BlockSpec(memory_space=pltpu.SMEM)],
    )(local, reach, sgate, act, one, two, norm_gain[None], place)
    got = swapped(give)
    r1, r2, r3 = [around(jnp.stack([mine[k], got[k]]), k, "y") for k in (1, 2, 3)]
    keep, s1, s2, s3 = call(
        grad_kernel,
        "grad",
        (shape((80, D)),) + (shape((80, D), BF16),) * 3,
        [],
        24,
        flops=2 * 10**9,
        moved=8 * 10**6,
    )(mine, got, r1, r2, r3, cots, c1, c2, c3)
    t1, t2, t3 = [around(v, k, "x") for k, v in ((1, s1), (2, s2), (3, s3))]
    packed = call(
        join_kernel,
        "join",
        shape((4, 200, LANES), BF16),
        [VMEM((80, D), F32), VMEM((4, 200, LANES), F32)],
        8,
        moved=10**6,
    )(keep, t1, t2, t3)
    pieces = lax.all_to_all(packed, "z", 0, 0)
    grad = call(sum_kernel, "total", shape((20, D)), [VMEM((200, LANES), F32)], 8, moved=10**6)(pieces)
    return (normed[None], grad)


def solution(mesh):
    fine = Mesh(mesh.devices.reshape(4, 4, 2, 4), ("y", "x", "c", "z"))
    dp = ("y", "x", "c")
    in_specs = (
        P(dp, "z", None),
        P(dp, "z", None),
        P(dp, None, "z"),
        P(),
        P(),
        P(),
        P(),
        P(),
        P(),
        P(dp, "z"),
        P(dp, "z", None),
    )
    out_specs = (P(dp, "z", None), P(dp + ("z",), None))
    return jax.shard_map(per_device, mesh=fine, in_specs=in_specs, out_specs=out_specs, check_vma=False)
```

time: 126 us -> 131 us (1.040)
  waiting for transfers between devices: 36.8 us -> 61.2 us
  between operations: 14.2 us -> 0.87 us
  blocking collectives: 22.3 us -> 11.4 us
  starting transfers between devices: 17.1 us -> 26.7 us
  matrix products: 3.68 us -> 0 us
  local copies, waits for them, and re-layouts: 8.32 us -> 5.12 us
  Pallas kernels: 21 us -> 23.3 us
    ppermute x1 -> x11, waiting for transfers between devices: 2.13 us -> 42.9 us  [the longest x9 42.9 us: around(): return lax.ppermute(value, ('y', 'x', 'c'), pairs)]
    all_to_all x1 -> x0, waiting for transfers between devices: 16.7 us -> none  [per_device(): rows = lax.all_to_all(parts, 'y', 0, 0)]
    ppermute x1 -> x11, starting transfers between devices: 0.09 us -> 15.2 us  [the longest x9 15.1 us: around(): return lax.ppermute(value, ('y', 'x', 'c'), pairs)]
    all_to_all x1, blocking collectives: 22.3 us -> 11.4 us  [per_device(): pieces = lax.all_to_all(packed, 'z', 0, 0)]
    all_to_all x1 -> x0, starting transfers between devices: 4.47 us -> none  [per_device(): rows = lax.all_to_all(parts, 'y', 0, 0)]
    dot_general x1 -> x0, matrix products: 3.68 us -> none  [per_device(): part = jnp.einsum('ytr,ytd->rd', rows, cots, preferred_element_type=F32)]
    pallas_call x3 -> x6, Pallas kernels: 12.2 us -> 14.6 us  [the longest x1 6.98 us: per_device(): call(back_kernel, 'back', (shape((T, INNER), BF16), shape(block, BF16), s...]
    broadcast_in_dim x4 -> x0, local copies, waits for them, and re-layouts: 1.65 us -> none  [the longest x1 0.74 us: per_device(): step_bias[:, None]]
  transfers between devices with their start and end apart: 6 -> 14, of which waited for: 4 -> 6; matrix products, arithmetic and copies ran while one was open for 4% -> 2% of each run, Pallas kernels for 16% -> 15%
where the time goes in v2:
time: 131 us; the launch traced here: 130 us
  waiting for transfers between devices  61.2 us (47%)
  starting transfers between devices  26.7 us (20%)
  Pallas kernels  23.3 us (18%)
  blocking collectives  11.4 us (9%)
  local copies, waits for them, and re-layouts  5.12 us (4%)
  other arithmetic  1.58 us (1%)
    ppermute x9, waiting for transfers between devices, around(): return lax.ppermute(value, ('y', 'x', 'c'), pairs)  42.9 us
    ppermute x3, waiting for transfers between devices, shifted(): return lax.ppermute(value, 'z', [(i, i + by) for i in range(4 - by)])  18.2 us
    ppermute x9, starting transfers between devices, around(): return lax.ppermute(value, ('y', 'x', 'c'), pairs)  15.1 us
    ppermute x3, starting transfers between devices, shifted(): return lax.ppermute(value, 'z', [(i, i + by) for i in range(4 - by)])  11.5 us
    all_to_all x1, blocking collectives, per_device(): pieces = lax.all_to_all(packed, 'z', 0, 0)  11.4 us
    pallas_call x1, Pallas kernels, per_device(): call(middle_kernel, 'middle', (shape((T, INNER)), shape((T, INNER)), shap...  8.03 us
    pallas_call x1, Pallas kernels, per_device(): call(back_kernel, 'back', (shape((T, INNER), BF16), shape(block, BF16), s...  6.98 us
    unnamed x22, local copies, waits for them, and re-layouts  4.17 us
  transfers between devices with their start and end apart: 14, of which 6 were waited for; matrix products, arithmetic and copies ran while one was open for 2% of the time, Pallas kernels for 15%

profile of v2, /device:TPU:0, one launch (start us, length us, event | category | flops | bytes accessed | tf_op | source)
XLA Modules:
  0.0 130.1 jit_solution(8231302364472954962)
XLA Ops:
  0.7 1.4 %copy-done = bf16[1,256,2816]{2,1,0:T(8,128)(2,1)S(1)} copy-done((bf16[1,256,2816]{2,1,0:T(8,128)(2,1)S(1)}, bf16[1,256,2816]{2,1,0:T(8,128)(2,1)}, u32[]{:S(2)}) %copy-start) | copy-done | bytes 1441816
  2.0 0.7 copy-done.3
  2.7 0.2 edge.1
  2.9 4.0 %collective-permute-start = (bf16[8,2944]{1,0:T(8,128)(2,1)S(1)}, bf16[8,2944]{1,0:T(8,128)(2,1)S(1)}, u32[]{:S(2)}, u32[]{:S(2)}) collective-permute-start(bf16[8,2944]{1,0:T(8,128)(2,1)S(1)} %edge.1), channel_id=1, source_target_pairs={{0,1},{1,2},{2,3},{4,5},{5,6},{6,7},{8,9},{9,10},{10,11},{12,13},{... | collective-permute-start | bytes 141320 | tf_op jit(solution)/shard_map/ppermute | solution.py:315
  6.9 0.7 broadcast_in_dim.19.cb
  7.7 0.0 copy-start.6
  7.7 0.8 copy-done.6
  8.5 3.9 %front.1 = (bf16[256,2816]{1,0:T(8,128)(2,1)S(1)}, f32[128,2560]{1,0:T(8,128)S(1)}, bf16[16,2560]{1,0:T(8,128)(2,1)S(1)}, f32[16,2560]{1,0:T(8,128)S(1)}, f32[40,256]{1,0:T(8,128)S(1)}, /*index=5*/f32[40,256]{1,0:T(8,128)S(1)}) custom-call(bf16[256,2816]{1,0:T(8,128)(2,1)S(1)} %bitcast.12, f32[40,256]{1,0:T(8,128)S(1)} %bitcast.15, f32[1,40]{1,0:T(1,128)S(1)} %bitcast.16, ...), custom_call_target="tpu_custom_call" | custom-call | flops 1000000000 | bytes 4000000 | tf_op jit(solution)/shard_map/front/pallas_call | solution.py:353
  12.4 0.0 collective-permute-done.halo
  12.4 0.0 copy-start.10
  12.4 0.0 copy-start.9
  12.4 0.0 copy-start.4
  12.4 1.5 %fix.1 = (bf16[256,2816]{1,0:T(8,128)(2,1)S(1)}, bf16[144,2560]{1,0:T(8,128)(2,1)}) custom-call(bf16[8,2944]{1,0:T(8,128)(2,1)S(1)} %collective-permute-done.halo, bf16[256,2816]{1,0:T(8,128)(2,1)S(1)} %bitcast.13, f32[4,2816]{1,0:T(4,128)S(1)} %copy-done.2, f32[1,2816]{1,0:T(1,128)S(1)} %broadcast_in_dim.19.cb, ...), custom_call_target="tpu_custom_call", output_to_operand_aliasing={{0}: (5, {})} | custom-call | bytes 2000000 | tf_op jit(solution)/shard_map/fix/pallas_call | solution.py:376
  13.9 3.9 %collective-permute-start.1 = (bf16[144,2560]{1,0:T(8,128)(2,1)}, bf16[144,2560]{1,0:T(8,128)(2,1)S(1)}, u32[]{:S(2)}, u32[]{:S(2)}) collective-permute-start(bf16[144,2560]{1,0:T(8,128)(2,1)} %get-tuple-element.30), channel_id=1, source_target_pairs={{0,1},{1,2},{2,3},{4,5},{5,6},{6,7},{8,9},{9,10},{10,11},{12,13},{... | collective-permute-start | bytes 2211848 | tf_op jit(solution)/shard_map/ppermute | solution.py:315
  17.8 3.6 %collective-permute-start.2 = (bf16[144,2560]{1,0:T(8,128)(2,1)}, bf16[144,2560]{1,0:T(8,128)(2,1)S(1)}, u32[]{:S(2)}, u32[]{:S(2)}) collective-permute-start(bf16[144,2560]{1,0:T(8,128)(2,1)} %get-tuple-element.30), channel_id=1, source_target_pairs={{0,2},{1,3},{4,6},{5,7},{8,10},{9,11},{12,14},{13,15},{16,18},{17,... | collective-permute-start | bytes 2211848 | tf_op jit(solution)/shard_map/ppermute | solution.py:315
  21.4 0.1 collective-permute-start.7
  21.5 0.1 broadcast_in_dim.22
  21.6 0.1 broadcast_in_dim_reshape.3.skip
  21.7 0.1 pad_add_fusion.place
  21.8 1.3 %copy-done.5 = bf16[1,256,2560]{2,1,0:T(8,128)(2,1)S(1)} copy-done((bf16[1,256,2560]{2,1,0:T(8,128)(2,1)S(1)}, bf16[1,256,2560]{2,1,0:T(8,128)(2,1)}, u32[]{:S(2)}) %copy-start.5) | copy-done | bytes 1310744
  23.1 8.0 %middle.1 = (f32[256,2560]{1,0:T(8,128)S(1)}, f32[256,2560]{1,0:T(8,128)S(1)}, f32[256,2560]{1,0:T(8,128)S(1)}) custom-call(bf16[256,2816]{1,0:T(8,128)(2,1)S(1)} %get-tuple-element.24.act, f32[40,256]{1,0:T(8,128)S(1)} %get-tuple-element.25.cum, f32[40,256]{1,0:T(8,128)S(1)} %get-tuple-element.26.step, s32[1,256]{1,0:T(1,128)S(1)} %copy-done.4, ...), custom_call_target="tpu_custom_call" | custom-call | flops 2000000000 | bytes 12000000 | tf_op jit(solution)/shard_map/middle/pallas_call | solution.py:401
  31.1 3.8 %collective-permute-done.1.one = bf16[144,2560]{1,0:T(8,128)(2,1)S(1)} collective-permute-done((bf16[144,2560]{1,0:T(8,128)(2,1)}, bf16[144,2560]{1,0:T(8,128)(2,1)S(1)}, u32[]{:S(2)}, u32[]{:S(2)}) %collective-permute-start.1) | collective-permute-done | bytes 737312 | tf_op jit(solution)/shard_map/ppermute | solution.py:315
  35.0 14.4 %collective-permute-done.2.two = bf16[144,2560]{1,0:T(8,128)(2,1)S(1)} collective-permute-done((bf16[144,2560]{1,0:T(8,128)(2,1)}, bf16[144,2560]{1,0:T(8,128)(2,1)S(1)}, u32[]{:S(2)}, u32[]{:S(2)}) %collective-permute-start.2) | collective-permute-done | bytes 737312 | tf_op jit(solution)/shard_map/ppermute | solution.py:315
  49.3 7.0 %back.1 = (bf16[256,2560]{1,0:T(8,128)(2,1)}, bf16[4,4,80,256]{3,2,1,0:T(8,128)(2,1)S(1)}, bf16[4,4,80,256]{3,2,1,0:T(8,128)(2,1)S(1)}) custom-call(f32[256,2560]{1,0:T(8,128)S(1)} %get-tuple-element.27.local, f32[256,2560]{1,0:T(8,128)S(1)} %get-tuple-element.28.reach, f32[256,2560]{1,0:T(8,128)S(1)} %get-tuple-element.29.sgate, ...), custom_call_target="tpu_custom_call" | custom-call | flops 1000000000 | bytes 12000000 | tf_op jit(solution)/shard_map/back/pallas_call | solution.py:413
  56.3 0.0 collective-permute-start.3
  56.3 0.0 collective-permute-done.7
  56.3 1.4 %pad_maximum_fusion.c0 = bf16[2,256,1280]{2,1,0:T(8,128)(2,1)S(1)} fusion(bf16[1,256,1280]{2,1,0:T(8,128)(2,1)} %bitcast.10, bf16[1,256,1280]{2,1,0:T(8,128)(2,1)} %param.21), kind=kLoop, calls=%fused_computation | loop fusion | flops 655360 | bytes 2621440 | tf_op jit(solution)/shard_map/stack | solution.py:351
  57.7 3.1 %collective-permute-start.10 = (bf16[2,256,1280]{2,1,0:T(8,128)(2,1)S(1)}, bf16[2,256,1280]{2,1,0:T(8,128)(2,1)S(1)}, u32[]{:S(2)}, u32[]{:S(2)}) collective-permute-start(bf16[2,256,1280]{2,1,0:T(8,128)(2,1)S(1)} %pad_maximum_fusion.c0), channel_id=1, source_target_pairs={{0,96},{4,28},{8,104},{12,4},{16,112},{20,12},{24,120},{28,20},{32... | collective-permute-start | bytes 3932168 | tf_op jit(solution)/shard_map/ppermute | solution.py:326
  60.8 0.0 collective-permute-start.8
  60.8 2.2 %collective-permute-start.9 = (bf16[2,256,1280]{2,1,0:T(8,128)(2,1)S(1)}, bf16[2,256,1280]{2,1,0:T(8,128)(2,1)S(1)}, u32[]{:S(2)}, u32[]{:S(2)}) collective-permute-start(bf16[2,256,1280]{2,1,0:T(8,128)(2,1)S(1)} %pad_maximum_fusion.c0), channel_id=1, source_target_pairs={{0,64},{4,20},{8,72},{12,28},{16,80},{20,4},{24,88},{28,12},{32,96... | collective-permute-start | bytes 3932168 | tf_op jit(solution)/shard_map/ppermute | solution.py:326
  63.1 0.0 collective-permute-done.3.got
  63.2 1.1 collective-permute-start.6
  64.3 3.0 %collective-permute-start.5 = (bf16[2,4,80,256]{3,2,1,0:T(8,128)(2,1)S(1)}, bf16[2,4,80,256]{3,2,1,0:T(8,128)(2,1)S(1)}, u32[]{:S(2)}, u32[]{:S(2)}) collective-permute-start(bf16[2,4,80,256]{3,2,1,0:T(8,128)(2,1)S(1)} %pad_maximum_fusion.2), channel_id=1, source_target_pairs={{0,64},{4,20},{8,72},{12,28},{16,80},{20,4},{24,88},{28,12},{32,96... | collective-permute-start | bytes 983048 | tf_op jit(solution)/shard_map/ppermute | solution.py:326
  67.3 29.7 %collective-permute-done.6.r3 = bf16[2,4,80,256]{3,2,1,0:T(8,128)(2,1)S(1)} collective-permute-done((bf16[2,4,80,256]{3,2,1,0:T(8,128)(2,1)S(1)}, bf16[2,4,80,256]{3,2,1,0:T(8,128)(2,1)S(1)}, u32[]{:S(2)}, u32[]{:S(2)}) %collective-permute-start.6) | collective-permute-done | bytes 327712 | tf_op jit(solution)/shard_map/ppermute | solution.py:326
  97.0 0.0 collective-permute-start.4
  97.0 0.0 collective-permute-done.5.r2
  97.0 8.7 %collective-permute-done.4.r1 = bf16[2,4,80,256]{3,2,1,0:T(8,128)(2,1)S(1)} collective-permute-done((bf16[2,4,80,256]{3,2,1,0:T(8,128)(2,1)S(1)}, bf16[2,4,80,256]{3,2,1,0:T(8,128)(2,1)S(1)}, u32[]{:S(2)}, u32[]{:S(2)}) %collective-permute-start.4) | collective-permute-done | bytes 327712 | tf_op jit(solution)/shard_map/ppermute | solution.py:326
  105.8 0.0 collective-permute-done.9.c2
  105.8 1.9 %grad.1 = (f32[80,1280]{1,0:T(8,128)S(1)}, bf16[80,1280]{1,0:T(8,128)(2,1)S(1)}, bf16[80,1280]{1,0:T(8,128)(2,1)S(1)}, bf16[80,1280]{1,0:T(8,128)(2,1)S(1)}) custom-call(bf16[4,4,80,256]{3,2,1,0:T(8,128)(2,1)S(1)} %get-tuple-element.32.mine, bf16[4,4,80,256]{3,2,1,0:T(8,128)(2,1)S(1)} %collective-permute-done.3.got, ...), custom_call_target="tpu_custom_call" | custom-call | flops 2000000000 | bytes 8000000 | tf_op jit(solution)/shard_map/grad/pallas_call | solution.py:425
  107.7 1.5 %collective-permute-start.11 = (bf16[80,1280]{1,0:T(8,128)(2,1)S(1)}, bf16[80,1280]{1,0:T(8,128)(2,1)S(1)}, u32[]{:S(2)}, u32[]{:S(2)}) collective-permute-start(bf16[80,1280]{1,0:T(8,128)(2,1)S(1)} %get-tuple-element.35), channel_id=1, source_target_pairs={{0,8},{4,36},{8,16},{12,44},{16,24},{20,52},{24,0},{28,60},{32,40}... | collective-permute-start | bytes 614408 | tf_op jit(solution)/shard_map/ppermute | solution.py:326
  109.2 2.7 %collective-permute-start.12 = (bf16[80,1280]{1,0:T(8,128)(2,1)S(1)}, bf16[80,1280]{1,0:T(8,128)(2,1)S(1)}, u32[]{:S(2)}, u32[]{:S(2)}) collective-permute-start(bf16[80,1280]{1,0:T(8,128)(2,1)S(1)} %get-tuple-element.36), channel_id=1, source_target_pairs={{0,16},{4,68},{8,24},{12,76},{16,0},{20,84},{24,8},{28,92},{32,48}... | collective-permute-start | bytes 614408 | tf_op jit(solution)/shard_map/ppermute | solution.py:326
  111.9 1.4 %collective-permute-start.13 = (bf16[80,1280]{1,0:T(8,128)(2,1)S(1)}, bf16[80,1280]{1,0:T(8,128)(2,1)S(1)}, u32[]{:S(2)}, u32[]{:S(2)}) collective-permute-start(bf16[80,1280]{1,0:T(8,128)(2,1)S(1)} %get-tuple-element.37), channel_id=1, source_target_pairs={{0,24},{4,100},{8,0},{12,108},{16,8},{20,116},{24,16},{28,124},{32... | collective-permute-start | bytes 614408 | tf_op jit(solution)/shard_map/ppermute | solution.py:326
  113.4 1.3 %collective-permute-done.11.r1 = bf16[80,1280]{1,0:T(8,128)(2,1)S(1)} collective-permute-done((bf16[80,1280]{1,0:T(8,128)(2,1)S(1)}, bf16[80,1280]{1,0:T(8,128)(2,1)S(1)}, u32[]{:S(2)}, u32[]{:S(2)}) %collective-permute-start.11) | collective-permute-done | bytes 204832 | tf_op jit(solution)/shard_map/ppermute | solution.py:326
  114.7 3.2 %collective-permute-done.12.r2 = bf16[80,1280]{1,0:T(8,128)(2,1)S(1)} collective-permute-done((bf16[80,1280]{1,0:T(8,128)(2,1)S(1)}, bf16[80,1280]{1,0:T(8,128)(2,1)S(1)}, u32[]{:S(2)}, u32[]{:S(2)}) %collective-permute-start.12) | collective-permute-done | bytes 204832 | tf_op jit(solution)/shard_map/ppermute | solution.py:326
  117.9 0.0 collective-permute-done.13.r3
  117.9 0.2 join.1
  118.0 11.4 %all_to_all.5.pieces = bf16[4,200,128]{2,1,0:T(8,128)(2,1)S(1)} all-to-all(bf16[4,200,128]{2,1,0:T(8,128)(2,1)S(1)} %join.1), channel_id=1, replica_groups=mesh['y'=4,'x'=4,'c'=2,'z'=4] {'z'}, dimensions={0} | all-to-all | bytes 409600 | tf_op jit(solution)/shard_map/all_to_all | solution.py:443
  129.5 0.7 total.1
  (22 shorter events, 0.2 us)
Async XLA Ops:
  0.6 7.0 %copy-start.7 = (f32[40]{0:T(128)S(1)}, f32[40]{0:T(128)}, u32[]{:S(2)}) copy-start(f32[40]{0:T(128)} %param.14) | copy-start | bytes 484
  0.6 7.0 %copy-start.8 = (f32[40]{0:T(128)S(1)}, f32[40]{0:T(128)}, u32[]{:S(2)}) copy-start(f32[40]{0:T(128)} %param.15) | copy-start | bytes 484
  0.7 1.4 %copy-start = (bf16[1,256,2816]{2,1,0:T(8,128)(2,1)S(1)}, bf16[1,256,2816]{2,1,0:T(8,128)(2,1)}, u32[]{:S(2)}) copy-start(bf16[1,256,2816]{2,1,0:T(8,128)(2,1)} %param.11) | copy-start | bytes 4325380
  2.0 0.7 copy-start.3
  2.7 5.0 %copy-start.1 = (bf16[1,256,2816]{2,1,0:T(8,128)(2,1)S(1)}, bf16[1,256,2816]{2,1,0:T(8,128)(2,1)}, u32[]{:S(2)}) copy-start(bf16[1,256,2816]{2,1,0:T(8,128)(2,1)} %param.11) | copy-start | bytes 4325380
  2.7 5.0 %copy-start.2 = (f32[4,2816]{1,0:T(4,128)S(1)}, f32[4,2816]{1,0:T(4,128)}, u32[]{:S(2)}) copy-start(f32[4,2816]{1,0:T(4,128)} %w.3) | copy-start | bytes 135172
  2.9 9.5 %collective-permute-start = (bf16[8,2944]{1,0:T(8,128)(2,1)S(1)}, bf16[8,2944]{1,0:T(8,128)(2,1)S(1)}, u32[]{:S(2)}, u32[]{:S(2)}) collective-permute-start(bf16[8,2944]{1,0:T(8,128)(2,1)S(1)} %edge.1), channel_id=1, source_target_pairs={{0,1},{1,2},{2,3},{4,5},{5,6},{6,7},{8,9},{9,10},{10,11},{12,13},{... | collective-permute-start | bytes 141320 | tf_op jit(solution)/shard_map/ppermute | solution.py:315
  7.7 0.8 copy-start.6
  12.4 9.1 %copy-start.10 = (f32[40]{0:T(128)S(1)}, f32[40]{0:T(128)}, u32[]{:S(2)}) copy-start(f32[40]{0:T(128)} %param.16) | copy-start | bytes 484
  12.4 9.2 %copy-start.9 = (f32[2560]{0:T(1024)S(1)}, f32[2560]{0:T(1024)}, u32[]{:S(2)}) copy-start(f32[2560]{0:T(1024)} %param.19) | copy-start | bytes 30724
  12.4 9.3 %copy-start.4 = (s32[1,256]{1,0:T(1,128)S(1)}, s32[1,256]{1,0:T(1,128)}, u32[]{:S(2)}) copy-start(s32[1,256]{1,0:T(1,128)} %docs.7) | copy-start | bytes 3076
  13.9 21.0 %collective-permute-start.1 = (bf16[144,2560]{1,0:T(8,128)(2,1)}, bf16[144,2560]{1,0:T(8,128)(2,1)S(1)}, u32[]{:S(2)}, u32[]{:S(2)}) collective-permute-start(bf16[144,2560]{1,0:T(8,128)(2,1)} %get-tuple-element.30), channel_id=1, source_target_pairs={{0,1},{1,2},{2,3},{4,5},{5,6},{6,7},{8,9},{9,10},{10,11},{12,13},{... | collective-permute-start | bytes 2211848 | tf_op jit(solution)/shard_map/ppermute | solution.py:315
  17.8 31.6 %collective-permute-start.2 = (bf16[144,2560]{1,0:T(8,128)(2,1)}, bf16[144,2560]{1,0:T(8,128)(2,1)S(1)}, u32[]{:S(2)}, u32[]{:S(2)}) collective-permute-start(bf16[144,2560]{1,0:T(8,128)(2,1)} %get-tuple-element.30), channel_id=1, source_target_pairs={{0,2},{1,3},{4,6},{5,7},{8,10},{9,11},{12,14},{13,15},{16,18},{17,... | collective-permute-start | bytes 2211848 | tf_op jit(solution)/shard_map/ppermute | solution.py:315
  21.4 35.0 %collective-permute-start.7 = (bf16[256,1280]{1,0:T(8,128)(2,1)}, bf16[256,1280]{1,0:T(8,128)(2,1)}, u32[]{:S(2)}, u32[]{:S(2)}) collective-permute-start(bf16[256,1280]{1,0:T(8,128)(2,1)} %bitcast.9), channel_id=1, source_target_pairs={{0,4},{4,0},{1,5},{5,1},{2,6},{6,2},{3,7},{7,3},{8,12},{12,8},{9,1... | collective-permute-start | bytes 1966088 | tf_op jit(solution)/shard_map/ppermute | solution.py:330
  21.8 1.3 %copy-start.5 = (bf16[1,256,2560]{2,1,0:T(8,128)(2,1)S(1)}, bf16[1,256,2560]{2,1,0:T(8,128)(2,1)}, u32[]{:S(2)}) copy-start(bf16[1,256,2560]{2,1,0:T(8,128)(2,1)} %param.12) | copy-start | bytes 3932164
  56.3 6.8 %collective-permute-start.3 = (bf16[4,4,80,256]{3,2,1,0:T(8,128)(2,1)S(1)}, bf16[4,4,80,256]{3,2,1,0:T(8,128)(2,1)S(1)}, u32[]{:S(2)}, u32[]{:S(2)}) collective-permute-start(bf16[4,4,80,256]{3,2,1,0:T(8,128)(2,1)S(1)} %get-tuple-element.33), channel_id=1, source_target_pairs={{0,4},{4,0},{1,5},{5,1},{2,6},{6,2},{3,7},{7,3},{8,12},{12,8},{9,1... | collective-permute-start | bytes 1966088 | tf_op jit(solution)/shard_map/ppermute | solution.py:330
  57.7 48.0 %collective-permute-start.10 = (bf16[2,256,1280]{2,1,0:T(8,128)(2,1)S(1)}, bf16[2,256,1280]{2,1,0:T(8,128)(2,1)S(1)}, u32[]{:S(2)}, u32[]{:S(2)}) collective-permute-start(bf16[2,256,1280]{2,1,0:T(8,128)(2,1)S(1)} %pad_maximum_fusion.c0), channel_id=1, source_target_pairs={{0,96},{4,28},{8,104},{12,4},{16,112},{20,12},{24,120},{28,20},{32... | collective-permute-start | bytes 3932168 | tf_op jit(solution)/shard_map/ppermute | solution.py:326
  60.8 44.9 %collective-permute-start.8 = (bf16[2,256,1280]{2,1,0:T(8,128)(2,1)S(1)}, bf16[2,256,1280]{2,1,0:T(8,128)(2,1)S(1)}, u32[]{:S(2)}, u32[]{:S(2)}) collective-permute-start(bf16[2,256,1280]{2,1,0:T(8,128)(2,1)S(1)} %pad_maximum_fusion.c0), channel_id=1, source_target_pairs={{0,32},{4,12},{8,40},{12,20},{16,48},{20,28},{24,56},{28,4},{32,64... | collective-permute-start | bytes 3932168 | tf_op jit(solution)/shard_map/ppermute | solution.py:326
  60.8 44.9 %collective-permute-start.9 = (bf16[2,256,1280]{2,1,0:T(8,128)(2,1)S(1)}, bf16[2,256,1280]{2,1,0:T(8,128)(2,1)S(1)}, u32[]{:S(2)}, u32[]{:S(2)}) collective-permute-start(bf16[2,256,1280]{2,1,0:T(8,128)(2,1)S(1)} %pad_maximum_fusion.c0), channel_id=1, source_target_pairs={{0,64},{4,20},{8,72},{12,28},{16,80},{20,4},{24,88},{28,12},{32,96... | collective-permute-start | bytes 3932168 | tf_op jit(solution)/shard_map/ppermute | solution.py:326
  63.2 33.9 %collective-permute-start.6 = (bf16[2,4,80,256]{3,2,1,0:T(8,128)(2,1)S(1)}, bf16[2,4,80,256]{3,2,1,0:T(8,128)(2,1)S(1)}, u32[]{:S(2)}, u32[]{:S(2)}) collective-permute-start(bf16[2,4,80,256]{3,2,1,0:T(8,128)(2,1)S(1)} %pad_maximum_fusion.3), channel_id=1, source_target_pairs={{0,96},{4,28},{8,104},{12,4},{16,112},{20,12},{24,120},{28,20},{32... | collective-permute-start | bytes 983048 | tf_op jit(solution)/shard_map/ppermute | solution.py:326
  64.3 32.7 %collective-permute-start.5 = (bf16[2,4,80,256]{3,2,1,0:T(8,128)(2,1)S(1)}, bf16[2,4,80,256]{3,2,1,0:T(8,128)(2,1)S(1)}, u32[]{:S(2)}, u32[]{:S(2)}) collective-permute-start(bf16[2,4,80,256]{3,2,1,0:T(8,128)(2,1)S(1)} %pad_maximum_fusion.2), channel_id=1, source_target_pairs={{0,64},{4,20},{8,72},{12,28},{16,80},{20,4},{24,88},{28,12},{32,96... | collective-permute-start | bytes 983048 | tf_op jit(solution)/shard_map/ppermute | solution.py:326
  97.0 8.7 %collective-permute-start.4 = (bf16[2,4,80,256]{3,2,1,0:T(8,128)(2,1)S(1)}, bf16[2,4,80,256]{3,2,1,0:T(8,128)(2,1)S(1)}, u32[]{:S(2)}, u32[]{:S(2)}) collective-permute-start(bf16[2,4,80,256]{3,2,1,0:T(8,128)(2,1)S(1)} %pad_maximum_fusion.1), channel_id=1, source_target_pairs={{0,32},{4,12},{8,40},{12,20},{16,48},{20,28},{24,56},{28,4},{32,64... | collective-permute-start | bytes 983048 | tf_op jit(solution)/shard_map/ppermute | solution.py:326
  107.7 7.0 %collective-permute-start.11 = (bf16[80,1280]{1,0:T(8,128)(2,1)S(1)}, bf16[80,1280]{1,0:T(8,128)(2,1)S(1)}, u32[]{:S(2)}, u32[]{:S(2)}) collective-permute-start(bf16[80,1280]{1,0:T(8,128)(2,1)S(1)} %get-tuple-element.35), channel_id=1, source_target_pairs={{0,8},{4,36},{8,16},{12,44},{16,24},{20,52},{24,0},{28,60},{32,40}... | collective-permute-start | bytes 614408 | tf_op jit(solution)/shard_map/ppermute | solution.py:326
  109.2 8.7 %collective-permute-start.12 = (bf16[80,1280]{1,0:T(8,128)(2,1)S(1)}, bf16[80,1280]{1,0:T(8,128)(2,1)S(1)}, u32[]{:S(2)}, u32[]{:S(2)}) collective-permute-start(bf16[80,1280]{1,0:T(8,128)(2,1)S(1)} %get-tuple-element.36), channel_id=1, source_target_pairs={{0,16},{4,68},{8,24},{12,76},{16,0},{20,84},{24,8},{28,92},{32,48}... | collective-permute-start | bytes 614408 | tf_op jit(solution)/shard_map/ppermute | solution.py:326
  111.9 5.9 %collective-permute-start.13 = (bf16[80,1280]{1,0:T(8,128)(2,1)S(1)}, bf16[80,1280]{1,0:T(8,128)(2,1)S(1)}, u32[]{:S(2)}, u32[]{:S(2)}) collective-permute-start(bf16[80,1280]{1,0:T(8,128)(2,1)S(1)} %get-tuple-element.37), channel_id=1, source_target_pairs={{0,24},{4,100},{8,0},{12,108},{16,8},{20,116},{24,16},{28,124},{32... | collective-permute-start | bytes 614408 | tf_op jit(solution)/shard_map/ppermute | solution.py:326

commit v3 on v2

--- a/solution.py
+++ b/solution.py
@@ -15,6 +15,7 @@
 D = 1280
 LANES = 128
 XCHUNKS = INNER // LANES
+EARLY = 4
 MSG = N + 16
 F32 = jnp.float32
 BF16 = jnp.bfloat16
@@ -60,26 +61,39 @@
     return jnp.sum(jnp.where(diag, jnp.broadcast_to(row, (n, n)), 0.0), axis=1, keepdims=True)
 
 
-def edge_kernel(rows, docs, out):
-    out[:, 0:C_ALL] = rows[8:16, :]
-    out[:, C_ALL:] = column(docs[...].astype(F32), LANES)[T - 8 :].astype(BF16)
-
-
-def front_kernel(conv, step_in, bias, rates, w, cb, docs, act, state, info, top, cum_o, step_o, win, dwin, masks, xs, fac):
+def steps(step_in, bias, rates):
     step = jax.nn.softplus(step_in[...] + upright(bias[...]))
     decay = -jnp.exp(upright(rates[...])) * step
     tri = (
         lax.broadcasted_iota(jnp.int32, (T, T), 0) <= lax.broadcasted_iota(jnp.int32, (T, T), 1)
     ).astype(F32)
-    cum = dot(decay, tri, precision=HIGH)
-    cum_o[...] = cum
-    step_o[...] = step
+    return step, dot(decay, tri, precision=HIGH)
+
+
+def edge_kernel(conv, docs, out, rows, ids, sems):
+    copies = [
+        pltpu.make_async_copy(conv.at[pl.ds(T - 16, 16), :], rows, sems.at[0]),
+        pltpu.make_async_copy(docs, ids, sems.at[1]),
+    ]
+    for copy in copies:
+        copy.start()
+    for copy in copies:
+        copy.wait()
+    out[:, 0:C_ALL] = rows[8:16, :]
+    last = ids[:, LANES:].astype(F32)
+    pick = lax.broadcasted_iota(jnp.int32, (8, LANES), 0) + LANES - 8 == lax.broadcasted_iota(jnp.int32, (8, LANES), 1)
+    docb = jnp.sum(jnp.where(pick, jnp.broadcast_to(last, (8, LANES)), 0.0), axis=1, keepdims=True)
+    out[:, C_ALL:] = jnp.broadcast_to(docb, (8, LANES)).astype(BF16)
+
+
+def tie_kernel(value, *rest):
+    del value, rest
+
+
+def front_kernel(conv, step_far, bias, rates, w, cb, docs, act, state, info, top, win, dwin, masks, xs, fac, step_in, sem):
+    fetch = pltpu.make_async_copy(step_far, step_in, sem)
+    fetch.start()
     doc_row = docs[...].astype(F32)
-    tail = (doc_row == doc_row[:, T - 1 : T]).astype(F32)
-    total = cum[:, T - 1 : T]
-    factor = step * jnp.exp(total - cum) * tail
-    whole = jnp.broadcast_to(jnp.exp(total), (H, LANES))
-    fac[...] = split_rows(jnp.concatenate([factor, whole], 1)).T.astype(BF16)
     docb = column(doc_row, LANES)
     dwin[0:8, :] = jnp.zeros((8, LANES), F32)
     dwin[8:, :] = docb
@@ -100,6 +114,16 @@
         act[:, at] = out
         return at, out
 
+    for slot in range(2):
+        conv_chunk(XCHUNKS + slot, slot)
+    fetch.wait()
+    step, cum = steps(step_in, bias, rates)
+    tail = (doc_row == doc_row[:, T - 1 : T]).astype(F32)
+    total = cum[:, T - 1 : T]
+    factor = step * jnp.exp(total - cum) * tail
+    whole = jnp.broadcast_to(jnp.exp(total), (H, LANES))
+    fac[...] = split_rows(jnp.concatenate([factor, whole], 1)).T.astype(BF16)
+
     def value_chunk(j, slot):
         at, out = conv_chunk(j, slot)
         wide = dot(fac[0 : T + 16, :], head_pick(j, LANES))
@@ -116,8 +140,6 @@
             value_chunk(2 * i + slot, slot)
         return carry
 
-    for slot in range(2):
-        conv_chunk(XCHUNKS + slot, slot)
     lax.fori_loop(0, XCHUNKS // 2, value_pair, 0)
     b_t = act[:, INNER : INNER + N].astype(F32).T.astype(BF16)
     for k in range(5):
@@ -151,8 +173,39 @@
         msg[N:, at] = info[:, at]
 
 
-def middle_kernel(act, cum, step, docs, halo, gate, skip, local, reach, sgate, scores, fac, efac):
+def pair_chunk(j, act, cum, step, scores, fac, skip):
+    half = T // 2
+    at = pl.ds(pl.multiple_of(j * LANES, LANES), LANES)
+    vals = act[:, at]
+    lanes = lax.broadcasted_iota(jnp.int32, (T, LANES), 1)
+    cols = dot(fac[...], head_pick(j, 2 * LANES))
+    top = skip[:, at] * vals[0:half].astype(F32)
+    low = skip[:, at] * vals[half:].astype(F32)
+    for k in range(2):
+        mine = jnp.where((lanes >= HD) == (k == 1), vals.astype(F32), 0.0).astype(BF16)
+        col = cols[:, k * LANES : (k + 1) * LANES]
+        row = cum[pl.ds(2 * j + k, 1), :]
+        size = step[pl.ds(2 * j + k, 1), :]
+
+        def weights(t, s):
+            ts = slice(t * half, t * half + half)
+            ss = slice(s * LANES, s * LANES + LANES)
+            spread = jnp.minimum(col[ts] - row[:, ss], 0.0)
+            return (scores[ts, ss] * jnp.exp(spread) * size[:, ss]).astype(BF16)
+
+        top = top + dot(weights(0, 0), mine[0:half])
+        low = low + dot(jnp.concatenate([weights(1, 0), weights(1, 1)], 1), mine)
+    return jnp.concatenate([top, low], 0)
+
+
+def early_kernel(act, step_in, bias, rates, docs, halo, skip, local, reach, cum, step, scores, fac, efac):
+    step[...], cum[...] = steps(step_in, bias, rates)
     doc_row = docs[...].astype(F32)
+    prev_tag = halo[:, C_ALL : C_ALL + LANES].astype(F32)[7:8, :]
+    prev_tag = jnp.concatenate([prev_tag, prev_tag], 1)
+    matched = (doc_row == prev_tag).astype(F32)
+    fac[...] = split_rows(cum[...]).T.astype(BF16)
+    efac[...] = split_rows(jnp.exp(cum[...]) * matched).T.astype(BF16)
     c_map = act[:, INNER + N :]
     b_map = act[:, INNER : INNER + N]
     doc_col = column(doc_row, LANES)
@@ -164,67 +217,63 @@
         )
         same = jnp.logical_and(order, doc_col == doc_row[:, at])
         scores[:, at] = jnp.where(same, g, 0.0)
-    all_cum = cum[...]
-    fac[...] = split_rows(all_cum).T.astype(BF16)
-    prev_tag = halo[:, C_ALL : C_ALL + LANES].astype(F32)[7:8, :]
-    prev_tag = jnp.concatenate([prev_tag, prev_tag], 1)
-    matched = (doc_row == prev_tag).astype(F32)
-    efac[...] = split_rows(jnp.exp(all_cum) * matched).T.astype(BF16)
-    half = T // 2
+
+    def chunk(j, carry):
+        at = pl.ds(pl.multiple_of(j * LANES, LANES), LANES)
+        reach[:, at] = dot(efac[...], head_pick(j, LANES))
+        return carry
+
+    lax.fori_loop(0, XCHUNKS, chunk, 0)
 
     def pair(j, carry):
         at = pl.ds(pl.multiple_of(j * LANES, LANES), LANES)
-        vals = act[:, at]
-        lanes = lax.broadcasted_iota(jnp.int32, (T, LANES), 1)
-        cols = dot(fac[...], head_pick(j, 2 * LANES))
-        top = jnp.zeros((half, LANES), F32)
-        low = jnp.zeros((half, LANES), F32)
-        for k in range(2):
-            mine = jnp.where((lanes >= HD) == (k == 1), vals.astype(F32), 0.0).astype(BF16)
-            col = cols[:, k * LANES : (k + 1) * LANES]
-            row = cum[pl.ds(2 * j + k, 1), :]
-            size = step[pl.ds(2 * j + k, 1), :]
-
-            def weights(t, s):
-                ts = slice(t * half, t * half + half)
-                ss = slice(s * LANES, s * LANES + LANES)
-                spread = jnp.minimum(col[ts] - row[:, ss], 0.0)
-                return (scores[ts, ss] * jnp.exp(spread) * size[:, ss]).astype(BF16)
-
-            top = top + dot(weights(0, 0), mine[0:half])
-            low = low + dot(jnp.concatenate([weights(1, 0), weights(1, 1)], 1), mine)
-        gain = skip[:, at]
-        local[0:half, at] = top + gain * vals[0:half].astype(F32)
-        local[half:, at] = low + gain * vals[half:].astype(F32)
-        reach[:, at] = dot(efac[...], head_pick(j, LANES))
+        local[:, at] = pair_chunk(j, act, cum, step, scores, fac, skip)
+        return carry
+
+    lax.fori_loop(0, EARLY, pair, 0)
+
+
+def late_kernel(act, cum, step, scores, fac, gate, skip, local, sgate):
+    def pair(j, carry):
+        at = pl.ds(pl.multiple_of(j * LANES, LANES), LANES)
+        local[:, at] = pair_chunk(j + EARLY, act, cum, step, scores, fac, skip)
+        return carry
+
+    lax.fori_loop(0, XCHUNKS - EARLY, pair, 0)
+
+    def gates(j, carry):
+        at = pl.ds(pl.multiple_of(j * 2 * LANES, 2 * LANES), 2 * LANES)
         sgate[:, at] = silu(gate[:, at].astype(F32))
         return carry
 
-    lax.fori_loop(0, XCHUNKS, pair, 0)
-
-
-def back_kernel(local, reach, sgate, act, one, two, gain, place, normed, mine, give, gated, squares, turned):
+    lax.fori_loop(0, XCHUNKS // 2, gates, 0)
+
+
+def back_kernel(early, late, reach, sgate, act, one, two, gain, place, normed, mine, give, gated, squares, turned, flat, sem):
     c_map = act[:, INNER + N :]
-    squares[...] = jnp.zeros_like(squares)
-
-    def first(j):
-        at = pl.ds(pl.multiple_of(j * LANES, LANES), LANES)
+    wide = 2 * LANES
+
+    def first(j, local, shift):
+        at = pl.ds(pl.multiple_of(j * wide, wide), wide)
         info = one[N:, at].astype(F32)
         other = two[N:, at].astype(F32)
         linked = (info[2:3] == other[2:3]).astype(F32)
         weight = (info[0:1] + info[1:2]) * linked
         state = one[0:N, at].astype(F32) + weight * two[0:N, at].astype(F32)
         reading = dot(c_map, state.astype(BF16))
-        mixed = local[:, at] + reading * reach[:, at]
+        here = pl.ds(pl.multiple_of((j - shift) * wide, wide), wide)
+        mixed = local[:, here] + reading * reach[:, at]
         value = mixed.astype(BF16).astype(F32) * sgate[:, at]
         gated[:, at] = value
-        return value * value
+        value = value * value
+        return value[:, 0:LANES] + value[:, LANES:]
 
     def first_pair(i, carry):
-        squares[...] += first(2 * i) + first(2 * i + 1)
-        return carry
-
-    lax.fori_loop(0, XCHUNKS // 2, first_pair, 0)
+        squares[...] += first(2 * i, late, EARLY // 2) + first(2 * i + 1, late, EARLY // 2)
+        return carry
+
+    squares[...] = first(0, early, 0) + first(1, early, 0)
+    lax.fori_loop(1, 5, first_pair, 0)
     mean = jnp.sum(squares[...], axis=1, keepdims=True) * (1.0 / INNER)
     squares[...] = jnp.broadcast_to(lax.rsqrt(mean + 1e-05), squares.shape)
     eye = (
@@ -232,33 +281,36 @@
     ).astype(BF16)
 
     def second(i, carry):
-        for k in range(2):
-            at = pl.ds(pl.multiple_of((2 * i + k) * LANES, LANES), LANES)
+        for k in range(4):
+            at = pl.ds(pl.multiple_of((4 * i + k) * LANES, LANES), LANES)
             value = (gated[:, at] * squares[...] * gain[:, at]).astype(BF16)
-            normed[:, at] = value
+            flat[:, at] = value
             turned[at, :] = dot(eye, value, ((1,), (1,))).astype(BF16)
         return carry
 
-    lax.fori_loop(0, XCHUNKS // 2, second, 0)
+    lax.fori_loop(0, 5, second, 0)
+    out = pltpu.make_async_copy(flat, normed, sem)
+    out.start()
     y, x, c = place[0], place[1], place[2]
-
-    def deal(i, carry):
-        far_y, far_x = lax.rem(i // 4 - y + 4, 4), lax.rem(lax.rem(i, 4) - x + 4, 4)
-        blocks = [turned[pl.ds(pl.multiple_of(160 * i + 80 * k, 16), 80), :] for k in range(2)]
-
-        @pl.when(c == 0)
-        def _():
-            mine[far_y, far_x] = blocks[0]
-            give[far_x, far_y] = blocks[1]
-
-        @pl.when(c == 1)
-        def _():
-            give[far_y, far_x] = blocks[0]
-            mine[far_x, far_y] = blocks[1]
-
-        return carry
-
-    lax.fori_loop(0, 16, deal, 0)
+    far_y = [lax.rem(i - y + 4, 4) for i in range(4)]
+    far_x = [lax.rem(i - x + 4, 4) for i in range(4)]
+
+    def deal(zero, other):
+        for i in range(4):
+            for j in range(4):
+                row = 80 * (2 * (4 * i + j))
+                zero[far_y[i], far_x[j]] = turned[row : row + 80, :]
+                other[far_x[j], far_y[i]] = turned[row + 80 : row + 160, :]
+
+    @pl.when(c == 0)
+    def _():
+        deal(mine, give)
+
+    @pl.when(c == 1)
+    def _():
+        deal(give, mine)
+
+    out.wait()
 
 
 def grad_kernel(mine, got, r1, r2, r3, c0, c1, c2, c3, keep, s1, s2, s3):
@@ -278,19 +330,19 @@
             out[:, at] = total[80 * k + 80 : 80 * k + 160].astype(BF16)
 
 
-def join_kernel(keep, r1, r2, r3, out, total, flat):
+def join_kernel(keep, r1, r2, r3, place, own, s1, s2, s3, total, flat):
     total[...] = keep[...] + r1[...].astype(F32) + r2[...].astype(F32) + r3[...].astype(F32)
     for z in range(4):
         for k in range(10):
             flat[z, 20 * k : 20 * k + 20, :] = total[20 * z : 20 * z + 20, k * LANES : k * LANES + LANES]
-        out[z] = flat[z].astype(BF16)
-
-
-def sum_kernel(pieces, out, flat):
-    total = pieces[0].astype(F32)
-    for i in range(1, 4):
-        total = total + pieces[i].astype(F32)
-    flat[...] = total
+    z = place[3]
+    own[...] = flat[z]
+    for k, out in enumerate((s1, s2, s3)):
+        out[...] = flat[lax.rem(z + k + 1, 4)].astype(BF16)
+
+
+def sum_kernel(own, r1, r2, r3, out, flat):
+    flat[...] = own[...] + r1[...].astype(F32) + r2[...].astype(F32) + r3[...].astype(F32)
     for k in range(10):
         out[:, k * LANES : k * LANES + LANES] = flat[20 * k : 20 * k + 20, :]
 
@@ -330,27 +382,40 @@
     return lax.ppermute(value, "c", [(0, 1), (1, 0)])
 
 
+def tied(value, *others):
+    anywhere = pl.BlockSpec(memory_space=pl.ANY)
+    return call(
+        tie_kernel,
+        "tie",
+        shape(value.shape, value.dtype),
+        [],
+        4,
+        in_specs=[anywhere] * (1 + len(others)),
+        out_specs=anywhere,
+        input_output_aliases={0: 0},
+    )(value, *others)
+
+
 def whole(dims):
     return pl.BlockSpec(dims, lambda i: (0,) * len(dims))
 
 
 def per_device(conv_input, gate_input, step_input, step_bias, log_rates, skip_gain, conv_weight, conv_bias, norm_gain, doc_ids, cotangent):
     conv = conv_input[0]
+    vmem = pl.BlockSpec(memory_space=VMEM)
     halo = call(
         edge_kernel,
         "edge",
         shape((8, C_ALL + LANES), BF16),
-        [],
-        8,
+        [VMEM((16, C_ALL), BF16), VMEM((1, T), jnp.int32), pltpu.SemaphoreType.DMA((2,))],
+        62,
         moved=10**5,
-        grid=(1,),
-        in_specs=[pl.BlockSpec((16, C_ALL), lambda i: (T // 16 - 1, 0)), whole((1, T))],
-        out_specs=whole((8, C_ALL + LANES)),
+        in_specs=[pl.BlockSpec(memory_space=pltpu.HBM)] * 2,
     )(conv, doc_ids)
     halo = shifted(halo, 1)
-    cots = jnp.stack([cotangent[0], swapped(cotangent[0])])
-    place = jnp.stack([lax.axis_index(a) for a in ("y", "x", "c")]).astype(jnp.int32)
-    act, state, info, top, cum, step = call(
+    cot_other = swapped(cotangent[0])
+    place = jnp.stack([lax.axis_index(a) for a in ("y", "x", "c", "z")]).astype(jnp.int32)
+    act, state, info, top = call(
         front_kernel,
         "front",
         (
@@ -358,8 +423,6 @@
             shape((N, INNER)),
             shape((16, INNER), BF16),
             shape((16, INNER)),
-            shape((H, T)),
-            shape((H, T)),
         ),
         [
             VMEM((2, T + 8, LANES), F32),
@@ -367,11 +430,14 @@
             VMEM((3, T, LANES), F32),
             VMEM((T, INNER), BF16),
             VMEM((T + LANES, LANES), BF16),
+            VMEM((H, T), F32),
+            pltpu.SemaphoreType.DMA,
         ],
         16,
         flops=10**9,
         moved=4 * 10**6,
         special=10**6,
+        in_specs=[vmem, pl.BlockSpec(memory_space=pltpu.HBM)] + [vmem] * 5,
     )(conv, step_input[0], step_bias[None], log_rates[None], conv_weight, conv_bias[None], doc_ids)
     act, msg = call(
         fix_kernel,
@@ -397,30 +463,43 @@
     )(halo, conv, conv_weight, conv_bias[None], doc_ids, act, state, info, top)
     one = shifted(msg, 1)
     two = shifted(msg, 2)
+    skip = jnp.repeat(skip_gain, HD)[None]
+    early, reach, cum, step, scores, fac = call(
+        early_kernel,
+        "early",
+        (
+            shape((T, EARLY * LANES)),
+            shape((T, INNER)),
+            shape((H, T)),
+            shape((H, T)),
+            shape((T, T)),
+            shape((T, LANES), BF16),
+        ),
+        [VMEM((T, LANES), BF16)],
+        16,
+    )(act, step_input[0], step_bias[None], log_rates[None], doc_ids, halo, skip)
+    cots = jnp.stack([cotangent[0], tied(cot_other, fac)])
     c1, c2, c3 = [around(cots, k, "y") for k in (1, 2, 3)]
-    local, reach, sgate = call(
-        middle_kernel,
-        "middle",
-        (shape((T, INNER)), shape((T, INNER)), shape((T, INNER))),
-        [VMEM((T, T), F32), VMEM((T, LANES), BF16), VMEM((T, LANES), BF16)],
-        24,
-        flops=2 * 10**9,
-        moved=12 * 10**6,
-        special=4 * 10**6,
-    )(act, cum, step, doc_ids, halo, gate_input[0], jnp.repeat(skip_gain, HD)[None])
+    late, sgate = call(
+        late_kernel, "late", (shape((T, INNER - EARLY * LANES)), shape((T, INNER))), [], 24
+    )(act, cum, step, scores, fac, gate_input[0], skip)
     block = (4, 4, 80, T)
-    vmem = pl.BlockSpec(memory_space=VMEM)
     normed, mine, give = call(
         back_kernel,
         "back",
         (shape((T, INNER), BF16), shape(block, BF16), shape(block, BF16)),
-        [VMEM((T, INNER), F32), VMEM((T, LANES), F32), VMEM((INNER, T), BF16)],
+        [
+            VMEM((T, INNER), F32),
+            VMEM((T, LANES), F32),
+            VMEM((INNER, T), BF16),
+            VMEM((T, INNER), BF16),
+            pltpu.SemaphoreType.DMA,
+        ],
         24,
-        flops=10**9,
-        moved=12 * 10**6,
-        in_specs=[vmem] * 7 + [pl.BlockSpec(memory_space=pltpu.SMEM)],
-    )(local, reach, sgate, act, one, two, norm_gain[None], place)
-    got = swapped(give)
+        in_specs=[vmem] * 8 + [pl.BlockSpec(memory_space=pltpu.SMEM)],
+        out_specs=(pl.BlockSpec(memory_space=pltpu.HBM), vmem, vmem),
+    )(early, late, reach, sgate, act, one, two, norm_gain[None], place)
+    got = tied(swapped(give), c1, c2, c3)
     r1, r2, r3 = [around(jnp.stack([mine[k], got[k]]), k, "y") for k in (1, 2, 3)]
     keep, s1, s2, s3 = call(
         grad_kernel,
@@ -432,16 +511,18 @@
         moved=8 * 10**6,
     )(mine, got, r1, r2, r3, cots, c1, c2, c3)
     t1, t2, t3 = [around(v, k, "x") for k, v in ((1, s1), (2, s2), (3, s3))]
-    packed = call(
+    small = (200, LANES)
+    own, s1, s2, s3 = call(
         join_kernel,
         "join",
-        shape((4, 200, LANES), BF16),
-        [VMEM((80, D), F32), VMEM((4, 200, LANES), F32)],
+        (shape(small),) + (shape(small, BF16),) * 3,
+        [VMEM((80, D), F32), VMEM((4,) + small, F32)],
         8,
         moved=10**6,
-    )(keep, t1, t2, t3)
-    pieces = lax.all_to_all(packed, "z", 0, 0)
-    grad = call(sum_kernel, "total", shape((20, D)), [VMEM((200, LANES), F32)], 8, moved=10**6)(pieces)
+        in_specs=[vmem] * 4 + [pl.BlockSpec(memory_space=pltpu.SMEM)],
+    )(keep, t1, t2, t3, place)
+    u1, u2, u3 = [lax.ppermute(v, "z", [(i, (i + k) % 4) for i in range(4)]) for k, v in ((1, s1), (2, s2), (3, s3))]
+    grad = call(sum_kernel, "total", shape((20, D)), [VMEM(small, F32)], 8, moved=10**6)(own, u1, u2, u3)
     return (normed[None], grad)
 
 

time: 131 us -> 102 us (0.78)
  waiting for transfers between devices: 61.2 us -> 29.4 us
  blocking collectives: 11.4 us -> 0 us
  Pallas kernels: 23.3 us -> 29.5 us
  starting transfers between devices: 26.7 us -> 31.8 us
  other arithmetic: 1.58 us -> 2.95 us
    ppermute x9, waiting for transfers between devices: 42.9 us -> 22.5 us  [around(): return lax.ppermute(value, ('y', 'x', 'c'), pairs)]
    ppermute x3, waiting for transfers between devices: 18.2 us -> 1.36 us  [shifted(): return lax.ppermute(value, 'z', [(i, i + by) for i in range(4 - by)])]
    all_to_all x1 -> x0, blocking collectives: 11.4 us -> none  [per_device(): pieces = lax.all_to_all(packed, 'z', 0, 0)]
    pallas_call x4 -> x7, Pallas kernels: 9.04 us -> 14.7 us  [the longest x1 6.53 us: per_device(): call(late_kernel, 'late', (shape((T, INNER - EARLY * LANES)), shape((T, I...]
    ppermute x0 -> x3, waiting for transfers between devices: none -> 3.49 us  [per_device(): lax.ppermute(v, 'z', [(i, (i + k) % 4) for i in range(4)])]
    ppermute x0 -> x3, starting transfers between devices: none -> 3.29 us  [per_device(): lax.ppermute(v, 'z', [(i, (i + k) % 4) for i in range(4)])]
    pallas_call x1, Pallas kernels: 1.86 us -> 3.96 us  [per_device(): call(grad_kernel, 'grad', (shape((80, D)),) + (shape((80, D), BF16),) * 3...]
    ppermute x2, waiting for transfers between devices: 0.01 us -> 2.04 us  [swapped(): return lax.ppermute(value, 'c', [(0, 1), (1, 0)])]
  transfers between devices with their start and end apart: 14 -> 17, of which waited for: 6 -> 10; matrix products, arithmetic and copies ran while one was open for 2% -> 4% of each run, Pallas kernels for 15% -> 24%
where the time goes in v3:
time: 102 us; the launch traced here: 101 us
  starting transfers between devices  31.8 us (31%)
  Pallas kernels  29.5 us (29%)
  waiting for transfers between devices  29.4 us (29%)
  local copies, waits for them, and re-layouts  6.18 us (6%)
  other arithmetic  2.95 us (3%)
  between operations  1.04 us (1%)
    ppermute x9, waiting for transfers between devices, around(): return lax.ppermute(value, ('y', 'x', 'c'), pairs)  22.5 us
    ppermute x9, starting transfers between devices, around(): return lax.ppermute(value, ('y', 'x', 'c'), pairs)  16.1 us
    ppermute x3, starting transfers between devices, shifted(): return lax.ppermute(value, 'z', [(i, i + by) for i in range(4 - by)])  12.2 us
    pallas_call x1, Pallas kernels, per_device(): call(late_kernel, 'late', (shape((T, INNER - EARLY * LANES)), shape((T, I...  6.53 us
    unnamed x52, local copies, waits for them, and re-layouts  5.24 us
    pallas_call x1, Pallas kernels, per_device(): call(back_kernel, 'back', (shape((T, INNER), BF16), shape(block, BF16), s...  5.12 us
    pallas_call x1, Pallas kernels, per_device(): call(early_kernel, 'early', (shape((T, EARLY * LANES)), shape((T, INNER))...  5.05 us
    pallas_call x1, Pallas kernels, per_device(): call(front_kernel, 'front', (shape((T, C_ALL), BF16), shape((N, INNER)),...  4.27 us
  transfers between devices with their start and end apart: 17, of which 10 were waited for; matrix products, arithmetic and copies ran while one was open for 4% of the time, Pallas kernels for 24%

profile of v3, /device:TPU:0, one launch (start us, length us, event | category | flops | bytes accessed | tf_op | source)
XLA Modules:
  0.0 100.9 jit_solution(3850826805301878348)
XLA Ops:
  0.6 0.0 copy-start.17
  0.7 0.1 collective-permute-start.4
  0.8 1.7 %edge.1 = bf16[8,2944]{1,0:T(8,128)(2,1)} custom-call(bf16[256,2816]{1,0:T(8,128)(2,1)} %bitcast.12, s32[1,256]{1,0:T(1,128)} %docs.7), custom_call_target="tpu_custom_call" | custom-call | bytes 100000 | tf_op jit(solution)/shard_map/edge/pallas_call | solution.py:406
  2.6 3.9 %collective-permute-start = (bf16[8,2944]{1,0:T(8,128)(2,1)}, bf16[8,2944]{1,0:T(8,128)(2,1)S(1)}, u32[]{:S(2)}, u32[]{:S(2)}) collective-permute-start(bf16[8,2944]{1,0:T(8,128)(2,1)} %edge.1), channel_id=1, source_target_pairs={{0,1},{1,2},{2,3},{4,5},{5,6},{6,7},{8,9},{9,10},{10,11},{12,13},{... | collective-permute-start | bytes 141320 | tf_op jit(solution)/shard_map/ppermute | solution.py:367
  6.5 0.1 broadcast_in_dim.24
  6.6 0.1 broadcast_in_dim_reshape.3.skip
  6.7 4.3 %front.1 = (bf16[256,2816]{1,0:T(8,128)(2,1)S(1)}, f32[128,2560]{1,0:T(8,128)S(1)}, bf16[16,2560]{1,0:T(8,128)(2,1)S(1)}, f32[16,2560]{1,0:T(8,128)S(1)}) custom-call(bf16[256,2816]{1,0:T(8,128)(2,1)S(1)} %bitcast.13, f32[40,256]{1,0:T(8,128)S(1)} %bitcast.16, f32[1,40]{1,0:T(1,128)S(1)} %bitcast.18, f32[1,40]{1,0:T(1,128)S(1)} %bitcast.20, ...), custom_call_target="tpu_custom_call" | custom-call | flops 1000000000 | bytes 4000000 | tf_op jit(solution)/shard_map/front/pallas_call | solution.py:418
  11.1 1.5 %fix.1 = (bf16[256,2816]{1,0:T(8,128)(2,1)S(1)}, bf16[144,2560]{1,0:T(8,128)(2,1)}) custom-call(bf16[8,2944]{1,0:T(8,128)(2,1)S(1)} %collective-permute-done.halo, bf16[256,2816]{1,0:T(8,128)(2,1)S(1)} %bitcast.14, f32[4,2816]{1,0:T(4,128)S(1)} %copy-done.10, f32[1,2816]{1,0:T(1,128)S(1)} %broadcast_in_dim.21.cb, ...), custom_call_target="tpu_custom_call", output_to_operand_aliasing={{0}: (5, {})} | custom-call | bytes 2000000 | tf_op jit(solution)/shard_map/fix/pallas_call | solution.py:442
  12.6 3.9 %collective-permute-start.1 = (bf16[144,2560]{1,0:T(8,128)(2,1)}, bf16[144,2560]{1,0:T(8,128)(2,1)S(1)}, u32[]{:S(2)}, u32[]{:S(2)}) collective-permute-start(bf16[144,2560]{1,0:T(8,128)(2,1)} %get-tuple-element.40), channel_id=1, source_target_pairs={{0,1},{1,2},{2,3},{4,5},{5,6},{6,7},{8,9},{9,10},{10,11},{12,13},{... | collective-permute-start | bytes 2211848 | tf_op jit(solution)/shard_map/ppermute | solution.py:367
  16.4 4.4 %collective-permute-start.2 = (bf16[144,2560]{1,0:T(8,128)(2,1)}, bf16[144,2560]{1,0:T(8,128)(2,1)}, u32[]{:S(2)}, u32[]{:S(2)}) collective-permute-start(bf16[144,2560]{1,0:T(8,128)(2,1)} %get-tuple-element.40), channel_id=1, source_target_pairs={{0,2},{1,3},{4,6},{5,7},{8,10},{9,11},{12,14},{13,15},{16,18},{17,... | collective-permute-start | bytes 2211848 | tf_op jit(solution)/shard_map/ppermute | solution.py:367
  20.9 5.0 %early.1 = (f32[256,512]{1,0:T(8,128)S(1)}, f32[256,2560]{1,0:T(8,128)S(1)}, f32[40,256]{1,0:T(8,128)S(1)}, f32[40,256]{1,0:T(8,128)S(1)}, f32[256,256]{1,0:T(8,128)S(1)}, /*index=5*/bf16[256,128]{1,0:T(8,128)(2,1)S(1)}) custom-call(bf16[256,2816]{1,0:T(8,128)(2,1)S(1)} %get-tuple-element.31.act, f32[40,256]{1,0:T(8,128)S(1)} %bitcast.17, ...), custom_call_target="tpu_custom_call" | custom-call | tf_op jit(solution)/shard_map/early/pallas_call | solution.py:467
  25.9 0.6 copy-done.13
  26.6 2.8 %pad_maximum_fusion.c0 = bf16[2,256,1280]{2,1,0:T(8,128)(2,1)} fusion(bf16[1,256,1280]{2,1,0:T(8,128)(2,1)} %bitcast.11, bf16[1,256,1280]{2,1,0:T(8,128)(2,1)S(1)} %copy-done.23), kind=kLoop, calls=%fused_computation | loop fusion | flops 655360 | bytes 2621440 | tf_op jit(solution)/shard_map/stack | solution.py:481
  29.4 1.6 %collective-permute-start.5 = (bf16[2,256,1280]{2,1,0:T(8,128)(2,1)}, bf16[2,256,1280]{2,1,0:T(8,128)(2,1)S(1)}, u32[]{:S(2)}, u32[]{:S(2)}) collective-permute-start(bf16[2,256,1280]{2,1,0:T(8,128)(2,1)} %pad_maximum_fusion.c0), channel_id=1, source_target_pairs={{0,32},{4,12},{8,40},{12,20},{16,48},{20,28},{24,56},{28,4},{32,64... | collective-permute-start | bytes 3932168 | tf_op jit(solution)/shard_map/ppermute | solution.py:378
  31.0 2.9 %collective-permute-start.6 = (bf16[2,256,1280]{2,1,0:T(8,128)(2,1)}, bf16[2,256,1280]{2,1,0:T(8,128)(2,1)}, u32[]{:S(2)}, u32[]{:S(2)}) collective-permute-start(bf16[2,256,1280]{2,1,0:T(8,128)(2,1)} %pad_maximum_fusion.c0), channel_id=1, source_target_pairs={{0,64},{4,20},{8,72},{12,28},{16,80},{20,4},{24,88},{28,12},{32,96... | collective-permute-start | bytes 3932168 | tf_op jit(solution)/shard_map/ppermute | solution.py:378
  33.9 1.3 %collective-permute-start.7 = (bf16[2,256,1280]{2,1,0:T(8,128)(2,1)}, bf16[2,256,1280]{2,1,0:T(8,128)(2,1)}, u32[]{:S(2)}, u32[]{:S(2)}) collective-permute-start(bf16[2,256,1280]{2,1,0:T(8,128)(2,1)} %pad_maximum_fusion.c0), channel_id=1, source_target_pairs={{0,96},{4,28},{8,104},{12,4},{16,112},{20,12},{24,120},{28,20},{32... | collective-permute-start | bytes 3932168 | tf_op jit(solution)/shard_map/ppermute | solution.py:378
  35.3 0.7 broadcast_in_dim.25.gain
  36.0 0.1 pad_add_fusion.place
  36.1 1.3 %copy-done.3 = bf16[1,256,2560]{2,1,0:T(8,128)(2,1)S(1)} copy-done((bf16[1,256,2560]{2,1,0:T(8,128)(2,1)S(1)}, bf16[1,256,2560]{2,1,0:T(8,128)(2,1)}, u32[]{:S(2)}) %copy-start.3) | copy-done | bytes 1310744
  37.4 0.9 copy-done.7
  38.3 0.7 copy-done.9
  39.0 0.8 copy-done.14
  39.8 0.8 copy-done.16
  40.6 6.5 %late.1 = (f32[256,2048]{1,0:T(8,128)S(1)}, f32[256,2560]{1,0:T(8,128)S(1)}) custom-call(bf16[256,2816]{1,0:T(8,128)(2,1)S(1)} %get-tuple-element.31.act, f32[40,256]{1,0:T(8,128)S(1)} %copy-done.14, f32[40,256]{1,0:T(8,128)S(1)} %copy-done.16, f32[256,256]{1,0:T(8,128)S(1)} %copy-done.7, bf16[256,128]{1,0:T(8,128)(2,1)S(1)} %get-tuple-element.36.fac.rest_0_, ...), custom_call_target="tpu_custom_call" | custom-call | tf_op jit(solution)/shard_map/late/pallas_call | solution.py:483
  47.2 1.4 %collective-permute-done.2.two = bf16[144,2560]{1,0:T(8,128)(2,1)} collective-permute-done((bf16[144,2560]{1,0:T(8,128)(2,1)}, bf16[144,2560]{1,0:T(8,128)(2,1)}, u32[]{:S(2)}, u32[]{:S(2)}) %collective-permute-start.2) | collective-permute-done | bytes 737312 | tf_op jit(solution)/shard_map/ppermute | solution.py:367
  48.5 5.1 %back.1 = (bf16[256,2560]{1,0:T(8,128)(2,1)}, bf16[4,4,80,256]{3,2,1,0:T(8,128)(2,1)S(1)}, bf16[4,4,80,256]{3,2,1,0:T(8,128)(2,1)S(1)}) custom-call(f32[256,512]{1,0:T(8,128)S(1)} %copy-done.5, f32[256,2048]{1,0:T(8,128)S(1)} %get-tuple-element.37.late, f32[256,2560]{1,0:T(8,128)S(1)} %copy-done.2, f32[256,2560]{1,0:T(8,128)S(1)} %get-tuple-element.39.sgate, ...), custom_call_target="tpu_custom_call" | custom-call | tf_op jit(solution)/shard_map/back/pallas_call | solution.py:487
  53.6 0.1 collective-permute-start.3
  53.8 2.0 %collective-permute-done.3.value = bf16[4,4,80,256]{3,2,1,0:T(8,128)(2,1)S(1)} collective-permute-done((bf16[4,4,80,256]{3,2,1,0:T(8,128)(2,1)S(1)}, bf16[4,4,80,256]{3,2,1,0:T(8,128)(2,1)S(1)}, u32[]{:S(2)}, u32[]{:S(2)}) %collective-permute-start.3) | collective-permute-done | bytes 655392 | tf_op jit(solution)/shard_map/ppermute | solution.py:382
  55.8 8.0 %collective-permute-done.6.rest_1_.c2 = bf16[2,256,1280]{2,1,0:T(8,128)(2,1)} collective-permute-done((bf16[2,256,1280]{2,1,0:T(8,128)(2,1)}, bf16[2,256,1280]{2,1,0:T(8,128)(2,1)}, u32[]{:S(2)}, u32[]{:S(2)}) %collective-permute-start.6) | collective-permute-done | bytes 1310752 | tf_op jit(solution)/shard_map/ppermute | solution.py:378
  64.0 2.4 %collective-permute-start.10 = (bf16[2,4,80,256]{3,2,1,0:T(8,128)(2,1)S(1)}, bf16[2,4,80,256]{3,2,1,0:T(8,128)(2,1)S(1)}, u32[]{:S(2)}, u32[]{:S(2)}) collective-permute-start(bf16[2,4,80,256]{3,2,1,0:T(8,128)(2,1)S(1)} %pad_maximum_fusion.3), channel_id=1, source_target_pairs={{0,96},{4,28},{8,104},{12,4},{16,112},{20,12},{24,120},{28,20},{32... | collective-permute-start | bytes 983048 | tf_op jit(solution)/shard_map/ppermute | solution.py:378
  66.3 1.5 %collective-permute-start.9 = (bf16[2,4,80,256]{3,2,1,0:T(8,128)(2,1)S(1)}, bf16[2,4,80,256]{3,2,1,0:T(8,128)(2,1)S(1)}, u32[]{:S(2)}, u32[]{:S(2)}) collective-permute-start(bf16[2,4,80,256]{3,2,1,0:T(8,128)(2,1)S(1)} %pad_maximum_fusion.2), channel_id=1, source_target_pairs={{0,64},{4,20},{8,72},{12,28},{16,80},{20,4},{24,88},{28,12},{32,96... | collective-permute-start | bytes 983048 | tf_op jit(solution)/shard_map/ppermute | solution.py:378
  67.9 0.6 collective-permute-start.8
  68.5 5.9 %collective-permute-done.10.r3 = bf16[2,4,80,256]{3,2,1,0:T(8,128)(2,1)S(1)} collective-permute-done((bf16[2,4,80,256]{3,2,1,0:T(8,128)(2,1)S(1)}, bf16[2,4,80,256]{3,2,1,0:T(8,128)(2,1)S(1)}, u32[]{:S(2)}, u32[]{:S(2)}) %collective-permute-start.10) | collective-permute-done | bytes 327712 | tf_op jit(solution)/shard_map/ppermute | solution.py:378
  74.4 0.7 collective-permute-done.9.r2
  75.1 3.4 %collective-permute-done.8.r1 = bf16[2,4,80,256]{3,2,1,0:T(8,128)(2,1)S(1)} collective-permute-done((bf16[2,4,80,256]{3,2,1,0:T(8,128)(2,1)S(1)}, bf16[2,4,80,256]{3,2,1,0:T(8,128)(2,1)S(1)}, u32[]{:S(2)}, u32[]{:S(2)}) %collective-permute-start.8) | collective-permute-done | bytes 327712 | tf_op jit(solution)/shard_map/ppermute | solution.py:378
  78.5 4.0 %grad.1 = (f32[80,1280]{1,0:T(8,128)S(1)}, bf16[80,1280]{1,0:T(8,128)(2,1)S(1)}, bf16[80,1280]{1,0:T(8,128)(2,1)S(1)}, bf16[80,1280]{1,0:T(8,128)(2,1)S(1)}) custom-call(bf16[4,4,80,256]{3,2,1,0:T(8,128)(2,1)S(1)} %get-tuple-element.42.mine, bf16[4,4,80,256]{3,2,1,0:T(8,128)(2,1)S(1)} %tie.3.got, bf16[2,4,80,256]{3,2,1,0:T(8,128)(2,1)S(1)} %collective-permute-done.8.r1, ...), custom_call_target="tpu_custom_call" | custom-call | flops 2000000000 | bytes 8000000 | tf_op jit(solution)/shard_map/grad/pallas_call | solution.py:504
  82.5 1.6 %collective-permute-start.11 = (bf16[80,1280]{1,0:T(8,128)(2,1)S(1)}, bf16[80,1280]{1,0:T(8,128)(2,1)S(1)}, u32[]{:S(2)}, u32[]{:S(2)}) collective-permute-start(bf16[80,1280]{1,0:T(8,128)(2,1)S(1)} %get-tuple-element.45), channel_id=1, source_target_pairs={{0,8},{4,36},{8,16},{12,44},{16,24},{20,52},{24,0},{28,60},{32,40}... | collective-permute-start | bytes 614408 | tf_op jit(solution)/shard_map/ppermute | solution.py:378
  84.0 2.7 %collective-permute-start.12 = (bf16[80,1280]{1,0:T(8,128)(2,1)S(1)}, bf16[80,1280]{1,0:T(8,128)(2,1)S(1)}, u32[]{:S(2)}, u32[]{:S(2)}) collective-permute-start(bf16[80,1280]{1,0:T(8,128)(2,1)S(1)} %get-tuple-element.46), channel_id=1, source_target_pairs={{0,16},{4,68},{8,24},{12,76},{16,0},{20,84},{24,8},{28,92},{32,48}... | collective-permute-start | bytes 614408 | tf_op jit(solution)/shard_map/ppermute | solution.py:378
  86.8 1.4 %collective-permute-start.13 = (bf16[80,1280]{1,0:T(8,128)(2,1)S(1)}, bf16[80,1280]{1,0:T(8,128)(2,1)S(1)}, u32[]{:S(2)}, u32[]{:S(2)}) collective-permute-start(bf16[80,1280]{1,0:T(8,128)(2,1)S(1)} %get-tuple-element.47), channel_id=1, source_target_pairs={{0,24},{4,100},{8,0},{12,108},{16,8},{20,116},{24,16},{28,124},{32... | collective-permute-start | bytes 614408 | tf_op jit(solution)/shard_map/ppermute | solution.py:378
  88.2 1.3 %collective-permute-done.11.r1 = bf16[80,1280]{1,0:T(8,128)(2,1)S(1)} collective-permute-done((bf16[80,1280]{1,0:T(8,128)(2,1)S(1)}, bf16[80,1280]{1,0:T(8,128)(2,1)S(1)}, u32[]{:S(2)}, u32[]{:S(2)}) %collective-permute-start.11) | collective-permute-done | bytes 204832 | tf_op jit(solution)/shard_map/ppermute | solution.py:378
  89.5 3.2 %collective-permute-done.12.r2 = bf16[80,1280]{1,0:T(8,128)(2,1)S(1)} collective-permute-done((bf16[80,1280]{1,0:T(8,128)(2,1)S(1)}, bf16[80,1280]{1,0:T(8,128)(2,1)S(1)}, u32[]{:S(2)}, u32[]{:S(2)}) %collective-permute-start.12) | collective-permute-done | bytes 204832 | tf_op jit(solution)/shard_map/ppermute | solution.py:378
  92.7 0.7 join.1
  93.4 0.1 collective-permute-start.14
  93.5 0.1 collective-permute-start.15
  93.6 3.1 %collective-permute-start.16 = (bf16[200,128]{1,0:T(8,128)(2,1)S(1)}, bf16[200,128]{1,0:T(8,128)(2,1)S(1)}, u32[]{:S(2)}, u32[]{:S(2)}) collective-permute-start(bf16[200,128]{1,0:T(8,128)(2,1)S(1)} %get-tuple-element.51), channel_id=1, source_target_pairs={{0,3},{1,0},{2,1},{3,2},{4,7},{5,4},{6,5},{7,6},{8,11},{9,8},{10,9... | collective-permute-start | bytes 153608 | tf_op jit(solution)/shard_map/ppermute | solution.py:524
  96.7 2.6 %collective-permute-done.14.r1 = bf16[200,128]{1,0:T(8,128)(2,1)S(1)} collective-permute-done((bf16[200,128]{1,0:T(8,128)(2,1)S(1)}, bf16[200,128]{1,0:T(8,128)(2,1)S(1)}, u32[]{:S(2)}, u32[]{:S(2)}) %collective-permute-start.14) | collective-permute-done | bytes 51232 | tf_op jit(solution)/shard_map/ppermute | solution.py:524
  99.3 0.9 collective-permute-done.16.r3
  100.2 0.7 total.1
  (60 shorter events, 0.3 us)
Async XLA Ops:
  0.6 6.1 %copy-start = (bf16[1,256,2816]{2,1,0:T(8,128)(2,1)S(1)}, bf16[1,256,2816]{2,1,0:T(8,128)(2,1)}, u32[]{:S(2)}) copy-start(bf16[1,256,2816]{2,1,0:T(8,128)(2,1)} %param.11) | copy-start | bytes 4325380
  0.6 6.1 %copy-start.17 = (s32[1,256]{1,0:T(1,128)S(1)}, s32[1,256]{1,0:T(1,128)}, u32[]{:S(2)}) copy-start(s32[1,256]{1,0:T(1,128)} %docs.7) | copy-start | bytes 3076
  0.7 5.8 %copy-start.24 = (f32[2816]{0:T(1024)S(1)}, f32[2816]{0:T(1024)}, u32[]{:S(2)}) copy-start(f32[2816]{0:T(1024)} %param.18) | copy-start | bytes 33796
  0.7 5.8 %copy-start.25 = (f32[40]{0:T(128)S(1)}, f32[40]{0:T(128)}, u32[]{:S(2)}) copy-start(f32[40]{0:T(128)} %param.16) | copy-start | bytes 484
  0.7 6.0 %copy-start.11 = (f32[1,40,256]{2,1,0:T(8,128)S(1)}, f32[1,40,256]{2,1,0:T(8,128)}, u32[]{:S(2)}) copy-start(f32[1,40,256]{2,1,0:T(8,128)} %param.13) | copy-start | bytes 122884
  0.7 6.0 %copy-start.19 = (f32[40]{0:T(128)S(1)}, f32[40]{0:T(128)}, u32[]{:S(2)}) copy-start(f32[40]{0:T(128)} %param.14) | copy-start | bytes 484
  0.7 6.0 %copy-start.21 = (f32[40]{0:T(128)S(1)}, f32[40]{0:T(128)}, u32[]{:S(2)}) copy-start(f32[40]{0:T(128)} %param.15) | copy-start | bytes 484
  0.7 6.0 %copy-start.10 = (f32[4,2816]{1,0:T(4,128)S(1)}, f32[4,2816]{1,0:T(4,128)}, u32[]{:S(2)}) copy-start(f32[4,2816]{1,0:T(4,128)} %w.3) | copy-start | bytes 135172
  0.7 25.8 %collective-permute-start.4 = (bf16[256,1280]{1,0:T(8,128)(2,1)}, bf16[256,1280]{1,0:T(8,128)(2,1)}, u32[]{:S(2)}, u32[]{:S(2)}) collective-permute-start(bf16[256,1280]{1,0:T(8,128)(2,1)} %bitcast.22), channel_id=1, source_target_pairs={{0,4},{4,0},{1,5},{5,1},{2,6},{6,2},{3,7},{7,3},{8,12},{12,8},{9,1... | collective-permute-start | bytes 1966088 | tf_op jit(solution)/shard_map/ppermute | solution.py:382
  2.6 8.5 %collective-permute-start = (bf16[8,2944]{1,0:T(8,128)(2,1)}, bf16[8,2944]{1,0:T(8,128)(2,1)S(1)}, u32[]{:S(2)}, u32[]{:S(2)}) collective-permute-start(bf16[8,2944]{1,0:T(8,128)(2,1)} %edge.1), channel_id=1, source_target_pairs={{0,1},{1,2},{2,3},{4,5},{5,6},{6,7},{8,9},{9,10},{10,11},{12,13},{... | collective-permute-start | bytes 141320 | tf_op jit(solution)/shard_map/ppermute | solution.py:367
  6.7 14.2 %copy-start.8 = (f32[1,2560]{1,0:T(1,128)}, f32[1,2560]{1,0:T(1,128)S(1)}, u32[]{:S(2)}) copy-start(f32[1,2560]{1,0:T(1,128)S(1)} %broadcast_in_dim_reshape.3.skip) | copy-start | bytes 30724
  11.0 9.8 %copy-start.12 = (f32[1,40,256]{2,1,0:T(8,128)S(1)}, f32[1,40,256]{2,1,0:T(8,128)}, u32[]{:S(2)}) copy-start(f32[1,40,256]{2,1,0:T(8,128)} %param.13) | copy-start | bytes 122884
  11.1 9.8 %copy-start.18 = (s32[1,256]{1,0:T(1,128)S(1)}, s32[1,256]{1,0:T(1,128)}, u32[]{:S(2)}) copy-start(s32[1,256]{1,0:T(1,128)} %docs.7) | copy-start | bytes 3076
  11.1 9.8 %copy-start.20 = (f32[40]{0:T(128)S(1)}, f32[40]{0:T(128)}, u32[]{:S(2)}) copy-start(f32[40]{0:T(128)} %param.14) | copy-start | bytes 484
  11.1 9.8 %copy-start.22 = (f32[40]{0:T(128)S(1)}, f32[40]{0:T(128)}, u32[]{:S(2)}) copy-start(f32[40]{0:T(128)} %param.15) | copy-start | bytes 484
  12.6 34.6 %collective-permute-start.1 = (bf16[144,2560]{1,0:T(8,128)(2,1)}, bf16[144,2560]{1,0:T(8,128)(2,1)S(1)}, u32[]{:S(2)}, u32[]{:S(2)}) collective-permute-start(bf16[144,2560]{1,0:T(8,128)(2,1)} %get-tuple-element.40), channel_id=1, source_target_pairs={{0,1},{1,2},{2,3},{4,5},{5,6},{6,7},{8,9},{9,10},{10,11},{12,13},{... | collective-permute-start | bytes 2211848 | tf_op jit(solution)/shard_map/ppermute | solution.py:367
  16.4 32.1 %collective-permute-start.2 = (bf16[144,2560]{1,0:T(8,128)(2,1)}, bf16[144,2560]{1,0:T(8,128)(2,1)}, u32[]{:S(2)}, u32[]{:S(2)}) collective-permute-start(bf16[144,2560]{1,0:T(8,128)(2,1)} %get-tuple-element.40), channel_id=1, source_target_pairs={{0,2},{1,3},{4,6},{5,7},{8,10},{9,11},{12,14},{13,15},{16,18},{17,... | collective-permute-start | bytes 2211848 | tf_op jit(solution)/shard_map/ppermute | solution.py:367
  20.9 5.7 %copy-start.23 = (bf16[1,256,1280]{2,1,0:T(8,128)(2,1)S(1)}, bf16[1,256,1280]{2,1,0:T(8,128)(2,1)}, u32[]{:S(2)}) copy-start(bf16[1,256,1280]{2,1,0:T(8,128)(2,1)} %param.21) | copy-start | bytes 1966084
  25.9 0.6 copy-start.13
  26.5 2.8 %copy-start.1 = (f32[256,2560]{1,0:T(8,128)}, f32[256,2560]{1,0:T(8,128)S(1)}, u32[]{:S(2)}) copy-start(f32[256,2560]{1,0:T(8,128)S(1)} %get-tuple-element.38.reach) | copy-start | bytes 7864324
  26.5 2.8 %copy-start.4 = (f32[256,512]{1,0:T(8,128)}, f32[256,512]{1,0:T(8,128)S(1)}, u32[]{:S(2)}) copy-start(f32[256,512]{1,0:T(8,128)S(1)} %get-tuple-element.32.early) | copy-start | bytes 1572868
  26.6 2.8 %copy-start.6 = (f32[256,256]{1,0:T(8,128)}, f32[256,256]{1,0:T(8,128)S(1)}, u32[]{:S(2)}) copy-start(f32[256,256]{1,0:T(8,128)S(1)} %get-tuple-element.35.scores) | copy-start | bytes 786436
  26.6 2.8 %copy-start.15 = (f32[40,256]{1,0:T(8,128)}, f32[40,256]{1,0:T(8,128)S(1)}, u32[]{:S(2)}) copy-start(f32[40,256]{1,0:T(8,128)S(1)} %get-tuple-element.34.step) | copy-start | bytes 122884
  29.4 26.4 %collective-permute-start.5 = (bf16[2,256,1280]{2,1,0:T(8,128)(2,1)}, bf16[2,256,1280]{2,1,0:T(8,128)(2,1)S(1)}, u32[]{:S(2)}, u32[]{:S(2)}) collective-permute-start(bf16[2,256,1280]{2,1,0:T(8,128)(2,1)} %pad_maximum_fusion.c0), channel_id=1, source_target_pairs={{0,32},{4,12},{8,40},{12,20},{16,48},{20,28},{24,56},{28,4},{32,64... | collective-permute-start | bytes 3932168 | tf_op jit(solution)/shard_map/ppermute | solution.py:378
  31.0 32.8 %collective-permute-start.6 = (bf16[2,256,1280]{2,1,0:T(8,128)(2,1)}, bf16[2,256,1280]{2,1,0:T(8,128)(2,1)}, u32[]{:S(2)}, u32[]{:S(2)}) collective-permute-start(bf16[2,256,1280]{2,1,0:T(8,128)(2,1)} %pad_maximum_fusion.c0), channel_id=1, source_target_pairs={{0,64},{4,20},{8,72},{12,28},{16,80},{20,4},{24,88},{28,12},{32,96... | collective-permute-start | bytes 3932168 | tf_op jit(solution)/shard_map/ppermute | solution.py:378
  33.9 29.9 %collective-permute-start.7 = (bf16[2,256,1280]{2,1,0:T(8,128)(2,1)}, bf16[2,256,1280]{2,1,0:T(8,128)(2,1)}, u32[]{:S(2)}, u32[]{:S(2)}) collective-permute-start(bf16[2,256,1280]{2,1,0:T(8,128)(2,1)} %pad_maximum_fusion.c0), channel_id=1, source_target_pairs={{0,96},{4,28},{8,104},{12,4},{16,112},{20,12},{24,120},{28,20},{32... | collective-permute-start | bytes 3932168 | tf_op jit(solution)/shard_map/ppermute | solution.py:378
  36.1 1.3 %copy-start.3 = (bf16[1,256,2560]{2,1,0:T(8,128)(2,1)S(1)}, bf16[1,256,2560]{2,1,0:T(8,128)(2,1)}, u32[]{:S(2)}) copy-start(bf16[1,256,2560]{2,1,0:T(8,128)(2,1)} %param.12) | copy-start | bytes 3932164
  37.4 0.9 copy-start.7
  38.3 0.7 copy-start.9
  39.0 0.8 copy-start.14
  39.8 0.8 copy-start.16
  40.6 7.9 %copy-start.2 = (f32[256,2560]{1,0:T(8,128)S(1)}, f32[256,2560]{1,0:T(8,128)}, u32[]{:S(2)}) copy-start(f32[256,2560]{1,0:T(8,128)} %copy-done.1) | copy-start | bytes 7864324
  40.6 7.9 %copy-start.5 = (f32[256,512]{1,0:T(8,128)S(1)}, f32[256,512]{1,0:T(8,128)}, u32[]{:S(2)}) copy-start(f32[256,512]{1,0:T(8,128)} %copy-done.4) | copy-start | bytes 1572868
  53.6 2.2 %collective-permute-start.3 = (bf16[4,4,80,256]{3,2,1,0:T(8,128)(2,1)S(1)}, bf16[4,4,80,256]{3,2,1,0:T(8,128)(2,1)S(1)}, u32[]{:S(2)}, u32[]{:S(2)}) collective-permute-start(bf16[4,4,80,256]{3,2,1,0:T(8,128)(2,1)S(1)} %get-tuple-element.43), channel_id=1, source_target_pairs={{0,4},{4,0},{1,5},{5,1},{2,6},{6,2},{3,7},{7,3},{8,12},{12,8},{9,1... | collective-permute-start | bytes 1966088 | tf_op jit(solution)/shard_map/ppermute | solution.py:382
  64.0 10.5 %collective-permute-start.10 = (bf16[2,4,80,256]{3,2,1,0:T(8,128)(2,1)S(1)}, bf16[2,4,80,256]{3,2,1,0:T(8,128)(2,1)S(1)}, u32[]{:S(2)}, u32[]{:S(2)}) collective-permute-start(bf16[2,4,80,256]{3,2,1,0:T(8,128)(2,1)S(1)} %pad_maximum_fusion.3), channel_id=1, source_target_pairs={{0,96},{4,28},{8,104},{12,4},{16,112},{20,12},{24,120},{28,20},{32... | collective-permute-start | bytes 983048 | tf_op jit(solution)/shard_map/ppermute | solution.py:378
  66.3 8.8 %collective-permute-start.9 = (bf16[2,4,80,256]{3,2,1,0:T(8,128)(2,1)S(1)}, bf16[2,4,80,256]{3,2,1,0:T(8,128)(2,1)S(1)}, u32[]{:S(2)}, u32[]{:S(2)}) collective-permute-start(bf16[2,4,80,256]{3,2,1,0:T(8,128)(2,1)S(1)} %pad_maximum_fusion.2), channel_id=1, source_target_pairs={{0,64},{4,20},{8,72},{12,28},{16,80},{20,4},{24,88},{28,12},{32,96... | collective-permute-start | bytes 983048 | tf_op jit(solution)/shard_map/ppermute | solution.py:378
  67.9 10.6 %collective-permute-start.8 = (bf16[2,4,80,256]{3,2,1,0:T(8,128)(2,1)S(1)}, bf16[2,4,80,256]{3,2,1,0:T(8,128)(2,1)S(1)}, u32[]{:S(2)}, u32[]{:S(2)}) collective-permute-start(bf16[2,4,80,256]{3,2,1,0:T(8,128)(2,1)S(1)} %pad_maximum_fusion.1), channel_id=1, source_target_pairs={{0,32},{4,12},{8,40},{12,20},{16,48},{20,28},{24,56},{28,4},{32,64... | collective-permute-start | bytes 983048 | tf_op jit(solution)/shard_map/ppermute | solution.py:378
  82.5 7.0 %collective-permute-start.11 = (bf16[80,1280]{1,0:T(8,128)(2,1)S(1)}, bf16[80,1280]{1,0:T(8,128)(2,1)S(1)}, u32[]{:S(2)}, u32[]{:S(2)}) collective-permute-start(bf16[80,1280]{1,0:T(8,128)(2,1)S(1)} %get-tuple-element.45), channel_id=1, source_target_pairs={{0,8},{4,36},{8,16},{12,44},{16,24},{20,52},{24,0},{28,60},{32,40}... | collective-permute-start | bytes 614408 | tf_op jit(solution)/shard_map/ppermute | solution.py:378
  84.0 8.7 %collective-permute-start.12 = (bf16[80,1280]{1,0:T(8,128)(2,1)S(1)}, bf16[80,1280]{1,0:T(8,128)(2,1)S(1)}, u32[]{:S(2)}, u32[]{:S(2)}) collective-permute-start(bf16[80,1280]{1,0:T(8,128)(2,1)S(1)} %get-tuple-element.46), channel_id=1, source_target_pairs={{0,16},{4,68},{8,24},{12,76},{16,0},{20,84},{24,8},{28,92},{32,48}... | collective-permute-start | bytes 614408 | tf_op jit(solution)/shard_map/ppermute | solution.py:378
  86.8 5.9 %collective-permute-start.13 = (bf16[80,1280]{1,0:T(8,128)(2,1)S(1)}, bf16[80,1280]{1,0:T(8,128)(2,1)S(1)}, u32[]{:S(2)}, u32[]{:S(2)}) collective-permute-start(bf16[80,1280]{1,0:T(8,128)(2,1)S(1)} %get-tuple-element.47), channel_id=1, source_target_pairs={{0,24},{4,100},{8,0},{12,108},{16,8},{20,116},{24,16},{28,124},{32... | collective-permute-start | bytes 614408 | tf_op jit(solution)/shard_map/ppermute | solution.py:378
  93.4 5.9 %collective-permute-start.14 = (bf16[200,128]{1,0:T(8,128)(2,1)S(1)}, bf16[200,128]{1,0:T(8,128)(2,1)S(1)}, u32[]{:S(2)}, u32[]{:S(2)}) collective-permute-start(bf16[200,128]{1,0:T(8,128)(2,1)S(1)} %get-tuple-element.49), channel_id=1, source_target_pairs={{0,1},{1,2},{2,3},{3,0},{4,5},{5,6},{6,7},{7,4},{8,9},{9,10},{10,1... | collective-permute-start | bytes 153608 | tf_op jit(solution)/shard_map/ppermute | solution.py:524
  93.5 5.9 %collective-permute-start.15 = (bf16[200,128]{1,0:T(8,128)(2,1)S(1)}, bf16[200,128]{1,0:T(8,128)(2,1)S(1)}, u32[]{:S(2)}, u32[]{:S(2)}) collective-permute-start(bf16[200,128]{1,0:T(8,128)(2,1)S(1)} %get-tuple-element.50), channel_id=1, source_target_pairs={{0,2},{1,3},{2,0},{3,1},{4,6},{5,7},{6,4},{7,5},{8,10},{9,11},{10,... | collective-permute-start | bytes 153608 | tf_op jit(solution)/shard_map/ppermute | solution.py:524
  93.6 6.6 %collective-permute-start.16 = (bf16[200,128]{1,0:T(8,128)(2,1)S(1)}, bf16[200,128]{1,0:T(8,128)(2,1)S(1)}, u32[]{:S(2)}, u32[]{:S(2)}) collective-permute-start(bf16[200,128]{1,0:T(8,128)(2,1)S(1)} %get-tuple-element.51), channel_id=1, source_target_pairs={{0,3},{1,0},{2,1},{3,2},{4,7},{5,4},{6,5},{7,6},{8,11},{9,8},{10,9... | collective-permute-start | bytes 153608 | tf_op jit(solution)/shard_map/ppermute | solution.py:524

commit v4 on v3

--- a/solution.py
+++ b/solution.py
@@ -86,13 +86,7 @@
     out[:, C_ALL:] = jnp.broadcast_to(docb, (8, LANES)).astype(BF16)
 
 
-def tie_kernel(value, *rest):
-    del value, rest
-
-
-def front_kernel(conv, step_far, bias, rates, w, cb, docs, act, state, info, top, win, dwin, masks, xs, fac, step_in, sem):
-    fetch = pltpu.make_async_copy(step_far, step_in, sem)
-    fetch.start()
+def front_kernel(conv, step_in, bias, rates, w, cb, docs, act, state, info, top, win, dwin, masks, xs, fac):
     doc_row = docs[...].astype(F32)
     docb = column(doc_row, LANES)
     dwin[0:8, :] = jnp.zeros((8, LANES), F32)
@@ -107,7 +101,7 @@
         at = pl.ds(pl.multiple_of(j * LANES, LANES), LANES)
         win[slot, 8:, :] = conv[:, at].astype(F32)
         taps = w[:, at]
-        total = cb[:, at] + taps[3:4] * win[slot, 8:, :]
+        total = cb[at].reshape(1, LANES) + taps[3:4] * win[slot, 8:, :]
         for k in range(3):
             total = total + (taps[k : k + 1] * win[slot, 5 + k : 5 + k + T, :]) * masks[k]
         out = silu(total).astype(BF16)
@@ -116,7 +110,6 @@
 
     for slot in range(2):
         conv_chunk(XCHUNKS + slot, slot)
-    fetch.wait()
     step, cum = steps(step_in, bias, rates)
     tail = (doc_row == doc_row[:, T - 1 : T]).astype(F32)
     total = cum[:, T - 1 : T]
@@ -155,7 +148,7 @@
     def chunk(j):
         at = slice(j * LANES, j * LANES + LANES)
         win = jnp.concatenate([halo[:, at].astype(F32), rows[:, at].astype(F32)], 0)
-        total = cb[:, at] + w[3:4, at] * win[8:24]
+        total = cb[at].reshape(1, LANES) + w[3:4, at] * win[8:24]
         for k in range(3):
             total = total + (w[k : k + 1, at] * win[5 + k : 21 + k]) * masks[k]
         out = silu(total).astype(BF16)
@@ -169,18 +162,20 @@
         at, out = chunk(j)
         scaled = (out.astype(F32) * top[:, at]).astype(BF16)
         scaled = jnp.concatenate([scaled, jnp.zeros((LANES - 16, LANES), BF16)], 0)
-        msg[0:N, at] = (state[:, at] + dot(b_t, scaled)).astype(BF16)
+        value = (state[:, at] + dot(b_t, scaled)).astype(BF16)
+        msg[0:N, at] = value
         msg[N:, at] = info[:, at]
 
 
-def pair_chunk(j, act, cum, step, scores, fac, skip):
+def pair_chunk(j, act, cum, step, scores, fac, sfac):
     half = T // 2
     at = pl.ds(pl.multiple_of(j * LANES, LANES), LANES)
     vals = act[:, at]
     lanes = lax.broadcasted_iota(jnp.int32, (T, LANES), 1)
     cols = dot(fac[...], head_pick(j, 2 * LANES))
-    top = skip[:, at] * vals[0:half].astype(F32)
-    low = skip[:, at] * vals[half:].astype(F32)
+    skip = dot(sfac[...], head_pick(j, LANES))[0:1]
+    top = skip * vals[0:half].astype(F32)
+    low = skip * vals[half:].astype(F32)
     for k in range(2):
         mine = jnp.where((lanes >= HD) == (k == 1), vals.astype(F32), 0.0).astype(BF16)
         col = cols[:, k * LANES : (k + 1) * LANES]
@@ -198,7 +193,10 @@
     return jnp.concatenate([top, low], 0)
 
 
-def early_kernel(act, step_in, bias, rates, docs, halo, skip, local, reach, cum, step, scores, fac, efac):
+def early_kernel(act, step_in, bias, rates, docs, halo, skip, cot, other, local, reach, cum, step, scores, fac, cots, sfac, efac):
+    cots[0] = cot[...]
+    cots[1] = other[...]
+    sfac[...] = split_rows(jnp.broadcast_to(upright(skip[...]), (H, LANES))).T[0:16].astype(BF16)
     step[...], cum[...] = steps(step_in, bias, rates)
     doc_row = docs[...].astype(F32)
     prev_tag = halo[:, C_ALL : C_ALL + LANES].astype(F32)[7:8, :]
@@ -227,16 +225,16 @@
 
     def pair(j, carry):
         at = pl.ds(pl.multiple_of(j * LANES, LANES), LANES)
-        local[:, at] = pair_chunk(j, act, cum, step, scores, fac, skip)
+        local[:, at] = pair_chunk(j, act, cum, step, scores, fac, sfac)
         return carry
 
     lax.fori_loop(0, EARLY, pair, 0)
 
 
-def late_kernel(act, cum, step, scores, fac, gate, skip, local, sgate):
+def late_kernel(act, cum, step, scores, fac, gate, sfac, local, sgate):
     def pair(j, carry):
         at = pl.ds(pl.multiple_of(j * LANES, LANES), LANES)
-        local[:, at] = pair_chunk(j + EARLY, act, cum, step, scores, fac, skip)
+        local[:, at] = pair_chunk(j + EARLY, act, cum, step, scores, fac, sfac)
         return carry
 
     lax.fori_loop(0, XCHUNKS - EARLY, pair, 0)
@@ -249,7 +247,7 @@
     lax.fori_loop(0, XCHUNKS // 2, gates, 0)
 
 
-def back_kernel(early, late, reach, sgate, act, one, two, gain, place, normed, mine, give, gated, squares, turned, flat, sem):
+def back_kernel(early, late, reach, sgate, act, one, two, gain, normed, mine, give, gated, squares, turned, flat, sem):
     c_map = act[:, INNER + N :]
     wide = 2 * LANES
 
@@ -283,7 +281,7 @@
     def second(i, carry):
         for k in range(4):
             at = pl.ds(pl.multiple_of((4 * i + k) * LANES, LANES), LANES)
-            value = (gated[:, at] * squares[...] * gain[:, at]).astype(BF16)
+            value = (gated[:, at] * squares[...] * gain[at].reshape(1, LANES)).astype(BF16)
             flat[:, at] = value
             turned[at, :] = dot(eye, value, ((1,), (1,))).astype(BF16)
         return carry
@@ -291,7 +289,7 @@
     lax.fori_loop(0, 5, second, 0)
     out = pltpu.make_async_copy(flat, normed, sem)
     out.start()
-    y, x, c = place[0], place[1], place[2]
+    y, x, c = [lax.axis_index(a) for a in ("y", "x", "c")]
     far_y = [lax.rem(i - y + 4, 4) for i in range(4)]
     far_x = [lax.rem(i - x + 4, 4) for i in range(4)]
 
@@ -299,8 +297,8 @@
         for i in range(4):
             for j in range(4):
                 row = 80 * (2 * (4 * i + j))
-                zero[far_y[i], far_x[j]] = turned[row : row + 80, :]
-                other[far_x[j], far_y[i]] = turned[row + 80 : row + 160, :]
+                zero[far_y[i], j] = turned[row : row + 80, :]
+                other[far_x[j], i] = turned[row + 80 : row + 160, :]
 
     @pl.when(c == 0)
     def _():
@@ -313,7 +311,14 @@
     out.wait()
 
 
-def grad_kernel(mine, got, r1, r2, r3, c0, c1, c2, c3, keep, s1, s2, s3):
+def load_kernel(mine, got, c1, c2, c3, *outs):
+    del c1, c2, c3
+    for k, out in enumerate(outs):
+        out[0] = mine[k + 1]
+        out[1] = got[k + 1]
+
+
+def grad_kernel(mine, got, r1, r2, r3, c0, c1, c2, c3, out, flat):
     left = [mine[0].reshape(320, T), got[0].reshape(320, T)]
     right = [c0[0], c0[1]]
     for r, c in ((r1, c1), (r2, c2), (r3, c3)):
@@ -325,24 +330,19 @@
         total = dot(left[0], right[0][:, at])
         for k in range(1, 8):
             total = total + dot(left[k], right[k][:, at])
-        keep[:, at] = total[0:80]
-        for k, out in enumerate((s1, s2, s3)):
-            out[:, at] = total[80 * k + 80 : 80 * k + 160].astype(BF16)
-
-
-def join_kernel(keep, r1, r2, r3, place, own, s1, s2, s3, total, flat):
-    total[...] = keep[...] + r1[...].astype(F32) + r2[...].astype(F32) + r3[...].astype(F32)
-    for z in range(4):
-        for k in range(10):
-            flat[z, 20 * k : 20 * k + 20, :] = total[20 * z : 20 * z + 20, k * LANES : k * LANES + LANES]
-    z = place[3]
-    own[...] = flat[z]
-    for k, out in enumerate((s1, s2, s3)):
-        out[...] = flat[lax.rem(z + k + 1, 4)].astype(BF16)
-
-
-def sum_kernel(own, r1, r2, r3, out, flat):
-    flat[...] = own[...] + r1[...].astype(F32) + r2[...].astype(F32) + r3[...].astype(F32)
+        for k in range(2):
+            row = 20 * (2 * n + k)
+            for i in range(16):
+                flat[i, row : row + 20, :] = total[20 * i : 20 * i + 20, k * LANES : k * LANES + LANES]
+    for i in range(16):
+        out[i] = flat[i].astype(BF16)
+
+
+def sum_kernel(pieces, out, flat):
+    total = pieces[0].astype(F32)
+    for i in range(1, 16):
+        total = total + pieces[i].astype(F32)
+    flat[...] = total
     for k in range(10):
         out[:, k * LANES : k * LANES + LANES] = flat[20 * k : 20 * k + 20, :]
 
@@ -378,22 +378,17 @@
     return lax.ppermute(value, ("y", "x", "c"), pairs)
 
 
+def place_of(y, x, c, z):
+    return ((y * 4 + x) * 2 + c) * 4 + z
+
+
+PLANES = [[place_of(y, k, 0, z) for k in range(4) for z in range(4)] for y in range(4)] + [
+    [place_of(k, x, 1, z) for k in range(4) for z in range(4)] for x in range(4)
+]
+
+
 def swapped(value):
     return lax.ppermute(value, "c", [(0, 1), (1, 0)])
-
-
-def tied(value, *others):
-    anywhere = pl.BlockSpec(memory_space=pl.ANY)
-    return call(
-        tie_kernel,
-        "tie",
-        shape(value.shape, value.dtype),
-        [],
-        4,
-        in_specs=[anywhere] * (1 + len(others)),
-        out_specs=anywhere,
-        input_output_aliases={0: 0},
-    )(value, *others)
 
 
 def whole(dims):
@@ -403,18 +398,19 @@
 def per_device(conv_input, gate_input, step_input, step_bias, log_rates, skip_gain, conv_weight, conv_bias, norm_gain, doc_ids, cotangent):
     conv = conv_input[0]
     vmem = pl.BlockSpec(memory_space=VMEM)
+    anywhere = pl.BlockSpec(memory_space=pl.ANY)
     halo = call(
         edge_kernel,
         "edge",
         shape((8, C_ALL + LANES), BF16),
         [VMEM((16, C_ALL), BF16), VMEM((1, T), jnp.int32), pltpu.SemaphoreType.DMA((2,))],
-        62,
+        63,
         moved=10**5,
-        in_specs=[pl.BlockSpec(memory_space=pltpu.HBM)] * 2,
+        in_specs=[anywhere] * 2,
     )(conv, doc_ids)
     halo = shifted(halo, 1)
+    step_in, bias, rates = step_input[0], step_bias[None], log_rates[None]
     cot_other = swapped(cotangent[0])
-    place = jnp.stack([lax.axis_index(a) for a in ("y", "x", "c", "z")]).astype(jnp.int32)
     act, state, info, top = call(
         front_kernel,
         "front",
@@ -430,15 +426,12 @@
             VMEM((3, T, LANES), F32),
             VMEM((T, INNER), BF16),
             VMEM((T + LANES, LANES), BF16),
-            VMEM((H, T), F32),
-            pltpu.SemaphoreType.DMA,
         ],
-        16,
+        8,
         flops=10**9,
         moved=4 * 10**6,
         special=10**6,
-        in_specs=[vmem, pl.BlockSpec(memory_space=pltpu.HBM)] + [vmem] * 5,
-    )(conv, step_input[0], step_bias[None], log_rates[None], conv_weight, conv_bias[None], doc_ids)
+    )(conv, step_in, bias, rates, conv_weight, conv_bias, doc_ids)
     act, msg = call(
         fix_kernel,
         "fix",
@@ -451,7 +444,7 @@
             whole((8, C_ALL + LANES)),
             whole((16, C_ALL)),
             whole((4, C_ALL)),
-            whole((1, C_ALL)),
+            whole((C_ALL,)),
             whole((1, T)),
             whole((16, C_ALL)),
             whole((N, INNER)),
@@ -460,11 +453,10 @@
         ],
         out_specs=(whole((16, C_ALL)), whole((MSG, INNER))),
         input_output_aliases={5: 0},
-    )(halo, conv, conv_weight, conv_bias[None], doc_ids, act, state, info, top)
+    )(halo, conv, conv_weight, conv_bias, doc_ids, act, state, info, top)
     one = shifted(msg, 1)
     two = shifted(msg, 2)
-    skip = jnp.repeat(skip_gain, HD)[None]
-    early, reach, cum, step, scores, fac = call(
+    early, reach, cum, step, scores, fac, cots, sfac = call(
         early_kernel,
         "early",
         (
@@ -474,15 +466,16 @@
             shape((H, T)),
             shape((T, T)),
             shape((T, LANES), BF16),
+            shape((2, T, D), BF16),
+            shape((16, LANES), BF16),
         ),
         [VMEM((T, LANES), BF16)],
-        16,
-    )(act, step_input[0], step_bias[None], log_rates[None], doc_ids, halo, skip)
-    cots = jnp.stack([cotangent[0], tied(cot_other, fac)])
+        8,
+    )(act, step_in, bias, rates, doc_ids, halo, skip_gain[None], cotangent[0], cot_other)
     c1, c2, c3 = [around(cots, k, "y") for k in (1, 2, 3)]
     late, sgate = call(
-        late_kernel, "late", (shape((T, INNER - EARLY * LANES)), shape((T, INNER))), [], 24
-    )(act, cum, step, scores, fac, gate_input[0], skip)
+        late_kernel, "late", (shape((T, INNER - EARLY * LANES)), shape((T, INNER))), [], 8
+    )(act, cum, step, scores, fac, gate_input[0], sfac)
     block = (4, 4, 80, T)
     normed, mine, give = call(
         back_kernel,
@@ -495,34 +488,30 @@
             VMEM((T, INNER), BF16),
             pltpu.SemaphoreType.DMA,
         ],
-        24,
-        in_specs=[vmem] * 8 + [pl.BlockSpec(memory_space=pltpu.SMEM)],
+        12,
         out_specs=(pl.BlockSpec(memory_space=pltpu.HBM), vmem, vmem),
-    )(early, late, reach, sgate, act, one, two, norm_gain[None], place)
-    got = tied(swapped(give), c1, c2, c3)
-    r1, r2, r3 = [around(jnp.stack([mine[k], got[k]]), k, "y") for k in (1, 2, 3)]
-    keep, s1, s2, s3 = call(
+    )(early, late, reach, sgate, act, one, two, norm_gain)
+    got = swapped(give)
+    sends = call(
+        load_kernel,
+        "load",
+        (shape((2, 4, 80, T), BF16),) * 3,
+        [],
+        4,
+        in_specs=[vmem] * 2 + [anywhere] * 3,
+    )(mine, got, c1, c2, c3)
+    r1, r2, r3 = [around(v, k + 1, "y") for k, v in enumerate(sends)]
+    packed = call(
         grad_kernel,
         "grad",
-        (shape((80, D)),) + (shape((80, D), BF16),) * 3,
-        [],
-        24,
+        shape((16, 200, LANES), BF16),
+        [VMEM((16, 200, LANES), F32)],
+        10,
         flops=2 * 10**9,
         moved=8 * 10**6,
     )(mine, got, r1, r2, r3, cots, c1, c2, c3)
-    t1, t2, t3 = [around(v, k, "x") for k, v in ((1, s1), (2, s2), (3, s3))]
-    small = (200, LANES)
-    own, s1, s2, s3 = call(
-        join_kernel,
-        "join",
-        (shape(small),) + (shape(small, BF16),) * 3,
-        [VMEM((80, D), F32), VMEM((4,) + small, F32)],
-        8,
-        moved=10**6,
-        in_specs=[vmem] * 4 + [pl.BlockSpec(memory_space=pltpu.SMEM)],
-    )(keep, t1, t2, t3, place)
-    u1, u2, u3 = [lax.ppermute(v, "z", [(i, (i + k) % 4) for i in range(4)]) for k, v in ((1, s1), (2, s2), (3, s3))]
-    grad = call(sum_kernel, "total", shape((20, D)), [VMEM(small, F32)], 8, moved=10**6)(own, u1, u2, u3)
+    pieces = lax.all_to_all(packed, ("y", "x", "c", "z"), 0, 0, axis_index_groups=PLANES)
+    grad = call(sum_kernel, "total", shape((20, D)), [VMEM((200, LANES), F32)], 8, moved=10**6)(pieces)
     return (normed[None], grad)
 
 

time: 102 us -> 92.6 us (0.908)
  blocking collectives: 0 us -> 16.2 us
  starting transfers between devices: 31.8 us -> 22.4 us
  Pallas kernels: 29.5 us -> 24.7 us
  local copies, waits for them, and re-layouts: 6.18 us -> 1.41 us
  other arithmetic: 2.95 us -> 0 us
  waiting for transfers between devices: 29.4 us -> 26.7 us
    all_to_all x0 -> x1, blocking collectives: none -> 16.2 us  [per_device(): lax.all_to_all(packed, ('y', 'x', 'c', 'z'), 0, 0, axis_index_groups=PLANES)]
    ppermute x3, waiting for transfers between devices: 1.36 us -> 10.6 us  [shifted(): return lax.ppermute(value, 'z', [(i, i + by) for i in range(4 - by)])]
    ppermute x9 -> x6, waiting for transfers between devices: 22.5 us -> 14 us  [around(): return lax.ppermute(value, ('y', 'x', 'c'), pairs)]
    ppermute x9 -> x6, starting transfers between devices: 16.1 us -> 10.8 us  [around(): return lax.ppermute(value, ('y', 'x', 'c'), pairs)]
    unnamed x52 -> x22, local copies, waits for them, and re-layouts: 5.24 us -> 1.41 us
    ppermute x3 -> x0, waiting for transfers between devices: 3.49 us -> none  [per_device(): lax.ppermute(v, 'z', [(i, (i + k) % 4) for i in range(4)])]
    ppermute x3 -> x0, starting transfers between devices: 3.29 us -> none  [per_device(): lax.ppermute(v, 'z', [(i, (i + k) % 4) for i in range(4)])]
    another operation x5 -> x0, other arithmetic: 2.95 us -> none  [the longest x1 2.77 us: per_device(): cots = jnp.stack([cotangent[0], tied(cot_other, fac)])]
  transfers between devices with their start and end apart: 17 -> 11, of which waited for: 10 -> 5; matrix products, arithmetic and copies ran while one was open for 4% -> 0% of each run, Pallas kernels for 24% -> 24%
where the time goes in v4:
time: 92.6 us; the launch traced here: 92.3 us
  waiting for transfers between devices  26.7 us (29%)
  Pallas kernels  24.7 us (27%)
  starting transfers between devices  22.4 us (24%)
  blocking collectives  16.2 us (17%)
  local copies, waits for them, and re-layouts  1.41 us (2%)
    all_to_all x1, blocking collectives, per_device(): lax.all_to_all(packed, ('y', 'x', 'c', 'z'), 0, 0, axis_index_groups=PLANES)  16.2 us
    ppermute x6, waiting for transfers between devices, around(): return lax.ppermute(value, ('y', 'x', 'c'), pairs)  14 us
    ppermute x3, starting transfers between devices, shifted(): return lax.ppermute(value, 'z', [(i, i + by) for i in range(4 - by)])  11.4 us
    ppermute x6, starting transfers between devices, around(): return lax.ppermute(value, ('y', 'x', 'c'), pairs)  10.8 us
    ppermute x3, waiting for transfers between devices, shifted(): return lax.ppermute(value, 'z', [(i, i + by) for i in range(4 - by)])  10.6 us
    pallas_call x1, Pallas kernels, per_device(): call(late_kernel, 'late', (shape((T, INNER - EARLY * LANES)), shape((T, I...  6.63 us
    pallas_call x1, Pallas kernels, per_device(): call(early_kernel, 'early', (shape((T, EARLY * LANES)), shape((T, INNER))...  5.13 us
    pallas_call x1, Pallas kernels, per_device(): call(back_kernel, 'back', (shape((T, INNER), BF16), shape(block, BF16), s...  4.07 us
  transfers between devices with their start and end apart: 11, of which 5 were waited for; matrix products, arithmetic and copies ran while one was open for 0% of the time, Pallas kernels for 24%

profile of v4, /device:TPU:0, one launch (start us, length us, event | category | flops | bytes accessed | tf_op | source)
XLA Modules:
  0.0 92.3 jit_solution(1784310855599146412)
XLA Ops:
  0.6 0.0 copy-start.7
  0.6 0.0 copy-start.4
  0.7 0.0 copy-start.8
  0.7 0.0 copy-start.9
  0.7 0.0 copy-start.3
  0.7 0.0 copy-start.6
  0.7 0.1 collective-permute-start.1
  0.8 1.6 %edge.1 = bf16[8,2944]{1,0:T(8,128)(2,1)} custom-call(bf16[256,2816]{1,0:T(8,128)(2,1)} %bitcast.8, s32[1,256]{1,0:T(1,128)} %docs.7), custom_call_target="tpu_custom_call" | custom-call | bytes 100000 | tf_op jit(solution)/shard_map/edge/pallas_call | solution.py:402
  2.4 3.9 %collective-permute-start = (bf16[8,2944]{1,0:T(8,128)(2,1)}, bf16[8,2944]{1,0:T(8,128)(2,1)S(1)}, u32[]{:S(2)}, u32[]{:S(2)}) collective-permute-start(bf16[8,2944]{1,0:T(8,128)(2,1)} %edge.1), channel_id=1, source_target_pairs={{0,1},{1,2},{2,3},{4,5},{5,6},{6,7},{8,9},{9,10},{10,11},{12,13},{... | collective-permute-start | bytes 141320 | tf_op jit(solution)/shard_map/ppermute | solution.py:367
  6.3 0.0 copy-done.7
  6.3 0.0 copy-done.4
  6.3 0.0 copy-done.8
  6.4 0.0 copy-start
  6.4 1.4 %copy-done = bf16[1,256,2816]{2,1,0:T(8,128)(2,1)S(1)} copy-done((bf16[1,256,2816]{2,1,0:T(8,128)(2,1)S(1)}, bf16[1,256,2816]{2,1,0:T(8,128)(2,1)}, u32[]{:S(2)}) %copy-start) | copy-done | bytes 1441816
  7.7 3.9 %front.1 = (bf16[256,2816]{1,0:T(8,128)(2,1)S(1)}, f32[128,2560]{1,0:T(8,128)S(1)}, bf16[16,2560]{1,0:T(8,128)(2,1)S(1)}, f32[16,2560]{1,0:T(8,128)S(1)}) custom-call(bf16[256,2816]{1,0:T(8,128)(2,1)S(1)} %bitcast.9, f32[40,256]{1,0:T(8,128)S(1)} %bitcast.14, f32[1,40]{1,0:T(1,128)S(1)} %bitcast.16, f32[1,40]{1,0:T(1,128)S(1)} %bitcast.18, ...), custom_call_target="tpu_custom_call" | custom-call | flops 1000000000 | bytes 4000000 | tf_op jit(solution)/shard_map/front/pallas_call | solution.py:414
  11.6 0.0 collective-permute-done.halo
  11.7 0.0 copy-start.2
  11.7 0.0 copy-start.10
  11.7 0.6 fix.1
  12.3 3.9 %collective-permute-start.2 = (bf16[144,2560]{1,0:T(8,128)(2,1)S(1)}, bf16[144,2560]{1,0:T(8,128)(2,1)S(1)}, u32[]{:S(2)}, u32[]{:S(2)}) collective-permute-start(bf16[144,2560]{1,0:T(8,128)(2,1)S(1)} %get-tuple-element.38), channel_id=1, source_target_pairs={{0,1},{1,2},{2,3},{4,5},{5,6},{6,7},{8,9},{9,10},{10,11},{12,13},{... | collective-permute-start | bytes 2211848 | tf_op jit(solution)/shard_map/ppermute | solution.py:367
  16.2 3.6 %collective-permute-start.3 = (bf16[144,2560]{1,0:T(8,128)(2,1)S(1)}, bf16[144,2560]{1,0:T(8,128)(2,1)S(1)}, u32[]{:S(2)}, u32[]{:S(2)}) collective-permute-start(bf16[144,2560]{1,0:T(8,128)(2,1)S(1)} %get-tuple-element.38), channel_id=1, source_target_pairs={{0,2},{1,3},{4,6},{5,7},{8,10},{9,11},{12,14},{13,15},{16,18},{17,... | collective-permute-start | bytes 2211848 | tf_op jit(solution)/shard_map/ppermute | solution.py:367
  19.8 0.0 collective-permute-done.1.other
  19.8 0.0 copy-done.2
  19.8 0.0 copy-done.10
  19.8 0.0 copy-start.1
  19.8 5.1 %early.1 = (f32[256,512]{1,0:T(8,128)S(1)}, f32[256,2560]{1,0:T(8,128)S(1)}, f32[40,256]{1,0:T(8,128)S(1)}, f32[40,256]{1,0:T(8,128)S(1)}, f32[256,256]{1,0:T(8,...) custom-call(bf16[256,2816]{1,0:T(8,128)(2,1)S(1)} %get-tuple-element.28.act, ...), custom_call_target="tpu_custom_call" | custom-call | tf_op jit(solution)/shard_map/early/pallas_call | solution.py:459
  24.9 1.6 %collective-permute-start.5 = (bf16[2,256,1280]{2,1,0:T(8,128)(2,1)S(1)}, bf16[2,256,1280]{2,1,0:T(8,128)(2,1)S(1)}, u32[]{:S(2)}, u32[]{:S(2)}) collective-permute-start(bf16[2,256,1280]{2,1,0:T(8,128)(2,1)S(1)} %get-tuple-element.42.c0), channel_id=1, source_target_pairs={{0,32},{4,12},{8,40},{12,20},{16,48},{20,28},{24,56},{28,4},{32,64... | collective-permute-start | bytes 3932168 | tf_op jit(solution)/shard_map/ppermute | solution.py:378
  26.6 2.9 %collective-permute-start.6 = (bf16[2,256,1280]{2,1,0:T(8,128)(2,1)S(1)}, bf16[2,256,1280]{2,1,0:T(8,128)(2,1)S(1)}, u32[]{:S(2)}, u32[]{:S(2)}) collective-permute-start(bf16[2,256,1280]{2,1,0:T(8,128)(2,1)S(1)} %get-tuple-element.42.c0), channel_id=1, source_target_pairs={{0,64},{4,20},{8,72},{12,28},{16,80},{20,4},{24,88},{28,12},{32,96... | collective-permute-start | bytes 3932168 | tf_op jit(solution)/shard_map/ppermute | solution.py:378
  29.5 1.3 %collective-permute-start.7 = (bf16[2,256,1280]{2,1,0:T(8,128)(2,1)S(1)}, bf16[2,256,1280]{2,1,0:T(8,128)(2,1)S(1)}, u32[]{:S(2)}, u32[]{:S(2)}) collective-permute-start(bf16[2,256,1280]{2,1,0:T(8,128)(2,1)S(1)} %get-tuple-element.42.c0), channel_id=1, source_target_pairs={{0,96},{4,28},{8,104},{12,4},{16,112},{20,12},{24,120},{28,20},{32... | collective-permute-start | bytes 3932168 | tf_op jit(solution)/shard_map/ppermute | solution.py:378
  30.8 6.6 %late.1 = (f32[256,2048]{1,0:T(8,128)S(1)}, f32[256,2560]{1,0:T(8,128)S(1)}) custom-call(bf16[256,2816]{1,0:T(8,128)(2,1)S(1)} %get-tuple-element.28.act, f32[40,256]{1,0:T(8,128)S(1)} %get-tuple-element.30.cum, f32[40,256]{1,0:T(8,128)S(1)} %get-tuple-element.31.step, f32[256,256]{1,0:T(8,128)S(1)} %get-tuple-element.32.scores, ...), custom_call_target="tpu_custom_call" | custom-call | tf_op jit(solution)/shard_map/late/pallas_call | solution.py:476
  37.5 0.0 collective-permute-done.2.one
  37.5 10.6 %collective-permute-done.3.two = bf16[144,2560]{1,0:T(8,128)(2,1)S(1)} collective-permute-done((bf16[144,2560]{1,0:T(8,128)(2,1)S(1)}, bf16[144,2560]{1,0:T(8,128)(2,1)S(1)}, u32[]{:S(2)}, u32[]{:S(2)}) %collective-permute-start.3) | collective-permute-done | bytes 737312 | tf_op jit(solution)/shard_map/ppermute | solution.py:367
  48.1 4.1 %back.1 = (bf16[256,2560]{1,0:T(8,128)(2,1)}, bf16[4,4,80,256]{3,2,1,0:T(8,128)(2,1)S(1)}, bf16[4,4,80,256]{3,2,1,0:T(8,128)(2,1)S(1)}) custom-call(f32[256,512]{1,0:T(8,128)S(1)} %get-tuple-element.29.early, f32[256,2048]{1,0:T(8,128)S(1)} %get-tuple-element.35.late, f32[256,2560]{1,0:T(8,128)S(1)} %get-tuple-element.36.reach, ...), custom_call_target="tpu_custom_call" | custom-call | tf_op jit(solution)/shard_map/back/pallas_call | solution.py:480
  52.2 0.1 collective-permute-start.4
  52.2 2.1 %collective-permute-done.4.got = bf16[4,4,80,256]{3,2,1,0:T(8,128)(2,1)S(1)} collective-permute-done((bf16[4,4,80,256]{3,2,1,0:T(8,128)(2,1)S(1)}, bf16[4,4,80,256]{3,2,1,0:T(8,128)(2,1)S(1)}, u32[]{:S(2)}, u32[]{:S(2)}) %collective-permute-start.4) | collective-permute-done | bytes 655392 | tf_op jit(solution)/shard_map/ppermute | solution.py:391
  54.3 0.0 collective-permute-done.5.c1
  54.3 4.8 %collective-permute-done.6.c2 = bf16[2,256,1280]{2,1,0:T(8,128)(2,1)S(1)} collective-permute-done((bf16[2,256,1280]{2,1,0:T(8,128)(2,1)S(1)}, bf16[2,256,1280]{2,1,0:T(8,128)(2,1)S(1)}, u32[]{:S(2)}, u32[]{:S(2)}) %collective-permute-start.6) | collective-permute-done | bytes 1310752 | tf_op jit(solution)/shard_map/ppermute | solution.py:378
  59.1 0.0 collective-permute-done.7.c3
  59.1 0.1 load.1
  59.2 2.4 %collective-permute-start.10 = (bf16[2,4,80,256]{3,2,1,0:T(8,128)(2,1)S(1)}, bf16[2,4,80,256]{3,2,1,0:T(8,128)(2,1)S(1)}, u32[]{:S(2)}, u32[]{:S(2)}) collective-permute-start(bf16[2,4,80,256]{3,2,1,0:T(8,128)(2,1)S(1)} %get-tuple-element.45), channel_id=1, source_target_pairs={{0,96},{4,28},{8,104},{12,4},{16,112},{20,12},{24,120},{28,20},{32... | collective-permute-start | bytes 983048 | tf_op jit(solution)/shard_map/ppermute | solution.py:378
  61.5 0.0 collective-permute-start.8
  61.5 2.6 %collective-permute-start.9 = (bf16[2,4,80,256]{3,2,1,0:T(8,128)(2,1)S(1)}, bf16[2,4,80,256]{3,2,1,0:T(8,128)(2,1)S(1)}, u32[]{:S(2)}, u32[]{:S(2)}) collective-permute-start(bf16[2,4,80,256]{3,2,1,0:T(8,128)(2,1)S(1)} %get-tuple-element.44), channel_id=1, source_target_pairs={{0,64},{4,20},{8,72},{12,28},{16,80},{20,4},{24,88},{28,12},{32,96... | collective-permute-start | bytes 983048 | tf_op jit(solution)/shard_map/ppermute | solution.py:378
  64.1 2.2 %collective-permute-done.10.r3 = bf16[2,4,80,256]{3,2,1,0:T(8,128)(2,1)S(1)} collective-permute-done((bf16[2,4,80,256]{3,2,1,0:T(8,128)(2,1)S(1)}, bf16[2,4,80,256]{3,2,1,0:T(8,128)(2,1)S(1)}, u32[]{:S(2)}, u32[]{:S(2)}) %collective-permute-start.10) | collective-permute-done | bytes 327712 | tf_op jit(solution)/shard_map/ppermute | solution.py:378
  66.3 7.0 %collective-permute-done.8.r1 = bf16[2,4,80,256]{3,2,1,0:T(8,128)(2,1)S(1)} collective-permute-done((bf16[2,4,80,256]{3,2,1,0:T(8,128)(2,1)S(1)}, bf16[2,4,80,256]{3,2,1,0:T(8,128)(2,1)S(1)}, u32[]{:S(2)}, u32[]{:S(2)}) %collective-permute-start.8) | collective-permute-done | bytes 327712 | tf_op jit(solution)/shard_map/ppermute | solution.py:378
  73.3 0.0 collective-permute-done.9.r2
  73.3 2.0 %grad.1 = bf16[16,200,128]{2,1,0:T(8,128)(2,1)S(1)} custom-call(bf16[4,4,80,256]{3,2,1,0:T(8,128)(2,1)S(1)} %get-tuple-element.40.mine, bf16[4,4,80,256]{3,2,1,0:T(8,128)(2,1)S(1)} %collective-permute-done.4.got, bf16[2,4,80,256]{3,2,1,0:T(8,128)(2,1)S(1)} %collective-permute-done.8.r1, bf16[2,4,80,256]{3,2,1,0:T(8,128)(2,1)S(1)} %collective-permute-done.9.r2, ...), custom_call_target="tpu_custom_call" | custom-call | flops 2000000000 | bytes 8000000 | tf_op jit(solution)/shard_map/grad/pallas_call | solution.py:504
  75.3 16.2 %all_to_all.5.pieces = bf16[16,200,128]{2,1,0:T(8,128)(2,1)S(1)} all-to-all(bf16[16,200,128]{2,1,0:T(8,128)(2,1)S(1)} %grad.1), channel_id=1, replica_groups={{0,1,2,3,8,9,10,11,16,17,18,19,24,25,26,27},{32,33,34,35,40,41,42,43,48..., dimensions={0} | all-to-all | bytes 1638400 | tf_op jit(solution)/shard_map/all_to_all | solution.py:513
  91.5 0.8 total.1
  (6 shorter events, 0.0 us)
Async XLA Ops:
  0.6 5.7 %copy-start.7 = (s32[1,256]{1,0:T(1,128)S(1)}, s32[1,256]{1,0:T(1,128)}, u32[]{:S(2)}) copy-start(s32[1,256]{1,0:T(1,128)} %docs.7) | copy-start | bytes 3076
  0.6 5.7 %copy-start.4 = (f32[1,40,256]{2,1,0:T(8,128)S(1)}, f32[1,40,256]{2,1,0:T(8,128)}, u32[]{:S(2)}) copy-start(f32[1,40,256]{2,1,0:T(8,128)} %param.13) | copy-start | bytes 122884
  0.7 5.7 %copy-start.8 = (f32[40]{0:T(128)S(1)}, f32[40]{0:T(128)}, u32[]{:S(2)}) copy-start(f32[40]{0:T(128)} %param.14) | copy-start | bytes 484
  0.7 5.7 %copy-start.9 = (f32[40]{0:T(128)S(1)}, f32[40]{0:T(128)}, u32[]{:S(2)}) copy-start(f32[40]{0:T(128)} %param.15) | copy-start | bytes 484
  0.7 5.7 %copy-start.3 = (f32[4,2816]{1,0:T(4,128)S(1)}, f32[4,2816]{1,0:T(4,128)}, u32[]{:S(2)}) copy-start(f32[4,2816]{1,0:T(4,128)} %w.3) | copy-start | bytes 135172
  0.7 5.7 %copy-start.6 = (f32[2816]{0:T(1024)S(1)}, f32[2816]{0:T(1024)}, u32[]{:S(2)}) copy-start(f32[2816]{0:T(1024)} %cb.3) | copy-start | bytes 33796
  0.7 19.1 %collective-permute-start.1 = (bf16[256,1280]{1,0:T(8,128)(2,1)}, bf16[256,1280]{1,0:T(8,128)(2,1)S(1)}, u32[]{:S(2)}, u32[]{:S(2)}) collective-permute-start(bf16[256,1280]{1,0:T(8,128)(2,1)} %bitcast.12), channel_id=1, source_target_pairs={{0,4},{4,0},{1,5},{5,1},{2,6},{6,2},{3,7},{7,3},{8,12},{12,8},{9,1... | collective-permute-start | bytes 1966088 | tf_op jit(solution)/shard_map/ppermute | solution.py:391
  2.4 9.2 %collective-permute-start = (bf16[8,2944]{1,0:T(8,128)(2,1)}, bf16[8,2944]{1,0:T(8,128)(2,1)S(1)}, u32[]{:S(2)}, u32[]{:S(2)}) collective-permute-start(bf16[8,2944]{1,0:T(8,128)(2,1)} %edge.1), channel_id=1, source_target_pairs={{0,1},{1,2},{2,3},{4,5},{5,6},{6,7},{8,9},{9,10},{10,11},{12,13},{... | collective-permute-start | bytes 141320 | tf_op jit(solution)/shard_map/ppermute | solution.py:367
  6.4 1.4 %copy-start = (bf16[1,256,2816]{2,1,0:T(8,128)(2,1)S(1)}, bf16[1,256,2816]{2,1,0:T(8,128)(2,1)}, u32[]{:S(2)}) copy-start(bf16[1,256,2816]{2,1,0:T(8,128)(2,1)} %param.11) | copy-start | bytes 4325380
  11.7 8.1 %copy-start.2 = (bf16[1,256,1280]{2,1,0:T(8,128)(2,1)S(1)}, bf16[1,256,1280]{2,1,0:T(8,128)(2,1)}, u32[]{:S(2)}) copy-start(bf16[1,256,1280]{2,1,0:T(8,128)(2,1)} %param.21) | copy-start | bytes 1966084
  11.7 8.1 %copy-start.10 = (f32[40]{0:T(128)S(1)}, f32[40]{0:T(128)}, u32[]{:S(2)}) copy-start(f32[40]{0:T(128)} %param.16) | copy-start | bytes 484
  12.3 25.2 %collective-permute-start.2 = (bf16[144,2560]{1,0:T(8,128)(2,1)S(1)}, bf16[144,2560]{1,0:T(8,128)(2,1)S(1)}, u32[]{:S(2)}, u32[]{:S(2)}) collective-permute-start(bf16[144,2560]{1,0:T(8,128)(2,1)S(1)} %get-tuple-element.38), channel_id=1, source_target_pairs={{0,1},{1,2},{2,3},{4,5},{5,6},{6,7},{8,9},{9,10},{10,11},{12,13},{... | collective-permute-start | bytes 2211848 | tf_op jit(solution)/shard_map/ppermute | solution.py:367
  16.2 31.9 %collective-permute-start.3 = (bf16[144,2560]{1,0:T(8,128)(2,1)S(1)}, bf16[144,2560]{1,0:T(8,128)(2,1)S(1)}, u32[]{:S(2)}, u32[]{:S(2)}) collective-permute-start(bf16[144,2560]{1,0:T(8,128)(2,1)S(1)} %get-tuple-element.38), channel_id=1, source_target_pairs={{0,2},{1,3},{4,6},{5,7},{8,10},{9,11},{12,14},{13,15},{16,18},{17,... | collective-permute-start | bytes 2211848 | tf_op jit(solution)/shard_map/ppermute | solution.py:367
  19.8 11.0 %copy-start.1 = (bf16[1,256,2560]{2,1,0:T(8,128)(2,1)S(1)}, bf16[1,256,2560]{2,1,0:T(8,128)(2,1)}, u32[]{:S(2)}) copy-start(bf16[1,256,2560]{2,1,0:T(8,128)(2,1)} %param.12) | copy-start | bytes 3932164
  24.9 29.4 %collective-permute-start.5 = (bf16[2,256,1280]{2,1,0:T(8,128)(2,1)S(1)}, bf16[2,256,1280]{2,1,0:T(8,128)(2,1)S(1)}, u32[]{:S(2)}, u32[]{:S(2)}) collective-permute-start(bf16[2,256,1280]{2,1,0:T(8,128)(2,1)S(1)} %get-tuple-element.42.c0), channel_id=1, source_target_pairs={{0,32},{4,12},{8,40},{12,20},{16,48},{20,28},{24,56},{28,4},{32,64... | collective-permute-start | bytes 3932168 | tf_op jit(solution)/shard_map/ppermute | solution.py:378
  26.6 32.5 %collective-permute-start.6 = (bf16[2,256,1280]{2,1,0:T(8,128)(2,1)S(1)}, bf16[2,256,1280]{2,1,0:T(8,128)(2,1)S(1)}, u32[]{:S(2)}, u32[]{:S(2)}) collective-permute-start(bf16[2,256,1280]{2,1,0:T(8,128)(2,1)S(1)} %get-tuple-element.42.c0), channel_id=1, source_target_pairs={{0,64},{4,20},{8,72},{12,28},{16,80},{20,4},{24,88},{28,12},{32,96... | collective-permute-start | bytes 3932168 | tf_op jit(solution)/shard_map/ppermute | solution.py:378
  29.5 29.6 %collective-permute-start.7 = (bf16[2,256,1280]{2,1,0:T(8,128)(2,1)S(1)}, bf16[2,256,1280]{2,1,0:T(8,128)(2,1)S(1)}, u32[]{:S(2)}, u32[]{:S(2)}) collective-permute-start(bf16[2,256,1280]{2,1,0:T(8,128)(2,1)S(1)} %get-tuple-element.42.c0), channel_id=1, source_target_pairs={{0,96},{4,28},{8,104},{12,4},{16,112},{20,12},{24,120},{28,20},{32... | collective-permute-start | bytes 3932168 | tf_op jit(solution)/shard_map/ppermute | solution.py:378
  30.8 17.2 %copy-start.5 = (f32[2560]{0:T(1024)S(1)}, f32[2560]{0:T(1024)}, u32[]{:S(2)}) copy-start(f32[2560]{0:T(1024)} %gain.1) | copy-start | bytes 30724
  52.2 2.2 %collective-permute-start.4 = (bf16[4,4,80,256]{3,2,1,0:T(8,128)(2,1)S(1)}, bf16[4,4,80,256]{3,2,1,0:T(8,128)(2,1)S(1)}, u32[]{:S(2)}, u32[]{:S(2)}) collective-permute-start(bf16[4,4,80,256]{3,2,1,0:T(8,128)(2,1)S(1)} %get-tuple-element.41), channel_id=1, source_target_pairs={{0,4},{4,0},{1,5},{5,1},{2,6},{6,2},{3,7},{7,3},{8,12},{12,8},{9,1... | collective-permute-start | bytes 1966088 | tf_op jit(solution)/shard_map/ppermute | solution.py:391
  59.2 7.1 %collective-permute-start.10 = (bf16[2,4,80,256]{3,2,1,0:T(8,128)(2,1)S(1)}, bf16[2,4,80,256]{3,2,1,0:T(8,128)(2,1)S(1)}, u32[]{:S(2)}, u32[]{:S(2)}) collective-permute-start(bf16[2,4,80,256]{3,2,1,0:T(8,128)(2,1)S(1)} %get-tuple-element.45), channel_id=1, source_target_pairs={{0,96},{4,28},{8,104},{12,4},{16,112},{20,12},{24,120},{28,20},{32... | collective-permute-start | bytes 983048 | tf_op jit(solution)/shard_map/ppermute | solution.py:378
  61.5 11.8 %collective-permute-start.8 = (bf16[2,4,80,256]{3,2,1,0:T(8,128)(2,1)S(1)}, bf16[2,4,80,256]{3,2,1,0:T(8,128)(2,1)S(1)}, u32[]{:S(2)}, u32[]{:S(2)}) collective-permute-start(bf16[2,4,80,256]{3,2,1,0:T(8,128)(2,1)S(1)} %get-tuple-element.43), channel_id=1, source_target_pairs={{0,32},{4,12},{8,40},{12,20},{16,48},{20,28},{24,56},{28,4},{32,64... | collective-permute-start | bytes 983048 | tf_op jit(solution)/shard_map/ppermute | solution.py:378
  61.5 11.8 %collective-permute-start.9 = (bf16[2,4,80,256]{3,2,1,0:T(8,128)(2,1)S(1)}, bf16[2,4,80,256]{3,2,1,0:T(8,128)(2,1)S(1)}, u32[]{:S(2)}, u32[]{:S(2)}) collective-permute-start(bf16[2,4,80,256]{3,2,1,0:T(8,128)(2,1)S(1)} %get-tuple-element.44), channel_id=1, source_target_pairs={{0,64},{4,20},{8,72},{12,28},{16,80},{20,4},{24,88},{28,12},{32,96... | collective-permute-start | bytes 983048 | tf_op jit(solution)/shard_map/ppermute | solution.py:378

commit v5 on v4

--- a/solution.py
+++ b/solution.py
@@ -15,7 +15,6 @@
 D = 1280
 LANES = 128
 XCHUNKS = INNER // LANES
-EARLY = 4
 MSG = N + 16
 F32 = jnp.float32
 BF16 = jnp.bfloat16
@@ -142,7 +141,8 @@
 
 def fix_kernel(halo, rows, w, cb, docs, old, state, info, top, act, msg):
     own = column(docs[...].astype(F32), LANES)[0:16]
-    joined = jnp.concatenate([halo[:, C_ALL:].astype(F32), own], 0)
+    before = jnp.where(lax.axis_index("z") > 0, halo[:, C_ALL:].astype(F32), -1.0)
+    joined = jnp.concatenate([before, own], 0)
     masks = [(joined[5 + k : 21 + k] == own).astype(F32) for k in range(3)]
 
     def chunk(j):
@@ -193,14 +193,14 @@
     return jnp.concatenate([top, low], 0)
 
 
-def early_kernel(act, step_in, bias, rates, docs, halo, skip, cot, other, local, reach, cum, step, scores, fac, cots, sfac, efac):
+def early_kernel(act, step_in, bias, rates, docs, halo, skip, cot, other, reach, cum, step, scores, fac, cots, sfac, efac):
     cots[0] = cot[...]
     cots[1] = other[...]
     sfac[...] = split_rows(jnp.broadcast_to(upright(skip[...]), (H, LANES))).T[0:16].astype(BF16)
     step[...], cum[...] = steps(step_in, bias, rates)
     doc_row = docs[...].astype(F32)
     prev_tag = halo[:, C_ALL : C_ALL + LANES].astype(F32)[7:8, :]
-    prev_tag = jnp.concatenate([prev_tag, prev_tag], 1)
+    prev_tag = jnp.where(lax.axis_index("z") > 0, jnp.concatenate([prev_tag, prev_tag], 1), -1.0)
     matched = (doc_row == prev_tag).astype(F32)
     fac[...] = split_rows(cum[...]).T.astype(BF16)
     efac[...] = split_rows(jnp.exp(cum[...]) * matched).T.astype(BF16)
@@ -223,21 +223,14 @@
 
     lax.fori_loop(0, XCHUNKS, chunk, 0)
 
+
+def late_kernel(act, cum, step, scores, fac, gate, sfac, local, sgate):
     def pair(j, carry):
         at = pl.ds(pl.multiple_of(j * LANES, LANES), LANES)
         local[:, at] = pair_chunk(j, act, cum, step, scores, fac, sfac)
         return carry
 
-    lax.fori_loop(0, EARLY, pair, 0)
-
-
-def late_kernel(act, cum, step, scores, fac, gate, sfac, local, sgate):
-    def pair(j, carry):
-        at = pl.ds(pl.multiple_of(j * LANES, LANES), LANES)
-        local[:, at] = pair_chunk(j + EARLY, act, cum, step, scores, fac, sfac)
-        return carry
-
-    lax.fori_loop(0, XCHUNKS - EARLY, pair, 0)
+    lax.fori_loop(0, XCHUNKS, pair, 0)
 
     def gates(j, carry):
         at = pl.ds(pl.multiple_of(j * 2 * LANES, 2 * LANES), 2 * LANES)
@@ -247,11 +240,11 @@
     lax.fori_loop(0, XCHUNKS // 2, gates, 0)
 
 
-def back_kernel(early, late, reach, sgate, act, one, two, gain, normed, mine, give, gated, squares, turned, flat, sem):
+def back_kernel(local, reach, sgate, act, one, two, gain, normed, mine, give, gated, squares, turned, flat, sem):
     c_map = act[:, INNER + N :]
     wide = 2 * LANES
 
-    def first(j, local, shift):
+    def first(j):
         at = pl.ds(pl.multiple_of(j * wide, wide), wide)
         info = one[N:, at].astype(F32)
         other = two[N:, at].astype(F32)
@@ -259,18 +252,17 @@
         weight = (info[0:1] + info[1:2]) * linked
         state = one[0:N, at].astype(F32) + weight * two[0:N, at].astype(F32)
         reading = dot(c_map, state.astype(BF16))
-        here = pl.ds(pl.multiple_of((j - shift) * wide, wide), wide)
-        mixed = local[:, here] + reading * reach[:, at]
+        mixed = local[:, at] + reading * reach[:, at]
         value = mixed.astype(BF16).astype(F32) * sgate[:, at]
         gated[:, at] = value
         value = value * value
         return value[:, 0:LANES] + value[:, LANES:]
 
     def first_pair(i, carry):
-        squares[...] += first(2 * i, late, EARLY // 2) + first(2 * i + 1, late, EARLY // 2)
+        squares[...] += first(2 * i) + first(2 * i + 1)
         return carry
 
-    squares[...] = first(0, early, 0) + first(1, early, 0)
+    squares[...] = first(0) + first(1)
     lax.fori_loop(1, 5, first_pair, 0)
     mean = jnp.sum(squares[...], axis=1, keepdims=True) * (1.0 / INNER)
     squares[...] = jnp.broadcast_to(lax.rsqrt(mean + 1e-05), squares.shape)
@@ -364,7 +356,7 @@
 
 
 def shifted(value, by):
-    return lax.ppermute(value, "z", [(i, i + by) for i in range(4 - by)])
+    return lax.ppermute(value, "z", [(i, (i + by) % 4) for i in range(4 if by == 1 else 4 - by)])
 
 
 def around(value, by, first_axis):
@@ -456,11 +448,10 @@
     )(halo, conv, conv_weight, conv_bias, doc_ids, act, state, info, top)
     one = shifted(msg, 1)
     two = shifted(msg, 2)
-    early, reach, cum, step, scores, fac, cots, sfac = call(
+    reach, cum, step, scores, fac, cots, sfac = call(
         early_kernel,
         "early",
         (
-            shape((T, EARLY * LANES)),
             shape((T, INNER)),
             shape((H, T)),
             shape((H, T)),
@@ -473,8 +464,8 @@
         8,
     )(act, step_in, bias, rates, doc_ids, halo, skip_gain[None], cotangent[0], cot_other)
     c1, c2, c3 = [around(cots, k, "y") for k in (1, 2, 3)]
-    late, sgate = call(
-        late_kernel, "late", (shape((T, INNER - EARLY * LANES)), shape((T, INNER))), [], 8
+    local, sgate = call(
+        late_kernel, "late", (shape((T, INNER)), shape((T, INNER))), [], 8
     )(act, cum, step, scores, fac, gate_input[0], sfac)
     block = (4, 4, 80, T)
     normed, mine, give = call(
@@ -490,7 +481,7 @@
         ],
         12,
         out_specs=(pl.BlockSpec(memory_space=pltpu.HBM), vmem, vmem),
-    )(early, late, reach, sgate, act, one, two, norm_gain)
+    )(local, reach, sgate, act, one, two, norm_gain)
     got = swapped(give)
     sends = call(
         load_kernel,

time: 92.6 us -> 88.6 us (0.957)
  starting transfers between devices: 22.4 us -> 18.7 us
  waiting for transfers between devices: 26.7 us -> 25.2 us
  blocking collectives: 16.2 us -> 17.5 us
    ppermute x3, starting transfers between devices: 11.4 us -> 7.7 us  [shifted(): lax.ppermute(value, 'z', [(i, (i + by) % 4) for i in range(4 if by == 1 e...]
    ppermute x6, waiting for transfers between devices: 14 us -> 12.5 us  [around(): return lax.ppermute(value, ('y', 'x', 'c'), pairs)]
    all_to_all x1, blocking collectives: 16.2 us -> 17.5 us  [per_device(): lax.all_to_all(packed, ('y', 'x', 'c', 'z'), 0, 0, axis_index_groups=PLANES)]
  transfers between devices with their start and end apart: 11 -> 11, of which waited for: 5 -> 5; matrix products, arithmetic and copies ran while one was open for 0% -> 0% of each run, Pallas kernels for 24% -> 25%
where the time goes in v5:
time: 88.6 us; the launch traced here: 88.4 us
  waiting for transfers between devices  25.2 us (28%)
  Pallas kernels  24.7 us (28%)
  starting transfers between devices  18.7 us (21%)
  blocking collectives  17.5 us (20%)
  local copies, waits for them, and re-layouts  1.41 us (2%)
    all_to_all x1, blocking collectives, per_device(): lax.all_to_all(packed, ('y', 'x', 'c', 'z'), 0, 0, axis_index_groups=PLANES)  17.5 us
    ppermute x6, waiting for transfers between devices, around(): return lax.ppermute(value, ('y', 'x', 'c'), pairs)  12.5 us
    ppermute x6, starting transfers between devices, around(): return lax.ppermute(value, ('y', 'x', 'c'), pairs)  10.8 us
    ppermute x3, waiting for transfers between devices, shifted(): lax.ppermute(value, 'z', [(i, (i + by) % 4) for i in range(4 if by == 1 e...  10.6 us
    pallas_call x1, Pallas kernels, per_device(): call(late_kernel, 'late', (shape((T, INNER)), shape((T, INNER))), [], 8)  8.15 us
    ppermute x3, starting transfers between devices, shifted(): lax.ppermute(value, 'z', [(i, (i + by) % 4) for i in range(4 if by == 1 e...  7.7 us
    pallas_call x1, Pallas kernels, per_device(): call(back_kernel, 'back', (shape((T, INNER), BF16), shape(block, BF16), s...  4.02 us
    pallas_call x1, Pallas kernels, per_device(): call(front_kernel, 'front', (shape((T, C_ALL), BF16), shape((N, INNER)),...  3.9 us
  transfers between devices with their start and end apart: 11, of which 5 were waited for; matrix products, arithmetic and copies ran while one was open for 0% of the time, Pallas kernels for 25%

profile of v5, /device:TPU:0, one launch (start us, length us, event | category | flops | bytes accessed | tf_op | source)
XLA Modules:
  0.0 88.4 jit_solution(10167452612720364077)
XLA Ops:
  0.6 0.0 copy-start.7
  0.6 0.0 copy-start.4
  0.7 0.0 copy-start.8
  0.7 0.0 copy-start.9
  0.7 0.0 copy-start.3
  0.7 0.0 copy-start.6
  0.7 0.1 collective-permute-start.1
  0.8 1.6 %edge.1 = bf16[8,2944]{1,0:T(8,128)(2,1)} custom-call(bf16[256,2816]{1,0:T(8,128)(2,1)} %bitcast.8, s32[1,256]{1,0:T(1,128)} %docs.7), custom_call_target="tpu_custom_call" | custom-call | bytes 100000 | tf_op jit(solution)/shard_map/edge/pallas_call | solution.py:394
  2.4 2.1 %collective-permute-start = (bf16[8,2944]{1,0:T(8,128)(2,1)}, bf16[8,2944]{1,0:T(8,128)(2,1)S(1)}, u32[]{:S(2)}, u32[]{:S(2)}) collective-permute-start(bf16[8,2944]{1,0:T(8,128)(2,1)} %edge.1), channel_id=1, source_target_pairs={{0,1},{1,2},{2,3},{3,0},{4,5},{5,6},{6,7},{7,4},{8,9},{9,10},{10,1... | collective-permute-start | bytes 141320 | tf_op jit(solution)/shard_map/ppermute | solution.py:359
  4.5 0.0 copy-done.7
  4.5 0.0 copy-done.4
  4.5 0.0 copy-done.8
  4.5 0.0 copy-done.9
  4.5 0.0 copy-done.3
  4.5 0.0 copy-start
  4.5 1.4 %copy-done = bf16[1,256,2816]{2,1,0:T(8,128)(2,1)S(1)} copy-done((bf16[1,256,2816]{2,1,0:T(8,128)(2,1)S(1)}, bf16[1,256,2816]{2,1,0:T(8,128)(2,1)}, u32[]{:S(2)}) %copy-start) | copy-done | bytes 1441816
  5.9 3.9 %front.1 = (bf16[256,2816]{1,0:T(8,128)(2,1)S(1)}, f32[128,2560]{1,0:T(8,128)S(1)}, bf16[16,2560]{1,0:T(8,128)(2,1)S(1)}, f32[16,2560]{1,0:T(8,128)S(1)}) custom-call(bf16[256,2816]{1,0:T(8,128)(2,1)S(1)} %bitcast.9, f32[40,256]{1,0:T(8,128)S(1)} %bitcast.14, f32[1,40]{1,0:T(1,128)S(1)} %bitcast.16, f32[1,40]{1,0:T(1,128)S(1)} %bitcast.18, ...), custom_call_target="tpu_custom_call" | custom-call | flops 1000000000 | bytes 4000000 | tf_op jit(solution)/shard_map/front/pallas_call | solution.py:406
  9.8 0.0 collective-permute-done.halo
  9.8 0.0 copy-start.2
  9.8 0.0 copy-start.10
  9.8 0.6 fix.1
  10.4 2.0 %collective-permute-start.2 = (bf16[144,2560]{1,0:T(8,128)(2,1)S(1)}, bf16[144,2560]{1,0:T(8,128)(2,1)S(1)}, u32[]{:S(2)}, u32[]{:S(2)}) collective-permute-start(bf16[144,2560]{1,0:T(8,128)(2,1)S(1)} %get-tuple-element.36), channel_id=1, source_target_pairs={{0,1},{1,2},{2,3},{3,0},{4,5},{5,6},{6,7},{7,4},{8,9},{9,10},{10,1... | collective-permute-start | bytes 2211848 | tf_op jit(solution)/shard_map/ppermute | solution.py:359
  12.4 3.6 %collective-permute-start.3 = (bf16[144,2560]{1,0:T(8,128)(2,1)S(1)}, bf16[144,2560]{1,0:T(8,128)(2,1)S(1)}, u32[]{:S(2)}, u32[]{:S(2)}) collective-permute-start(bf16[144,2560]{1,0:T(8,128)(2,1)S(1)} %get-tuple-element.36), channel_id=1, source_target_pairs={{0,2},{1,3},{4,6},{5,7},{8,10},{9,11},{12,14},{13,15},{16,18},{17,... | collective-permute-start | bytes 2211848 | tf_op jit(solution)/shard_map/ppermute | solution.py:359
  16.1 0.0 collective-permute-done.1.other
  16.1 0.0 copy-start.1
  16.1 3.6 %early.1 = (f32[256,2560]{1,0:T(8,128)S(1)}, f32[40,256]{1,0:T(8,128)S(1)}, f32[40,256]{1,0:T(8,128)S(1)}, f32[256,256]{1,0:T(8,128)S(1)}, bf16[256,128]{1,0:T(8...) custom-call(bf16[256,2816]{1,0:T(8,128)(2,1)S(1)} %get-tuple-element.27.act, ...), custom_call_target="tpu_custom_call" | custom-call | tf_op jit(solution)/shard_map/early/pallas_call | solution.py:451
  19.7 1.6 %collective-permute-start.5 = (bf16[2,256,1280]{2,1,0:T(8,128)(2,1)S(1)}, bf16[2,256,1280]{2,1,0:T(8,128)(2,1)S(1)}, u32[]{:S(2)}, u32[]{:S(2)}) collective-permute-start(bf16[2,256,1280]{2,1,0:T(8,128)(2,1)S(1)} %get-tuple-element.40.c0), channel_id=1, source_target_pairs={{0,32},{4,12},{8,40},{12,20},{16,48},{20,28},{24,56},{28,4},{32,64... | collective-permute-start | bytes 3932168 | tf_op jit(solution)/shard_map/ppermute | solution.py:370
  21.3 2.9 %collective-permute-start.6 = (bf16[2,256,1280]{2,1,0:T(8,128)(2,1)S(1)}, bf16[2,256,1280]{2,1,0:T(8,128)(2,1)S(1)}, u32[]{:S(2)}, u32[]{:S(2)}) collective-permute-start(bf16[2,256,1280]{2,1,0:T(8,128)(2,1)S(1)} %get-tuple-element.40.c0), channel_id=1, source_target_pairs={{0,64},{4,20},{8,72},{12,28},{16,80},{20,4},{24,88},{28,12},{32,96... | collective-permute-start | bytes 3932168 | tf_op jit(solution)/shard_map/ppermute | solution.py:370
  24.2 1.3 %collective-permute-start.7 = (bf16[2,256,1280]{2,1,0:T(8,128)(2,1)S(1)}, bf16[2,256,1280]{2,1,0:T(8,128)(2,1)S(1)}, u32[]{:S(2)}, u32[]{:S(2)}) collective-permute-start(bf16[2,256,1280]{2,1,0:T(8,128)(2,1)S(1)} %get-tuple-element.40.c0), channel_id=1, source_target_pairs={{0,96},{4,28},{8,104},{12,4},{16,112},{20,12},{24,120},{28,20},{32... | collective-permute-start | bytes 3932168 | tf_op jit(solution)/shard_map/ppermute | solution.py:370
  25.6 8.2 %late.1 = (f32[256,2560]{1,0:T(8,128)S(1)}, f32[256,2560]{1,0:T(8,128)S(1)}) custom-call(bf16[256,2816]{1,0:T(8,128)(2,1)S(1)} %get-tuple-element.27.act, f32[40,256]{1,0:T(8,128)S(1)} %get-tuple-element.28.cum, f32[40,256]{1,0:T(8,128)S(1)} %get-tuple-element.29.step, f32[256,256]{1,0:T(8,128)S(1)} %get-tuple-element.30.scores, ...), custom_call_target="tpu_custom_call" | custom-call | tf_op jit(solution)/shard_map/late/pallas_call | solution.py:467
  33.8 0.0 collective-permute-done.2.one
  33.8 10.6 %collective-permute-done.3.two = bf16[144,2560]{1,0:T(8,128)(2,1)S(1)} collective-permute-done((bf16[144,2560]{1,0:T(8,128)(2,1)S(1)}, bf16[144,2560]{1,0:T(8,128)(2,1)S(1)}, u32[]{:S(2)}, u32[]{:S(2)}) %collective-permute-start.3) | collective-permute-done | bytes 737312 | tf_op jit(solution)/shard_map/ppermute | solution.py:359
  44.4 4.0 %back.1 = (bf16[256,2560]{1,0:T(8,128)(2,1)}, bf16[4,4,80,256]{3,2,1,0:T(8,128)(2,1)S(1)}, bf16[4,4,80,256]{3,2,1,0:T(8,128)(2,1)S(1)}) custom-call(f32[256,2560]{1,0:T(8,128)S(1)} %get-tuple-element.33.local, f32[256,2560]{1,0:T(8,128)S(1)} %get-tuple-element.34.reach, f32[256,2560]{1,0:T(8,128)S(1)} %get-tuple-element.35.sgate, ...), custom_call_target="tpu_custom_call" | custom-call | tf_op jit(solution)/shard_map/back/pallas_call | solution.py:471
  48.4 0.1 collective-permute-start.4
  48.5 2.1 %collective-permute-done.4.got = bf16[4,4,80,256]{3,2,1,0:T(8,128)(2,1)S(1)} collective-permute-done((bf16[4,4,80,256]{3,2,1,0:T(8,128)(2,1)S(1)}, bf16[4,4,80,256]{3,2,1,0:T(8,128)(2,1)S(1)}, u32[]{:S(2)}, u32[]{:S(2)}) %collective-permute-start.4) | collective-permute-done | bytes 655392 | tf_op jit(solution)/shard_map/ppermute | solution.py:383
  50.6 0.0 collective-permute-done.5.c1
  50.6 3.3 %collective-permute-done.6.c2 = bf16[2,256,1280]{2,1,0:T(8,128)(2,1)S(1)} collective-permute-done((bf16[2,256,1280]{2,1,0:T(8,128)(2,1)S(1)}, bf16[2,256,1280]{2,1,0:T(8,128)(2,1)S(1)}, u32[]{:S(2)}, u32[]{:S(2)}) %collective-permute-start.6) | collective-permute-done | bytes 1310752 | tf_op jit(solution)/shard_map/ppermute | solution.py:370
  53.9 0.0 collective-permute-done.7.c3
  53.9 0.1 load.1
  53.9 2.4 %collective-permute-start.10 = (bf16[2,4,80,256]{3,2,1,0:T(8,128)(2,1)S(1)}, bf16[2,4,80,256]{3,2,1,0:T(8,128)(2,1)S(1)}, u32[]{:S(2)}, u32[]{:S(2)}) collective-permute-start(bf16[2,4,80,256]{3,2,1,0:T(8,128)(2,1)S(1)} %get-tuple-element.43), channel_id=1, source_target_pairs={{0,96},{4,28},{8,104},{12,4},{16,112},{20,12},{24,120},{28,20},{32... | collective-permute-start | bytes 983048 | tf_op jit(solution)/shard_map/ppermute | solution.py:370
  56.3 0.0 collective-permute-start.8
  56.3 2.6 %collective-permute-start.9 = (bf16[2,4,80,256]{3,2,1,0:T(8,128)(2,1)S(1)}, bf16[2,4,80,256]{3,2,1,0:T(8,128)(2,1)S(1)}, u32[]{:S(2)}, u32[]{:S(2)}) collective-permute-start(bf16[2,4,80,256]{3,2,1,0:T(8,128)(2,1)S(1)} %get-tuple-element.42), channel_id=1, source_target_pairs={{0,64},{4,20},{8,72},{12,28},{16,80},{20,4},{24,88},{28,12},{32,96... | collective-permute-start | bytes 983048 | tf_op jit(solution)/shard_map/ppermute | solution.py:370
  58.9 2.2 %collective-permute-done.10.r3 = bf16[2,4,80,256]{3,2,1,0:T(8,128)(2,1)S(1)} collective-permute-done((bf16[2,4,80,256]{3,2,1,0:T(8,128)(2,1)S(1)}, bf16[2,4,80,256]{3,2,1,0:T(8,128)(2,1)S(1)}, u32[]{:S(2)}, u32[]{:S(2)}) %collective-permute-start.10) | collective-permute-done | bytes 327712 | tf_op jit(solution)/shard_map/ppermute | solution.py:370
  61.1 7.0 %collective-permute-done.8.r1 = bf16[2,4,80,256]{3,2,1,0:T(8,128)(2,1)S(1)} collective-permute-done((bf16[2,4,80,256]{3,2,1,0:T(8,128)(2,1)S(1)}, bf16[2,4,80,256]{3,2,1,0:T(8,128)(2,1)S(1)}, u32[]{:S(2)}, u32[]{:S(2)}) %collective-permute-start.8) | collective-permute-done | bytes 327712 | tf_op jit(solution)/shard_map/ppermute | solution.py:370
  68.1 0.0 collective-permute-done.9.r2
  68.1 2.0 %grad.1 = bf16[16,200,128]{2,1,0:T(8,128)(2,1)S(1)} custom-call(bf16[4,4,80,256]{3,2,1,0:T(8,128)(2,1)S(1)} %get-tuple-element.38.mine, bf16[4,4,80,256]{3,2,1,0:T(8,128)(2,1)S(1)} %collective-permute-done.4.got, bf16[2,4,80,256]{3,2,1,0:T(8,128)(2,1)S(1)} %collective-permute-done.8.r1, bf16[2,4,80,256]{3,2,1,0:T(8,128)(2,1)S(1)} %collective-permute-done.9.r2, ...), custom_call_target="tpu_custom_call" | custom-call | flops 2000000000 | bytes 8000000 | tf_op jit(solution)/shard_map/grad/pallas_call | solution.py:495
  70.1 17.5 %all_to_all.5.pieces = bf16[16,200,128]{2,1,0:T(8,128)(2,1)S(1)} all-to-all(bf16[16,200,128]{2,1,0:T(8,128)(2,1)S(1)} %grad.1), channel_id=1, replica_groups={{0,1,2,3,8,9,10,11,16,17,18,19,24,25,26,27},{32,33,34,35,40,41,42,43,48..., dimensions={0} | all-to-all | bytes 1638400 | tf_op jit(solution)/shard_map/all_to_all | solution.py:504
  87.6 0.8 total.1
  (6 shorter events, 0.0 us)
Async XLA Ops:
  0.6 3.8 %copy-start.7 = (s32[1,256]{1,0:T(1,128)S(1)}, s32[1,256]{1,0:T(1,128)}, u32[]{:S(2)}) copy-start(s32[1,256]{1,0:T(1,128)} %docs.7) | copy-start | bytes 3076
  0.6 3.8 %copy-start.4 = (f32[1,40,256]{2,1,0:T(8,128)S(1)}, f32[1,40,256]{2,1,0:T(8,128)}, u32[]{:S(2)}) copy-start(f32[1,40,256]{2,1,0:T(8,128)} %param.13) | copy-start | bytes 122884
  0.7 3.8 %copy-start.8 = (f32[40]{0:T(128)S(1)}, f32[40]{0:T(128)}, u32[]{:S(2)}) copy-start(f32[40]{0:T(128)} %param.14) | copy-start | bytes 484
  0.7 3.8 %copy-start.9 = (f32[40]{0:T(128)S(1)}, f32[40]{0:T(128)}, u32[]{:S(2)}) copy-start(f32[40]{0:T(128)} %param.15) | copy-start | bytes 484
  0.7 3.8 %copy-start.3 = (f32[4,2816]{1,0:T(4,128)S(1)}, f32[4,2816]{1,0:T(4,128)}, u32[]{:S(2)}) copy-start(f32[4,2816]{1,0:T(4,128)} %w.3) | copy-start | bytes 135172
  0.7 3.8 %copy-start.6 = (f32[2816]{0:T(1024)S(1)}, f32[2816]{0:T(1024)}, u32[]{:S(2)}) copy-start(f32[2816]{0:T(1024)} %cb.3) | copy-start | bytes 33796
  0.7 15.4 %collective-permute-start.1 = (bf16[256,1280]{1,0:T(8,128)(2,1)}, bf16[256,1280]{1,0:T(8,128)(2,1)S(1)}, u32[]{:S(2)}, u32[]{:S(2)}) collective-permute-start(bf16[256,1280]{1,0:T(8,128)(2,1)} %bitcast.12), channel_id=1, source_target_pairs={{0,4},{4,0},{1,5},{5,1},{2,6},{6,2},{3,7},{7,3},{8,12},{12,8},{9,1... | collective-permute-start | bytes 1966088 | tf_op jit(solution)/shard_map/ppermute | solution.py:383
  2.4 7.4 %collective-permute-start = (bf16[8,2944]{1,0:T(8,128)(2,1)}, bf16[8,2944]{1,0:T(8,128)(2,1)S(1)}, u32[]{:S(2)}, u32[]{:S(2)}) collective-permute-start(bf16[8,2944]{1,0:T(8,128)(2,1)} %edge.1), channel_id=1, source_target_pairs={{0,1},{1,2},{2,3},{3,0},{4,5},{5,6},{6,7},{7,4},{8,9},{9,10},{10,1... | collective-permute-start | bytes 141320 | tf_op jit(solution)/shard_map/ppermute | solution.py:359
  4.5 1.4 %copy-start = (bf16[1,256,2816]{2,1,0:T(8,128)(2,1)S(1)}, bf16[1,256,2816]{2,1,0:T(8,128)(2,1)}, u32[]{:S(2)}) copy-start(bf16[1,256,2816]{2,1,0:T(8,128)(2,1)} %param.11) | copy-start | bytes 4325380
  9.8 6.3 %copy-start.2 = (bf16[1,256,1280]{2,1,0:T(8,128)(2,1)S(1)}, bf16[1,256,1280]{2,1,0:T(8,128)(2,1)}, u32[]{:S(2)}) copy-start(bf16[1,256,1280]{2,1,0:T(8,128)(2,1)} %param.21) | copy-start | bytes 1966084
  9.8 6.3 %copy-start.10 = (f32[40]{0:T(128)S(1)}, f32[40]{0:T(128)}, u32[]{:S(2)}) copy-start(f32[40]{0:T(128)} %param.16) | copy-start | bytes 484
  10.4 23.3 %collective-permute-start.2 = (bf16[144,2560]{1,0:T(8,128)(2,1)S(1)}, bf16[144,2560]{1,0:T(8,128)(2,1)S(1)}, u32[]{:S(2)}, u32[]{:S(2)}) collective-permute-start(bf16[144,2560]{1,0:T(8,128)(2,1)S(1)} %get-tuple-element.36), channel_id=1, source_target_pairs={{0,1},{1,2},{2,3},{3,0},{4,5},{5,6},{6,7},{7,4},{8,9},{9,10},{10,1... | collective-permute-start | bytes 2211848 | tf_op jit(solution)/shard_map/ppermute | solution.py:359
  12.4 32.0 %collective-permute-start.3 = (bf16[144,2560]{1,0:T(8,128)(2,1)S(1)}, bf16[144,2560]{1,0:T(8,128)(2,1)S(1)}, u32[]{:S(2)}, u32[]{:S(2)}) collective-permute-start(bf16[144,2560]{1,0:T(8,128)(2,1)S(1)} %get-tuple-element.36), channel_id=1, source_target_pairs={{0,2},{1,3},{4,6},{5,7},{8,10},{9,11},{12,14},{13,15},{16,18},{17,... | collective-permute-start | bytes 2211848 | tf_op jit(solution)/shard_map/ppermute | solution.py:359
  16.1 9.5 %copy-start.1 = (bf16[1,256,2560]{2,1,0:T(8,128)(2,1)S(1)}, bf16[1,256,2560]{2,1,0:T(8,128)(2,1)}, u32[]{:S(2)}) copy-start(bf16[1,256,2560]{2,1,0:T(8,128)(2,1)} %param.12) | copy-start | bytes 3932164
  19.7 30.9 %collective-permute-start.5 = (bf16[2,256,1280]{2,1,0:T(8,128)(2,1)S(1)}, bf16[2,256,1280]{2,1,0:T(8,128)(2,1)S(1)}, u32[]{:S(2)}, u32[]{:S(2)}) collective-permute-start(bf16[2,256,1280]{2,1,0:T(8,128)(2,1)S(1)} %get-tuple-element.40.c0), channel_id=1, source_target_pairs={{0,32},{4,12},{8,40},{12,20},{16,48},{20,28},{24,56},{28,4},{32,64... | collective-permute-start | bytes 3932168 | tf_op jit(solution)/shard_map/ppermute | solution.py:370
  21.3 32.5 %collective-permute-start.6 = (bf16[2,256,1280]{2,1,0:T(8,128)(2,1)S(1)}, bf16[2,256,1280]{2,1,0:T(8,128)(2,1)S(1)}, u32[]{:S(2)}, u32[]{:S(2)}) collective-permute-start(bf16[2,256,1280]{2,1,0:T(8,128)(2,1)S(1)} %get-tuple-element.40.c0), channel_id=1, source_target_pairs={{0,64},{4,20},{8,72},{12,28},{16,80},{20,4},{24,88},{28,12},{32,96... | collective-permute-start | bytes 3932168 | tf_op jit(solution)/shard_map/ppermute | solution.py:370
  24.2 29.6 %collective-permute-start.7 = (bf16[2,256,1280]{2,1,0:T(8,128)(2,1)S(1)}, bf16[2,256,1280]{2,1,0:T(8,128)(2,1)S(1)}, u32[]{:S(2)}, u32[]{:S(2)}) collective-permute-start(bf16[2,256,1280]{2,1,0:T(8,128)(2,1)S(1)} %get-tuple-element.40.c0), channel_id=1, source_target_pairs={{0,96},{4,28},{8,104},{12,4},{16,112},{20,12},{24,120},{28,20},{32... | collective-permute-start | bytes 3932168 | tf_op jit(solution)/shard_map/ppermute | solution.py:370
  25.6 18.8 %copy-start.5 = (f32[2560]{0:T(1024)S(1)}, f32[2560]{0:T(1024)}, u32[]{:S(2)}) copy-start(f32[2560]{0:T(1024)} %gain.1) | copy-start | bytes 30724
  48.4 2.2 %collective-permute-start.4 = (bf16[4,4,80,256]{3,2,1,0:T(8,128)(2,1)S(1)}, bf16[4,4,80,256]{3,2,1,0:T(8,128)(2,1)S(1)}, u32[]{:S(2)}, u32[]{:S(2)}) collective-permute-start(bf16[4,4,80,256]{3,2,1,0:T(8,128)(2,1)S(1)} %get-tuple-element.39), channel_id=1, source_target_pairs={{0,4},{4,0},{1,5},{5,1},{2,6},{6,2},{3,7},{7,3},{8,12},{12,8},{9,1... | collective-permute-start | bytes 1966088 | tf_op jit(solution)/shard_map/ppermute | solution.py:383
  53.9 7.1 %collective-permute-start.10 = (bf16[2,4,80,256]{3,2,1,0:T(8,128)(2,1)S(1)}, bf16[2,4,80,256]{3,2,1,0:T(8,128)(2,1)S(1)}, u32[]{:S(2)}, u32[]{:S(2)}) collective-permute-start(bf16[2,4,80,256]{3,2,1,0:T(8,128)(2,1)S(1)} %get-tuple-element.43), channel_id=1, source_target_pairs={{0,96},{4,28},{8,104},{12,4},{16,112},{20,12},{24,120},{28,20},{32... | collective-permute-start | bytes 983048 | tf_op jit(solution)/shard_map/ppermute | solution.py:370
  56.3 11.8 %collective-permute-start.8 = (bf16[2,4,80,256]{3,2,1,0:T(8,128)(2,1)S(1)}, bf16[2,4,80,256]{3,2,1,0:T(8,128)(2,1)S(1)}, u32[]{:S(2)}, u32[]{:S(2)}) collective-permute-start(bf16[2,4,80,256]{3,2,1,0:T(8,128)(2,1)S(1)} %get-tuple-element.41), channel_id=1, source_target_pairs={{0,32},{4,12},{8,40},{12,20},{16,48},{20,28},{24,56},{28,4},{32,64... | collective-permute-start | bytes 983048 | tf_op jit(solution)/shard_map/ppermute | solution.py:370
  56.3 11.8 %collective-permute-start.9 = (bf16[2,4,80,256]{3,2,1,0:T(8,128)(2,1)S(1)}, bf16[2,4,80,256]{3,2,1,0:T(8,128)(2,1)S(1)}, u32[]{:S(2)}, u32[]{:S(2)}) collective-permute-start(bf16[2,4,80,256]{3,2,1,0:T(8,128)(2,1)S(1)} %get-tuple-element.42), channel_id=1, source_target_pairs={{0,64},{4,20},{8,72},{12,28},{16,80},{20,4},{24,88},{28,12},{32,96... | collective-permute-start | bytes 983048 | tf_op jit(solution)/shard_map/ppermute | solution.py:370

commit v6 on v5

--- a/solution.py
+++ b/solution.py
@@ -193,9 +193,7 @@
     return jnp.concatenate([top, low], 0)
 
 
-def early_kernel(act, step_in, bias, rates, docs, halo, skip, cot, other, reach, cum, step, scores, fac, cots, sfac, efac):
-    cots[0] = cot[...]
-    cots[1] = other[...]
+def early_kernel(act, step_in, bias, rates, docs, halo, skip, reach, cum, step, scores, fac, sfac, efac):
     sfac[...] = split_rows(jnp.broadcast_to(upright(skip[...]), (H, LANES))).T[0:16].astype(BF16)
     step[...], cum[...] = steps(step_in, bias, rates)
     doc_row = docs[...].astype(F32)
@@ -240,7 +238,7 @@
     lax.fori_loop(0, XCHUNKS // 2, gates, 0)
 
 
-def back_kernel(local, reach, sgate, act, one, two, gain, normed, mine, give, gated, squares, turned, flat, sem):
+def back_kernel(local, reach, sgate, act, one, two, gain, normed, give, m0, m1, m2, m3, gated, squares, turned, flat, sem):
     c_map = act[:, INNER + N :]
     wide = 2 * LANES
 
@@ -282,41 +280,36 @@
     out = pltpu.make_async_copy(flat, normed, sem)
     out.start()
     y, x, c = [lax.axis_index(a) for a in ("y", "x", "c")]
-    far_y = [lax.rem(i - y + 4, 4) for i in range(4)]
-    far_x = [lax.rem(i - x + 4, 4) for i in range(4)]
-
-    def deal(zero, other):
-        for i in range(4):
-            for j in range(4):
-                row = 80 * (2 * (4 * i + j))
-                zero[far_y[i], j] = turned[row : row + 80, :]
-                other[far_x[j], i] = turned[row + 80 : row + 160, :]
-
-    @pl.when(c == 0)
-    def _():
-        deal(mine, give)
-
-    @pl.when(c == 1)
-    def _():
-        deal(give, mine)
-
+
+    def block(core, k, m):
+        i = jnp.where(core == 0, lax.rem(y + k, 4), m)
+        j = jnp.where(core == 0, m, lax.rem(x + k, 4))
+        return turned[pl.ds(pl.multiple_of(80 * (2 * (4 * i + j) + core), 16), 80), :]
+
+    for k, mine in enumerate((m0, m1, m2, m3)):
+        for m in range(4):
+            give[k, m] = block(1 - c, k, m)
+            mine[m] = block(c, k, m)
     out.wait()
 
 
-def load_kernel(mine, got, c1, c2, c3, *outs):
-    del c1, c2, c3
-    for k, out in enumerate(outs):
-        out[0] = mine[k + 1]
-        out[1] = got[k + 1]
-
-
-def grad_kernel(mine, got, r1, r2, r3, c0, c1, c2, c3, out, flat):
-    left = [mine[0].reshape(320, T), got[0].reshape(320, T)]
+def stack_kernel(one, two, after, out):
+    del after
+    out[0] = one[...]
+    out[1] = two[...]
+
+
+def load_kernel(got, *rest):
+    for k, out in enumerate(rest[-3:]):
+        out[...] = got[k + 1]
+
+
+def grad_kernel(m0, got, m1, m2, m3, r1, r2, r3, c0, c1, c2, c3, out, flat):
+    left = [m0[...].reshape(320, T), got[0].reshape(320, T)]
     right = [c0[0], c0[1]]
-    for r, c in ((r1, c1), (r2, c2), (r3, c3)):
-        for k in range(2):
-            left.append(r[k].reshape(320, T))
-            right.append(c[k])
+    for m, r, c in ((m1, r1, c1), (m2, r2, c2), (m3, r3, c3)):
+        left += [m[...].reshape(320, T), r[...].reshape(320, T)]
+        right += [c[0], c[1]]
     for n in range(5):
         at = slice(256 * n, 256 * n + 256)
         total = dot(left[0], right[0][:, at])
@@ -448,7 +441,7 @@
     )(halo, conv, conv_weight, conv_bias, doc_ids, act, state, info, top)
     one = shifted(msg, 1)
     two = shifted(msg, 2)
-    reach, cum, step, scores, fac, cots, sfac = call(
+    reach, cum, step, scores, fac, sfac = call(
         early_kernel,
         "early",
         (
@@ -457,21 +450,23 @@
             shape((H, T)),
             shape((T, T)),
             shape((T, LANES), BF16),
-            shape((2, T, D), BF16),
             shape((16, LANES), BF16),
         ),
         [VMEM((T, LANES), BF16)],
         8,
-    )(act, step_in, bias, rates, doc_ids, halo, skip_gain[None], cotangent[0], cot_other)
+    )(act, step_in, bias, rates, doc_ids, halo, skip_gain[None])
+    cots = call(
+        stack_kernel, "stack", shape((2, T, D), BF16), [], 4, in_specs=[vmem] * 2 + [anywhere]
+    )(cotangent[0], cot_other, act)
     c1, c2, c3 = [around(cots, k, "y") for k in (1, 2, 3)]
     local, sgate = call(
         late_kernel, "late", (shape((T, INNER)), shape((T, INNER))), [], 8
     )(act, cum, step, scores, fac, gate_input[0], sfac)
     block = (4, 4, 80, T)
-    normed, mine, give = call(
+    normed, give, m0, *mine = call(
         back_kernel,
         "back",
-        (shape((T, INNER), BF16), shape(block, BF16), shape(block, BF16)),
+        (shape((T, INNER), BF16), shape(block, BF16)) + (shape(block[1:], BF16),) * 4,
         [
             VMEM((T, INNER), F32),
             VMEM((T, LANES), F32),
@@ -480,18 +475,14 @@
             pltpu.SemaphoreType.DMA,
         ],
         12,
-        out_specs=(pl.BlockSpec(memory_space=pltpu.HBM), vmem, vmem),
+        out_specs=(pl.BlockSpec(memory_space=pltpu.HBM),) + (vmem,) * 5,
     )(local, reach, sgate, act, one, two, norm_gain)
     got = swapped(give)
+    mine = [around(v, k + 1, "y") for k, v in enumerate(mine)]
     sends = call(
-        load_kernel,
-        "load",
-        (shape((2, 4, 80, T), BF16),) * 3,
-        [],
-        4,
-        in_specs=[vmem] * 2 + [anywhere] * 3,
-    )(mine, got, c1, c2, c3)
-    r1, r2, r3 = [around(v, k + 1, "y") for k, v in enumerate(sends)]
+        load_kernel, "load", (shape(block[1:], BF16),) * 3, [], 4, in_specs=[vmem] + [anywhere] * 3
+    )(got, c1, c2, c3)
+    got_far = [around(v, k + 1, "y") for k, v in enumerate(sends)]
     packed = call(
         grad_kernel,
         "grad",
@@ -500,7 +491,7 @@
         10,
         flops=2 * 10**9,
         moved=8 * 10**6,
-    )(mine, got, r1, r2, r3, cots, c1, c2, c3)
+    )(m0, got, *mine, *got_far, cots, c1, c2, c3)
     pieces = lax.all_to_all(packed, ("y", "x", "c", "z"), 0, 0, axis_index_groups=PLANES)
     grad = call(sum_kernel, "total", shape((20, D)), [VMEM((200, LANES), F32)], 8, moved=10**6)(pieces)
     return (normed[None], grad)

time: 88.6 us -> 87 us (0.982)
  waiting for transfers between devices: 25.2 us -> 16.4 us
  starting transfers between devices: 18.7 us -> 23.4 us
  blocking collectives: 17.5 us -> 20.1 us
    ppermute x6 -> x9, waiting for transfers between devices: 12.5 us -> 4.82 us  [around(): return lax.ppermute(value, ('y', 'x', 'c'), pairs)]
    ppermute x6 -> x9, starting transfers between devices: 10.8 us -> 15.6 us  [around(): return lax.ppermute(value, ('y', 'x', 'c'), pairs)]
    all_to_all x1, blocking collectives: 17.5 us -> 20.1 us  [per_device(): lax.all_to_all(packed, ('y', 'x', 'c', 'z'), 0, 0, axis_index_groups=PLANES)]
    ppermute x2, waiting for transfers between devices: 2.09 us -> 0.44 us  [swapped(): return lax.ppermute(value, 'c', [(0, 1), (1, 0)])]
    pallas_call x2 -> x3, Pallas kernels: 4.09 us -> 4.09 us  [the longest x1 3.97 us: per_device(): call(back_kernel, 'back', (shape((T, INNER), BF16), shape(block, BF16)) +...]
  transfers between devices with their start and end apart: 11 -> 14, of which waited for: 5 -> 5; matrix products, arithmetic and copies ran while one was open for 0% -> 0% of each run, Pallas kernels for 25% -> 25%
where the time goes in v6:
time: 87 us; the launch traced here: 86.8 us
  Pallas kernels  24.6 us (28%)
  starting transfers between devices  23.4 us (27%)
  blocking collectives  20.1 us (23%)
  waiting for transfers between devices  16.4 us (19%)
  local copies, waits for them, and re-layouts  1.41 us (2%)
  between operations  0.88 us (1%)
    all_to_all x1, blocking collectives, per_device(): lax.all_to_all(packed, ('y', 'x', 'c', 'z'), 0, 0, axis_index_groups=PLANES)  20.1 us
    ppermute x9, starting transfers between devices, around(): return lax.ppermute(value, ('y', 'x', 'c'), pairs)  15.6 us
    ppermute x3, waiting for transfers between devices, shifted(): lax.ppermute(value, 'z', [(i, (i + by) % 4) for i in range(4 if by == 1 e...  11.1 us
    pallas_call x1, Pallas kernels, per_device(): call(late_kernel, 'late', (shape((T, INNER)), shape((T, INNER))), [], 8)  8.16 us
    ppermute x3, starting transfers between devices, shifted(): lax.ppermute(value, 'z', [(i, (i + by) % 4) for i in range(4 if by == 1 e...  7.7 us
    ppermute x9, waiting for transfers between devices, around(): return lax.ppermute(value, ('y', 'x', 'c'), pairs)  4.82 us
    pallas_call x1, Pallas kernels, per_device(): call(back_kernel, 'back', (shape((T, INNER), BF16), shape(block, BF16)) +...  3.97 us
    pallas_call x1, Pallas kernels, per_device(): call(front_kernel, 'front', (shape((T, C_ALL), BF16), shape((N, INNER)),...  3.9 us
  transfers between devices with their start and end apart: 14, of which 5 were waited for; matrix products, arithmetic and copies ran while one was open for 0% of the time, Pallas kernels for 25%

profile of v6, /device:TPU:0, one launch (start us, length us, event | category | flops | bytes accessed | tf_op | source)
XLA Modules:
  0.0 86.8 jit_solution(8575910304529254085)
XLA Ops:
  0.6 0.0 copy-start.7
  0.6 0.0 copy-start.4
  0.7 0.1 collective-permute-start.7
  0.8 1.6 %edge.1 = bf16[8,2944]{1,0:T(8,128)(2,1)} custom-call(bf16[256,2816]{1,0:T(8,128)(2,1)} %bitcast.8, s32[1,256]{1,0:T(1,128)} %docs.7), custom_call_target="tpu_custom_call" | custom-call | bytes 100000 | tf_op jit(solution)/shard_map/edge/pallas_call | solution.py:387
  2.4 2.1 %collective-permute-start = (bf16[8,2944]{1,0:T(8,128)(2,1)}, bf16[8,2944]{1,0:T(8,128)(2,1)S(1)}, u32[]{:S(2)}, u32[]{:S(2)}) collective-permute-start(bf16[8,2944]{1,0:T(8,128)(2,1)} %edge.1), channel_id=1, source_target_pairs={{0,1},{1,2},{2,3},{3,0},{4,5},{5,6},{6,7},{7,4},{8,9},{9,10},{10,1... | collective-permute-start | bytes 141320 | tf_op jit(solution)/shard_map/ppermute | solution.py:352
  4.5 0.0 copy-done.4
  4.5 0.0 copy-start
  4.5 1.4 %copy-done = bf16[1,256,2816]{2,1,0:T(8,128)(2,1)S(1)} copy-done((bf16[1,256,2816]{2,1,0:T(8,128)(2,1)S(1)}, bf16[1,256,2816]{2,1,0:T(8,128)(2,1)}, u32[]{:S(2)}) %copy-start) | copy-done | bytes 1441816
  5.9 3.9 %front.1 = (bf16[256,2816]{1,0:T(8,128)(2,1)S(1)}, f32[128,2560]{1,0:T(8,128)S(1)}, bf16[16,2560]{1,0:T(8,128)(2,1)S(1)}, f32[16,2560]{1,0:T(8,128)S(1)}) custom-call(bf16[256,2816]{1,0:T(8,128)(2,1)S(1)} %bitcast.9, f32[40,256]{1,0:T(8,128)S(1)} %bitcast.14, f32[1,40]{1,0:T(1,128)S(1)} %bitcast.16, f32[1,40]{1,0:T(1,128)S(1)} %bitcast.18, ...), custom_call_target="tpu_custom_call" | custom-call | flops 1000000000 | bytes 4000000 | tf_op jit(solution)/shard_map/front/pallas_call | solution.py:399
  9.8 0.0 collective-permute-done.halo
  9.8 0.0 copy-start.2
  9.8 0.6 fix.1
  10.4 2.0 %collective-permute-start.1 = (bf16[144,2560]{1,0:T(8,128)(2,1)S(1)}, bf16[144,2560]{1,0:T(8,128)(2,1)S(1)}, u32[]{:S(2)}, u32[]{:S(2)}) collective-permute-start(bf16[144,2560]{1,0:T(8,128)(2,1)S(1)} %get-tuple-element.38), channel_id=1, source_target_pairs={{0,1},{1,2},{2,3},{3,0},{4,5},{5,6},{6,7},{7,4},{8,9},{9,10},{10,1... | collective-permute-start | bytes 2211848 | tf_op jit(solution)/shard_map/ppermute | solution.py:352
  12.4 3.6 %collective-permute-start.2 = (bf16[144,2560]{1,0:T(8,128)(2,1)S(1)}, bf16[144,2560]{1,0:T(8,128)(2,1)S(1)}, u32[]{:S(2)}, u32[]{:S(2)}) collective-permute-start(bf16[144,2560]{1,0:T(8,128)(2,1)S(1)} %get-tuple-element.38), channel_id=1, source_target_pairs={{0,2},{1,3},{4,6},{5,7},{8,10},{9,11},{12,14},{13,15},{16,18},{17,... | collective-permute-start | bytes 2211848 | tf_op jit(solution)/shard_map/ppermute | solution.py:352
  16.0 0.0 collective-permute-done.7.two
  16.1 0.0 copy-start.10
  16.1 0.1 stack.1.c0
  16.2 0.0 copy-start.1
  16.2 3.1 %collective-permute-start.10 = (bf16[2,256,1280]{2,1,0:T(8,128)(2,1)S(1)}, bf16[2,256,1280]{2,1,0:T(8,128)(2,1)S(1)}, u32[]{:S(2)}, u32[]{:S(2)}) collective-permute-start(bf16[2,256,1280]{2,1,0:T(8,128)(2,1)S(1)} %stack.1.c0), channel_id=1, source_target_pairs={{0,96},{4,28},{8,104},{12,4},{16,112},{20,12},{24,120},{28,20},{32... | collective-permute-start | bytes 3932168 | tf_op jit(solution)/shard_map/ppermute | solution.py:363
  19.3 0.0 collective-permute-start.8
  19.3 2.2 %collective-permute-start.9 = (bf16[2,256,1280]{2,1,0:T(8,128)(2,1)S(1)}, bf16[2,256,1280]{2,1,0:T(8,128)(2,1)S(1)}, u32[]{:S(2)}, u32[]{:S(2)}) collective-permute-start(bf16[2,256,1280]{2,1,0:T(8,128)(2,1)S(1)} %stack.1.c0), channel_id=1, source_target_pairs={{0,64},{4,20},{8,72},{12,28},{16,80},{20,4},{24,88},{28,12},{32,96... | collective-permute-start | bytes 3932168 | tf_op jit(solution)/shard_map/ppermute | solution.py:363
  21.5 3.5 %early.1 = (f32[256,2560]{1,0:T(8,128)S(1)}, f32[40,256]{1,0:T(8,128)S(1)}, f32[40,256]{1,0:T(8,128)S(1)}, f32[256,256]{1,0:T(8,128)S(1)}, bf16[256,128]{1,0:T(8,128)(2,1)S(1)}, /*index=5*/bf16[16,128]{1,0:T(8,128)(2,1)S(1)}) custom-call(bf16[256,2816]{1,0:T(8,128)(2,1)S(1)} %get-tuple-element.29.act.after, f32[40,256]{1,0:T(8,128)S(1)} %bitcast.15, ...), custom_call_target="tpu_custom_call" | custom-call | tf_op jit(solution)/shard_map/early/pallas_call | solution.py:444
  25.0 0.0 copy-start.5
  25.0 8.2 %late.1 = (f32[256,2560]{1,0:T(8,128)S(1)}, f32[256,2560]{1,0:T(8,128)S(1)}) custom-call(bf16[256,2816]{1,0:T(8,128)(2,1)S(1)} %get-tuple-element.29.act.after, f32[40,256]{1,0:T(8,128)S(1)} %get-tuple-element.30.cum, f32[40,256]{1,0:T(8,128)S(1)} %get-tuple-element.31.step, f32[256,256]{1,0:T(8,128)S(1)} %get-tuple-element.32.scores, ...), custom_call_target="tpu_custom_call" | custom-call | tf_op jit(solution)/shard_map/late/pallas_call | solution.py:462
  33.2 0.0 collective-permute-done.1.one
  33.2 11.1 %collective-permute-done.2.two = bf16[144,2560]{1,0:T(8,128)(2,1)S(1)} collective-permute-done((bf16[144,2560]{1,0:T(8,128)(2,1)S(1)}, bf16[144,2560]{1,0:T(8,128)(2,1)S(1)}, u32[]{:S(2)}, u32[]{:S(2)}) %collective-permute-start.2) | collective-permute-done | bytes 737312 | tf_op jit(solution)/shard_map/ppermute | solution.py:352
  44.4 0.0 copy-done.5
  44.4 4.0 %back.1 = (bf16[256,2560]{1,0:T(8,128)(2,1)}, bf16[4,4,80,256]{3,2,1,0:T(8,128)(2,1)S(1)}, bf16[4,80,256]{2,1,0:T(8,128)(2,1)S(1)}, bf16[4,80,256]{2,1,0:T(8,128...) custom-call(f32[256,2560]{1,0:T(8,128)S(1)} %get-tuple-element.35.local, ...), custom_call_target="tpu_custom_call" | custom-call | tf_op jit(solution)/shard_map/back/pallas_call | solution.py:466
  48.3 0.1 collective-permute-start.3
  48.4 1.6 %collective-permute-start.4 = (bf16[4,80,256]{2,1,0:T(8,128)(2,1)S(1)}, bf16[4,80,256]{2,1,0:T(8,128)(2,1)S(1)}, u32[]{:S(2)}, u32[]{:S(2)}) collective-permute-start(bf16[4,80,256]{2,1,0:T(8,128)(2,1)S(1)} %get-tuple-element.42), channel_id=1, source_target_pairs={{0,32},{4,12},{8,40},{12,20},{16,48},{20,28},{24,56},{28,4},{32,64... | collective-permute-start | bytes 491528 | tf_op jit(solution)/shard_map/ppermute | solution.py:363
  50.1 0.4 collective-permute-done.3.got
  50.5 3.2 %collective-permute-start.5 = (bf16[4,80,256]{2,1,0:T(8,128)(2,1)S(1)}, bf16[4,80,256]{2,1,0:T(8,128)(2,1)S(1)}, u32[]{:S(2)}, u32[]{:S(2)}) collective-permute-start(bf16[4,80,256]{2,1,0:T(8,128)(2,1)S(1)} %get-tuple-element.43), channel_id=1, source_target_pairs={{0,64},{4,20},{8,72},{12,28},{16,80},{20,4},{24,88},{28,12},{32,96... | collective-permute-start | bytes 491528 | tf_op jit(solution)/shard_map/ppermute | solution.py:363
  53.7 0.0 collective-permute-done.10.rest_2_.c3
  53.7 1.1 %collective-permute-start.6 = (bf16[4,80,256]{2,1,0:T(8,128)(2,1)S(1)}, bf16[4,80,256]{2,1,0:T(8,128)(2,1)S(1)}, u32[]{:S(2)}, u32[]{:S(2)}) collective-permute-start(bf16[4,80,256]{2,1,0:T(8,128)(2,1)S(1)} %get-tuple-element.44), channel_id=1, source_target_pairs={{0,96},{4,28},{8,104},{12,4},{16,112},{20,12},{24,120},{28,20},{32... | collective-permute-start | bytes 491528 | tf_op jit(solution)/shard_map/ppermute | solution.py:363
  54.8 0.0 collective-permute-done.8.rest_0_.c1
  54.8 0.0 collective-permute-done.9.rest_1_.c2
  54.8 1.0 %collective-permute-start.11 = (bf16[4,80,256]{2,1,0:T(8,128)(2,1)S(1)}, bf16[4,80,256]{2,1,0:T(8,128)(2,1)S(1)}, u32[]{:S(2)}, u32[]{:S(2)}) collective-permute-start(bf16[4,80,256]{2,1,0:T(8,128)(2,1)S(1)} %get-tuple-element.45), channel_id=1, source_target_pairs={{0,32},{4,12},{8,40},{12,20},{16,48},{20,28},{24,56},{28,4},{32,64... | collective-permute-start | bytes 491528 | tf_op jit(solution)/shard_map/ppermute | solution.py:363
  55.9 0.8 collective-permute-start.12
  56.7 0.0 collective-permute-done.4.m1
  56.7 2.5 %collective-permute-start.13 = (bf16[4,80,256]{2,1,0:T(8,128)(2,1)S(1)}, bf16[4,80,256]{2,1,0:T(8,128)(2,1)S(1)}, u32[]{:S(2)}, u32[]{:S(2)}) collective-permute-start(bf16[4,80,256]{2,1,0:T(8,128)(2,1)S(1)} %get-tuple-element.47), channel_id=1, source_target_pairs={{0,96},{4,28},{8,104},{12,4},{16,112},{20,12},{24,120},{28,20},{32... | collective-permute-start | bytes 491528 | tf_op jit(solution)/shard_map/ppermute | solution.py:363
  59.2 0.0 collective-permute-done.5.m2
  59.2 0.2 collective-permute-done.6.m3
  59.4 3.7 %collective-permute-done.11.r1 = bf16[4,80,256]{2,1,0:T(8,128)(2,1)S(1)} collective-permute-done((bf16[4,80,256]{2,1,0:T(8,128)(2,1)S(1)}, bf16[4,80,256]{2,1,0:T(8,128)(2,1)S(1)}, u32[]{:S(2)}, u32[]{:S(2)}) %collective-permute-start.11) | collective-permute-done | bytes 163872 | tf_op jit(solution)/shard_map/ppermute | solution.py:363
  63.2 0.0 collective-permute-done.12.r2
  63.2 0.9 collective-permute-done.13.r3
  64.0 1.9 %grad.1 = bf16[16,200,128]{2,1,0:T(8,128)(2,1)S(1)} custom-call(bf16[4,80,256]{2,1,0:T(8,128)(2,1)S(1)} %get-tuple-element.40.m0, bf16[4,4,80,256]{3,2,1,0:T(8,128)(2,1)S(1)} %collective-permute-done.3.got, bf16[4,80,256]{2,1,0:T(8,128)(2,1)S(1)} %collective-permute-done.4.m1, bf16[4,80,256]{2,1,0:T(8,128)(2,1)S(1)} %collective-permute-done.5.m2, ...), custom_call_target="tpu_custom_call" | custom-call | flops 2000000000 | bytes 8000000 | tf_op jit(solution)/shard_map/grad/pallas_call | solution.py:486
  66.0 20.1 %all_to_all.5.pieces = bf16[16,200,128]{2,1,0:T(8,128)(2,1)S(1)} all-to-all(bf16[16,200,128]{2,1,0:T(8,128)(2,1)S(1)} %grad.1), channel_id=1, replica_groups={{0,1,2,3,8,9,10,11,16,17,18,19,24,25,26,27},{32,33,34,35,40,41,42,43,48..., dimensions={0} | all-to-all | bytes 1638400 | tf_op jit(solution)/shard_map/all_to_all | solution.py:495
  86.0 0.8 total.1
  (13 shorter events, 0.1 us)
Async XLA Ops:
  0.6 3.8 %copy-start.7 = (s32[1,256]{1,0:T(1,128)S(1)}, s32[1,256]{1,0:T(1,128)}, u32[]{:S(2)}) copy-start(s32[1,256]{1,0:T(1,128)} %docs.7) | copy-start | bytes 3076
  0.6 3.8 %copy-start.4 = (f32[1,40,256]{2,1,0:T(8,128)S(1)}, f32[1,40,256]{2,1,0:T(8,128)}, u32[]{:S(2)}) copy-start(f32[1,40,256]{2,1,0:T(8,128)} %param.13) | copy-start | bytes 122884
  0.7 3.8 %copy-start.8 = (f32[40]{0:T(128)S(1)}, f32[40]{0:T(128)}, u32[]{:S(2)}) copy-start(f32[40]{0:T(128)} %param.14) | copy-start | bytes 484
  0.7 3.8 %copy-start.9 = (f32[40]{0:T(128)S(1)}, f32[40]{0:T(128)}, u32[]{:S(2)}) copy-start(f32[40]{0:T(128)} %param.15) | copy-start | bytes 484
  0.7 3.8 %copy-start.3 = (f32[4,2816]{1,0:T(4,128)S(1)}, f32[4,2816]{1,0:T(4,128)}, u32[]{:S(2)}) copy-start(f32[4,2816]{1,0:T(4,128)} %w.3) | copy-start | bytes 135172
  0.7 3.8 %copy-start.6 = (f32[2816]{0:T(1024)S(1)}, f32[2816]{0:T(1024)}, u32[]{:S(2)}) copy-start(f32[2816]{0:T(1024)} %cb.3) | copy-start | bytes 33796
  0.7 15.4 %collective-permute-start.7 = (bf16[256,1280]{1,0:T(8,128)(2,1)}, bf16[256,1280]{1,0:T(8,128)(2,1)S(1)}, u32[]{:S(2)}, u32[]{:S(2)}) collective-permute-start(bf16[256,1280]{1,0:T(8,128)(2,1)} %bitcast.12), channel_id=1, source_target_pairs={{0,4},{4,0},{1,5},{5,1},{2,6},{6,2},{3,7},{7,3},{8,12},{12,8},{9,1... | collective-permute-start | bytes 1966088 | tf_op jit(solution)/shard_map/ppermute | solution.py:376
  2.4 7.4 %collective-permute-start = (bf16[8,2944]{1,0:T(8,128)(2,1)}, bf16[8,2944]{1,0:T(8,128)(2,1)S(1)}, u32[]{:S(2)}, u32[]{:S(2)}) collective-permute-start(bf16[8,2944]{1,0:T(8,128)(2,1)} %edge.1), channel_id=1, source_target_pairs={{0,1},{1,2},{2,3},{3,0},{4,5},{5,6},{6,7},{7,4},{8,9},{9,10},{10,1... | collective-permute-start | bytes 141320 | tf_op jit(solution)/shard_map/ppermute | solution.py:352
  4.5 1.4 %copy-start = (bf16[1,256,2816]{2,1,0:T(8,128)(2,1)S(1)}, bf16[1,256,2816]{2,1,0:T(8,128)(2,1)}, u32[]{:S(2)}) copy-start(bf16[1,256,2816]{2,1,0:T(8,128)(2,1)} %param.11) | copy-start | bytes 4325380
  9.8 6.3 %copy-start.2 = (bf16[1,256,1280]{2,1,0:T(8,128)(2,1)S(1)}, bf16[1,256,1280]{2,1,0:T(8,128)(2,1)}, u32[]{:S(2)}) copy-start(bf16[1,256,1280]{2,1,0:T(8,128)(2,1)} %param.21) | copy-start | bytes 1966084
  10.4 22.8 %collective-permute-start.1 = (bf16[144,2560]{1,0:T(8,128)(2,1)S(1)}, bf16[144,2560]{1,0:T(8,128)(2,1)S(1)}, u32[]{:S(2)}, u32[]{:S(2)}) collective-permute-start(bf16[144,2560]{1,0:T(8,128)(2,1)S(1)} %get-tuple-element.38), channel_id=1, source_target_pairs={{0,1},{1,2},{2,3},{3,0},{4,5},{5,6},{6,7},{7,4},{8,9},{9,10},{10,1... | collective-permute-start | bytes 2211848 | tf_op jit(solution)/shard_map/ppermute | solution.py:352
  12.4 32.0 %collective-permute-start.2 = (bf16[144,2560]{1,0:T(8,128)(2,1)S(1)}, bf16[144,2560]{1,0:T(8,128)(2,1)S(1)}, u32[]{:S(2)}, u32[]{:S(2)}) collective-permute-start(bf16[144,2560]{1,0:T(8,128)(2,1)S(1)} %get-tuple-element.38), channel_id=1, source_target_pairs={{0,2},{1,3},{4,6},{5,7},{8,10},{9,11},{12,14},{13,15},{16,18},{17,... | collective-permute-start | bytes 2211848 | tf_op jit(solution)/shard_map/ppermute | solution.py:352
  16.1 5.4 %copy-start.10 = (f32[40]{0:T(128)S(1)}, f32[40]{0:T(128)}, u32[]{:S(2)}) copy-start(f32[40]{0:T(128)} %param.16) | copy-start | bytes 484
  16.2 8.9 %copy-start.1 = (bf16[1,256,2560]{2,1,0:T(8,128)(2,1)S(1)}, bf16[1,256,2560]{2,1,0:T(8,128)(2,1)}, u32[]{:S(2)}) copy-start(bf16[1,256,2560]{2,1,0:T(8,128)(2,1)} %param.12) | copy-start | bytes 3932164
  16.2 37.5 %collective-permute-start.10 = (bf16[2,256,1280]{2,1,0:T(8,128)(2,1)S(1)}, bf16[2,256,1280]{2,1,0:T(8,128)(2,1)S(1)}, u32[]{:S(2)}, u32[]{:S(2)}) collective-permute-start(bf16[2,256,1280]{2,1,0:T(8,128)(2,1)S(1)} %stack.1.c0), channel_id=1, source_target_pairs={{0,96},{4,28},{8,104},{12,4},{16,112},{20,12},{24,120},{28,20},{32... | collective-permute-start | bytes 3932168 | tf_op jit(solution)/shard_map/ppermute | solution.py:363
  19.3 35.5 %collective-permute-start.8 = (bf16[2,256,1280]{2,1,0:T(8,128)(2,1)S(1)}, bf16[2,256,1280]{2,1,0:T(8,128)(2,1)S(1)}, u32[]{:S(2)}, u32[]{:S(2)}) collective-permute-start(bf16[2,256,1280]{2,1,0:T(8,128)(2,1)S(1)} %stack.1.c0), channel_id=1, source_target_pairs={{0,32},{4,12},{8,40},{12,20},{16,48},{20,28},{24,56},{28,4},{32,64... | collective-permute-start | bytes 3932168 | tf_op jit(solution)/shard_map/ppermute | solution.py:363
  19.3 35.5 %collective-permute-start.9 = (bf16[2,256,1280]{2,1,0:T(8,128)(2,1)S(1)}, bf16[2,256,1280]{2,1,0:T(8,128)(2,1)S(1)}, u32[]{:S(2)}, u32[]{:S(2)}) collective-permute-start(bf16[2,256,1280]{2,1,0:T(8,128)(2,1)S(1)} %stack.1.c0), channel_id=1, source_target_pairs={{0,64},{4,20},{8,72},{12,28},{16,80},{20,4},{24,88},{28,12},{32,96... | collective-permute-start | bytes 3932168 | tf_op jit(solution)/shard_map/ppermute | solution.py:363
  25.0 19.3 %copy-start.5 = (f32[2560]{0:T(1024)S(1)}, f32[2560]{0:T(1024)}, u32[]{:S(2)}) copy-start(f32[2560]{0:T(1024)} %gain.1) | copy-start | bytes 30724
  48.3 2.2 %collective-permute-start.3 = (bf16[4,4,80,256]{3,2,1,0:T(8,128)(2,1)S(1)}, bf16[4,4,80,256]{3,2,1,0:T(8,128)(2,1)S(1)}, u32[]{:S(2)}, u32[]{:S(2)}) collective-permute-start(bf16[4,4,80,256]{3,2,1,0:T(8,128)(2,1)S(1)} %get-tuple-element.41), channel_id=1, source_target_pairs={{0,4},{4,0},{1,5},{5,1},{2,6},{6,2},{3,7},{7,3},{8,12},{12,8},{9,1... | collective-permute-start | bytes 1966088 | tf_op jit(solution)/shard_map/ppermute | solution.py:376
  48.4 8.2 %collective-permute-start.4 = (bf16[4,80,256]{2,1,0:T(8,128)(2,1)S(1)}, bf16[4,80,256]{2,1,0:T(8,128)(2,1)S(1)}, u32[]{:S(2)}, u32[]{:S(2)}) collective-permute-start(bf16[4,80,256]{2,1,0:T(8,128)(2,1)S(1)} %get-tuple-element.42), channel_id=1, source_target_pairs={{0,32},{4,12},{8,40},{12,20},{16,48},{20,28},{24,56},{28,4},{32,64... | collective-permute-start | bytes 491528 | tf_op jit(solution)/shard_map/ppermute | solution.py:363
  50.5 8.7 %collective-permute-start.5 = (bf16[4,80,256]{2,1,0:T(8,128)(2,1)S(1)}, bf16[4,80,256]{2,1,0:T(8,128)(2,1)S(1)}, u32[]{:S(2)}, u32[]{:S(2)}) collective-permute-start(bf16[4,80,256]{2,1,0:T(8,128)(2,1)S(1)} %get-tuple-element.43), channel_id=1, source_target_pairs={{0,64},{4,20},{8,72},{12,28},{16,80},{20,4},{24,88},{28,12},{32,96... | collective-permute-start | bytes 491528 | tf_op jit(solution)/shard_map/ppermute | solution.py:363
  53.7 5.7 %collective-permute-start.6 = (bf16[4,80,256]{2,1,0:T(8,128)(2,1)S(1)}, bf16[4,80,256]{2,1,0:T(8,128)(2,1)S(1)}, u32[]{:S(2)}, u32[]{:S(2)}) collective-permute-start(bf16[4,80,256]{2,1,0:T(8,128)(2,1)S(1)} %get-tuple-element.44), channel_id=1, source_target_pairs={{0,96},{4,28},{8,104},{12,4},{16,112},{20,12},{24,120},{28,20},{32... | collective-permute-start | bytes 491528 | tf_op jit(solution)/shard_map/ppermute | solution.py:363
  54.8 8.4 %collective-permute-start.11 = (bf16[4,80,256]{2,1,0:T(8,128)(2,1)S(1)}, bf16[4,80,256]{2,1,0:T(8,128)(2,1)S(1)}, u32[]{:S(2)}, u32[]{:S(2)}) collective-permute-start(bf16[4,80,256]{2,1,0:T(8,128)(2,1)S(1)} %get-tuple-element.45), channel_id=1, source_target_pairs={{0,32},{4,12},{8,40},{12,20},{16,48},{20,28},{24,56},{28,4},{32,64... | collective-permute-start | bytes 491528 | tf_op jit(solution)/shard_map/ppermute | solution.py:363
  55.9 7.3 %collective-permute-start.12 = (bf16[4,80,256]{2,1,0:T(8,128)(2,1)S(1)}, bf16[4,80,256]{2,1,0:T(8,128)(2,1)S(1)}, u32[]{:S(2)}, u32[]{:S(2)}) collective-permute-start(bf16[4,80,256]{2,1,0:T(8,128)(2,1)S(1)} %get-tuple-element.46), channel_id=1, source_target_pairs={{0,64},{4,20},{8,72},{12,28},{16,80},{20,4},{24,88},{28,12},{32,96... | collective-permute-start | bytes 491528 | tf_op jit(solution)/shard_map/ppermute | solution.py:363
  56.7 7.4 %collective-permute-start.13 = (bf16[4,80,256]{2,1,0:T(8,128)(2,1)S(1)}, bf16[4,80,256]{2,1,0:T(8,128)(2,1)S(1)}, u32[]{:S(2)}, u32[]{:S(2)}) collective-permute-start(bf16[4,80,256]{2,1,0:T(8,128)(2,1)S(1)} %get-tuple-element.47), channel_id=1, source_target_pairs={{0,96},{4,28},{8,104},{12,4},{16,112},{20,12},{24,120},{28,20},{32... | collective-permute-start | bytes 491528 | tf_op jit(solution)/shard_map/ppermute | solution.py:363

commit v7 on v6

--- a/solution.py
+++ b/solution.py
@@ -85,14 +85,24 @@
     out[:, C_ALL:] = jnp.broadcast_to(docb, (8, LANES)).astype(BF16)
 
 
-def front_kernel(conv, step_in, bias, rates, w, cb, docs, act, state, info, top, win, dwin, masks, xs, fac):
+def prep_kernel(step_in, bias, rates, docs, cum_o, step_o, masks, fac, dwin):
     doc_row = docs[...].astype(F32)
     docb = column(doc_row, LANES)
     dwin[0:8, :] = jnp.zeros((8, LANES), F32)
     dwin[8:, :] = docb
     for k in range(3):
         masks[k] = (dwin[5 + k : 5 + k + T, :] == docb).astype(F32)
-    tag = docb[T - 8 :][7:8]
+    step, cum = steps(step_in, bias, rates)
+    step_o[...], cum_o[...] = step, cum
+    tail = (doc_row == doc_row[:, T - 1 : T]).astype(F32)
+    total = cum[:, T - 1 : T]
+    factor = step * jnp.exp(total - cum) * tail
+    whole = jnp.broadcast_to(jnp.exp(total), (H, LANES))
+    fac[...] = split_rows(jnp.concatenate([factor, whole], 1)).T.astype(BF16)
+
+
+def front_kernel(conv, w, cb, docs, masks, fac, act, state, info, top, win, xs):
+    tag = jnp.broadcast_to(docs[:, T - 1 : T].astype(F32), (1, LANES))
     win[:, 0:8, :] = jnp.zeros((2, 8, LANES), F32)
     xs[0:16, :] = jnp.zeros((16, INNER), BF16)
 
@@ -109,12 +119,6 @@
 
     for slot in range(2):
         conv_chunk(XCHUNKS + slot, slot)
-    step, cum = steps(step_in, bias, rates)
-    tail = (doc_row == doc_row[:, T - 1 : T]).astype(F32)
-    total = cum[:, T - 1 : T]
-    factor = step * jnp.exp(total - cum) * tail
-    whole = jnp.broadcast_to(jnp.exp(total), (H, LANES))
-    fac[...] = split_rows(jnp.concatenate([factor, whole], 1)).T.astype(BF16)
 
     def value_chunk(j, slot):
         at, out = conv_chunk(j, slot)
@@ -193,9 +197,8 @@
     return jnp.concatenate([top, low], 0)
 
 
-def early_kernel(act, step_in, bias, rates, docs, halo, skip, reach, cum, step, scores, fac, sfac, efac):
+def early_kernel(act, cum, docs, halo, skip, reach, scores, fac, sfac, efac):
     sfac[...] = split_rows(jnp.broadcast_to(upright(skip[...]), (H, LANES))).T[0:16].astype(BF16)
-    step[...], cum[...] = steps(step_in, bias, rates)
     doc_row = docs[...].astype(F32)
     prev_tag = halo[:, C_ALL : C_ALL + LANES].astype(F32)[7:8, :]
     prev_tag = jnp.where(lax.axis_index("z") > 0, jnp.concatenate([prev_tag, prev_tag], 1), -1.0)
@@ -256,12 +259,13 @@
         value = value * value
         return value[:, 0:LANES] + value[:, LANES:]
 
-    def first_pair(i, carry):
-        squares[...] += first(2 * i) + first(2 * i + 1)
+    def first_group(i, carry):
+        parts = [first(5 * i + k) for k in range(5)]
+        squares[...] += (parts[0] + parts[1]) + (parts[2] + parts[3]) + parts[4]
         return carry
 
-    squares[...] = first(0) + first(1)
-    lax.fori_loop(1, 5, first_pair, 0)
+    squares[...] = jnp.zeros_like(squares)
+    lax.fori_loop(0, 2, first_group, 0)
     mean = jnp.sum(squares[...], axis=1, keepdims=True) * (1.0 / INNER)
     squares[...] = jnp.broadcast_to(lax.rsqrt(mean + 1e-05), squares.shape)
     eye = (
@@ -396,27 +400,26 @@
     halo = shifted(halo, 1)
     step_in, bias, rates = step_input[0], step_bias[None], log_rates[None]
     cot_other = swapped(cotangent[0])
+    cum, step, masks, spread = call(
+        prep_kernel,
+        "prep",
+        (shape((H, T)), shape((H, T)), shape((3, T, LANES)), shape((T + LANES, LANES), BF16)),
+        [VMEM((T + 8, LANES), F32)],
+        4,
+        flops=10**9,
+        moved=10**7,
+        special=10**5,
+    )(step_in, bias, rates, doc_ids)
     act, state, info, top = call(
         front_kernel,
         "front",
-        (
-            shape((T, C_ALL), BF16),
-            shape((N, INNER)),
-            shape((16, INNER), BF16),
-            shape((16, INNER)),
-        ),
-        [
-            VMEM((2, T + 8, LANES), F32),
-            VMEM((T + 8, LANES), F32),
-            VMEM((3, T, LANES), F32),
-            VMEM((T, INNER), BF16),
-            VMEM((T + LANES, LANES), BF16),
-        ],
+        (shape((T, C_ALL), BF16), shape((N, INNER)), shape((16, INNER), BF16), shape((16, INNER))),
+        [VMEM((2, T + 8, LANES), F32), VMEM((T, INNER), BF16)],
         8,
         flops=10**9,
         moved=4 * 10**6,
         special=10**6,
-    )(conv, step_in, bias, rates, conv_weight, conv_bias, doc_ids)
+    )(conv, conv_weight, conv_bias, doc_ids, masks, spread)
     act, msg = call(
         fix_kernel,
         "fix",
@@ -441,20 +444,18 @@
     )(halo, conv, conv_weight, conv_bias, doc_ids, act, state, info, top)
     one = shifted(msg, 1)
     two = shifted(msg, 2)
-    reach, cum, step, scores, fac, sfac = call(
+    reach, scores, fac, sfac = call(
         early_kernel,
         "early",
         (
             shape((T, INNER)),
-            shape((H, T)),
-            shape((H, T)),
             shape((T, T)),
             shape((T, LANES), BF16),
             shape((16, LANES), BF16),
         ),
         [VMEM((T, LANES), BF16)],
         8,
-    )(act, step_in, bias, rates, doc_ids, halo, skip_gain[None])
+    )(act, cum, doc_ids, halo, skip_gain[None])
     cots = call(
         stack_kernel, "stack", shape((2, T, D), BF16), [], 4, in_specs=[vmem] * 2 + [anywhere]
     )(cotangent[0], cot_other, act)

time: 87 us -> 86.3 us (level)
    pallas_call x1 -> x2, Pallas kernels: 3.54 us -> 3.79 us  [the longest x1 3.24 us: per_device(): call(early_kernel, 'early', (shape((T, INNER)), shape((T, T)), shape((T,...]
where the time goes in v7:
time: 86.3 us; the launch traced here: 86.1 us
  Pallas kernels  24.1 us (28%)
  starting transfers between devices  23.4 us (27%)
  blocking collectives  20 us (23%)
  waiting for transfers between devices  16.7 us (19%)
  between operations  0.87 us (1%)
    all_to_all x1, blocking collectives, per_device(): lax.all_to_all(packed, ('y', 'x', 'c', 'z'), 0, 0, axis_index_groups=PLANES)  20 us
    ppermute x9, starting transfers between devices, around(): return lax.ppermute(value, ('y', 'x', 'c'), pairs)  15.6 us
    ppermute x3, waiting for transfers between devices, shifted(): lax.ppermute(value, 'z', [(i, (i + by) % 4) for i in range(4 if by == 1 e...  11.5 us
    pallas_call x1, Pallas kernels, per_device(): call(late_kernel, 'late', (shape((T, INNER)), shape((T, INNER))), [], 8)  8.15 us
    ppermute x3, starting transfers between devices, shifted(): lax.ppermute(value, 'z', [(i, (i + by) % 4) for i in range(4 if by == 1 e...  7.7 us
    ppermute x9, waiting for transfers between devices, around(): return lax.ppermute(value, ('y', 'x', 'c'), pairs)  4.82 us
    pallas_call x1, Pallas kernels, per_device(): call(back_kernel, 'back', (shape((T, INNER), BF16), shape(block, BF16)) +...  3.59 us
    pallas_call x1, Pallas kernels, per_device(): call(front_kernel, 'front', (shape((T, C_ALL), BF16), shape((N, INNER)),...  3.53 us
  transfers between devices with their start and end apart: 14, of which 5 were waited for; matrix products, arithmetic and copies ran while one was open for 0% of the time, Pallas kernels for 25%

profile of v7, /device:TPU:0, one launch (start us, length us, event | category | flops | bytes accessed | tf_op | source)
XLA Modules:
  0.0 86.1 jit_solution(1108781045843433742)
XLA Ops:
  0.6 0.0 copy-start.6
  0.7 0.1 collective-permute-start.7
  0.8 1.6 %edge.1 = bf16[8,2944]{1,0:T(8,128)(2,1)} custom-call(bf16[256,2816]{1,0:T(8,128)(2,1)} %bitcast.8, s32[1,256]{1,0:T(1,128)} %docs.9), custom_call_target="tpu_custom_call" | custom-call | bytes 100000 | tf_op jit(solution)/shard_map/edge/pallas_call | solution.py:391
  2.4 2.1 %collective-permute-start = (bf16[8,2944]{1,0:T(8,128)(2,1)}, bf16[8,2944]{1,0:T(8,128)(2,1)S(1)}, u32[]{:S(2)}, u32[]{:S(2)}) collective-permute-start(bf16[8,2944]{1,0:T(8,128)(2,1)} %edge.1), channel_id=1, source_target_pairs={{0,1},{1,2},{2,3},{3,0},{4,5},{5,6},{6,7},{7,4},{8,9},{9,10},{10,1... | collective-permute-start | bytes 141320 | tf_op jit(solution)/shard_map/ppermute | solution.py:356
  4.5 0.0 copy-start
  4.5 0.0 copy-start.3
  4.5 0.0 copy-start.5
  4.5 0.5 prep.1
  5.1 0.8 copy-done
  5.8 3.5 %front.1 = (bf16[256,2816]{1,0:T(8,128)(2,1)S(1)}, f32[128,2560]{1,0:T(8,128)S(1)}, bf16[16,2560]{1,0:T(8,128)(2,1)S(1)}, f32[16,2560]{1,0:T(8,128)S(1)}) custom-call(bf16[256,2816]{1,0:T(8,128)(2,1)S(1)} %bitcast.9, f32[4,2816]{1,0:T(4,128)S(1)} %copy-done.3, f32[2816]{0:T(1024)S(1)} %copy-done.5, s32[1,256]{1,0:T(1,128)S(1)} %copy-done.6, ...), custom_call_target="tpu_custom_call" | custom-call | flops 1000000000 | bytes 4000000 | tf_op jit(solution)/shard_map/front/pallas_call | solution.py:413
  9.4 0.0 collective-permute-done.halo
  9.4 0.0 copy-start.2
  9.4 0.6 fix.1
  10.0 2.0 %collective-permute-start.1 = (bf16[144,2560]{1,0:T(8,128)(2,1)S(1)}, bf16[144,2560]{1,0:T(8,128)(2,1)S(1)}, u32[]{:S(2)}, u32[]{:S(2)}) collective-permute-start(bf16[144,2560]{1,0:T(8,128)(2,1)S(1)} %get-tuple-element.42), channel_id=1, source_target_pairs={{0,1},{1,2},{2,3},{3,0},{4,5},{5,6},{6,7},{7,4},{8,9},{9,10},{10,1... | collective-permute-start | bytes 2211848 | tf_op jit(solution)/shard_map/ppermute | solution.py:356
  12.0 3.6 %collective-permute-start.2 = (bf16[144,2560]{1,0:T(8,128)(2,1)S(1)}, bf16[144,2560]{1,0:T(8,128)(2,1)S(1)}, u32[]{:S(2)}, u32[]{:S(2)}) collective-permute-start(bf16[144,2560]{1,0:T(8,128)(2,1)S(1)} %get-tuple-element.42), channel_id=1, source_target_pairs={{0,2},{1,3},{4,6},{5,7},{8,10},{9,11},{12,14},{13,15},{16,18},{17,... | collective-permute-start | bytes 2211848 | tf_op jit(solution)/shard_map/ppermute | solution.py:356
  15.6 0.0 collective-permute-done.7.two
  15.7 0.0 copy-start.7
  15.7 0.1 stack.1.c0
  15.8 0.0 copy-start.1
  15.8 3.1 %collective-permute-start.10 = (bf16[2,256,1280]{2,1,0:T(8,128)(2,1)S(1)}, bf16[2,256,1280]{2,1,0:T(8,128)(2,1)S(1)}, u32[]{:S(2)}, u32[]{:S(2)}) collective-permute-start(bf16[2,256,1280]{2,1,0:T(8,128)(2,1)S(1)} %stack.1.c0), channel_id=1, source_target_pairs={{0,96},{4,28},{8,104},{12,4},{16,112},{20,12},{24,120},{28,20},{32... | collective-permute-start | bytes 3932168 | tf_op jit(solution)/shard_map/ppermute | solution.py:367
  18.9 0.0 collective-permute-start.8
  18.9 2.2 %collective-permute-start.9 = (bf16[2,256,1280]{2,1,0:T(8,128)(2,1)S(1)}, bf16[2,256,1280]{2,1,0:T(8,128)(2,1)S(1)}, u32[]{:S(2)}, u32[]{:S(2)}) collective-permute-start(bf16[2,256,1280]{2,1,0:T(8,128)(2,1)S(1)} %stack.1.c0), channel_id=1, source_target_pairs={{0,64},{4,20},{8,72},{12,28},{16,80},{20,4},{24,88},{28,12},{32,96... | collective-permute-start | bytes 3932168 | tf_op jit(solution)/shard_map/ppermute | solution.py:367
  21.1 3.2 %early.1 = (f32[256,2560]{1,0:T(8,128)S(1)}, f32[256,256]{1,0:T(8,128)S(1)}, bf16[256,128]{1,0:T(8,128)(2,1)S(1)}, bf16[16,128]{1,0:T(8,128)(2,1)S(1)}) custom-call(bf16[256,2816]{1,0:T(8,128)(2,1)S(1)} %get-tuple-element.33.act.after, f32[40,256]{1,0:T(8,128)S(1)} %get-tuple-element.34.cum, s32[1,256]{1,0:T(1,128)S(1)} %copy-done.6, ...), custom_call_target="tpu_custom_call" | custom-call | tf_op jit(solution)/shard_map/early/pallas_call | solution.py:447
  24.3 0.0 copy-start.4
  24.3 8.2 %late.1 = (f32[256,2560]{1,0:T(8,128)S(1)}, f32[256,2560]{1,0:T(8,128)S(1)}) custom-call(bf16[256,2816]{1,0:T(8,128)(2,1)S(1)} %get-tuple-element.33.act.after, f32[40,256]{1,0:T(8,128)S(1)} %get-tuple-element.34.cum, f32[40,256]{1,0:T(8,128)S(1)} %get-tuple-element.35.step, f32[256,256]{1,0:T(8,128)S(1)} %get-tuple-element.36.scores, ...), custom_call_target="tpu_custom_call" | custom-call | tf_op jit(solution)/shard_map/late/pallas_call | solution.py:463
  32.5 0.0 collective-permute-done.1.one
  32.5 11.4 %collective-permute-done.2.two = bf16[144,2560]{1,0:T(8,128)(2,1)S(1)} collective-permute-done((bf16[144,2560]{1,0:T(8,128)(2,1)S(1)}, bf16[144,2560]{1,0:T(8,128)(2,1)S(1)}, u32[]{:S(2)}, u32[]{:S(2)}) %collective-permute-start.2) | collective-permute-done | bytes 737312 | tf_op jit(solution)/shard_map/ppermute | solution.py:356
  44.0 3.6 %back.1 = (bf16[256,2560]{1,0:T(8,128)(2,1)}, bf16[4,4,80,256]{3,2,1,0:T(8,128)(2,1)S(1)}, bf16[4,80,256]{2,1,0:T(8,128)(2,1)S(1)}, bf16[4,80,256]{2,1,0:T(8,128...) custom-call(f32[256,2560]{1,0:T(8,128)S(1)} %get-tuple-element.39.local, ...), custom_call_target="tpu_custom_call" | custom-call | tf_op jit(solution)/shard_map/back/pallas_call | solution.py:467
  47.6 0.1 collective-permute-start.3
  47.7 1.6 %collective-permute-start.4 = (bf16[4,80,256]{2,1,0:T(8,128)(2,1)S(1)}, bf16[4,80,256]{2,1,0:T(8,128)(2,1)S(1)}, u32[]{:S(2)}, u32[]{:S(2)}) collective-permute-start(bf16[4,80,256]{2,1,0:T(8,128)(2,1)S(1)} %get-tuple-element.46), channel_id=1, source_target_pairs={{0,32},{4,12},{8,40},{12,20},{16,48},{20,28},{24,56},{28,4},{32,64... | collective-permute-start | bytes 491528 | tf_op jit(solution)/shard_map/ppermute | solution.py:367
  49.3 0.4 collective-permute-done.3.got
  49.7 3.2 %collective-permute-start.5 = (bf16[4,80,256]{2,1,0:T(8,128)(2,1)S(1)}, bf16[4,80,256]{2,1,0:T(8,128)(2,1)S(1)}, u32[]{:S(2)}, u32[]{:S(2)}) collective-permute-start(bf16[4,80,256]{2,1,0:T(8,128)(2,1)S(1)} %get-tuple-element.47), channel_id=1, source_target_pairs={{0,64},{4,20},{8,72},{12,28},{16,80},{20,4},{24,88},{28,12},{32,96... | collective-permute-start | bytes 491528 | tf_op jit(solution)/shard_map/ppermute | solution.py:367
  52.9 0.0 collective-permute-done.10.rest_2_.c3
  52.9 1.1 %collective-permute-start.6 = (bf16[4,80,256]{2,1,0:T(8,128)(2,1)S(1)}, bf16[4,80,256]{2,1,0:T(8,128)(2,1)S(1)}, u32[]{:S(2)}, u32[]{:S(2)}) collective-permute-start(bf16[4,80,256]{2,1,0:T(8,128)(2,1)S(1)} %get-tuple-element.48), channel_id=1, source_target_pairs={{0,96},{4,28},{8,104},{12,4},{16,112},{20,12},{24,120},{28,20},{32... | collective-permute-start | bytes 491528 | tf_op jit(solution)/shard_map/ppermute | solution.py:367
  54.0 0.0 collective-permute-done.8.rest_0_.c1
  54.0 0.0 collective-permute-done.9.rest_1_.c2
  54.0 1.0 %collective-permute-start.11 = (bf16[4,80,256]{2,1,0:T(8,128)(2,1)S(1)}, bf16[4,80,256]{2,1,0:T(8,128)(2,1)S(1)}, u32[]{:S(2)}, u32[]{:S(2)}) collective-permute-start(bf16[4,80,256]{2,1,0:T(8,128)(2,1)S(1)} %get-tuple-element.49), channel_id=1, source_target_pairs={{0,32},{4,12},{8,40},{12,20},{16,48},{20,28},{24,56},{28,4},{32,64... | collective-permute-start | bytes 491528 | tf_op jit(solution)/shard_map/ppermute | solution.py:367
  55.1 0.8 collective-permute-start.12
  55.9 0.0 collective-permute-done.4.m1
  55.9 2.5 %collective-permute-start.13 = (bf16[4,80,256]{2,1,0:T(8,128)(2,1)S(1)}, bf16[4,80,256]{2,1,0:T(8,128)(2,1)S(1)}, u32[]{:S(2)}, u32[]{:S(2)}) collective-permute-start(bf16[4,80,256]{2,1,0:T(8,128)(2,1)S(1)} %get-tuple-element.51), channel_id=1, source_target_pairs={{0,96},{4,28},{8,104},{12,4},{16,112},{20,12},{24,120},{28,20},{32... | collective-permute-start | bytes 491528 | tf_op jit(solution)/shard_map/ppermute | solution.py:367
  58.4 0.0 collective-permute-done.5.m2
  58.4 0.2 collective-permute-done.6.m3
  58.7 3.7 %collective-permute-done.11.r1 = bf16[4,80,256]{2,1,0:T(8,128)(2,1)S(1)} collective-permute-done((bf16[4,80,256]{2,1,0:T(8,128)(2,1)S(1)}, bf16[4,80,256]{2,1,0:T(8,128)(2,1)S(1)}, u32[]{:S(2)}, u32[]{:S(2)}) %collective-permute-start.11) | collective-permute-done | bytes 163872 | tf_op jit(solution)/shard_map/ppermute | solution.py:367
  62.4 0.0 collective-permute-done.12.r2
  62.4 0.9 collective-permute-done.13.r3
  63.3 2.0 %grad.1 = bf16[16,200,128]{2,1,0:T(8,128)(2,1)S(1)} custom-call(bf16[4,80,256]{2,1,0:T(8,128)(2,1)S(1)} %get-tuple-element.44.m0, bf16[4,4,80,256]{3,2,1,0:T(8,128)(2,1)S(1)} %collective-permute-done.3.got, bf16[4,80,256]{2,1,0:T(8,128)(2,1)S(1)} %collective-permute-done.4.m1, bf16[4,80,256]{2,1,0:T(8,128)(2,1)S(1)} %collective-permute-done.5.m2, ...), custom_call_target="tpu_custom_call" | custom-call | flops 2000000000 | bytes 8000000 | tf_op jit(solution)/shard_map/grad/pallas_call | solution.py:487
  65.2 20.0 %all_to_all.5.pieces = bf16[16,200,128]{2,1,0:T(8,128)(2,1)S(1)} all-to-all(bf16[16,200,128]{2,1,0:T(8,128)(2,1)S(1)} %grad.1), channel_id=1, replica_groups={{0,1,2,3,8,9,10,11,16,17,18,19,24,25,26,27},{32,33,34,35,40,41,42,43,48..., dimensions={0} | all-to-all | bytes 1638400 | tf_op jit(solution)/shard_map/all_to_all | solution.py:496
  85.3 0.8 total.1
  (14 shorter events, 0.1 us)
Async XLA Ops:
  0.6 3.8 %copy-start.6 = (s32[1,256]{1,0:T(1,128)S(1)}, s32[1,256]{1,0:T(1,128)}, u32[]{:S(2)}) copy-start(s32[1,256]{1,0:T(1,128)} %docs.9) | copy-start | bytes 3076
  0.6 3.8 %copy-start.8 = (f32[1,40,256]{2,1,0:T(8,128)S(1)}, f32[1,40,256]{2,1,0:T(8,128)}, u32[]{:S(2)}) copy-start(f32[1,40,256]{2,1,0:T(8,128)} %param.13) | copy-start | bytes 122884
  0.7 3.8 %copy-start.9 = (f32[40]{0:T(128)S(1)}, f32[40]{0:T(128)}, u32[]{:S(2)}) copy-start(f32[40]{0:T(128)} %param.14) | copy-start | bytes 484
  0.7 3.8 %copy-start.10 = (f32[40]{0:T(128)S(1)}, f32[40]{0:T(128)}, u32[]{:S(2)}) copy-start(f32[40]{0:T(128)} %param.15) | copy-start | bytes 484
  0.7 15.0 %collective-permute-start.7 = (bf16[256,1280]{1,0:T(8,128)(2,1)}, bf16[256,1280]{1,0:T(8,128)(2,1)S(1)}, u32[]{:S(2)}, u32[]{:S(2)}) collective-permute-start(bf16[256,1280]{1,0:T(8,128)(2,1)} %bitcast.12), channel_id=1, source_target_pairs={{0,4},{4,0},{1,5},{5,1},{2,6},{6,2},{3,7},{7,3},{8,12},{12,8},{9,1... | collective-permute-start | bytes 1966088 | tf_op jit(solution)/shard_map/ppermute | solution.py:380
  2.4 7.0 %collective-permute-start = (bf16[8,2944]{1,0:T(8,128)(2,1)}, bf16[8,2944]{1,0:T(8,128)(2,1)S(1)}, u32[]{:S(2)}, u32[]{:S(2)}) collective-permute-start(bf16[8,2944]{1,0:T(8,128)(2,1)} %edge.1), channel_id=1, source_target_pairs={{0,1},{1,2},{2,3},{3,0},{4,5},{5,6},{6,7},{7,4},{8,9},{9,10},{10,1... | collective-permute-start | bytes 141320 | tf_op jit(solution)/shard_map/ppermute | solution.py:356
  4.5 1.4 %copy-start = (bf16[1,256,2816]{2,1,0:T(8,128)(2,1)S(1)}, bf16[1,256,2816]{2,1,0:T(8,128)(2,1)}, u32[]{:S(2)}) copy-start(bf16[1,256,2816]{2,1,0:T(8,128)(2,1)} %param.11) | copy-start | bytes 4325380
  4.5 1.4 %copy-start.3 = (f32[4,2816]{1,0:T(4,128)S(1)}, f32[4,2816]{1,0:T(4,128)}, u32[]{:S(2)}) copy-start(f32[4,2816]{1,0:T(4,128)} %w.3) | copy-start | bytes 135172
  4.5 1.3 %copy-start.5 = (f32[2816]{0:T(1024)S(1)}, f32[2816]{0:T(1024)}, u32[]{:S(2)}) copy-start(f32[2816]{0:T(1024)} %cb.3) | copy-start | bytes 33796
  9.4 6.3 %copy-start.2 = (bf16[1,256,1280]{2,1,0:T(8,128)(2,1)S(1)}, bf16[1,256,1280]{2,1,0:T(8,128)(2,1)}, u32[]{:S(2)}) copy-start(bf16[1,256,1280]{2,1,0:T(8,128)(2,1)} %param.21) | copy-start | bytes 1966084
  10.0 22.5 %collective-permute-start.1 = (bf16[144,2560]{1,0:T(8,128)(2,1)S(1)}, bf16[144,2560]{1,0:T(8,128)(2,1)S(1)}, u32[]{:S(2)}, u32[]{:S(2)}) collective-permute-start(bf16[144,2560]{1,0:T(8,128)(2,1)S(1)} %get-tuple-element.42), channel_id=1, source_target_pairs={{0,1},{1,2},{2,3},{3,0},{4,5},{5,6},{6,7},{7,4},{8,9},{9,10},{10,1... | collective-permute-start | bytes 2211848 | tf_op jit(solution)/shard_map/ppermute | solution.py:356
  12.0 32.0 %collective-permute-start.2 = (bf16[144,2560]{1,0:T(8,128)(2,1)S(1)}, bf16[144,2560]{1,0:T(8,128)(2,1)S(1)}, u32[]{:S(2)}, u32[]{:S(2)}) collective-permute-start(bf16[144,2560]{1,0:T(8,128)(2,1)S(1)} %get-tuple-element.42), channel_id=1, source_target_pairs={{0,2},{1,3},{4,6},{5,7},{8,10},{9,11},{12,14},{13,15},{16,18},{17,... | collective-permute-start | bytes 2211848 | tf_op jit(solution)/shard_map/ppermute | solution.py:356
  15.7 5.4 %copy-start.7 = (f32[40]{0:T(128)S(1)}, f32[40]{0:T(128)}, u32[]{:S(2)}) copy-start(f32[40]{0:T(128)} %param.16) | copy-start | bytes 484
  15.8 8.6 %copy-start.1 = (bf16[1,256,2560]{2,1,0:T(8,128)(2,1)S(1)}, bf16[1,256,2560]{2,1,0:T(8,128)(2,1)}, u32[]{:S(2)}) copy-start(bf16[1,256,2560]{2,1,0:T(8,128)(2,1)} %param.12) | copy-start | bytes 3932164
  15.8 37.2 %collective-permute-start.10 = (bf16[2,256,1280]{2,1,0:T(8,128)(2,1)S(1)}, bf16[2,256,1280]{2,1,0:T(8,128)(2,1)S(1)}, u32[]{:S(2)}, u32[]{:S(2)}) collective-permute-start(bf16[2,256,1280]{2,1,0:T(8,128)(2,1)S(1)} %stack.1.c0), channel_id=1, source_target_pairs={{0,96},{4,28},{8,104},{12,4},{16,112},{20,12},{24,120},{28,20},{32... | collective-permute-start | bytes 3932168 | tf_op jit(solution)/shard_map/ppermute | solution.py:367
  18.9 35.1 %collective-permute-start.8 = (bf16[2,256,1280]{2,1,0:T(8,128)(2,1)S(1)}, bf16[2,256,1280]{2,1,0:T(8,128)(2,1)S(1)}, u32[]{:S(2)}, u32[]{:S(2)}) collective-permute-start(bf16[2,256,1280]{2,1,0:T(8,128)(2,1)S(1)} %stack.1.c0), channel_id=1, source_target_pairs={{0,32},{4,12},{8,40},{12,20},{16,48},{20,28},{24,56},{28,4},{32,64... | collective-permute-start | bytes 3932168 | tf_op jit(solution)/shard_map/ppermute | solution.py:367
  18.9 35.1 %collective-permute-start.9 = (bf16[2,256,1280]{2,1,0:T(8,128)(2,1)S(1)}, bf16[2,256,1280]{2,1,0:T(8,128)(2,1)S(1)}, u32[]{:S(2)}, u32[]{:S(2)}) collective-permute-start(bf16[2,256,1280]{2,1,0:T(8,128)(2,1)S(1)} %stack.1.c0), channel_id=1, source_target_pairs={{0,64},{4,20},{8,72},{12,28},{16,80},{20,4},{24,88},{28,12},{32,96... | collective-permute-start | bytes 3932168 | tf_op jit(solution)/shard_map/ppermute | solution.py:367
  24.3 19.6 %copy-start.4 = (f32[2560]{0:T(1024)S(1)}, f32[2560]{0:T(1024)}, u32[]{:S(2)}) copy-start(f32[2560]{0:T(1024)} %gain.1) | copy-start | bytes 30724
  47.6 2.2 %collective-permute-start.3 = (bf16[4,4,80,256]{3,2,1,0:T(8,128)(2,1)S(1)}, bf16[4,4,80,256]{3,2,1,0:T(8,128)(2,1)S(1)}, u32[]{:S(2)}, u32[]{:S(2)}) collective-permute-start(bf16[4,4,80,256]{3,2,1,0:T(8,128)(2,1)S(1)} %get-tuple-element.45), channel_id=1, source_target_pairs={{0,4},{4,0},{1,5},{5,1},{2,6},{6,2},{3,7},{7,3},{8,12},{12,8},{9,1... | collective-permute-start | bytes 1966088 | tf_op jit(solution)/shard_map/ppermute | solution.py:380
  47.7 8.2 %collective-permute-start.4 = (bf16[4,80,256]{2,1,0:T(8,128)(2,1)S(1)}, bf16[4,80,256]{2,1,0:T(8,128)(2,1)S(1)}, u32[]{:S(2)}, u32[]{:S(2)}) collective-permute-start(bf16[4,80,256]{2,1,0:T(8,128)(2,1)S(1)} %get-tuple-element.46), channel_id=1, source_target_pairs={{0,32},{4,12},{8,40},{12,20},{16,48},{20,28},{24,56},{28,4},{32,64... | collective-permute-start | bytes 491528 | tf_op jit(solution)/shard_map/ppermute | solution.py:367
  49.7 8.7 %collective-permute-start.5 = (bf16[4,80,256]{2,1,0:T(8,128)(2,1)S(1)}, bf16[4,80,256]{2,1,0:T(8,128)(2,1)S(1)}, u32[]{:S(2)}, u32[]{:S(2)}) collective-permute-start(bf16[4,80,256]{2,1,0:T(8,128)(2,1)S(1)} %get-tuple-element.47), channel_id=1, source_target_pairs={{0,64},{4,20},{8,72},{12,28},{16,80},{20,4},{24,88},{28,12},{32,96... | collective-permute-start | bytes 491528 | tf_op jit(solution)/shard_map/ppermute | solution.py:367
  52.9 5.7 %collective-permute-start.6 = (bf16[4,80,256]{2,1,0:T(8,128)(2,1)S(1)}, bf16[4,80,256]{2,1,0:T(8,128)(2,1)S(1)}, u32[]{:S(2)}, u32[]{:S(2)}) collective-permute-start(bf16[4,80,256]{2,1,0:T(8,128)(2,1)S(1)} %get-tuple-element.48), channel_id=1, source_target_pairs={{0,96},{4,28},{8,104},{12,4},{16,112},{20,12},{24,120},{28,20},{32... | collective-permute-start | bytes 491528 | tf_op jit(solution)/shard_map/ppermute | solution.py:367
  54.0 8.4 %collective-permute-start.11 = (bf16[4,80,256]{2,1,0:T(8,128)(2,1)S(1)}, bf16[4,80,256]{2,1,0:T(8,128)(2,1)S(1)}, u32[]{:S(2)}, u32[]{:S(2)}) collective-permute-start(bf16[4,80,256]{2,1,0:T(8,128)(2,1)S(1)} %get-tuple-element.49), channel_id=1, source_target_pairs={{0,32},{4,12},{8,40},{12,20},{16,48},{20,28},{24,56},{28,4},{32,64... | collective-permute-start | bytes 491528 | tf_op jit(solution)/shard_map/ppermute | solution.py:367
  55.1 7.3 %collective-permute-start.12 = (bf16[4,80,256]{2,1,0:T(8,128)(2,1)S(1)}, bf16[4,80,256]{2,1,0:T(8,128)(2,1)S(1)}, u32[]{:S(2)}, u32[]{:S(2)}) collective-permute-start(bf16[4,80,256]{2,1,0:T(8,128)(2,1)S(1)} %get-tuple-element.50), channel_id=1, source_target_pairs={{0,64},{4,20},{8,72},{12,28},{16,80},{20,4},{24,88},{28,12},{32,96... | collective-permute-start | bytes 491528 | tf_op jit(solution)/shard_map/ppermute | solution.py:367
  55.9 7.4 %collective-permute-start.13 = (bf16[4,80,256]{2,1,0:T(8,128)(2,1)S(1)}, bf16[4,80,256]{2,1,0:T(8,128)(2,1)S(1)}, u32[]{:S(2)}, u32[]{:S(2)}) collective-permute-start(bf16[4,80,256]{2,1,0:T(8,128)(2,1)S(1)} %get-tuple-element.51), channel_id=1, source_target_pairs={{0,96},{4,28},{8,104},{12,4},{16,112},{20,12},{24,120},{28,20},{32... | collective-permute-start | bytes 491528 | tf_op jit(solution)/shard_map/ppermute | solution.py:367

commit v8 on v7

--- a/solution.py
+++ b/solution.py
@@ -103,7 +103,7 @@
 
 def front_kernel(conv, w, cb, docs, masks, fac, act, state, info, top, win, xs):
     tag = jnp.broadcast_to(docs[:, T - 1 : T].astype(F32), (1, LANES))
-    win[:, 0:8, :] = jnp.zeros((2, 8, LANES), F32)
+    win[:, 0:8, :] = jnp.zeros((5, 8, LANES), F32)
     xs[0:16, :] = jnp.zeros((16, INNER), BF16)
 
     def conv_chunk(j, slot):
@@ -131,12 +131,12 @@
         rows = jnp.where(row == 0, hi, jnp.where(row == 1, end - hi, jnp.where(row == 2, tag, 0.0)))
         info[:, at] = rows.astype(BF16)
 
-    def value_pair(i, carry):
-        for slot in range(2):
-            value_chunk(2 * i + slot, slot)
+    def value_group(i, carry):
+        for slot in range(5):
+            value_chunk(5 * i + slot, slot)
         return carry
 
-    lax.fori_loop(0, XCHUNKS // 2, value_pair, 0)
+    lax.fori_loop(0, XCHUNKS // 5, value_group, 0)
     b_t = act[:, INNER : INNER + N].astype(F32).T.astype(BF16)
     for k in range(5):
         at = slice(512 * k, 512 * k + 512)
@@ -273,14 +273,14 @@
     ).astype(BF16)
 
     def second(i, carry):
-        for k in range(4):
-            at = pl.ds(pl.multiple_of((4 * i + k) * LANES, LANES), LANES)
+        for k in range(10):
+            at = pl.ds(pl.multiple_of((10 * i + k) * LANES, LANES), LANES)
             value = (gated[:, at] * squares[...] * gain[at].reshape(1, LANES)).astype(BF16)
             flat[:, at] = value
             turned[at, :] = dot(eye, value, ((1,), (1,))).astype(BF16)
         return carry
 
-    lax.fori_loop(0, 5, second, 0)
+    lax.fori_loop(0, 2, second, 0)
     out = pltpu.make_async_copy(flat, normed, sem)
     out.start()
     y, x, c = [lax.axis_index(a) for a in ("y", "x", "c")]
@@ -414,7 +414,7 @@
         front_kernel,
         "front",
         (shape((T, C_ALL), BF16), shape((N, INNER)), shape((16, INNER), BF16), shape((16, INNER))),
-        [VMEM((2, T + 8, LANES), F32), VMEM((T, INNER), BF16)],
+        [VMEM((5, T + 8, LANES), F32), VMEM((T, INNER), BF16)],
         8,
         flops=10**9,
         moved=4 * 10**6,

time: 86.3 us -> 85.3 us (0.988)
  Pallas kernels: 24.1 us -> 23.2 us
  transfers between devices with their start and end apart: 14 -> 14, of which waited for: 5 -> 6; matrix products, arithmetic and copies ran while one was open for 0% -> 0% of each run, Pallas kernels for 25% -> 24%
where the time goes in v8:
time: 85.3 us; the launch traced here: 85.1 us
  starting transfers between devices  23.2 us (27%)
  Pallas kernels  23.2 us (27%)
  blocking collectives  20 us (23%)
  waiting for transfers between devices  17 us (20%)
  between operations  0.86 us (1%)
    all_to_all x1, blocking collectives, per_device(): lax.all_to_all(packed, ('y', 'x', 'c', 'z'), 0, 0, axis_index_groups=PLANES)  20 us
    ppermute x9, starting transfers between devices, around(): return lax.ppermute(value, ('y', 'x', 'c'), pairs)  15.6 us
    ppermute x3, waiting for transfers between devices, shifted(): lax.ppermute(value, 'z', [(i, (i + by) % 4) for i in range(4 if by == 1 e...  11.7 us
    pallas_call x1, Pallas kernels, per_device(): call(late_kernel, 'late', (shape((T, INNER)), shape((T, INNER))), [], 8)  8.15 us
    ppermute x3, starting transfers between devices, shifted(): lax.ppermute(value, 'z', [(i, (i + by) % 4) for i in range(4 if by == 1 e...  7.43 us
    ppermute x9, waiting for transfers between devices, around(): return lax.ppermute(value, ('y', 'x', 'c'), pairs)  4.83 us
    pallas_call x1, Pallas kernels, per_device(): call(early_kernel, 'early', (shape((T, INNER)), shape((T, T)), shape((T,...  3.25 us
    pallas_call x1, Pallas kernels, per_device(): call(back_kernel, 'back', (shape((T, INNER), BF16), shape(block, BF16)) +...  3.19 us
  transfers between devices with their start and end apart: 14, of which 6 were waited for; matrix products, arithmetic and copies ran while one was open for 0% of the time, Pallas kernels for 24%

profile of v8, /device:TPU:0, one launch (start us, length us, event | category | flops | bytes accessed | tf_op | source)
XLA Modules:
  0.0 85.1 jit_solution(10350211937404186373)
XLA Ops:
  0.6 0.0 copy-start.6
  0.7 0.1 collective-permute-start.7
  0.8 1.6 %edge.1 = bf16[8,2944]{1,0:T(8,128)(2,1)} custom-call(bf16[256,2816]{1,0:T(8,128)(2,1)} %bitcast.8, s32[1,256]{1,0:T(1,128)} %docs.9), custom_call_target="tpu_custom_call" | custom-call | bytes 100000 | tf_op jit(solution)/shard_map/edge/pallas_call | solution.py:391
  2.4 2.1 %collective-permute-start = (bf16[8,2944]{1,0:T(8,128)(2,1)}, bf16[8,2944]{1,0:T(8,128)(2,1)S(1)}, u32[]{:S(2)}, u32[]{:S(2)}) collective-permute-start(bf16[8,2944]{1,0:T(8,128)(2,1)} %edge.1), channel_id=1, source_target_pairs={{0,1},{1,2},{2,3},{3,0},{4,5},{5,6},{6,7},{7,4},{8,9},{9,10},{10,1... | collective-permute-start | bytes 141320 | tf_op jit(solution)/shard_map/ppermute | solution.py:356
  4.5 0.0 copy-start
  4.5 0.0 copy-start.3
  4.5 0.0 copy-start.5
  4.5 0.5 prep.1
  5.1 0.8 copy-done
  5.8 0.0 copy-done.3
  5.8 3.0 %front.1 = (bf16[256,2816]{1,0:T(8,128)(2,1)S(1)}, f32[128,2560]{1,0:T(8,128)S(1)}, bf16[16,2560]{1,0:T(8,128)(2,1)S(1)}, f32[16,2560]{1,0:T(8,128)S(1)}) custom-call(bf16[256,2816]{1,0:T(8,128)(2,1)S(1)} %bitcast.9, f32[4,2816]{1,0:T(4,128)S(1)} %copy-done.3, f32[2816]{0:T(1024)S(1)} %copy-done.5, s32[1,256]{1,0:T(1,128)S(1)} %copy-done.6, ...), custom_call_target="tpu_custom_call" | custom-call | flops 1000000000 | bytes 4000000 | tf_op jit(solution)/shard_map/front/pallas_call | solution.py:413
  8.8 0.3 collective-permute-done.halo
  9.1 0.6 fix.1
  9.7 1.7 %collective-permute-start.1 = (bf16[144,2560]{1,0:T(8,128)(2,1)S(1)}, bf16[144,2560]{1,0:T(8,128)(2,1)S(1)}, u32[]{:S(2)}, u32[]{:S(2)}) collective-permute-start(bf16[144,2560]{1,0:T(8,128)(2,1)S(1)} %get-tuple-element.42), channel_id=1, source_target_pairs={{0,1},{1,2},{2,3},{3,0},{4,5},{5,6},{6,7},{7,4},{8,9},{9,10},{10,1... | collective-permute-start | bytes 2211848 | tf_op jit(solution)/shard_map/ppermute | solution.py:356
  11.5 3.6 %collective-permute-start.2 = (bf16[144,2560]{1,0:T(8,128)(2,1)S(1)}, bf16[144,2560]{1,0:T(8,128)(2,1)S(1)}, u32[]{:S(2)}, u32[]{:S(2)}) collective-permute-start(bf16[144,2560]{1,0:T(8,128)(2,1)S(1)} %get-tuple-element.42), channel_id=1, source_target_pairs={{0,2},{1,3},{4,6},{5,7},{8,10},{9,11},{12,14},{13,15},{16,18},{17,... | collective-permute-start | bytes 2211848 | tf_op jit(solution)/shard_map/ppermute | solution.py:356
  15.1 0.0 collective-permute-done.7.two
  15.1 0.0 copy-start.7
  15.1 0.1 stack.1.c0
  15.2 0.0 copy-start.1
  15.3 3.1 %collective-permute-start.10 = (bf16[2,256,1280]{2,1,0:T(8,128)(2,1)S(1)}, bf16[2,256,1280]{2,1,0:T(8,128)(2,1)S(1)}, u32[]{:S(2)}, u32[]{:S(2)}) collective-permute-start(bf16[2,256,1280]{2,1,0:T(8,128)(2,1)S(1)} %stack.1.c0), channel_id=1, source_target_pairs={{0,96},{4,28},{8,104},{12,4},{16,112},{20,12},{24,120},{28,20},{32... | collective-permute-start | bytes 3932168 | tf_op jit(solution)/shard_map/ppermute | solution.py:367
  18.3 0.0 collective-permute-start.8
  18.3 2.2 %collective-permute-start.9 = (bf16[2,256,1280]{2,1,0:T(8,128)(2,1)S(1)}, bf16[2,256,1280]{2,1,0:T(8,128)(2,1)S(1)}, u32[]{:S(2)}, u32[]{:S(2)}) collective-permute-start(bf16[2,256,1280]{2,1,0:T(8,128)(2,1)S(1)} %stack.1.c0), channel_id=1, source_target_pairs={{0,64},{4,20},{8,72},{12,28},{16,80},{20,4},{24,88},{28,12},{32,96... | collective-permute-start | bytes 3932168 | tf_op jit(solution)/shard_map/ppermute | solution.py:367
  20.5 3.2 %early.1 = (f32[256,2560]{1,0:T(8,128)S(1)}, f32[256,256]{1,0:T(8,128)S(1)}, bf16[256,128]{1,0:T(8,128)(2,1)S(1)}, bf16[16,128]{1,0:T(8,128)(2,1)S(1)}) custom-call(bf16[256,2816]{1,0:T(8,128)(2,1)S(1)} %get-tuple-element.33.act.after, f32[40,256]{1,0:T(8,128)S(1)} %get-tuple-element.34.cum, s32[1,256]{1,0:T(1,128)S(1)} %copy-done.6, ...), custom_call_target="tpu_custom_call" | custom-call | tf_op jit(solution)/shard_map/early/pallas_call | solution.py:447
  23.8 0.0 copy-start.4
  23.8 8.2 %late.1 = (f32[256,2560]{1,0:T(8,128)S(1)}, f32[256,2560]{1,0:T(8,128)S(1)}) custom-call(bf16[256,2816]{1,0:T(8,128)(2,1)S(1)} %get-tuple-element.33.act.after, f32[40,256]{1,0:T(8,128)S(1)} %get-tuple-element.34.cum, f32[40,256]{1,0:T(8,128)S(1)} %get-tuple-element.35.step, f32[256,256]{1,0:T(8,128)S(1)} %get-tuple-element.36.scores, ...), custom_call_target="tpu_custom_call" | custom-call | tf_op jit(solution)/shard_map/late/pallas_call | solution.py:463
  32.0 0.0 collective-permute-done.1.one
  32.0 11.4 %collective-permute-done.2.two = bf16[144,2560]{1,0:T(8,128)(2,1)S(1)} collective-permute-done((bf16[144,2560]{1,0:T(8,128)(2,1)S(1)}, bf16[144,2560]{1,0:T(8,128)(2,1)S(1)}, u32[]{:S(2)}, u32[]{:S(2)}) %collective-permute-start.2) | collective-permute-done | bytes 737312 | tf_op jit(solution)/shard_map/ppermute | solution.py:356
  43.4 3.2 %back.1 = (bf16[256,2560]{1,0:T(8,128)(2,1)}, bf16[4,4,80,256]{3,2,1,0:T(8,128)(2,1)S(1)}, bf16[4,80,256]{2,1,0:T(8,128)(2,1)S(1)}, bf16[4,80,256]{2,1,0:T(8,128...) custom-call(f32[256,2560]{1,0:T(8,128)S(1)} %get-tuple-element.39.local, ...), custom_call_target="tpu_custom_call" | custom-call | tf_op jit(solution)/shard_map/back/pallas_call | solution.py:467
  46.6 0.1 collective-permute-start.3
  46.7 1.6 %collective-permute-start.4 = (bf16[4,80,256]{2,1,0:T(8,128)(2,1)S(1)}, bf16[4,80,256]{2,1,0:T(8,128)(2,1)S(1)}, u32[]{:S(2)}, u32[]{:S(2)}) collective-permute-start(bf16[4,80,256]{2,1,0:T(8,128)(2,1)S(1)} %get-tuple-element.46), channel_id=1, source_target_pairs={{0,32},{4,12},{8,40},{12,20},{16,48},{20,28},{24,56},{28,4},{32,64... | collective-permute-start | bytes 491528 | tf_op jit(solution)/shard_map/ppermute | solution.py:367
  48.4 0.4 collective-permute-done.3.got
  48.8 3.2 %collective-permute-start.5 = (bf16[4,80,256]{2,1,0:T(8,128)(2,1)S(1)}, bf16[4,80,256]{2,1,0:T(8,128)(2,1)S(1)}, u32[]{:S(2)}, u32[]{:S(2)}) collective-permute-start(bf16[4,80,256]{2,1,0:T(8,128)(2,1)S(1)} %get-tuple-element.47), channel_id=1, source_target_pairs={{0,64},{4,20},{8,72},{12,28},{16,80},{20,4},{24,88},{28,12},{32,96... | collective-permute-start | bytes 491528 | tf_op jit(solution)/shard_map/ppermute | solution.py:367
  52.0 0.0 collective-permute-done.10.rest_2_.c3
  52.0 1.1 %collective-permute-start.6 = (bf16[4,80,256]{2,1,0:T(8,128)(2,1)S(1)}, bf16[4,80,256]{2,1,0:T(8,128)(2,1)S(1)}, u32[]{:S(2)}, u32[]{:S(2)}) collective-permute-start(bf16[4,80,256]{2,1,0:T(8,128)(2,1)S(1)} %get-tuple-element.48), channel_id=1, source_target_pairs={{0,96},{4,28},{8,104},{12,4},{16,112},{20,12},{24,120},{28,20},{32... | collective-permute-start | bytes 491528 | tf_op jit(solution)/shard_map/ppermute | solution.py:367
  53.1 0.0 collective-permute-done.8.rest_0_.c1
  53.1 0.0 collective-permute-done.9.rest_1_.c2
  53.1 1.0 %collective-permute-start.11 = (bf16[4,80,256]{2,1,0:T(8,128)(2,1)S(1)}, bf16[4,80,256]{2,1,0:T(8,128)(2,1)S(1)}, u32[]{:S(2)}, u32[]{:S(2)}) collective-permute-start(bf16[4,80,256]{2,1,0:T(8,128)(2,1)S(1)} %get-tuple-element.49), channel_id=1, source_target_pairs={{0,32},{4,12},{8,40},{12,20},{16,48},{20,28},{24,56},{28,4},{32,64... | collective-permute-start | bytes 491528 | tf_op jit(solution)/shard_map/ppermute | solution.py:367
  54.2 0.8 collective-permute-start.12
  55.0 0.0 collective-permute-done.4.m1
  55.0 2.5 %collective-permute-start.13 = (bf16[4,80,256]{2,1,0:T(8,128)(2,1)S(1)}, bf16[4,80,256]{2,1,0:T(8,128)(2,1)S(1)}, u32[]{:S(2)}, u32[]{:S(2)}) collective-permute-start(bf16[4,80,256]{2,1,0:T(8,128)(2,1)S(1)} %get-tuple-element.51), channel_id=1, source_target_pairs={{0,96},{4,28},{8,104},{12,4},{16,112},{20,12},{24,120},{28,20},{32... | collective-permute-start | bytes 491528 | tf_op jit(solution)/shard_map/ppermute | solution.py:367
  57.5 0.0 collective-permute-done.5.m2
  57.5 0.2 collective-permute-done.6.m3
  57.7 3.7 %collective-permute-done.11.r1 = bf16[4,80,256]{2,1,0:T(8,128)(2,1)S(1)} collective-permute-done((bf16[4,80,256]{2,1,0:T(8,128)(2,1)S(1)}, bf16[4,80,256]{2,1,0:T(8,128)(2,1)S(1)}, u32[]{:S(2)}, u32[]{:S(2)}) %collective-permute-start.11) | collective-permute-done | bytes 163872 | tf_op jit(solution)/shard_map/ppermute | solution.py:367
  61.5 0.0 collective-permute-done.12.r2
  61.5 0.9 %collective-permute-done.13.r3 = bf16[4,80,256]{2,1,0:T(8,128)(2,1)S(1)} collective-permute-done((bf16[4,80,256]{2,1,0:T(8,128)(2,1)S(1)}, bf16[4,80,256]{2,1,0:T(8,128)(2,1)S(1)}, u32[]{:S(2)}, u32[]{:S(2)}) %collective-permute-start.13) | collective-permute-done | bytes 163872 | tf_op jit(solution)/shard_map/ppermute | solution.py:367
  62.3 2.0 %grad.1 = bf16[16,200,128]{2,1,0:T(8,128)(2,1)S(1)} custom-call(bf16[4,80,256]{2,1,0:T(8,128)(2,1)S(1)} %get-tuple-element.44.m0, bf16[4,4,80,256]{3,2,1,0:T(8,128)(2,1)S(1)} %collective-permute-done.3.got, bf16[4,80,256]{2,1,0:T(8,128)(2,1)S(1)} %collective-permute-done.4.m1, bf16[4,80,256]{2,1,0:T(8,128)(2,1)S(1)} %collective-permute-done.5.m2, ...), custom_call_target="tpu_custom_call" | custom-call | flops 2000000000 | bytes 8000000 | tf_op jit(solution)/shard_map/grad/pallas_call | solution.py:487
  64.3 20.0 %all_to_all.5.pieces = bf16[16,200,128]{2,1,0:T(8,128)(2,1)S(1)} all-to-all(bf16[16,200,128]{2,1,0:T(8,128)(2,1)S(1)} %grad.1), channel_id=1, replica_groups={{0,1,2,3,8,9,10,11,16,17,18,19,24,25,26,27},{32,33,34,35,40,41,42,43,48..., dimensions={0} | all-to-all | bytes 1638400 | tf_op jit(solution)/shard_map/all_to_all | solution.py:496
  84.3 0.8 total.1
  (14 shorter events, 0.1 us)
Async XLA Ops:
  0.6 3.8 %copy-start.6 = (s32[1,256]{1,0:T(1,128)S(1)}, s32[1,256]{1,0:T(1,128)}, u32[]{:S(2)}) copy-start(s32[1,256]{1,0:T(1,128)} %docs.9) | copy-start | bytes 3076
  0.6 3.8 %copy-start.8 = (f32[1,40,256]{2,1,0:T(8,128)S(1)}, f32[1,40,256]{2,1,0:T(8,128)}, u32[]{:S(2)}) copy-start(f32[1,40,256]{2,1,0:T(8,128)} %param.13) | copy-start | bytes 122884
  0.7 3.8 %copy-start.9 = (f32[40]{0:T(128)S(1)}, f32[40]{0:T(128)}, u32[]{:S(2)}) copy-start(f32[40]{0:T(128)} %param.14) | copy-start | bytes 484
  0.7 3.8 %copy-start.10 = (f32[40]{0:T(128)S(1)}, f32[40]{0:T(128)}, u32[]{:S(2)}) copy-start(f32[40]{0:T(128)} %param.15) | copy-start | bytes 484
  0.7 14.4 %collective-permute-start.7 = (bf16[256,1280]{1,0:T(8,128)(2,1)}, bf16[256,1280]{1,0:T(8,128)(2,1)S(1)}, u32[]{:S(2)}, u32[]{:S(2)}) collective-permute-start(bf16[256,1280]{1,0:T(8,128)(2,1)} %bitcast.12), channel_id=1, source_target_pairs={{0,4},{4,0},{1,5},{5,1},{2,6},{6,2},{3,7},{7,3},{8,12},{12,8},{9,1... | collective-permute-start | bytes 1966088 | tf_op jit(solution)/shard_map/ppermute | solution.py:380
  2.4 6.8 %collective-permute-start = (bf16[8,2944]{1,0:T(8,128)(2,1)}, bf16[8,2944]{1,0:T(8,128)(2,1)S(1)}, u32[]{:S(2)}, u32[]{:S(2)}) collective-permute-start(bf16[8,2944]{1,0:T(8,128)(2,1)} %edge.1), channel_id=1, source_target_pairs={{0,1},{1,2},{2,3},{3,0},{4,5},{5,6},{6,7},{7,4},{8,9},{9,10},{10,1... | collective-permute-start | bytes 141320 | tf_op jit(solution)/shard_map/ppermute | solution.py:356
  4.5 1.4 %copy-start = (bf16[1,256,2816]{2,1,0:T(8,128)(2,1)S(1)}, bf16[1,256,2816]{2,1,0:T(8,128)(2,1)}, u32[]{:S(2)}) copy-start(bf16[1,256,2816]{2,1,0:T(8,128)(2,1)} %param.11) | copy-start | bytes 4325380
  4.5 1.4 %copy-start.3 = (f32[4,2816]{1,0:T(4,128)S(1)}, f32[4,2816]{1,0:T(4,128)}, u32[]{:S(2)}) copy-start(f32[4,2816]{1,0:T(4,128)} %w.3) | copy-start | bytes 135172
  4.5 1.3 %copy-start.5 = (f32[2816]{0:T(1024)S(1)}, f32[2816]{0:T(1024)}, u32[]{:S(2)}) copy-start(f32[2816]{0:T(1024)} %cb.3) | copy-start | bytes 33796
  9.1 6.0 %copy-start.2 = (bf16[1,256,1280]{2,1,0:T(8,128)(2,1)S(1)}, bf16[1,256,1280]{2,1,0:T(8,128)(2,1)}, u32[]{:S(2)}) copy-start(bf16[1,256,1280]{2,1,0:T(8,128)(2,1)} %param.21) | copy-start | bytes 1966084
  9.7 22.2 %collective-permute-start.1 = (bf16[144,2560]{1,0:T(8,128)(2,1)S(1)}, bf16[144,2560]{1,0:T(8,128)(2,1)S(1)}, u32[]{:S(2)}, u32[]{:S(2)}) collective-permute-start(bf16[144,2560]{1,0:T(8,128)(2,1)S(1)} %get-tuple-element.42), channel_id=1, source_target_pairs={{0,1},{1,2},{2,3},{3,0},{4,5},{5,6},{6,7},{7,4},{8,9},{9,10},{10,1... | collective-permute-start | bytes 2211848 | tf_op jit(solution)/shard_map/ppermute | solution.py:356
  11.5 32.0 %collective-permute-start.2 = (bf16[144,2560]{1,0:T(8,128)(2,1)S(1)}, bf16[144,2560]{1,0:T(8,128)(2,1)S(1)}, u32[]{:S(2)}, u32[]{:S(2)}) collective-permute-start(bf16[144,2560]{1,0:T(8,128)(2,1)S(1)} %get-tuple-element.42), channel_id=1, source_target_pairs={{0,2},{1,3},{4,6},{5,7},{8,10},{9,11},{12,14},{13,15},{16,18},{17,... | collective-permute-start | bytes 2211848 | tf_op jit(solution)/shard_map/ppermute | solution.py:356
  15.1 5.4 %copy-start.7 = (f32[40]{0:T(128)S(1)}, f32[40]{0:T(128)}, u32[]{:S(2)}) copy-start(f32[40]{0:T(128)} %param.16) | copy-start | bytes 484
  15.2 8.6 %copy-start.1 = (bf16[1,256,2560]{2,1,0:T(8,128)(2,1)S(1)}, bf16[1,256,2560]{2,1,0:T(8,128)(2,1)}, u32[]{:S(2)}) copy-start(bf16[1,256,2560]{2,1,0:T(8,128)(2,1)} %param.12) | copy-start | bytes 3932164
  15.3 36.8 %collective-permute-start.10 = (bf16[2,256,1280]{2,1,0:T(8,128)(2,1)S(1)}, bf16[2,256,1280]{2,1,0:T(8,128)(2,1)S(1)}, u32[]{:S(2)}, u32[]{:S(2)}) collective-permute-start(bf16[2,256,1280]{2,1,0:T(8,128)(2,1)S(1)} %stack.1.c0), channel_id=1, source_target_pairs={{0,96},{4,28},{8,104},{12,4},{16,112},{20,12},{24,120},{28,20},{32... | collective-permute-start | bytes 3932168 | tf_op jit(solution)/shard_map/ppermute | solution.py:367
  18.3 34.7 %collective-permute-start.8 = (bf16[2,256,1280]{2,1,0:T(8,128)(2,1)S(1)}, bf16[2,256,1280]{2,1,0:T(8,128)(2,1)S(1)}, u32[]{:S(2)}, u32[]{:S(2)}) collective-permute-start(bf16[2,256,1280]{2,1,0:T(8,128)(2,1)S(1)} %stack.1.c0), channel_id=1, source_target_pairs={{0,32},{4,12},{8,40},{12,20},{16,48},{20,28},{24,56},{28,4},{32,64... | collective-permute-start | bytes 3932168 | tf_op jit(solution)/shard_map/ppermute | solution.py:367
  18.3 34.7 %collective-permute-start.9 = (bf16[2,256,1280]{2,1,0:T(8,128)(2,1)S(1)}, bf16[2,256,1280]{2,1,0:T(8,128)(2,1)S(1)}, u32[]{:S(2)}, u32[]{:S(2)}) collective-permute-start(bf16[2,256,1280]{2,1,0:T(8,128)(2,1)S(1)} %stack.1.c0), channel_id=1, source_target_pairs={{0,64},{4,20},{8,72},{12,28},{16,80},{20,4},{24,88},{28,12},{32,96... | collective-permute-start | bytes 3932168 | tf_op jit(solution)/shard_map/ppermute | solution.py:367
  23.8 19.6 %copy-start.4 = (f32[2560]{0:T(1024)S(1)}, f32[2560]{0:T(1024)}, u32[]{:S(2)}) copy-start(f32[2560]{0:T(1024)} %gain.1) | copy-start | bytes 30724
  46.6 2.2 %collective-permute-start.3 = (bf16[4,4,80,256]{3,2,1,0:T(8,128)(2,1)S(1)}, bf16[4,4,80,256]{3,2,1,0:T(8,128)(2,1)S(1)}, u32[]{:S(2)}, u32[]{:S(2)}) collective-permute-start(bf16[4,4,80,256]{3,2,1,0:T(8,128)(2,1)S(1)} %get-tuple-element.45), channel_id=1, source_target_pairs={{0,4},{4,0},{1,5},{5,1},{2,6},{6,2},{3,7},{7,3},{8,12},{12,8},{9,1... | collective-permute-start | bytes 1966088 | tf_op jit(solution)/shard_map/ppermute | solution.py:380
  46.7 8.2 %collective-permute-start.4 = (bf16[4,80,256]{2,1,0:T(8,128)(2,1)S(1)}, bf16[4,80,256]{2,1,0:T(8,128)(2,1)S(1)}, u32[]{:S(2)}, u32[]{:S(2)}) collective-permute-start(bf16[4,80,256]{2,1,0:T(8,128)(2,1)S(1)} %get-tuple-element.46), channel_id=1, source_target_pairs={{0,32},{4,12},{8,40},{12,20},{16,48},{20,28},{24,56},{28,4},{32,64... | collective-permute-start | bytes 491528 | tf_op jit(solution)/shard_map/ppermute | solution.py:367
  48.8 8.7 %collective-permute-start.5 = (bf16[4,80,256]{2,1,0:T(8,128)(2,1)S(1)}, bf16[4,80,256]{2,1,0:T(8,128)(2,1)S(1)}, u32[]{:S(2)}, u32[]{:S(2)}) collective-permute-start(bf16[4,80,256]{2,1,0:T(8,128)(2,1)S(1)} %get-tuple-element.47), channel_id=1, source_target_pairs={{0,64},{4,20},{8,72},{12,28},{16,80},{20,4},{24,88},{28,12},{32,96... | collective-permute-start | bytes 491528 | tf_op jit(solution)/shard_map/ppermute | solution.py:367
  52.0 5.7 %collective-permute-start.6 = (bf16[4,80,256]{2,1,0:T(8,128)(2,1)S(1)}, bf16[4,80,256]{2,1,0:T(8,128)(2,1)S(1)}, u32[]{:S(2)}, u32[]{:S(2)}) collective-permute-start(bf16[4,80,256]{2,1,0:T(8,128)(2,1)S(1)} %get-tuple-element.48), channel_id=1, source_target_pairs={{0,96},{4,28},{8,104},{12,4},{16,112},{20,12},{24,120},{28,20},{32... | collective-permute-start | bytes 491528 | tf_op jit(solution)/shard_map/ppermute | solution.py:367
  53.1 8.4 %collective-permute-start.11 = (bf16[4,80,256]{2,1,0:T(8,128)(2,1)S(1)}, bf16[4,80,256]{2,1,0:T(8,128)(2,1)S(1)}, u32[]{:S(2)}, u32[]{:S(2)}) collective-permute-start(bf16[4,80,256]{2,1,0:T(8,128)(2,1)S(1)} %get-tuple-element.49), channel_id=1, source_target_pairs={{0,32},{4,12},{8,40},{12,20},{16,48},{20,28},{24,56},{28,4},{32,64... | collective-permute-start | bytes 491528 | tf_op jit(solution)/shard_map/ppermute | solution.py:367
  54.2 7.3 %collective-permute-start.12 = (bf16[4,80,256]{2,1,0:T(8,128)(2,1)S(1)}, bf16[4,80,256]{2,1,0:T(8,128)(2,1)S(1)}, u32[]{:S(2)}, u32[]{:S(2)}) collective-permute-start(bf16[4,80,256]{2,1,0:T(8,128)(2,1)S(1)} %get-tuple-element.50), channel_id=1, source_target_pairs={{0,64},{4,20},{8,72},{12,28},{16,80},{20,4},{24,88},{28,12},{32,96... | collective-permute-start | bytes 491528 | tf_op jit(solution)/shard_map/ppermute | solution.py:367
  55.0 7.4 %collective-permute-start.13 = (bf16[4,80,256]{2,1,0:T(8,128)(2,1)S(1)}, bf16[4,80,256]{2,1,0:T(8,128)(2,1)S(1)}, u32[]{:S(2)}, u32[]{:S(2)}) collective-permute-start(bf16[4,80,256]{2,1,0:T(8,128)(2,1)S(1)} %get-tuple-element.51), channel_id=1, source_target_pairs={{0,96},{4,28},{8,104},{12,4},{16,112},{20,12},{24,120},{28,20},{32... | collective-permute-start | bytes 491528 | tf_op jit(solution)/shard_map/ppermute | solution.py:367

commit v9 on v8

--- a/solution.py
+++ b/solution.py
@@ -260,12 +260,14 @@
         return value[:, 0:LANES] + value[:, LANES:]
 
     def first_group(i, carry):
-        parts = [first(5 * i + k) for k in range(5)]
-        squares[...] += (parts[0] + parts[1]) + (parts[2] + parts[3]) + parts[4]
+        parts = first(10 * i)
+        for k in range(1, 10):
+            parts = parts + first(10 * i + k)
+        squares[...] += parts
         return carry
 
     squares[...] = jnp.zeros_like(squares)
-    lax.fori_loop(0, 2, first_group, 0)
+    lax.fori_loop(0, 1, first_group, 0)
     mean = jnp.sum(squares[...], axis=1, keepdims=True) * (1.0 / INNER)
     squares[...] = jnp.broadcast_to(lax.rsqrt(mean + 1e-05), squares.shape)
     eye = (

time: 85.3 us -> 85.2 us (level)
  no operation moved by 1% of the time
where the time goes in v9:
time: 85.2 us; the launch traced here: 84.9 us
  starting transfers between devices  23.2 us (27%)
  Pallas kernels  23 us (27%)
  blocking collectives  20 us (23%)
  waiting for transfers between devices  17 us (20%)
  between operations  0.86 us (1%)
    all_to_all x1, blocking collectives, per_device(): lax.all_to_all(packed, ('y', 'x', 'c', 'z'), 0, 0, axis_index_groups=PLANES)  20 us
    ppermute x9, starting transfers between devices, around(): return lax.ppermute(value, ('y', 'x', 'c'), pairs)  15.6 us
    ppermute x3, waiting for transfers between devices, shifted(): lax.ppermute(value, 'z', [(i, (i + by) % 4) for i in range(4 if by == 1 e...  11.7 us
    pallas_call x1, Pallas kernels, per_device(): call(late_kernel, 'late', (shape((T, INNER)), shape((T, INNER))), [], 8)  8.15 us
    ppermute x3, starting transfers between devices, shifted(): lax.ppermute(value, 'z', [(i, (i + by) % 4) for i in range(4 if by == 1 e...  7.43 us
    ppermute x9, waiting for transfers between devices, around(): return lax.ppermute(value, ('y', 'x', 'c'), pairs)  4.84 us
    pallas_call x1, Pallas kernels, per_device(): call(early_kernel, 'early', (shape((T, INNER)), shape((T, T)), shape((T,...  3.25 us
    pallas_call x1, Pallas kernels, per_device(): call(front_kernel, 'front', (shape((T, C_ALL), BF16), shape((N, INNER)),...  3.01 us
  transfers between devices with their start and end apart: 14, of which 6 were waited for; matrix products, arithmetic and copies ran while one was open for 0% of the time, Pallas kernels for 24%

profile of v9, /device:TPU:0, one launch (start us, length us, event | category | flops | bytes accessed | tf_op | source)
XLA Modules:
  0.0 84.9 jit_solution(15499998241764379906)
XLA Ops:
  0.6 0.0 copy-start.6
  0.7 0.1 collective-permute-start.7
  0.8 1.6 %edge.1 = bf16[8,2944]{1,0:T(8,128)(2,1)} custom-call(bf16[256,2816]{1,0:T(8,128)(2,1)} %bitcast.8, s32[1,256]{1,0:T(1,128)} %docs.9), custom_call_target="tpu_custom_call" | custom-call | bytes 100000 | tf_op jit(solution)/shard_map/edge/pallas_call | solution.py:393
  2.4 2.1 %collective-permute-start = (bf16[8,2944]{1,0:T(8,128)(2,1)}, bf16[8,2944]{1,0:T(8,128)(2,1)S(1)}, u32[]{:S(2)}, u32[]{:S(2)}) collective-permute-start(bf16[8,2944]{1,0:T(8,128)(2,1)} %edge.1), channel_id=1, source_target_pairs={{0,1},{1,2},{2,3},{3,0},{4,5},{5,6},{6,7},{7,4},{8,9},{9,10},{10,1... | collective-permute-start | bytes 141320 | tf_op jit(solution)/shard_map/ppermute | solution.py:358
  4.5 0.0 copy-start
  4.5 0.0 copy-start.3
  4.5 0.0 copy-start.5
  4.5 0.5 prep.1
  5.1 0.8 copy-done
  5.8 0.0 copy-done.3
  5.8 3.0 %front.1 = (bf16[256,2816]{1,0:T(8,128)(2,1)S(1)}, f32[128,2560]{1,0:T(8,128)S(1)}, bf16[16,2560]{1,0:T(8,128)(2,1)S(1)}, f32[16,2560]{1,0:T(8,128)S(1)}) custom-call(bf16[256,2816]{1,0:T(8,128)(2,1)S(1)} %bitcast.9, f32[4,2816]{1,0:T(4,128)S(1)} %copy-done.3, f32[2816]{0:T(1024)S(1)} %copy-done.5, s32[1,256]{1,0:T(1,128)S(1)} %copy-done.6, ...), custom_call_target="tpu_custom_call" | custom-call | flops 1000000000 | bytes 4000000 | tf_op jit(solution)/shard_map/front/pallas_call | solution.py:415
  8.8 0.3 collective-permute-done.halo
  9.1 0.6 fix.1
  9.7 1.7 %collective-permute-start.1 = (bf16[144,2560]{1,0:T(8,128)(2,1)S(1)}, bf16[144,2560]{1,0:T(8,128)(2,1)S(1)}, u32[]{:S(2)}, u32[]{:S(2)}) collective-permute-start(bf16[144,2560]{1,0:T(8,128)(2,1)S(1)} %get-tuple-element.42), channel_id=1, source_target_pairs={{0,1},{1,2},{2,3},{3,0},{4,5},{5,6},{6,7},{7,4},{8,9},{9,10},{10,1... | collective-permute-start | bytes 2211848 | tf_op jit(solution)/shard_map/ppermute | solution.py:358
  11.5 3.6 %collective-permute-start.2 = (bf16[144,2560]{1,0:T(8,128)(2,1)S(1)}, bf16[144,2560]{1,0:T(8,128)(2,1)S(1)}, u32[]{:S(2)}, u32[]{:S(2)}) collective-permute-start(bf16[144,2560]{1,0:T(8,128)(2,1)S(1)} %get-tuple-element.42), channel_id=1, source_target_pairs={{0,2},{1,3},{4,6},{5,7},{8,10},{9,11},{12,14},{13,15},{16,18},{17,... | collective-permute-start | bytes 2211848 | tf_op jit(solution)/shard_map/ppermute | solution.py:358
  15.1 0.0 collective-permute-done.7.two
  15.1 0.0 copy-start.7
  15.1 0.1 stack.1.c0
  15.2 0.0 copy-start.1
  15.3 3.1 %collective-permute-start.10 = (bf16[2,256,1280]{2,1,0:T(8,128)(2,1)S(1)}, bf16[2,256,1280]{2,1,0:T(8,128)(2,1)S(1)}, u32[]{:S(2)}, u32[]{:S(2)}) collective-permute-start(bf16[2,256,1280]{2,1,0:T(8,128)(2,1)S(1)} %stack.1.c0), channel_id=1, source_target_pairs={{0,96},{4,28},{8,104},{12,4},{16,112},{20,12},{24,120},{28,20},{32... | collective-permute-start | bytes 3932168 | tf_op jit(solution)/shard_map/ppermute | solution.py:369
  18.3 0.0 collective-permute-start.8
  18.3 2.2 %collective-permute-start.9 = (bf16[2,256,1280]{2,1,0:T(8,128)(2,1)S(1)}, bf16[2,256,1280]{2,1,0:T(8,128)(2,1)S(1)}, u32[]{:S(2)}, u32[]{:S(2)}) collective-permute-start(bf16[2,256,1280]{2,1,0:T(8,128)(2,1)S(1)} %stack.1.c0), channel_id=1, source_target_pairs={{0,64},{4,20},{8,72},{12,28},{16,80},{20,4},{24,88},{28,12},{32,96... | collective-permute-start | bytes 3932168 | tf_op jit(solution)/shard_map/ppermute | solution.py:369
  20.5 3.2 %early.1 = (f32[256,2560]{1,0:T(8,128)S(1)}, f32[256,256]{1,0:T(8,128)S(1)}, bf16[256,128]{1,0:T(8,128)(2,1)S(1)}, bf16[16,128]{1,0:T(8,128)(2,1)S(1)}) custom-call(bf16[256,2816]{1,0:T(8,128)(2,1)S(1)} %get-tuple-element.33.act.after, f32[40,256]{1,0:T(8,128)S(1)} %get-tuple-element.34.cum, s32[1,256]{1,0:T(1,128)S(1)} %copy-done.6, ...), custom_call_target="tpu_custom_call" | custom-call | tf_op jit(solution)/shard_map/early/pallas_call | solution.py:449
  23.8 0.0 copy-start.4
  23.8 8.2 %late.1 = (f32[256,2560]{1,0:T(8,128)S(1)}, f32[256,2560]{1,0:T(8,128)S(1)}) custom-call(bf16[256,2816]{1,0:T(8,128)(2,1)S(1)} %get-tuple-element.33.act.after, f32[40,256]{1,0:T(8,128)S(1)} %get-tuple-element.34.cum, f32[40,256]{1,0:T(8,128)S(1)} %get-tuple-element.35.step, f32[256,256]{1,0:T(8,128)S(1)} %get-tuple-element.36.scores, ...), custom_call_target="tpu_custom_call" | custom-call | tf_op jit(solution)/shard_map/late/pallas_call | solution.py:465
  32.0 0.0 collective-permute-done.1.one
  32.0 11.4 %collective-permute-done.2.two = bf16[144,2560]{1,0:T(8,128)(2,1)S(1)} collective-permute-done((bf16[144,2560]{1,0:T(8,128)(2,1)S(1)}, bf16[144,2560]{1,0:T(8,128)(2,1)S(1)}, u32[]{:S(2)}, u32[]{:S(2)}) %collective-permute-start.2) | collective-permute-done | bytes 737312 | tf_op jit(solution)/shard_map/ppermute | solution.py:358
  43.4 3.0 %back.1 = (bf16[256,2560]{1,0:T(8,128)(2,1)}, bf16[4,4,80,256]{3,2,1,0:T(8,128)(2,1)S(1)}, bf16[4,80,256]{2,1,0:T(8,128)(2,1)S(1)}, bf16[4,80,256]{2,1,0:T(8,128...) custom-call(f32[256,2560]{1,0:T(8,128)S(1)} %get-tuple-element.39.local, ...), custom_call_target="tpu_custom_call" | custom-call | tf_op jit(solution)/shard_map/back/pallas_call | solution.py:469
  46.4 0.1 collective-permute-start.3
  46.5 1.6 %collective-permute-start.4 = (bf16[4,80,256]{2,1,0:T(8,128)(2,1)S(1)}, bf16[4,80,256]{2,1,0:T(8,128)(2,1)S(1)}, u32[]{:S(2)}, u32[]{:S(2)}) collective-permute-start(bf16[4,80,256]{2,1,0:T(8,128)(2,1)S(1)} %get-tuple-element.46), channel_id=1, source_target_pairs={{0,32},{4,12},{8,40},{12,20},{16,48},{20,28},{24,56},{28,4},{32,64... | collective-permute-start | bytes 491528 | tf_op jit(solution)/shard_map/ppermute | solution.py:369
  48.2 0.4 collective-permute-done.3.got
  48.6 3.2 %collective-permute-start.5 = (bf16[4,80,256]{2,1,0:T(8,128)(2,1)S(1)}, bf16[4,80,256]{2,1,0:T(8,128)(2,1)S(1)}, u32[]{:S(2)}, u32[]{:S(2)}) collective-permute-start(bf16[4,80,256]{2,1,0:T(8,128)(2,1)S(1)} %get-tuple-element.47), channel_id=1, source_target_pairs={{0,64},{4,20},{8,72},{12,28},{16,80},{20,4},{24,88},{28,12},{32,96... | collective-permute-start | bytes 491528 | tf_op jit(solution)/shard_map/ppermute | solution.py:369
  51.8 0.0 collective-permute-done.10.rest_2_.c3
  51.8 1.1 %collective-permute-start.6 = (bf16[4,80,256]{2,1,0:T(8,128)(2,1)S(1)}, bf16[4,80,256]{2,1,0:T(8,128)(2,1)S(1)}, u32[]{:S(2)}, u32[]{:S(2)}) collective-permute-start(bf16[4,80,256]{2,1,0:T(8,128)(2,1)S(1)} %get-tuple-element.48), channel_id=1, source_target_pairs={{0,96},{4,28},{8,104},{12,4},{16,112},{20,12},{24,120},{28,20},{32... | collective-permute-start | bytes 491528 | tf_op jit(solution)/shard_map/ppermute | solution.py:369
  52.9 0.0 collective-permute-done.8.rest_0_.c1
  52.9 0.0 collective-permute-done.9.rest_1_.c2
  52.9 1.0 %collective-permute-start.11 = (bf16[4,80,256]{2,1,0:T(8,128)(2,1)S(1)}, bf16[4,80,256]{2,1,0:T(8,128)(2,1)S(1)}, u32[]{:S(2)}, u32[]{:S(2)}) collective-permute-start(bf16[4,80,256]{2,1,0:T(8,128)(2,1)S(1)} %get-tuple-element.49), channel_id=1, source_target_pairs={{0,32},{4,12},{8,40},{12,20},{16,48},{20,28},{24,56},{28,4},{32,64... | collective-permute-start | bytes 491528 | tf_op jit(solution)/shard_map/ppermute | solution.py:369
  54.0 0.8 collective-permute-start.12
  54.8 0.0 collective-permute-done.4.m1
  54.8 2.5 %collective-permute-start.13 = (bf16[4,80,256]{2,1,0:T(8,128)(2,1)S(1)}, bf16[4,80,256]{2,1,0:T(8,128)(2,1)S(1)}, u32[]{:S(2)}, u32[]{:S(2)}) collective-permute-start(bf16[4,80,256]{2,1,0:T(8,128)(2,1)S(1)} %get-tuple-element.51), channel_id=1, source_target_pairs={{0,96},{4,28},{8,104},{12,4},{16,112},{20,12},{24,120},{28,20},{32... | collective-permute-start | bytes 491528 | tf_op jit(solution)/shard_map/ppermute | solution.py:369
  57.3 0.0 collective-permute-done.5.m2
  57.3 0.2 collective-permute-done.6.m3
  57.5 3.7 %collective-permute-done.11.r1 = bf16[4,80,256]{2,1,0:T(8,128)(2,1)S(1)} collective-permute-done((bf16[4,80,256]{2,1,0:T(8,128)(2,1)S(1)}, bf16[4,80,256]{2,1,0:T(8,128)(2,1)S(1)}, u32[]{:S(2)}, u32[]{:S(2)}) %collective-permute-start.11) | collective-permute-done | bytes 163872 | tf_op jit(solution)/shard_map/ppermute | solution.py:369
  61.3 0.0 collective-permute-done.12.r2
  61.3 0.9 %collective-permute-done.13.r3 = bf16[4,80,256]{2,1,0:T(8,128)(2,1)S(1)} collective-permute-done((bf16[4,80,256]{2,1,0:T(8,128)(2,1)S(1)}, bf16[4,80,256]{2,1,0:T(8,128)(2,1)S(1)}, u32[]{:S(2)}, u32[]{:S(2)}) %collective-permute-start.13) | collective-permute-done | bytes 163872 | tf_op jit(solution)/shard_map/ppermute | solution.py:369
  62.1 2.0 %grad.1 = bf16[16,200,128]{2,1,0:T(8,128)(2,1)S(1)} custom-call(bf16[4,80,256]{2,1,0:T(8,128)(2,1)S(1)} %get-tuple-element.44.m0, bf16[4,4,80,256]{3,2,1,0:T(8,128)(2,1)S(1)} %collective-permute-done.3.got, bf16[4,80,256]{2,1,0:T(8,128)(2,1)S(1)} %collective-permute-done.4.m1, bf16[4,80,256]{2,1,0:T(8,128)(2,1)S(1)} %collective-permute-done.5.m2, ...), custom_call_target="tpu_custom_call" | custom-call | flops 2000000000 | bytes 8000000 | tf_op jit(solution)/shard_map/grad/pallas_call | solution.py:489
  64.1 20.0 %all_to_all.5.pieces = bf16[16,200,128]{2,1,0:T(8,128)(2,1)S(1)} all-to-all(bf16[16,200,128]{2,1,0:T(8,128)(2,1)S(1)} %grad.1), channel_id=1, replica_groups={{0,1,2,3,8,9,10,11,16,17,18,19,24,25,26,27},{32,33,34,35,40,41,42,43,48..., dimensions={0} | all-to-all | bytes 1638400 | tf_op jit(solution)/shard_map/all_to_all | solution.py:498
  84.2 0.8 total.1
  (14 shorter events, 0.1 us)
Async XLA Ops:
  0.6 3.8 %copy-start.6 = (s32[1,256]{1,0:T(1,128)S(1)}, s32[1,256]{1,0:T(1,128)}, u32[]{:S(2)}) copy-start(s32[1,256]{1,0:T(1,128)} %docs.9) | copy-start | bytes 3076
  0.6 3.8 %copy-start.8 = (f32[1,40,256]{2,1,0:T(8,128)S(1)}, f32[1,40,256]{2,1,0:T(8,128)}, u32[]{:S(2)}) copy-start(f32[1,40,256]{2,1,0:T(8,128)} %param.13) | copy-start | bytes 122884
  0.7 3.8 %copy-start.9 = (f32[40]{0:T(128)S(1)}, f32[40]{0:T(128)}, u32[]{:S(2)}) copy-start(f32[40]{0:T(128)} %param.14) | copy-start | bytes 484
  0.7 3.8 %copy-start.10 = (f32[40]{0:T(128)S(1)}, f32[40]{0:T(128)}, u32[]{:S(2)}) copy-start(f32[40]{0:T(128)} %param.15) | copy-start | bytes 484
  0.7 14.4 %collective-permute-start.7 = (bf16[256,1280]{1,0:T(8,128)(2,1)}, bf16[256,1280]{1,0:T(8,128)(2,1)S(1)}, u32[]{:S(2)}, u32[]{:S(2)}) collective-permute-start(bf16[256,1280]{1,0:T(8,128)(2,1)} %bitcast.12), channel_id=1, source_target_pairs={{0,4},{4,0},{1,5},{5,1},{2,6},{6,2},{3,7},{7,3},{8,12},{12,8},{9,1... | collective-permute-start | bytes 1966088 | tf_op jit(solution)/shard_map/ppermute | solution.py:382
  2.4 6.8 %collective-permute-start = (bf16[8,2944]{1,0:T(8,128)(2,1)}, bf16[8,2944]{1,0:T(8,128)(2,1)S(1)}, u32[]{:S(2)}, u32[]{:S(2)}) collective-permute-start(bf16[8,2944]{1,0:T(8,128)(2,1)} %edge.1), channel_id=1, source_target_pairs={{0,1},{1,2},{2,3},{3,0},{4,5},{5,6},{6,7},{7,4},{8,9},{9,10},{10,1... | collective-permute-start | bytes 141320 | tf_op jit(solution)/shard_map/ppermute | solution.py:358
  4.5 1.4 %copy-start = (bf16[1,256,2816]{2,1,0:T(8,128)(2,1)S(1)}, bf16[1,256,2816]{2,1,0:T(8,128)(2,1)}, u32[]{:S(2)}) copy-start(bf16[1,256,2816]{2,1,0:T(8,128)(2,1)} %param.11) | copy-start | bytes 4325380
  4.5 1.4 %copy-start.3 = (f32[4,2816]{1,0:T(4,128)S(1)}, f32[4,2816]{1,0:T(4,128)}, u32[]{:S(2)}) copy-start(f32[4,2816]{1,0:T(4,128)} %w.3) | copy-start | bytes 135172
  4.5 1.3 %copy-start.5 = (f32[2816]{0:T(1024)S(1)}, f32[2816]{0:T(1024)}, u32[]{:S(2)}) copy-start(f32[2816]{0:T(1024)} %cb.3) | copy-start | bytes 33796
  9.1 6.0 %copy-start.2 = (bf16[1,256,1280]{2,1,0:T(8,128)(2,1)S(1)}, bf16[1,256,1280]{2,1,0:T(8,128)(2,1)}, u32[]{:S(2)}) copy-start(bf16[1,256,1280]{2,1,0:T(8,128)(2,1)} %param.21) | copy-start | bytes 1966084
  9.7 22.2 %collective-permute-start.1 = (bf16[144,2560]{1,0:T(8,128)(2,1)S(1)}, bf16[144,2560]{1,0:T(8,128)(2,1)S(1)}, u32[]{:S(2)}, u32[]{:S(2)}) collective-permute-start(bf16[144,2560]{1,0:T(8,128)(2,1)S(1)} %get-tuple-element.42), channel_id=1, source_target_pairs={{0,1},{1,2},{2,3},{3,0},{4,5},{5,6},{6,7},{7,4},{8,9},{9,10},{10,1... | collective-permute-start | bytes 2211848 | tf_op jit(solution)/shard_map/ppermute | solution.py:358
  11.5 32.0 %collective-permute-start.2 = (bf16[144,2560]{1,0:T(8,128)(2,1)S(1)}, bf16[144,2560]{1,0:T(8,128)(2,1)S(1)}, u32[]{:S(2)}, u32[]{:S(2)}) collective-permute-start(bf16[144,2560]{1,0:T(8,128)(2,1)S(1)} %get-tuple-element.42), channel_id=1, source_target_pairs={{0,2},{1,3},{4,6},{5,7},{8,10},{9,11},{12,14},{13,15},{16,18},{17,... | collective-permute-start | bytes 2211848 | tf_op jit(solution)/shard_map/ppermute | solution.py:358
  15.1 5.4 %copy-start.7 = (f32[40]{0:T(128)S(1)}, f32[40]{0:T(128)}, u32[]{:S(2)}) copy-start(f32[40]{0:T(128)} %param.16) | copy-start | bytes 484
  15.2 8.6 %copy-start.1 = (bf16[1,256,2560]{2,1,0:T(8,128)(2,1)S(1)}, bf16[1,256,2560]{2,1,0:T(8,128)(2,1)}, u32[]{:S(2)}) copy-start(bf16[1,256,2560]{2,1,0:T(8,128)(2,1)} %param.12) | copy-start | bytes 3932164
  15.3 36.6 %collective-permute-start.10 = (bf16[2,256,1280]{2,1,0:T(8,128)(2,1)S(1)}, bf16[2,256,1280]{2,1,0:T(8,128)(2,1)S(1)}, u32[]{:S(2)}, u32[]{:S(2)}) collective-permute-start(bf16[2,256,1280]{2,1,0:T(8,128)(2,1)S(1)} %stack.1.c0), channel_id=1, source_target_pairs={{0,96},{4,28},{8,104},{12,4},{16,112},{20,12},{24,120},{28,20},{32... | collective-permute-start | bytes 3932168 | tf_op jit(solution)/shard_map/ppermute | solution.py:369
  18.3 34.5 %collective-permute-start.8 = (bf16[2,256,1280]{2,1,0:T(8,128)(2,1)S(1)}, bf16[2,256,1280]{2,1,0:T(8,128)(2,1)S(1)}, u32[]{:S(2)}, u32[]{:S(2)}) collective-permute-start(bf16[2,256,1280]{2,1,0:T(8,128)(2,1)S(1)} %stack.1.c0), channel_id=1, source_target_pairs={{0,32},{4,12},{8,40},{12,20},{16,48},{20,28},{24,56},{28,4},{32,64... | collective-permute-start | bytes 3932168 | tf_op jit(solution)/shard_map/ppermute | solution.py:369
  18.3 34.5 %collective-permute-start.9 = (bf16[2,256,1280]{2,1,0:T(8,128)(2,1)S(1)}, bf16[2,256,1280]{2,1,0:T(8,128)(2,1)S(1)}, u32[]{:S(2)}, u32[]{:S(2)}) collective-permute-start(bf16[2,256,1280]{2,1,0:T(8,128)(2,1)S(1)} %stack.1.c0), channel_id=1, source_target_pairs={{0,64},{4,20},{8,72},{12,28},{16,80},{20,4},{24,88},{28,12},{32,96... | collective-permute-start | bytes 3932168 | tf_op jit(solution)/shard_map/ppermute | solution.py:369
  23.8 19.6 %copy-start.4 = (f32[2560]{0:T(1024)S(1)}, f32[2560]{0:T(1024)}, u32[]{:S(2)}) copy-start(f32[2560]{0:T(1024)} %gain.1) | copy-start | bytes 30724
  46.4 2.2 %collective-permute-start.3 = (bf16[4,4,80,256]{3,2,1,0:T(8,128)(2,1)S(1)}, bf16[4,4,80,256]{3,2,1,0:T(8,128)(2,1)S(1)}, u32[]{:S(2)}, u32[]{:S(2)}) collective-permute-start(bf16[4,4,80,256]{3,2,1,0:T(8,128)(2,1)S(1)} %get-tuple-element.45), channel_id=1, source_target_pairs={{0,4},{4,0},{1,5},{5,1},{2,6},{6,2},{3,7},{7,3},{8,12},{12,8},{9,1... | collective-permute-start | bytes 1966088 | tf_op jit(solution)/shard_map/ppermute | solution.py:382
  46.5 8.2 %collective-permute-start.4 = (bf16[4,80,256]{2,1,0:T(8,128)(2,1)S(1)}, bf16[4,80,256]{2,1,0:T(8,128)(2,1)S(1)}, u32[]{:S(2)}, u32[]{:S(2)}) collective-permute-start(bf16[4,80,256]{2,1,0:T(8,128)(2,1)S(1)} %get-tuple-element.46), channel_id=1, source_target_pairs={{0,32},{4,12},{8,40},{12,20},{16,48},{20,28},{24,56},{28,4},{32,64... | collective-permute-start | bytes 491528 | tf_op jit(solution)/shard_map/ppermute | solution.py:369
  48.6 8.7 %collective-permute-start.5 = (bf16[4,80,256]{2,1,0:T(8,128)(2,1)S(1)}, bf16[4,80,256]{2,1,0:T(8,128)(2,1)S(1)}, u32[]{:S(2)}, u32[]{:S(2)}) collective-permute-start(bf16[4,80,256]{2,1,0:T(8,128)(2,1)S(1)} %get-tuple-element.47), channel_id=1, source_target_pairs={{0,64},{4,20},{8,72},{12,28},{16,80},{20,4},{24,88},{28,12},{32,96... | collective-permute-start | bytes 491528 | tf_op jit(solution)/shard_map/ppermute | solution.py:369
  51.8 5.7 %collective-permute-start.6 = (bf16[4,80,256]{2,1,0:T(8,128)(2,1)S(1)}, bf16[4,80,256]{2,1,0:T(8,128)(2,1)S(1)}, u32[]{:S(2)}, u32[]{:S(2)}) collective-permute-start(bf16[4,80,256]{2,1,0:T(8,128)(2,1)S(1)} %get-tuple-element.48), channel_id=1, source_target_pairs={{0,96},{4,28},{8,104},{12,4},{16,112},{20,12},{24,120},{28,20},{32... | collective-permute-start | bytes 491528 | tf_op jit(solution)/shard_map/ppermute | solution.py:369
  52.9 8.4 %collective-permute-start.11 = (bf16[4,80,256]{2,1,0:T(8,128)(2,1)S(1)}, bf16[4,80,256]{2,1,0:T(8,128)(2,1)S(1)}, u32[]{:S(2)}, u32[]{:S(2)}) collective-permute-start(bf16[4,80,256]{2,1,0:T(8,128)(2,1)S(1)} %get-tuple-element.49), channel_id=1, source_target_pairs={{0,32},{4,12},{8,40},{12,20},{16,48},{20,28},{24,56},{28,4},{32,64... | collective-permute-start | bytes 491528 | tf_op jit(solution)/shard_map/ppermute | solution.py:369
  54.0 7.3 %collective-permute-start.12 = (bf16[4,80,256]{2,1,0:T(8,128)(2,1)S(1)}, bf16[4,80,256]{2,1,0:T(8,128)(2,1)S(1)}, u32[]{:S(2)}, u32[]{:S(2)}) collective-permute-start(bf16[4,80,256]{2,1,0:T(8,128)(2,1)S(1)} %get-tuple-element.50), channel_id=1, source_target_pairs={{0,64},{4,20},{8,72},{12,28},{16,80},{20,4},{24,88},{28,12},{32,96... | collective-permute-start | bytes 491528 | tf_op jit(solution)/shard_map/ppermute | solution.py:369
  54.8 7.4 %collective-permute-start.13 = (bf16[4,80,256]{2,1,0:T(8,128)(2,1)S(1)}, bf16[4,80,256]{2,1,0:T(8,128)(2,1)S(1)}, u32[]{:S(2)}, u32[]{:S(2)}) collective-permute-start(bf16[4,80,256]{2,1,0:T(8,128)(2,1)S(1)} %get-tuple-element.51), channel_id=1, source_target_pairs={{0,96},{4,28},{8,104},{12,4},{16,112},{20,12},{24,120},{28,20},{32... | collective-permute-start | bytes 491528 | tf_op jit(solution)/shard_map/ppermute | solution.py:369

commit v10 on v9

--- a/solution.py
+++ b/solution.py
@@ -275,14 +275,14 @@
     ).astype(BF16)
 
     def second(i, carry):
-        for k in range(10):
-            at = pl.ds(pl.multiple_of((10 * i + k) * LANES, LANES), LANES)
+        for k in range(20):
+            at = pl.ds(pl.multiple_of((20 * i + k) * LANES, LANES), LANES)
             value = (gated[:, at] * squares[...] * gain[at].reshape(1, LANES)).astype(BF16)
             flat[:, at] = value
             turned[at, :] = dot(eye, value, ((1,), (1,))).astype(BF16)
         return carry
 
-    lax.fori_loop(0, 2, second, 0)
+    lax.fori_loop(0, 1, second, 0)
     out = pltpu.make_async_copy(flat, normed, sem)
     out.start()
     y, x, c = [lax.axis_index(a) for a in ("y", "x", "c")]

time: 85.2 us -> 85 us (level)
  no operation moved by 1% of the time
where the time goes in v10:
time: 85 us; the launch traced here: 84.7 us
  starting transfers between devices  23.2 us (27%)
  Pallas kernels  22.8 us (27%)
  blocking collectives  20 us (24%)
  waiting for transfers between devices  17 us (20%)
  between operations  0.86 us (1%)
    all_to_all x1, blocking collectives, per_device(): lax.all_to_all(packed, ('y', 'x', 'c', 'z'), 0, 0, axis_index_groups=PLANES)  20 us
    ppermute x9, starting transfers between devices, around(): return lax.ppermute(value, ('y', 'x', 'c'), pairs)  15.6 us
    ppermute x3, waiting for transfers between devices, shifted(): lax.ppermute(value, 'z', [(i, (i + by) % 4) for i in range(4 if by == 1 e...  11.7 us
    pallas_call x1, Pallas kernels, per_device(): call(late_kernel, 'late', (shape((T, INNER)), shape((T, INNER))), [], 8)  8.15 us
    ppermute x3, starting transfers between devices, shifted(): lax.ppermute(value, 'z', [(i, (i + by) % 4) for i in range(4 if by == 1 e...  7.43 us
    ppermute x9, waiting for transfers between devices, around(): return lax.ppermute(value, ('y', 'x', 'c'), pairs)  4.84 us
    pallas_call x1, Pallas kernels, per_device(): call(early_kernel, 'early', (shape((T, INNER)), shape((T, T)), shape((T,...  3.25 us
    pallas_call x1, Pallas kernels, per_device(): call(front_kernel, 'front', (shape((T, C_ALL), BF16), shape((N, INNER)),...  3.01 us
  transfers between devices with their start and end apart: 14, of which 6 were waited for; matrix products, arithmetic and copies ran while one was open for 0% of the time, Pallas kernels for 24%

profile of v10, /device:TPU:0, one launch (start us, length us, event | category | flops | bytes accessed | tf_op | source)
XLA Modules:
  0.0 84.7 jit_solution(686847046632872191)
XLA Ops:
  0.6 0.0 copy-start.6
  0.6 0.0 copy-start.8
  0.7 0.1 collective-permute-start.7
  0.8 1.6 %edge.1 = bf16[8,2944]{1,0:T(8,128)(2,1)} custom-call(bf16[256,2816]{1,0:T(8,128)(2,1)} %bitcast.8, s32[1,256]{1,0:T(1,128)} %docs.9), custom_call_target="tpu_custom_call" | custom-call | bytes 100000 | tf_op jit(solution)/shard_map/edge/pallas_call | solution.py:393
  2.4 2.1 %collective-permute-start = (bf16[8,2944]{1,0:T(8,128)(2,1)}, bf16[8,2944]{1,0:T(8,128)(2,1)S(1)}, u32[]{:S(2)}, u32[]{:S(2)}) collective-permute-start(bf16[8,2944]{1,0:T(8,128)(2,1)} %edge.1), channel_id=1, source_target_pairs={{0,1},{1,2},{2,3},{3,0},{4,5},{5,6},{6,7},{7,4},{8,9},{9,10},{10,1... | collective-permute-start | bytes 141320 | tf_op jit(solution)/shard_map/ppermute | solution.py:358
  4.5 0.0 copy-start
  4.5 0.0 copy-start.3
  4.5 0.0 copy-start.5
  4.5 0.5 prep.1
  5.1 0.8 copy-done
  5.8 3.0 %front.1 = (bf16[256,2816]{1,0:T(8,128)(2,1)S(1)}, f32[128,2560]{1,0:T(8,128)S(1)}, bf16[16,2560]{1,0:T(8,128)(2,1)S(1)}, f32[16,2560]{1,0:T(8,128)S(1)}) custom-call(bf16[256,2816]{1,0:T(8,128)(2,1)S(1)} %bitcast.9, f32[4,2816]{1,0:T(4,128)S(1)} %copy-done.3, f32[2816]{0:T(1024)S(1)} %copy-done.5, s32[1,256]{1,0:T(1,128)S(1)} %copy-done.6, ...), custom_call_target="tpu_custom_call" | custom-call | flops 1000000000 | bytes 4000000 | tf_op jit(solution)/shard_map/front/pallas_call | solution.py:415
  8.8 0.3 collective-permute-done.halo
  9.1 0.6 fix.1
  9.7 1.7 %collective-permute-start.1 = (bf16[144,2560]{1,0:T(8,128)(2,1)S(1)}, bf16[144,2560]{1,0:T(8,128)(2,1)S(1)}, u32[]{:S(2)}, u32[]{:S(2)}) collective-permute-start(bf16[144,2560]{1,0:T(8,128)(2,1)S(1)} %get-tuple-element.42), channel_id=1, source_target_pairs={{0,1},{1,2},{2,3},{3,0},{4,5},{5,6},{6,7},{7,4},{8,9},{9,10},{10,1... | collective-permute-start | bytes 2211848 | tf_op jit(solution)/shard_map/ppermute | solution.py:358
  11.5 3.6 %collective-permute-start.2 = (bf16[144,2560]{1,0:T(8,128)(2,1)S(1)}, bf16[144,2560]{1,0:T(8,128)(2,1)S(1)}, u32[]{:S(2)}, u32[]{:S(2)}) collective-permute-start(bf16[144,2560]{1,0:T(8,128)(2,1)S(1)} %get-tuple-element.42), channel_id=1, source_target_pairs={{0,2},{1,3},{4,6},{5,7},{8,10},{9,11},{12,14},{13,15},{16,18},{17,... | collective-permute-start | bytes 2211848 | tf_op jit(solution)/shard_map/ppermute | solution.py:358
  15.1 0.0 collective-permute-done.7.two
  15.1 0.0 copy-start.7
  15.1 0.1 stack.1.c0
  15.2 0.0 copy-start.1
  15.3 3.1 %collective-permute-start.10 = (bf16[2,256,1280]{2,1,0:T(8,128)(2,1)S(1)}, bf16[2,256,1280]{2,1,0:T(8,128)(2,1)S(1)}, u32[]{:S(2)}, u32[]{:S(2)}) collective-permute-start(bf16[2,256,1280]{2,1,0:T(8,128)(2,1)S(1)} %stack.1.c0), channel_id=1, source_target_pairs={{0,96},{4,28},{8,104},{12,4},{16,112},{20,12},{24,120},{28,20},{32... | collective-permute-start | bytes 3932168 | tf_op jit(solution)/shard_map/ppermute | solution.py:369
  18.3 0.0 collective-permute-start.8
  18.3 2.2 %collective-permute-start.9 = (bf16[2,256,1280]{2,1,0:T(8,128)(2,1)S(1)}, bf16[2,256,1280]{2,1,0:T(8,128)(2,1)S(1)}, u32[]{:S(2)}, u32[]{:S(2)}) collective-permute-start(bf16[2,256,1280]{2,1,0:T(8,128)(2,1)S(1)} %stack.1.c0), channel_id=1, source_target_pairs={{0,64},{4,20},{8,72},{12,28},{16,80},{20,4},{24,88},{28,12},{32,96... | collective-permute-start | bytes 3932168 | tf_op jit(solution)/shard_map/ppermute | solution.py:369
  20.5 3.2 %early.1 = (f32[256,2560]{1,0:T(8,128)S(1)}, f32[256,256]{1,0:T(8,128)S(1)}, bf16[256,128]{1,0:T(8,128)(2,1)S(1)}, bf16[16,128]{1,0:T(8,128)(2,1)S(1)}) custom-call(bf16[256,2816]{1,0:T(8,128)(2,1)S(1)} %get-tuple-element.33.act.after, f32[40,256]{1,0:T(8,128)S(1)} %get-tuple-element.34.cum, s32[1,256]{1,0:T(1,128)S(1)} %copy-done.6, ...), custom_call_target="tpu_custom_call" | custom-call | tf_op jit(solution)/shard_map/early/pallas_call | solution.py:449
  23.8 0.0 copy-start.4
  23.8 8.2 %late.1 = (f32[256,2560]{1,0:T(8,128)S(1)}, f32[256,2560]{1,0:T(8,128)S(1)}) custom-call(bf16[256,2816]{1,0:T(8,128)(2,1)S(1)} %get-tuple-element.33.act.after, f32[40,256]{1,0:T(8,128)S(1)} %get-tuple-element.34.cum, f32[40,256]{1,0:T(8,128)S(1)} %get-tuple-element.35.step, f32[256,256]{1,0:T(8,128)S(1)} %get-tuple-element.36.scores, ...), custom_call_target="tpu_custom_call" | custom-call | tf_op jit(solution)/shard_map/late/pallas_call | solution.py:465
  32.0 0.0 collective-permute-done.1.one
  32.0 11.4 %collective-permute-done.2.two = bf16[144,2560]{1,0:T(8,128)(2,1)S(1)} collective-permute-done((bf16[144,2560]{1,0:T(8,128)(2,1)S(1)}, bf16[144,2560]{1,0:T(8,128)(2,1)S(1)}, u32[]{:S(2)}, u32[]{:S(2)}) %collective-permute-start.2) | collective-permute-done | bytes 737312 | tf_op jit(solution)/shard_map/ppermute | solution.py:358
  43.4 2.8 %back.1 = (bf16[256,2560]{1,0:T(8,128)(2,1)}, bf16[4,4,80,256]{3,2,1,0:T(8,128)(2,1)S(1)}, bf16[4,80,256]{2,1,0:T(8,128)(2,1)S(1)}, bf16[4,80,256]{2,1,0:T(8,128...) custom-call(f32[256,2560]{1,0:T(8,128)S(1)} %get-tuple-element.39.local, ...), custom_call_target="tpu_custom_call" | custom-call | tf_op jit(solution)/shard_map/back/pallas_call | solution.py:469
  46.2 0.1 collective-permute-start.3
  46.3 1.7 %collective-permute-start.4 = (bf16[4,80,256]{2,1,0:T(8,128)(2,1)S(1)}, bf16[4,80,256]{2,1,0:T(8,128)(2,1)S(1)}, u32[]{:S(2)}, u32[]{:S(2)}) collective-permute-start(bf16[4,80,256]{2,1,0:T(8,128)(2,1)S(1)} %get-tuple-element.46), channel_id=1, source_target_pairs={{0,32},{4,12},{8,40},{12,20},{16,48},{20,28},{24,56},{28,4},{32,64... | collective-permute-start | bytes 491528 | tf_op jit(solution)/shard_map/ppermute | solution.py:369
  48.0 0.4 collective-permute-done.3.got
  48.4 3.2 %collective-permute-start.5 = (bf16[4,80,256]{2,1,0:T(8,128)(2,1)S(1)}, bf16[4,80,256]{2,1,0:T(8,128)(2,1)S(1)}, u32[]{:S(2)}, u32[]{:S(2)}) collective-permute-start(bf16[4,80,256]{2,1,0:T(8,128)(2,1)S(1)} %get-tuple-element.47), channel_id=1, source_target_pairs={{0,64},{4,20},{8,72},{12,28},{16,80},{20,4},{24,88},{28,12},{32,96... | collective-permute-start | bytes 491528 | tf_op jit(solution)/shard_map/ppermute | solution.py:369
  51.6 0.0 collective-permute-done.10.rest_2_.c3
  51.6 1.1 %collective-permute-start.6 = (bf16[4,80,256]{2,1,0:T(8,128)(2,1)S(1)}, bf16[4,80,256]{2,1,0:T(8,128)(2,1)S(1)}, u32[]{:S(2)}, u32[]{:S(2)}) collective-permute-start(bf16[4,80,256]{2,1,0:T(8,128)(2,1)S(1)} %get-tuple-element.48), channel_id=1, source_target_pairs={{0,96},{4,28},{8,104},{12,4},{16,112},{20,12},{24,120},{28,20},{32... | collective-permute-start | bytes 491528 | tf_op jit(solution)/shard_map/ppermute | solution.py:369
  52.7 0.0 collective-permute-done.8.rest_0_.c1
  52.7 0.0 collective-permute-done.9.rest_1_.c2
  52.7 1.0 %collective-permute-start.11 = (bf16[4,80,256]{2,1,0:T(8,128)(2,1)S(1)}, bf16[4,80,256]{2,1,0:T(8,128)(2,1)S(1)}, u32[]{:S(2)}, u32[]{:S(2)}) collective-permute-start(bf16[4,80,256]{2,1,0:T(8,128)(2,1)S(1)} %get-tuple-element.49), channel_id=1, source_target_pairs={{0,32},{4,12},{8,40},{12,20},{16,48},{20,28},{24,56},{28,4},{32,64... | collective-permute-start | bytes 491528 | tf_op jit(solution)/shard_map/ppermute | solution.py:369
  53.8 0.8 collective-permute-start.12
  54.6 0.0 collective-permute-done.4.m1
  54.6 2.5 %collective-permute-start.13 = (bf16[4,80,256]{2,1,0:T(8,128)(2,1)S(1)}, bf16[4,80,256]{2,1,0:T(8,128)(2,1)S(1)}, u32[]{:S(2)}, u32[]{:S(2)}) collective-permute-start(bf16[4,80,256]{2,1,0:T(8,128)(2,1)S(1)} %get-tuple-element.51), channel_id=1, source_target_pairs={{0,96},{4,28},{8,104},{12,4},{16,112},{20,12},{24,120},{28,20},{32... | collective-permute-start | bytes 491528 | tf_op jit(solution)/shard_map/ppermute | solution.py:369
  57.1 0.0 collective-permute-done.5.m2
  57.1 0.2 collective-permute-done.6.m3
  57.3 3.7 %collective-permute-done.11.r1 = bf16[4,80,256]{2,1,0:T(8,128)(2,1)S(1)} collective-permute-done((bf16[4,80,256]{2,1,0:T(8,128)(2,1)S(1)}, bf16[4,80,256]{2,1,0:T(8,128)(2,1)S(1)}, u32[]{:S(2)}, u32[]{:S(2)}) %collective-permute-start.11) | collective-permute-done | bytes 163872 | tf_op jit(solution)/shard_map/ppermute | solution.py:369
  61.1 0.0 collective-permute-done.12.r2
  61.1 0.9 %collective-permute-done.13.r3 = bf16[4,80,256]{2,1,0:T(8,128)(2,1)S(1)} collective-permute-done((bf16[4,80,256]{2,1,0:T(8,128)(2,1)S(1)}, bf16[4,80,256]{2,1,0:T(8,128)(2,1)S(1)}, u32[]{:S(2)}, u32[]{:S(2)}) %collective-permute-start.13) | collective-permute-done | bytes 163872 | tf_op jit(solution)/shard_map/ppermute | solution.py:369
  61.9 2.0 %grad.1 = bf16[16,200,128]{2,1,0:T(8,128)(2,1)S(1)} custom-call(bf16[4,80,256]{2,1,0:T(8,128)(2,1)S(1)} %get-tuple-element.44.m0, bf16[4,4,80,256]{3,2,1,0:T(8,128)(2,1)S(1)} %collective-permute-done.3.got, bf16[4,80,256]{2,1,0:T(8,128)(2,1)S(1)} %collective-permute-done.4.m1, bf16[4,80,256]{2,1,0:T(8,128)(2,1)S(1)} %collective-permute-done.5.m2, ...), custom_call_target="tpu_custom_call" | custom-call | flops 2000000000 | bytes 8000000 | tf_op jit(solution)/shard_map/grad/pallas_call | solution.py:489
  63.9 20.0 %all_to_all.5.pieces = bf16[16,200,128]{2,1,0:T(8,128)(2,1)S(1)} all-to-all(bf16[16,200,128]{2,1,0:T(8,128)(2,1)S(1)} %grad.1), channel_id=1, replica_groups={{0,1,2,3,8,9,10,11,16,17,18,19,24,25,26,27},{32,33,34,35,40,41,42,43,48..., dimensions={0} | all-to-all | bytes 1638400 | tf_op jit(solution)/shard_map/all_to_all | solution.py:498
  84.0 0.8 total.1
  (14 shorter events, 0.1 us)
Async XLA Ops:
  0.6 3.8 %copy-start.6 = (s32[1,256]{1,0:T(1,128)S(1)}, s32[1,256]{1,0:T(1,128)}, u32[]{:S(2)}) copy-start(s32[1,256]{1,0:T(1,128)} %docs.9) | copy-start | bytes 3076
  0.6 3.8 %copy-start.8 = (f32[1,40,256]{2,1,0:T(8,128)S(1)}, f32[1,40,256]{2,1,0:T(8,128)}, u32[]{:S(2)}) copy-start(f32[1,40,256]{2,1,0:T(8,128)} %param.13) | copy-start | bytes 122884
  0.7 3.8 %copy-start.9 = (f32[40]{0:T(128)S(1)}, f32[40]{0:T(128)}, u32[]{:S(2)}) copy-start(f32[40]{0:T(128)} %param.14) | copy-start | bytes 484
  0.7 3.8 %copy-start.10 = (f32[40]{0:T(128)S(1)}, f32[40]{0:T(128)}, u32[]{:S(2)}) copy-start(f32[40]{0:T(128)} %param.15) | copy-start | bytes 484
  0.7 14.4 %collective-permute-start.7 = (bf16[256,1280]{1,0:T(8,128)(2,1)}, bf16[256,1280]{1,0:T(8,128)(2,1)S(1)}, u32[]{:S(2)}, u32[]{:S(2)}) collective-permute-start(bf16[256,1280]{1,0:T(8,128)(2,1)} %bitcast.12), channel_id=1, source_target_pairs={{0,4},{4,0},{1,5},{5,1},{2,6},{6,2},{3,7},{7,3},{8,12},{12,8},{9,1... | collective-permute-start | bytes 1966088 | tf_op jit(solution)/shard_map/ppermute | solution.py:382
  2.4 6.8 %collective-permute-start = (bf16[8,2944]{1,0:T(8,128)(2,1)}, bf16[8,2944]{1,0:T(8,128)(2,1)S(1)}, u32[]{:S(2)}, u32[]{:S(2)}) collective-permute-start(bf16[8,2944]{1,0:T(8,128)(2,1)} %edge.1), channel_id=1, source_target_pairs={{0,1},{1,2},{2,3},{3,0},{4,5},{5,6},{6,7},{7,4},{8,9},{9,10},{10,1... | collective-permute-start | bytes 141320 | tf_op jit(solution)/shard_map/ppermute | solution.py:358
  4.5 1.4 %copy-start = (bf16[1,256,2816]{2,1,0:T(8,128)(2,1)S(1)}, bf16[1,256,2816]{2,1,0:T(8,128)(2,1)}, u32[]{:S(2)}) copy-start(bf16[1,256,2816]{2,1,0:T(8,128)(2,1)} %param.11) | copy-start | bytes 4325380
  4.5 1.4 %copy-start.3 = (f32[4,2816]{1,0:T(4,128)S(1)}, f32[4,2816]{1,0:T(4,128)}, u32[]{:S(2)}) copy-start(f32[4,2816]{1,0:T(4,128)} %w.3) | copy-start | bytes 135172
  4.5 1.3 %copy-start.5 = (f32[2816]{0:T(1024)S(1)}, f32[2816]{0:T(1024)}, u32[]{:S(2)}) copy-start(f32[2816]{0:T(1024)} %cb.3) | copy-start | bytes 33796
  9.1 6.0 %copy-start.2 = (bf16[1,256,1280]{2,1,0:T(8,128)(2,1)S(1)}, bf16[1,256,1280]{2,1,0:T(8,128)(2,1)}, u32[]{:S(2)}) copy-start(bf16[1,256,1280]{2,1,0:T(8,128)(2,1)} %param.21) | copy-start | bytes 1966084
  9.7 22.2 %collective-permute-start.1 = (bf16[144,2560]{1,0:T(8,128)(2,1)S(1)}, bf16[144,2560]{1,0:T(8,128)(2,1)S(1)}, u32[]{:S(2)}, u32[]{:S(2)}) collective-permute-start(bf16[144,2560]{1,0:T(8,128)(2,1)S(1)} %get-tuple-element.42), channel_id=1, source_target_pairs={{0,1},{1,2},{2,3},{3,0},{4,5},{5,6},{6,7},{7,4},{8,9},{9,10},{10,1... | collective-permute-start | bytes 2211848 | tf_op jit(solution)/shard_map/ppermute | solution.py:358
  11.5 32.0 %collective-permute-start.2 = (bf16[144,2560]{1,0:T(8,128)(2,1)S(1)}, bf16[144,2560]{1,0:T(8,128)(2,1)S(1)}, u32[]{:S(2)}, u32[]{:S(2)}) collective-permute-start(bf16[144,2560]{1,0:T(8,128)(2,1)S(1)} %get-tuple-element.42), channel_id=1, source_target_pairs={{0,2},{1,3},{4,6},{5,7},{8,10},{9,11},{12,14},{13,15},{16,18},{17,... | collective-permute-start | bytes 2211848 | tf_op jit(solution)/shard_map/ppermute | solution.py:358
  15.1 5.4 %copy-start.7 = (f32[40]{0:T(128)S(1)}, f32[40]{0:T(128)}, u32[]{:S(2)}) copy-start(f32[40]{0:T(128)} %param.16) | copy-start | bytes 484
  15.2 8.6 %copy-start.1 = (bf16[1,256,2560]{2,1,0:T(8,128)(2,1)S(1)}, bf16[1,256,2560]{2,1,0:T(8,128)(2,1)}, u32[]{:S(2)}) copy-start(bf16[1,256,2560]{2,1,0:T(8,128)(2,1)} %param.12) | copy-start | bytes 3932164
  15.3 36.4 %collective-permute-start.10 = (bf16[2,256,1280]{2,1,0:T(8,128)(2,1)S(1)}, bf16[2,256,1280]{2,1,0:T(8,128)(2,1)S(1)}, u32[]{:S(2)}, u32[]{:S(2)}) collective-permute-start(bf16[2,256,1280]{2,1,0:T(8,128)(2,1)S(1)} %stack.1.c0), channel_id=1, source_target_pairs={{0,96},{4,28},{8,104},{12,4},{16,112},{20,12},{24,120},{28,20},{32... | collective-permute-start | bytes 3932168 | tf_op jit(solution)/shard_map/ppermute | solution.py:369
  18.3 34.3 %collective-permute-start.8 = (bf16[2,256,1280]{2,1,0:T(8,128)(2,1)S(1)}, bf16[2,256,1280]{2,1,0:T(8,128)(2,1)S(1)}, u32[]{:S(2)}, u32[]{:S(2)}) collective-permute-start(bf16[2,256,1280]{2,1,0:T(8,128)(2,1)S(1)} %stack.1.c0), channel_id=1, source_target_pairs={{0,32},{4,12},{8,40},{12,20},{16,48},{20,28},{24,56},{28,4},{32,64... | collective-permute-start | bytes 3932168 | tf_op jit(solution)/shard_map/ppermute | solution.py:369
  18.3 34.3 %collective-permute-start.9 = (bf16[2,256,1280]{2,1,0:T(8,128)(2,1)S(1)}, bf16[2,256,1280]{2,1,0:T(8,128)(2,1)S(1)}, u32[]{:S(2)}, u32[]{:S(2)}) collective-permute-start(bf16[2,256,1280]{2,1,0:T(8,128)(2,1)S(1)} %stack.1.c0), channel_id=1, source_target_pairs={{0,64},{4,20},{8,72},{12,28},{16,80},{20,4},{24,88},{28,12},{32,96... | collective-permute-start | bytes 3932168 | tf_op jit(solution)/shard_map/ppermute | solution.py:369
  23.8 19.6 %copy-start.4 = (f32[2560]{0:T(1024)S(1)}, f32[2560]{0:T(1024)}, u32[]{:S(2)}) copy-start(f32[2560]{0:T(1024)} %gain.1) | copy-start | bytes 30724
  46.2 2.2 %collective-permute-start.3 = (bf16[4,4,80,256]{3,2,1,0:T(8,128)(2,1)S(1)}, bf16[4,4,80,256]{3,2,1,0:T(8,128)(2,1)S(1)}, u32[]{:S(2)}, u32[]{:S(2)}) collective-permute-start(bf16[4,4,80,256]{3,2,1,0:T(8,128)(2,1)S(1)} %get-tuple-element.45), channel_id=1, source_target_pairs={{0,4},{4,0},{1,5},{5,1},{2,6},{6,2},{3,7},{7,3},{8,12},{12,8},{9,1... | collective-permute-start | bytes 1966088 | tf_op jit(solution)/shard_map/ppermute | solution.py:382
  46.3 8.2 %collective-permute-start.4 = (bf16[4,80,256]{2,1,0:T(8,128)(2,1)S(1)}, bf16[4,80,256]{2,1,0:T(8,128)(2,1)S(1)}, u32[]{:S(2)}, u32[]{:S(2)}) collective-permute-start(bf16[4,80,256]{2,1,0:T(8,128)(2,1)S(1)} %get-tuple-element.46), channel_id=1, source_target_pairs={{0,32},{4,12},{8,40},{12,20},{16,48},{20,28},{24,56},{28,4},{32,64... | collective-permute-start | bytes 491528 | tf_op jit(solution)/shard_map/ppermute | solution.py:369
  48.4 8.7 %collective-permute-start.5 = (bf16[4,80,256]{2,1,0:T(8,128)(2,1)S(1)}, bf16[4,80,256]{2,1,0:T(8,128)(2,1)S(1)}, u32[]{:S(2)}, u32[]{:S(2)}) collective-permute-start(bf16[4,80,256]{2,1,0:T(8,128)(2,1)S(1)} %get-tuple-element.47), channel_id=1, source_target_pairs={{0,64},{4,20},{8,72},{12,28},{16,80},{20,4},{24,88},{28,12},{32,96... | collective-permute-start | bytes 491528 | tf_op jit(solution)/shard_map/ppermute | solution.py:369
  51.6 5.7 %collective-permute-start.6 = (bf16[4,80,256]{2,1,0:T(8,128)(2,1)S(1)}, bf16[4,80,256]{2,1,0:T(8,128)(2,1)S(1)}, u32[]{:S(2)}, u32[]{:S(2)}) collective-permute-start(bf16[4,80,256]{2,1,0:T(8,128)(2,1)S(1)} %get-tuple-element.48), channel_id=1, source_target_pairs={{0,96},{4,28},{8,104},{12,4},{16,112},{20,12},{24,120},{28,20},{32... | collective-permute-start | bytes 491528 | tf_op jit(solution)/shard_map/ppermute | solution.py:369
  52.7 8.4 %collective-permute-start.11 = (bf16[4,80,256]{2,1,0:T(8,128)(2,1)S(1)}, bf16[4,80,256]{2,1,0:T(8,128)(2,1)S(1)}, u32[]{:S(2)}, u32[]{:S(2)}) collective-permute-start(bf16[4,80,256]{2,1,0:T(8,128)(2,1)S(1)} %get-tuple-element.49), channel_id=1, source_target_pairs={{0,32},{4,12},{8,40},{12,20},{16,48},{20,28},{24,56},{28,4},{32,64... | collective-permute-start | bytes 491528 | tf_op jit(solution)/shard_map/ppermute | solution.py:369
  53.8 7.3 %collective-permute-start.12 = (bf16[4,80,256]{2,1,0:T(8,128)(2,1)S(1)}, bf16[4,80,256]{2,1,0:T(8,128)(2,1)S(1)}, u32[]{:S(2)}, u32[]{:S(2)}) collective-permute-start(bf16[4,80,256]{2,1,0:T(8,128)(2,1)S(1)} %get-tuple-element.50), channel_id=1, source_target_pairs={{0,64},{4,20},{8,72},{12,28},{16,80},{20,4},{24,88},{28,12},{32,96... | collective-permute-start | bytes 491528 | tf_op jit(solution)/shard_map/ppermute | solution.py:369
  54.6 7.4 %collective-permute-start.13 = (bf16[4,80,256]{2,1,0:T(8,128)(2,1)S(1)}, bf16[4,80,256]{2,1,0:T(8,128)(2,1)S(1)}, u32[]{:S(2)}, u32[]{:S(2)}) collective-permute-start(bf16[4,80,256]{2,1,0:T(8,128)(2,1)S(1)} %get-tuple-element.51), channel_id=1, source_target_pairs={{0,96},{4,28},{8,104},{12,4},{16,112},{20,12},{24,120},{28,20},{32... | collective-permute-start | bytes 491528 | tf_op jit(solution)/shard_map/ppermute | solution.py:369
